TPU v7x, 32 devices: a whole 2x2x4 slice. The times are simulated.
32 devices in a mesh: dp: 8 (over z, x), mp: 4 (over y, core).
Axes of the slice: x: 2, y: 2, z: 4, core: 2. Of those that a mesh axis runs over, the one named last changes fastest.
Arguments:
- tokens: bfloat16 [8192, 768], P('dp'), may hold values from -6 to 6
- cotangent: bfloat16 [8192, 768], P('dp'), may hold values from -6 to 6
- doc_lengths: int32 [8, 4], P('dp'), may hold values from 0 to 1024, as said below
- outer_norms: float32 [4, 768], replicated
- attn_norm: float32 [2, 768], P(None, 'mp')
- ffn_norm: float32 [2, 3072], P(None, 'mp')
- w_qkv: float32 [4, 768, 576], P('mp', 'dp')
- left_qkv: float32 [4, 768, 768], P('mp', 'dp')
- right_qkv: float32 [4, 576, 576], P('mp', 'dp')
- left_root_qkv: float32 [4, 768, 768], P('mp', 'dp')
- right_root_qkv: float32 [4, 576, 576], P('mp')
- w_out: float32 [4, 192, 768], P('mp', 'dp')
- left_out: float32 [4, 192, 192], P('mp', 'dp')
- right_out: float32 [4, 768, 768], P('mp', 'dp')
- left_root_out: float32 [4, 192, 192], P('mp', 'dp')
- right_root_out: float32 [4, 768, 768], P('mp')
- w_up: float32 [4, 768, 768], P('mp', 'dp')
- left_up: float32 [4, 768, 768], P('mp', 'dp')
- right_up: float32 [4, 768, 768], P('mp', 'dp')
- left_root_up: float32 [4, 768, 768], P('mp', 'dp')
- right_root_up: float32 [4, 768, 768], P('mp')
- w_down: float32 [4, 768, 768], P('mp', 'dp')
- left_down: float32 [4, 768, 768], P('mp', 'dp')
- right_down: float32 [4, 768, 768], P('mp', 'dp')
- left_root_down: float32 [4, 768, 768], P('mp', 'dp')
- right_root_down: float32 [4, 768, 768], P('mp')
Outputs:
- block_out: bfloat16 [8192, 768], P('dp')
- grad_tokens: bfloat16 [8192, 768], P('dp')
- grad_outer: float32 [4, 768], replicated
- grad_attn_norm: float32 [2, 768], P(None, 'mp')
- grad_ffn_norm: float32 [2, 3072], P(None, 'mp')
- new_outer: float32 [4, 768], replicated
- new_attn_norm: float32 [2, 768], P(None, 'mp')
- new_ffn_norm: float32 [2, 3072], P(None, 'mp')
- grad_qkv: float32 [4, 768, 576], P('mp')
- new_left_qkv: float32 [4, 768, 768], P('mp', 'dp')
- new_right_qkv: float32 [4, 576, 576], P('mp', 'dp')
- new_w_qkv: float32 [4, 768, 576], P('mp', 'dp')
- copy_qkv: bfloat16 [4, 768, 576], P('mp', 'dp')
- grad_out: float32 [4, 192, 768], P('mp')
- new_left_out: float32 [4, 192, 192], P('mp', 'dp')
- new_right_out: float32 [4, 768, 768], P('mp', 'dp')
- new_w_out: float32 [4, 192, 768], P('mp', 'dp')
- copy_out: bfloat16 [4, 192, 768], P('mp', 'dp')
- grad_up: float32 [4, 768, 768], P('mp')
- new_left_up: float32 [4, 768, 768], P('mp', 'dp')
- new_right_up: float32 [4, 768, 768], P('mp', 'dp')
- new_w_up: float32 [4, 768, 768], P('mp', 'dp')
- copy_up: bfloat16 [4, 768, 768], P('mp', 'dp')
- grad_down: float32 [4, 768, 768], P('mp')
- new_left_down: float32 [4, 768, 768], P('mp', 'dp')
- new_right_down: float32 [4, 768, 768], P('mp', 'dp')
- new_w_down: float32 [4, 768, 768], P('mp', 'dp')
- copy_down: bfloat16 [4, 768, 768], P('mp', 'dp')
Inputs may be any that keep to these rules, and one draw needn't show every extreme that they name: `doc_lengths`: each row sums to 1024: either one document of 1024 tokens followed by zeros, or 4 documents of 128 to 384 tokens; both kinds of rows occur in every draw.
All inputs are finite; a program needn't handle non-finite values.
Results may differ from a plain program's by a relative error of at most 0.017.
The roundings to bfloat16 on the way count: a program that leaves them out, or rounds other values in their place, can miss the bound.
Values may be sent and summed in bfloat16 or wider, within the bound.
No kernel may reach another device: no remote copies, remote signals or barrier semaphores. Data moves between devices by JAX's collectives and lax.ppermute only.
A program may use at most 128 MiB of HBM per device.

v0:
```python
from functools import partial
import math

import jax
import jax.numpy as jnp
from jax import lax
from jax.sharding import PartitionSpec as P

HD = 64


EPS = 1e-05
DECAY = 0.5
MAT_RATE = 0.5
VEC_RATE = 0.05
UNIT_RATE = 0.3
HIGH = lax.Precision.HIGHEST


def outer_norm(values_in, gain_row, bias_row):
    center = jnp.mean(values_in, -1, keepdims=True)
    offset = values_in - center
    factor = lax.rsqrt(jnp.mean(offset * offset, -1, keepdims=True) + EPS)
    normed = offset * factor
    return (normed * gain_row + bias_row, normed, factor)


def inner_norm(values_in, gain_row, bias_row, full_width):
    center = lax.psum(jnp.sum(values_in, -1), "mp")[:, None] / full_width
    offset = values_in - center
    spread = lax.psum(jnp.sum(offset * offset, -1), "mp")[:, None] / full_width
    factor = lax.rsqrt(spread + EPS)
    normed = offset * factor
    return (normed * gain_row + bias_row, normed, factor)


def norm_back(incoming, normed, factor, gain_row, full_width, shared):
    weighted = incoming * gain_row
    partial_sums = (jnp.sum(weighted, -1), jnp.sum(weighted * normed, -1))
    if shared:
        sum_plain, sum_normed = lax.psum((partial_sums[0], partial_sums[1]), "mp")
    else:
        sum_plain, sum_normed = partial_sums
    result = factor * (
        weighted - sum_plain[:, None] / full_width - normed * (sum_normed[:, None] / full_width)
    )
    return (result, jnp.stack([jnp.sum(incoming * normed, 0), jnp.sum(incoming, 0)]))


def branch_sum(part_out):
    return lax.psum(part_out, "mp")


def input_back(part_grad):
    return lax.psum(part_grad, "mp")


def shampoo_rows(grad_sum, master, left_stat, right_stat, left_root, right_root, total_tokens):
    owner_place = lax.axis_index("dp")
    mean_grad = grad_sum / total_tokens
    height = master.shape[1]
    breadth = right_stat.shape[1]
    row_part = lax.dynamic_slice_in_dim(mean_grad, owner_place * height, height, 0)
    col_part = lax.dynamic_slice_in_dim(mean_grad, owner_place * breadth, breadth, 1)
    new_left = DECAY * left_stat[0] + (1.0 - DECAY) * jnp.dot(row_part, mean_grad.T, precision=HIGH)
    new_right = DECAY * right_stat[0] + (1.0 - DECAY) * jnp.dot(
        col_part.T, mean_grad, precision=HIGH
    )
    left_part = jnp.dot(left_root[0], mean_grad, precision=HIGH)
    step_size = jnp.dot(left_part, right_root[0], precision=HIGH)
    new_master = master[0] - MAT_RATE * step_size
    return (
        new_left[None],
        new_right[None],
        new_master[None],
        new_master.astype(jnp.bfloat16)[None],
    )


def body(
    tokens,
    cotangent,
    doc_lengths,
    outer_norms,
    attn_norm,
    ffn_norm,
    w_qkv,
    left_qkv,
    right_qkv,
    left_root_qkv,
    right_root_qkv,
    w_out,
    left_out,
    right_out,
    left_root_out,
    right_root_out,
    w_up,
    left_up,
    right_up,
    left_root_up,
    right_root_up,
    w_down,
    left_down,
    right_down,
    left_root_down,
    right_root_down,
):
    row_count = tokens.shape[0]
    total_tokens = row_count * lax.axis_size("dp")
    mp_count = lax.axis_size("mp")
    qkv_whole, out_whole, up_whole, down_whole = (
        lax.all_gather(w_qkv.astype(jnp.bfloat16), "dp", axis=1, tiled=True),
        lax.all_gather(w_out.astype(jnp.bfloat16), "dp", axis=1, tiled=True),
        lax.all_gather(w_up.astype(jnp.bfloat16), "dp", axis=1, tiled=True),
        lax.all_gather(w_down.astype(jnp.bfloat16), "dp", axis=1, tiled=True),
    )
    qkv_mat = qkv_whole[0]
    out_mat = out_whole[0]
    up_mat = up_whole[0]
    down_mat = down_whole[0]
    head_width = out_mat.shape[0]
    head_count = head_width // HD
    unit_width = up_mat.shape[1]
    inv_root = HD ** (-0.5)
    ends = jnp.cumsum(doc_lengths[0])
    places = jnp.arange(row_count, dtype=jnp.int32)
    member = jnp.sum((places[:, None] >= ends[None, :]).astype(jnp.int32), axis=1)
    visible = (member[:, None] == member[None, :]) & (places[None, :] <= places[:, None])
    inputs = tokens.astype(jnp.float32)
    normed_a, a_hat, a_factor = outer_norm(inputs, outer_norms[0], outer_norms[1])
    a_low = normed_a.astype(jnp.bfloat16)
    qkv_low = jnp.dot(a_low, qkv_mat, preferred_element_type=jnp.float32).astype(jnp.bfloat16)
    query_rows = qkv_low[:, :head_width].reshape(row_count, head_count, HD)
    key_rows = qkv_low[:, head_width : 2 * head_width].reshape(row_count, head_count, HD)
    value_rows = qkv_low[:, 2 * head_width :].reshape(row_count, head_count, HD)

    def masked_scores(query_in, key_in):
        raw_scores = (
            jnp.einsum("qhe,khe->hqk", query_in, key_in, preferred_element_type=jnp.float32)
            * inv_root
        )
        return jnp.where(visible[None], raw_scores, -1e30)

    scores = masked_scores(query_rows, key_rows)
    top_score = jnp.max(scores, -1, keepdims=True)
    log_total = top_score + jnp.log(jnp.sum(jnp.exp(scores - top_score), -1, keepdims=True))
    probs_low = jnp.exp(scores - log_total).astype(jnp.bfloat16)
    attended = jnp.einsum(
        "hqk,khe->qhe", probs_low, value_rows, preferred_element_type=jnp.float32
    ).reshape(row_count, head_width)
    normed_y, y_hat, y_factor = inner_norm(
        attended, attn_norm[0], attn_norm[1], head_width * mp_count
    )
    y_low = normed_y.astype(jnp.bfloat16)
    hidden = inputs + branch_sum(jnp.dot(y_low, out_mat, preferred_element_type=jnp.float32))
    normed_c, c_hat, c_factor = outer_norm(hidden, outer_norms[2], outer_norms[3])
    c_low = normed_c.astype(jnp.bfloat16)
    up_vals = jnp.dot(c_low, up_mat, preferred_element_type=jnp.float32)
    activated = jax.nn.gelu(up_vals, approximate=True)
    normed_w, w_hat, w_factor = inner_norm(
        activated, ffn_norm[0], ffn_norm[1], unit_width * mp_count
    )
    w_low = normed_w.astype(jnp.bfloat16)
    block_out = (
        hidden + branch_sum(jnp.dot(w_low, down_mat, preferred_element_type=jnp.float32))
    ).astype(jnp.bfloat16)
    grad_down = jnp.einsum("tf,td->fd", w_low, cotangent, preferred_element_type=jnp.float32)
    grad_w = jnp.einsum("td,fd->tf", cotangent, down_mat, preferred_element_type=jnp.float32)
    grad_z, ffn_grads = norm_back(grad_w, w_hat, w_factor, ffn_norm[0], unit_width * mp_count, True)
    gelu_out, gelu_back = jax.vjp(partial(jax.nn.gelu, approximate=True), up_vals)
    grad_u = gelu_back(grad_z)[0].astype(jnp.bfloat16)
    grad_up = jnp.einsum("td,tf->df", c_low, grad_u, preferred_element_type=jnp.float32)
    grad_c = input_back(jnp.einsum("tf,df->td", grad_u, up_mat, preferred_element_type=jnp.float32))
    grad_h_norm, outer_late = norm_back(
        grad_c, c_hat, c_factor, outer_norms[2], grad_c.shape[-1], False
    )
    grad_hidden = cotangent.astype(jnp.float32) + grad_h_norm
    hidden_low = grad_hidden.astype(jnp.bfloat16)
    grad_out = jnp.einsum("ti,td->id", y_low, hidden_low, preferred_element_type=jnp.float32)
    grad_y = jnp.einsum("td,id->ti", hidden_low, out_mat, preferred_element_type=jnp.float32)
    grad_att, attn_grads = norm_back(
        grad_y, y_hat, y_factor, attn_norm[0], head_width * mp_count, True
    )
    grad_att_low = grad_att.astype(jnp.bfloat16).reshape(row_count, head_count, HD)
    probs_again = jnp.exp(masked_scores(query_rows, key_rows) - log_total)
    probs_again_low = probs_again.astype(jnp.bfloat16)
    grad_probs = jnp.einsum(
        "qhe,khe->hqk", grad_att_low, value_rows, preferred_element_type=jnp.float32
    )
    grad_scores = (
        probs_again * (grad_probs - jnp.sum(probs_again * grad_probs, -1, keepdims=True))
    ).astype(jnp.bfloat16)
    grad_query = (
        jnp.einsum("hqk,khe->qhe", grad_scores, key_rows, preferred_element_type=jnp.float32)
        * inv_root
    )
    grad_key = (
        jnp.einsum("hqk,qhe->khe", grad_scores, query_rows, preferred_element_type=jnp.float32)
        * inv_root
    )
    grad_value = jnp.einsum(
        "hqk,qhe->khe", probs_again_low, grad_att_low, preferred_element_type=jnp.float32
    )
    grad_qkv_low = jnp.concatenate(
        [
            grad_query.reshape(row_count, head_width),
            grad_key.reshape(row_count, head_width),
            grad_value.reshape(row_count, head_width),
        ],
        axis=1,
    ).astype(jnp.bfloat16)
    grad_qkv = jnp.einsum("td,tc->dc", a_low, grad_qkv_low, preferred_element_type=jnp.float32)
    grad_a = input_back(
        jnp.einsum("tc,dc->td", grad_qkv_low, qkv_mat, preferred_element_type=jnp.float32)
    )
    grad_x_norm, outer_early = norm_back(
        grad_a, a_hat, a_factor, outer_norms[0], grad_a.shape[-1], False
    )
    grad_tokens = (grad_hidden + grad_x_norm).astype(jnp.bfloat16)
    outer_grads = jnp.concatenate([outer_early, outer_late], axis=0)
    grad_qkv, grad_out, grad_up, grad_down, attn_grads, ffn_grads, outer_grads = lax.psum(
        (grad_qkv, grad_out, grad_up, grad_down, attn_grads, ffn_grads, outer_grads), "dp"
    )
    factor = VEC_RATE / math.sqrt(total_tokens)
    unit_factor = UNIT_RATE / math.sqrt(total_tokens)
    qkv_left, qkv_right, qkv_new, qkv_copy = shampoo_rows(
        grad_qkv, w_qkv, left_qkv, right_qkv, left_root_qkv, right_root_qkv, total_tokens
    )
    out_left, out_right, out_new, out_copy = shampoo_rows(
        grad_out, w_out, left_out, right_out, left_root_out, right_root_out, total_tokens
    )
    up_left, up_right, up_new, up_copy = shampoo_rows(
        grad_up, w_up, left_up, right_up, left_root_up, right_root_up, total_tokens
    )
    down_left, down_right, down_new, down_copy = shampoo_rows(
        grad_down, w_down, left_down, right_down, left_root_down, right_root_down, total_tokens
    )
    return (
        block_out,
        grad_tokens,
        outer_grads,
        attn_grads,
        ffn_grads,
        outer_norms - factor * outer_grads,
        attn_norm - factor * attn_grads,
        ffn_norm - unit_factor * ffn_grads,
        grad_qkv[None],
        qkv_left,
        qkv_right,
        qkv_new,
        qkv_copy,
        grad_out[None],
        out_left,
        out_right,
        out_new,
        out_copy,
        grad_up[None],
        up_left,
        up_right,
        up_new,
        up_copy,
        grad_down[None],
        down_left,
        down_right,
        down_new,
        down_copy,
    )


def solution(mesh):
    return jax.shard_map(
        body,
        mesh=mesh,
        in_specs=(
            P("dp", None),
            P("dp", None),
            P("dp", None),
            P(),
            P(None, "mp"),
            P(None, "mp"),
            P("mp", "dp", None),
            P("mp", "dp", None),
            P("mp", "dp", None),
            P("mp", "dp", None),
            P("mp", None, None),
            P("mp", "dp", None),
            P("mp", "dp", None),
            P("mp", "dp", None),
            P("mp", "dp", None),
            P("mp", None, None),
            P("mp", "dp", None),
            P("mp", "dp", None),
            P("mp", "dp", None),
            P("mp", "dp", None),
            P("mp", None, None),
            P("mp", "dp", None),
            P("mp", "dp", None),
            P("mp", "dp", None),
            P("mp", "dp", None),
            P("mp", None, None),
        ),
        out_specs=(
            P("dp", None),
            P("dp", None),
            P(),
            P(None, "mp"),
            P(None, "mp"),
            P(),
            P(None, "mp"),
            P(None, "mp"),
            P("mp", None, None),
            P("mp", "dp", None),
            P("mp", "dp", None),
            P("mp", "dp", None),
            P("mp", "dp", None),
            P("mp", None, None),
            P("mp", "dp", None),
            P("mp", "dp", None),
            P("mp", "dp", None),
            P("mp", "dp", None),
            P("mp", None, None),
            P("mp", "dp", None),
            P("mp", "dp", None),
            P("mp", "dp", None),
            P("mp", "dp", None),
            P("mp", None, None),
            P("mp", "dp", None),
            P("mp", "dp", None),
            P("mp", "dp", None),
            P("mp", "dp", None),
        ),
        check_vma=False,
    )
```

profile of v0, /device:TPU:0, one launch (start us, length us, event | category | flops | bytes accessed | tf_op | source)
XLA Modules:
  0.0 786.1 jit_solution(8546946648870703262)
XLA Ops:
  12.1 34.4 %all_gather.12 = bf16[1,768,576]{2,1,0:T(8,128)(2,1)S(1)} all-gather(bf16[1,96,576]{2,1,0:T(8,128)(2,1)S(1)} %convert_element_type.78), channel_id=1, replica_groups=mesh['dp'=8,'mp'=4] {'dp'}, dimensions={1}, use_global_device_ids=true | all-gather | bytes 995328 | tf_op jit(solution)/shard_map/all_gather | solution.py:112
  49.9 8.2 %fusion = (f32[3,1024]{1,0:T(4,128)S(1)}, f32[3,1024,1024]{1,2,0:T(8,128)}) fusion(pred[1024,1024]{0,1:T(8,128)(4,1)S(1)} %fusion.2, bf16[1024,3,64]{0,2,1:T(8,128)(2,1)} %bitcast.192, bf16[1024,3,64]{0,2,1:T(8,128)(2,1)} %bitcast.194), kind=kOutput, calls=%fused_computation.5 | convolution fusion | flops 412087296 | bytes 14430208 | tf_op jit(solution)/shard_map/qhe,khe->hqk/dot_general | solution.py:139
  58.1 7.4 exponential_reduce_fusion
  65.5 7.3 fusion.131
  72.9 5.6 psum.133
  79.7 6.7 psum.134
  87.2 31.3 %all_gather.13 = bf16[1,192,768]{2,1,0:T(8,128)(2,1)S(1)} all-gather(bf16[1,24,768]{2,1,0:T(8,128)(2,1)S(1)} %convert_element_type.84), channel_id=1, replica_groups=mesh['dp'=8,'mp'=4] {'dp'}, dimensions={1}, use_global_device_ids=true | all-gather | bytes 331776 | tf_op jit(solution)/shard_map/all_gather | solution.py:113
  119.9 2.3 fusion.103
  127.1 64.2 %all-reduce.10.cloned.1.call-done = f32[1024,768]{1,0:T(8,128)} async-done(((f32[1024,768]{1,0:T(8,128)}), f32[1024,768]{1,0:T(8,128)}) %all-reduce.10.cloned.1.call-update) | async-done | bytes 3145744 | tf_op jit(solution)/shard_map/psum | solution.py:51
  191.3 2.7 fusion.129
  197.5 5.6 fusion.128
  203.1 6.1 psum.136
  209.2 3.1 multiply_reduce_fusion.5
  212.3 6.3 psum.137
  219.2 5.4 fusion.132
  224.7 3.6 copy.61
  228.3 4.6 multiply_reduce_fusion.1
  232.9 7.7 all-reduce.3
  241.2 6.5 fusion.24
  248.9 3.1 fusion.39
  252.1 2.1 fusion.86
  254.2 4.9 fusion.37
  259.1 61.8 %all-reduce.12.cloned.1.call-done = f32[1024,768]{1,0:T(8,128)} async-done(((f32[1024,768]{1,0:T(8,128)}), f32[1024,768]{1,0:T(8,128)}) %all-reduce.12.cloned.1.call-update) | async-done | bytes 3145744 | tf_op jit(solution)/shard_map/psum | solution.py:55
  320.9 4.3 multiply_reduce_fusion.2
  325.6 2.5 multiply_add_fusion
  329.8 2.3 multiply_reduce_fusion.10
  332.1 6.1 all-reduce.2
  339.8 11.2 %multiply_reduce_fusion = (f32[3,1024]{1,0:T(4,128)S(1)}, f32[3,1024,1024]{1,2,0:T(8,128)}) fusion(f32[3,1024,1024]{1,2,0:T(8,128)} %get-tuple-element.74, f32[3,1024]{1,0:T(4,128)S(1)} %log_add_fusion, pred[1024,1024]{0,1:T(8,128)(4,1)S(1)} %fusion.2, bf16[1024,3,64]{0,2,1:T(8,128)(2,1)S(1)} %bitcast.198, bf16[1024,3,64]{0,2,1:T(8,128)(2,1)} %bitcast.196), kind=kOutput, calls=%fused_computation.1 | convolution fusion | flops 418378752 | bytes 27025408 | tf_op jit(solution)/shard_map/qhe,khe->hqk/dot_general | solution.py:187
  352.6 7.0 multiply_convert_fusion
  362.9 3.8 convolution_convert_fusion.1
  367.4 3.2 fusion.83
  370.9 4.9 fusion.133
  375.8 2.8 fusion.134
  380.9 2.6 fusion.91
  384.3 106.9 %all-reduce.16.cloned.1.call-done = (f32[1024,768]{1,0:T(8,128)}, f32[1024,768]{1,0:T(8,128)}) async-done(((f32[1024,768]{1,0:T(8,128)}, f32[1024,768]{1,0:T(8,128)}), (f32[1024,768]{1,0:T(8,128)}, f32[1024,768]{1,0:T(8,128)})) %all-reduce.16.cloned.1.call-update) | async-done | bytes 6291472 | tf_op jit(solution)/shard_map/psum | solution.py:51
  491.1 3.2 fusion.16
  494.4 39.0 %all-reduce = (f32[4,768]{1,0:T(4,128)S(1)}, f32[2,192]{1,0:T(2,128)S(1)}, f32[2,768]{1,0:T(2,128)S(1)}) all-reduce(f32[4,768]{1,0:T(4,128)S(1)} %pad_maximum_fusion.3, f32[2,192]{1,0:T(2,128)S(1)} %pad_maximum_fusion.5, f32[2,768]{1,0:T(2,128)S(1)} %pad_maximum_fusion.4), channel_id=1, replica_groups=mesh['dp'=8,'mp'=4] {'dp'}, use_global_device_ids=true, to_apply=%region_37.38 | all-reduce | flops 4992 | bytes 39936 | tf_op jit(solution)/shard_map/psum | solution.py:221
  535.2 4.7 add_convert_fusion
  541.3 2.5 fusion.15
  543.8 189.3 %all-reduce.14.cloned.1.call-done = (f32[768,576]{0,1:T(8,128)}, f32[192,768]{1,0:T(8,128)}, f32[768,768]{1,0:T(8,128)}, f32[768,768]{1,0:T(8,128)}) async-done(((f32[768,576]{0,1:T(8,128)}, f32[192,768]{1,0:T(8,128)}, f32[768,768]{1,0:T(8,128)}, f32[768,768]{1,0:T(8,128)}), (f32[768,576]{0,1:T(8,128)}, f32[192,768]{1,0:T(8,128)}, f32[768,768]{1,0:T(8,128)}, ...) | async-done | bytes 7077904 | tf_op jit(solution)/shard_map/psum | solution.py:221
  736.2 3.1 fusion.52
  739.3 2.4 fusion.56
  741.7 3.1 fusion.54
  744.8 2.4 fusion.58
  747.4 3.8 fusion.96
  753.7 3.8 fusion.98
  766.8 2.3 fusion.66
  769.1 2.4 fusion.74
  (245 shorter events, 59.3 us)
Async XLA Ops:
  8.0 743.2 %copy-start = (f32[1,768,768]{2,1,0:T(8,128)S(1)}, f32[1,768,768]{2,1,0:T(8,128)}, u32[]{:S(2)}) copy-start(f32[1,768,768]{2,1,0:T(8,128)} %param.51) | copy-start | bytes 7077892
  8.1 183.2 %all-reduce.10.cloned.1.call-start = ((), (), s32[]{:S(2)}) async-start(), calls=%async_computation | async-start | bytes 6291456 | tf_op jit(solution)/shard_map/psum | solution.py:51
  8.1 38.4 %copy-start.6 = (bf16[1024,768]{1,0:T(8,128)(2,1)S(1)}, bf16[1024,768]{1,0:T(8,128)(2,1)}, u32[]{:S(2)}) copy-start(bf16[1024,768]{1,0:T(8,128)(2,1)} %param.26) | copy-start | bytes 4718596
  12.1 35.9 %copy-start.67 = (f32[768]{0:T(1024)}, f32[768]{0:T(1024)S(1)}, u32[]{:S(2)}) copy-start(f32[768]{0:T(1024)S(1)} %get-tuple-element.44) | copy-start | bytes 9220
  58.1 7.4 copy-start.23
  65.5 20.9 %copy-start.62 = (f32[2,192]{1,0:T(2,128)S(1)}, f32[2,192]{1,0:T(2,128)}, u32[]{:S(2)}) copy-start(f32[2,192]{1,0:T(2,128)} %param.30) | copy-start | bytes 4612
  65.5 21.6 %copy-start.49 = (f32[1,24,768]{2,1,0:T(8,128)S(1)}, f32[1,24,768]{2,1,0:T(8,128)}, u32[]{:S(2)}) copy-start(f32[1,24,768]{2,1,0:T(8,128)} %param.37) | copy-start | bytes 221188
  122.3 75.3 %all-gather.3.cloned.1.call-start = ((), (), s32[]{:S(2)}) async-start(), calls=%async_computation.1 | async-start | bytes 1327104 | tf_op jit(solution)/shard_map/all_gather | solution.py:114
  124.0 95.3 %all-gather.5.cloned.1.call-start = ((), (), s32[]{:S(2)}) async-start(), calls=%async_computation.2 | async-start | bytes 1327104 | tf_op jit(solution)/shard_map/all_gather | solution.py:115
  125.7 195.2 %all-reduce.12.cloned.1.call-start = ((), (), s32[]{:S(2)}) async-start(), calls=%async_computation.3 | async-start | bytes 6291456 | tf_op jit(solution)/shard_map/psum | solution.py:55
  241.2 7.7 copy-start.72
  252.0 239.1 %all-reduce.16.cloned.1.call-start = ((), (), s32[]{:S(2)}) async-start(), calls=%async_computation.5 | async-start | bytes 12582912 | tf_op jit(solution)/shard_map/psum | solution.py:51
  320.9 4.3 copy-start.2
  320.9 4.7 copy-start.13
  339.8 11.2 %slice-start = ((s8[12582912]{0:T(1024)(128)(4,1)}), s8[4194304]{0:T(1024)(128)(4,1)S(1)}, s32[]{:S(2)}) async-start(s8[12582912]{0:T(1024)(128)(4,1)} %bitcast.186), calls=%async_computation.6 | async-start | bytes 8388608
  339.8 11.2 %slice-start.1 = ((s8[12582912]{0:T(1024)(128)(4,1)}), s8[4194304]{0:T(1024)(128)(4,1)S(1)}, s32[]{:S(2)}) async-start(s8[12582912]{0:T(1024)(128)(4,1)} %bitcast.186), calls=%async_computation.7 | async-start | bytes 8388608
  339.8 12.7 %slice-start.2 = ((s8[12582912]{0:T(1024)(128)(4,1)}), s8[4194304]{0:T(1024)(128)(4,1)S(1)}, s32[]{:S(2)}) async-start(s8[12582912]{0:T(1024)(128)(4,1)} %bitcast.186), calls=%async_computation.8 | async-start | bytes 8388608
  352.6 7.0 copy-start.18
  360.8 5.8 copy-start.37
  362.8 4.5 copy-start.33
  370.6 362.6 %all-reduce.14.cloned.1.call-start = ((), (), s32[]{:S(2)}) async-start(), calls=%async_computation.4 | async-start | bytes 14155776 | tf_op jit(solution)/shard_map/psum | solution.py:221
  370.9 4.9 copy-start.24
  370.9 4.9 copy-start.25
  383.5 149.8 %copy-start.63 = (f32[2,192]{1,0:T(2,128)S(1)}, f32[2,192]{1,0:T(2,128)}, u32[]{:S(2)}) copy-start(f32[2,192]{1,0:T(2,128)} %param.30) | copy-start | bytes 4612
  383.5 150.4 %copy-start.55 = (f32[2,768]{1,0:T(2,128)S(1)}, f32[2,768]{1,0:T(2,128)}, u32[]{:S(2)}) copy-start(f32[2,768]{1,0:T(2,128)} %param.31) | copy-start | bytes 18436
  533.4 6.5 copy-start.61
  533.4 6.5 copy-start.64
  533.4 6.5 copy-start.71
  535.2 4.7 copy-start.5
  535.2 4.7 copy-start.8
  535.2 6.1 copy-start.12
  736.2 5.5 copy-start.43
  739.3 5.5 copy-start.44
  741.7 5.5 copy-start.11
  747.3 6.3 copy-start.10
  747.4 6.3 copy-start.46
  751.2 6.3 copy-start.21
  751.2 6.3 copy-start.29
  752.9 6.2 copy-start.30
  753.7 6.2 copy-start.47
  759.1 5.6 copy-start.31
  759.2 5.6 copy-start.22
  761.4 5.4 copy-start.48
  762.6 6.5 copy-start.36
  763.3 5.8 copy-start.52
  764.8 6.7 copy-start.51
  766.1 7.8 copy-start.50
  766.1 6.6 copy-start.54
  (37 other events, 90.7 us)
Sparse Core Ops, SparseCore 0:
  122.4 68.9 all-reduce.9
  252.2 68.7 all-reduce.11
  370.7 120.4 all-reduce.15
  496.6 236.5 all-reduce.13
Sparse Core Ops, SparseCore 1:
  125.5 41.8 all-gather.2
  170.0 39.8 all-gather.4
where the time goes:
time: 795 us; the launch traced here: 786 us
  waiting for transfers between devices  422 us (53%)
  blocking collectives  143 us (18%)
  matrix products  108 us (14%)
  other arithmetic  73.4 us (9%)
  local copies, waits for them, and re-layouts  22.3 us (3%)
  between operations  16.4 us (2%)
    psum x1, waiting for transfers between devices, body(): lax.psum((grad_qkv, grad_out, grad_up, grad_down, attn_grads, ffn_grads,...  189 us
    psum x2, waiting for transfers between devices, branch_sum(): return lax.psum(part_out, 'mp')  171 us
    psum x1, waiting for transfers between devices, input_back(): return lax.psum(part_grad, 'mp')  61.8 us
    psum x1, blocking collectives, body(): lax.psum((grad_qkv, grad_out, grad_up, grad_down, attn_grads, ffn_grads,...  39 us
    all_gather x1, blocking collectives, body(): lax.all_gather(w_qkv.astype(jnp.bfloat16), 'dp', axis=1, tiled=True)  34.4 us
    all_gather x1, blocking collectives, body(): lax.all_gather(w_out.astype(jnp.bfloat16), 'dp', axis=1, tiled=True)  31.3 us
  transfers between devices with their start and end apart: 6, of which 4 were waited for; matrix products, arithmetic and copies ran while one was open for 6% of the time, Pallas kernels for 0%

commit v1 on v0

v1 whole, which is shorter than its diff:
```python
import math

import jax
import jax.numpy as jnp
from jax import lax
from jax.experimental import pallas as pl
from jax.experimental.pallas import tpu as pltpu
from jax.sharding import PartitionSpec as P

HD = 64
EPS = 1e-05
DECAY = 0.5
MAT_RATE = 0.5
VEC_RATE = 0.05
UNIT_RATE = 0.3
GELU_A = math.sqrt(2.0 / math.pi)
GELU_B = 0.044715
BF = jnp.bfloat16
F32 = jnp.float32
VMEM = 48 * 1024 * 1024
WAYS = 8
BLK = 256


def full(shape):
    return pl.BlockSpec(shape, lambda *args: (0,) * len(shape))


def fulls(arrays):
    return [full(x.shape) for x in arrays]


def run(kernel, grid, ins, in_specs, outs, out_specs, idx, name, flops, scratch=()):
    traffic = sum(x.size * x.dtype.itemsize for x in ins)
    traffic += sum(math.prod(o.shape) * o.dtype.itemsize for o in outs)
    return pl.pallas_call(
        kernel,
        grid_spec=pltpu.PrefetchScalarGridSpec(
            num_scalar_prefetch=1,
            grid=grid,
            in_specs=in_specs,
            out_specs=out_specs,
            scratch_shapes=list(scratch),
        ),
        out_shape=outs,
        compiler_params=pltpu.CompilerParams(vmem_limit_bytes=VMEM),
        cost_estimate=pl.CostEstimate(
            flops=int(flops), bytes_accessed=int(traffic), transcendentals=0
        ),
        name=name,
    )(idx, *ins)


def sds(shape, dtype):
    return jax.ShapeDtypeStruct(shape, dtype)


def dot(x, y):
    return jnp.dot(x, y, preferred_element_type=F32)


def dot_nt(x, y):
    return lax.dot_general(x, y, (((1,), (1,)), ((), ())), preferred_element_type=F32)


def dot_tn(x, y):
    return lax.dot_general(x, y, (((0,), (0,)), ((), ())), preferred_element_type=F32)


def rowsum(x):
    return jnp.sum(x, -1, keepdims=True)


def normalize(x):
    n = x.shape[-1]
    off = x - rowsum(x) / n
    r = lax.rsqrt(rowsum(off * off) / n + EPS)
    return off * r, r


def gelu_parts(u):
    t = jnp.tanh(GELU_A * (u + GELU_B * (u * u * u)))
    return 0.5 * u * (1.0 + t), t


def unpack_rows(tail, narrow):
    n = tail.shape[-1]
    low = tail.shape[0] * n // (n + narrow)
    rest = tail[low:]
    step = tail.shape[0] - low
    side = jnp.concatenate([rest[:, i * narrow : (i + 1) * narrow] for i in range(low // step)], axis=0)
    return jnp.concatenate([tail[:low], side], axis=1)


def pack_rows(block, wide):
    rows, n = block.shape
    narrow = n - wide
    step = rows * narrow // wide
    side = block[:, wide:]
    rest = jnp.concatenate([side[i * step : (i + 1) * step] for i in range(rows // step)], axis=1)
    return jnp.concatenate([block[:, :wide], rest], axis=0)


def project_kernel(idx, a_ref, *refs):
    pieces = refs[:WAYS]
    q_ref, k_ref, v_ref, wq_ref, wo_ref, scr = refs[WAYS:]
    rows = wq_ref.shape[0] // WAYS
    orows = wo_ref.shape[0] // WAYS
    hw = q_ref.shape[1]

    @pl.when(pl.program_id(0) == 0)
    def _():
        for k in range(WAYS):
            j = jnp.bitwise_xor(idx[0], k)
            wq_ref[pl.ds(pl.multiple_of(j * rows, rows), rows), :] = pieces[k][:rows, :]
            tail = pieces[k][rows:, :].astype(F32)
            scr[pl.ds(pl.multiple_of(j * orows, orows), orows), :] = unpack_rows(
                tail, wo_ref.shape[1] - wq_ref.shape[1]
            )
        wo_ref[...] = scr[...].astype(BF)

    res = dot(a_ref[...], wq_ref[...]).astype(BF)
    q_ref[...] = res[:, :hw] * BF(HD ** (-0.5))
    k_ref[...] = res[:, hw : 2 * hw]
    v_ref[...] = res[:, 2 * hw :]


def project(a, pieces, hw, idx):
    rows, d = a.shape
    n = 3 * hw
    blk = lambda w: pl.BlockSpec((BLK, w), lambda s, i: (s, 0))
    return run(
        project_kernel,
        (rows // BLK,),
        [a, *pieces],
        [blk(d)] + fulls(pieces),
        [sds((rows, hw), BF)] * 3 + [sds((d, n), BF), sds((hw, d), BF)],
        [blk(hw)] * 3 + [full((d, n)), full((hw, d))],
        idx,
        "project",
        2 * rows * d * n,
        [pltpu.VMEM((hw, d), F32)],
    )


def attend_kernel(idx, start_ref, q_ref, k_ref, v_ref, o_ref, p_ref):
    h = pl.program_id(0)
    rows, hw = q_ref.shape
    lane = (lax.broadcasted_iota(jnp.int32, (1, hw), 1) // HD) == h
    for i in range(rows // BLK):
        lo, hi = i * BLK, (i + 1) * BLK
        qb = jnp.where(lane, q_ref[lo:hi, :], BF(0))
        s = dot_nt(qb, k_ref[:hi, :])
        kpos = lax.broadcasted_iota(jnp.int32, (BLK, hi), 1)
        qpos = lo + lax.broadcasted_iota(jnp.int32, (BLK, hi), 0)
        s = jnp.where((kpos >= start_ref[lo:hi, :]) & (kpos <= qpos), s, -1e30)
        p = jnp.exp(s - jnp.max(s, -1, keepdims=True))
        p = (p * (1.0 / rowsum(p))).astype(BF)
        p_ref[0, lo:hi, :hi] = p
        ob = dot(p, v_ref[:hi, :]).astype(BF)
        o_ref[lo:hi, :] = jnp.where(lane, ob, o_ref[lo:hi, :])


def attend(start, q, k, v, idx):
    rows, hw = q.shape
    heads = hw // HD
    return run(
        attend_kernel,
        (heads,),
        [start, q, k, v],
        fulls([start, q, k, v]),
        [sds((rows, hw), BF), sds((heads, rows, rows), BF)],
        [full((rows, hw)), pl.BlockSpec((1, rows, rows), lambda s, i: (s, 0, 0))],
        idx,
        "attend",
        heads * rows * rows * 256 * 4,
    )


def wide_norm(o_refs):
    parts = [x[...].astype(F32) for x in o_refs]
    n = sum(x.shape[-1] for x in parts)
    mean = sum(rowsum(x) for x in parts) / n
    parts = [x - mean for x in parts]
    r = lax.rsqrt(sum(rowsum(x * x) for x in parts) / n + EPS)
    return [x * r for x in parts], r


def outproj_kernel(idx, an_ref, on_ref, tok_ref, *refs):
    g = (len(refs) - 2) // 2
    o_refs, w_refs = refs[:g], refs[g : 2 * g]
    h_ref, c_ref = refs[2 * g :]
    hats, _ = wide_norm(o_refs)
    acc = tok_ref[...].astype(F32)
    for k in range(g):
        norm = an_ref[jnp.bitwise_xor(idx[1], k)]
        y = (hats[k] * norm[0:1] + norm[1:2]).astype(BF)
        acc = acc + dot(y, w_refs[k][...])
    h_ref[...] = acc
    hat, _ = normalize(acc)
    c_ref[...] = (hat * on_ref[2:3, :] + on_ref[3:4, :]).astype(BF)


def outproj(an, on, tok, o, w, idx):
    rows, d = tok.shape
    hw = o[0].shape[1]
    blk = lambda n: pl.BlockSpec((BLK, n), lambda s, i: (s, 0))
    return run(
        outproj_kernel,
        (rows // BLK,),
        [an, on, tok, *o, *w],
        fulls([an, on]) + [blk(d)] + [blk(hw)] * len(o) + fulls(w),
        [sds((rows, d), F32), sds((rows, d), BF)],
        [blk(d), blk(d)],
        idx,
        "outproj",
        2 * rows * d * hw * len(o),
    )


def ffn_up_kernel(idx, c_ref, e_ref, fn_ref, *refs):
    up, down = refs[:WAYS], refs[WAYS : 2 * WAYS]
    u_ref, dw_ref, st_ref, wu_ref, wd_ref = refs[2 * WAYS :]
    rows = up[0].shape[0]

    @pl.when(pl.program_id(0) == 0)
    def _():
        for k in range(WAYS):
            j = jnp.bitwise_xor(idx[0], k)
            at = pl.ds(pl.multiple_of(j * rows, rows), rows)
            wu_ref[at, :] = up[k][...]
            wd_ref[at, :] = down[k][...]

    u = dot(c_ref[...], wu_ref[...])
    u_ref[...] = u
    z, _ = gelu_parts(u)
    mean = rowsum(z) / z.shape[-1]
    z = z - mean
    dw = dot_nt(e_ref[...], wd_ref[...])
    dw_ref[...] = dw
    eg = dw * fn_ref[0:1, :]
    stats = [mean, rowsum(z * z), rowsum(eg), rowsum(eg * z)]
    place = lax.broadcasted_iota(jnp.int32, (BLK, 128), 1)
    tile = jnp.zeros((BLK, 128), F32)
    for i, x in enumerate(stats):
        tile = jnp.where(place == i, x, tile)
    st_ref[...] = tile.T[:8, :]


def ffn_up(c, e, fn, up, down, idx):
    rows, d = c.shape
    fl = up[0].shape[1]
    rblk = lambda n: pl.BlockSpec((BLK, n), lambda s, i: (s, 0))
    return run(
        ffn_up_kernel,
        (rows // BLK,),
        [c, e, fn, *up, *down],
        [rblk(d), rblk(d), full(fn.shape)] + fulls(up) + fulls(down),
        [sds((rows, fl), F32), sds((rows, fl), F32), sds((8, rows), F32), sds((d, fl), BF), sds((fl, d), BF)],
        [rblk(fl), rblk(fl), pl.BlockSpec((8, BLK), lambda s, i: (0, s)), full((d, fl)), full((fl, d))],
        idx,
        "ffn_up",
        4 * rows * d * fl,
    )


def rel_of(s):
    return jnp.where(s < 2, 2 * s + 1, 2 * s - 4)


def rel_block(s, i):
    return jnp.bitwise_xor(rel_of(s), i[1])


def rel_spec(n):
    return pl.BlockSpec((BLK, n), lambda s, i: (rel_block(s, i), 0))


SEND_SPEC = lambda n: pl.BlockSpec((1, BLK, n), lambda s, i: (jnp.minimum(s, 1), 0, 0))
KEEP_SPEC = lambda n: pl.BlockSpec((1, BLK, n), lambda s, i: (jnp.maximum(s - 2, 0), 0, 0))


def put_rel(send_ref, keep_ref, value):
    @pl.when(pl.program_id(0) < 2)
    def _():
        send_ref[0] = value.astype(BF)

    @pl.when(pl.program_id(0) >= 2)
    def _():
        keep_ref[0] = value


def ffn_mid_kernel(idx, u_ref, dw_ref, st_ref, fn_ref, wu_ref, w_ref, du_ref, send_ref, keep_ref, fg_ref):
    g = st_ref.shape[0]
    fl = u_ref.shape[1]
    n = g * fl
    st = [st_ref[k] for k in range(g)]
    mean = sum(x[0:1] for x in st) / g
    gap = [x[0:1] - mean for x in st]
    spread = sum(x[1:2] + fl * (gp * gp) for x, gp in zip(st, gap)) / n
    r = lax.rsqrt(spread + EPS)
    s_plain = sum(x[2:3] for x in st) / n
    s_norm = r * (sum(x[3:4] + gp * x[2:3] for x, gp in zip(st, gap)) / n)
    cols = jnp.concatenate([mean, r, s_plain, s_norm, jnp.zeros((124, BLK), F32)], axis=0).T
    mean, r, s_plain, s_norm = (cols[:, i : i + 1] for i in range(4))
    u = u_ref[...]
    z, t = gelu_parts(u)
    hat = (z - mean) * r
    w_ref[...] = (hat * fn_ref[0:1, :] + fn_ref[1:2, :]).astype(BF)
    dw = dw_ref[...]
    dz = r * (dw * fn_ref[0:1, :] - s_plain - hat * s_norm)
    slope = 0.5 * (1.0 + t) + 0.5 * u * (1.0 - t * t) * (GELU_A * (1.0 + (3.0 * GELU_B) * (u * u)))
    du = (dz * slope).astype(BF)
    du_ref[...] = du
    put_rel(send_ref, keep_ref, dot_nt(du, wu_ref[...]))
    grads = jnp.concatenate([jnp.sum(dw * hat, 0, keepdims=True), jnp.sum(dw, 0, keepdims=True)], axis=0)

    @pl.when(pl.program_id(0) == 0)
    def _():
        fg_ref[...] = grads

    @pl.when(pl.program_id(0) > 0)
    def _():
        fg_ref[...] += grads


def ffn_mid(u, dw, st, fn, wu, idx):
    rows, fl = u.shape
    d = wu.shape[0]
    return run(
        ffn_mid_kernel,
        (rows // BLK,),
        [u, dw, st, fn, wu],
        [rel_spec(fl), rel_spec(fl), pl.BlockSpec((st.shape[0], 8, BLK), lambda s, i: (0, 0, rel_block(s, i)))]
        + fulls([fn, wu]),
        [sds((rows, fl), BF), sds((rows, fl), BF), sds((2, BLK, d), BF), sds((2, BLK, d), F32), sds((2, fl), F32)],
        [rel_spec(fl), rel_spec(fl), SEND_SPEC(d), KEEP_SPEC(d), full((2, fl))],
        idx,
        "ffn_mid",
        2 * rows * d * fl,
    )


def rel_matmul(x, w, transposed, idx, name):
    rows, depth = x.shape
    d = w.shape[0] if transposed else w.shape[1]

    def kernel(idx, x_ref, w_ref, send_ref, keep_ref):
        op = dot_nt if transposed else dot
        put_rel(send_ref, keep_ref, op(x_ref[...], w_ref[...]))

    return run(
        kernel,
        (rows // BLK,),
        [x, w],
        [rel_spec(depth), full(w.shape)],
        [sds((2, BLK, d), BF), sds((2, BLK, d), F32)],
        [SEND_SPEC(d), KEEP_SPEC(d)],
        idx,
        name,
        2 * rows * d * depth,
    )


def weight_grad(x, y, idx, name, extra=None):
    rows, d = x.shape
    n = y.shape[1]
    step = d // WAYS
    steps = d // BLK
    extra_rows = 0 if extra is None else extra.size // (WAYS * n)
    out = step + extra_rows

    def kernel(idx, x_ref, y_ref, *refs):
        send_ref, keep_ref, scr = refs[-3:]
        s = pl.program_id(0)
        scr[pl.ds(pl.multiple_of(s * BLK, BLK), BLK), :] = dot_tn(x_ref[...], y_ref[...])

        @pl.when(s == steps - 1)
        def _():
            for k in range(WAYS):
                j = jnp.bitwise_xor(idx[0], k)
                value = scr[pl.ds(pl.multiple_of(j * step, step), step), :]
                dest = send_ref if k % 2 else keep_ref
                dest[k // 2, :step, :] = value.astype(dest.dtype)
                if extra_rows:
                    er = refs[0].shape[0] // WAYS
                    tail = pack_rows(refs[0][pl.ds(pl.multiple_of(j * er, er), er), :], n)
                    dest[k // 2, step:, :] = tail.astype(dest.dtype)

    ins = [x, y] + ([] if extra is None else [extra])
    return run(
        kernel,
        (steps,),
        ins,
        [pl.BlockSpec((rows, BLK), lambda s, i: (0, s))] + fulls(ins[1:]),
        [sds((WAYS // 2, out, n), BF), sds((WAYS // 2, out, n), F32)],
        [full((WAYS // 2, out, n))] * 2,
        idx,
        name,
        2 * rows * d * n,
        [pltpu.VMEM((d, n), F32)],
    )


def shard_back_kernel(idx, dc0_ref, dc1_ref, dc2_ref, h_ref, e_ref, an_ref, on_ref, *refs):
    g = 4
    o_refs, w_refs = refs[:g], refs[g : 2 * g]
    dh_ref, ol_ref, ag_ref, *do_refs = refs[2 * g :]
    do_refs, (gs_ref, gk_ref) = do_refs[:g], do_refs[g:]
    dc = dc0_ref[0] + dc1_ref[0].astype(F32) + dc2_ref[...].astype(F32)
    hat, r = normalize(h_ref[...])
    wgt = dc * on_ref[2:3, :]
    n = dc.shape[-1]
    dh = e_ref[...].astype(F32) + r * (wgt - rowsum(wgt) / n - hat * (rowsum(wgt * hat) / n))
    dh_ref[...] = dh
    ol_ref[...] = jnp.concatenate([jnp.sum(dc * hat, 0, keepdims=True), jnp.sum(dc, 0, keepdims=True)], axis=0)
    dhb = dh.astype(BF)
    hats, r = wide_norm(o_refs)
    norms = [an_ref[jnp.bitwise_xor(idx[1], k)] for k in range(g)]
    dys = [dot_nt(dhb, w_refs[k][...]) for k in range(g)]
    wgts = [dys[k] * norms[k][0:1] for k in range(g)]
    s_plain = sum(rowsum(x) for x in wgts) / n
    s_norm = sum(rowsum(x * y) for x, y in zip(wgts, hats)) / n
    for k in range(g):
        do_refs[k][...] = (r * (wgts[k] - s_plain - hats[k] * s_norm)).astype(BF)
        ag_ref[jnp.bitwise_xor(idx[1], k)] = jnp.concatenate(
            [jnp.sum(dys[k] * hats[k], 0, keepdims=True), jnp.sum(dys[k], 0, keepdims=True)], axis=0
        )
    for k in range(g):
        y = (hats[k] * norms[k][0:1] + norms[k][1:2]).astype(BF)
        dest = gs_ref if k % 2 else gk_ref
        dest[k // 2] = dot_tn(y, dhb).astype(dest.dtype)


def shard_back(dc_keep, dc_one, dc_two, h, e, an, on, o, w, idx):
    rows, d = h.shape
    g = len(o)
    hw = o[0].shape[1]
    mine = lambda n: pl.BlockSpec((BLK, n), lambda s, i: (i[1], 0))
    lead = pl.BlockSpec((1, BLK, d), lambda s, i: (0, 0, 0))
    ins = [dc_keep, dc_one, dc_two, h, e, an, on, *o, *w]
    return run(
        shard_back_kernel,
        (1,),
        ins,
        [lead, lead, full((BLK, d)), mine(d), mine(d)] + fulls([an, on]) + [mine(hw)] * g + fulls(w),
        [sds((BLK, d), F32), sds((2, d), F32), sds((g, 2, hw), F32)]
        + [sds((BLK, hw), BF)] * g
        + [sds((2, hw, d), BF), sds((2, hw, d), F32)],
        [full((BLK, d)), full((2, d)), full((g, 2, hw))]
        + [full((BLK, hw))] * g
        + [full((2, hw, d))] * 2,
        idx,
        "shard_back",
        4 * BLK * d * d,
    )


def attend_back_kernel(idx, q_ref, k_ref, v_ref, p_ref, *refs):
    d_refs = refs[:4]
    out_ref, do_scr, dq_scr, dk_scr, dv_scr = refs[4:]
    h = pl.program_id(0)
    rows, hw = q_ref.shape

    @pl.when(h == 0)
    def _():
        for k in range(4):
            j = jnp.bitwise_xor(idx[1], k)
            do_scr[pl.ds(pl.multiple_of(j * BLK, BLK), BLK), :] = d_refs[k][...]
        dk_scr[...] = jnp.zeros_like(dk_scr)
        dv_scr[...] = jnp.zeros_like(dv_scr)
        dq_scr[...] = jnp.zeros_like(dq_scr)

    lane = (lax.broadcasted_iota(jnp.int32, (1, hw), 1) // HD) == h
    for i in range(rows // BLK):
        lo, hi = i * BLK, (i + 1) * BLK
        dob = jnp.where(lane, do_scr[lo:hi, :], BF(0))
        qb = jnp.where(lane, q_ref[lo:hi, :], BF(0))
        pb = p_ref[0, lo:hi, :hi]
        p = pb.astype(F32)
        dp = dot_nt(dob, v_ref[:hi, :])
        ds = (p * (dp - rowsum(p * dp))).astype(BF)
        dq_scr[lo:hi, :] = jnp.where(lane, dot(ds, k_ref[:hi, :]), dq_scr[lo:hi, :])
        dk_scr[:hi, :] += dot_tn(ds, qb)
        dv_scr[:hi, :] += dot_tn(pb, dob)

    @pl.when(h == pl.num_programs(0) - 1)
    def _():
        out_ref[...] = jnp.concatenate([dq_scr[...] * HD ** (-0.5), dk_scr[...], dv_scr[...]], axis=1).astype(BF)


def attend_back(q, k, v, p, do, idx):
    rows, hw = q.shape
    heads = hw // HD
    return run(
        attend_back_kernel,
        (heads,),
        [q, k, v, p, *do],
        fulls([q, k, v]) + [pl.BlockSpec((1, rows, rows), lambda s, i: (s, 0, 0))] + fulls(do),
        [sds((rows, 3 * hw), BF)],
        [full((rows, 3 * hw))],
        idx,
        "attend_back",
        heads * rows * rows * 256 * 8,
        [pltpu.VMEM((rows, hw), BF)] + [pltpu.VMEM((rows, hw), F32)] * 3,
    )[0]


def shard_end_kernel(idx, da0_ref, da1_ref, da2_ref, tok_ref, on_ref, dh_ref, gt_ref, oe_ref):
    da = da0_ref[0] + da1_ref[0].astype(F32) + da2_ref[...].astype(F32)
    hat, r = normalize(tok_ref[...].astype(F32))
    wgt = da * on_ref[0:1, :]
    n = da.shape[-1]
    grad = r * (wgt - rowsum(wgt) / n - hat * (rowsum(wgt * hat) / n))
    gt_ref[...] = (dh_ref[...] + grad).astype(BF)
    oe_ref[...] = jnp.concatenate([jnp.sum(da * hat, 0, keepdims=True), jnp.sum(da, 0, keepdims=True)], axis=0)


def shard_end(da_keep, da_one, da_two, tok, on, dh, idx):
    d = tok.shape[1]
    lead = pl.BlockSpec((1, BLK, d), lambda s, i: (0, 0, 0))
    return run(
        shard_end_kernel,
        (1,),
        [da_keep, da_one, da_two, tok, on, dh],
        [lead, lead, full((BLK, d)), pl.BlockSpec((BLK, d), lambda s, i: (i[1], 0)), full(on.shape), full((BLK, d))],
        [sds((BLK, d), BF), sds((2, d), F32)],
        [full((BLK, d)), full((2, d))],
        idx,
        "shard_end",
        0,
    )


def spread_rows(parts, idx, name):
    d = parts[0].shape[1]

    def kernel(idx, *refs):
        for k in range(len(parts)):

            @pl.when(pl.program_id(0) == k)
            def _():
                refs[-1][...] = refs[k][...]

    return run(
        kernel,
        (len(parts),),
        parts,
        fulls(parts),
        [sds((BLK * len(parts), d), BF)],
        [pl.BlockSpec((BLK, d), lambda s, i: (jnp.bitwise_xor(s, i[1]), 0))],
        idx,
        name,
        0,
    )[0]


def precondition(pieces, w, left, right, left_root, right_root, total, packed, idx, name):
    rows, n = w.shape
    d = left.shape[1]
    side = right.shape[0]
    step = d // WAYS

    def kernel(idx, w_ref, l_ref, r_ref, lr_ref, rr_ref, *refs):
        parts = refs[:WAYS]
        g_ref, nl_ref, nr_ref, nw_ref, copy_ref = refs[WAYS:]
        for k in range(WAYS):
            j = jnp.bitwise_xor(idx[0], k)
            if packed == "head":
                value = parts[k][:step, :].astype(F32)
            elif packed == "tail":
                wide = parts[k].shape[1]
                head = parts[k].shape[0] - step * n // wide
                value = unpack_rows(parts[k][head:, :].astype(F32), n - wide)
            else:
                value = parts[k][...].astype(F32)
            g_ref[pl.ds(pl.multiple_of(j * step, step), step), :] = value
        grad = g_ref[...].astype(BF)
        place = idx[2]

        def one_hot(count, width):
            at = lax.broadcasted_iota(jnp.int32, (count, width), 1)
            want = place * count + lax.broadcasted_iota(jnp.int32, (count, width), 0)
            return jnp.where(at == want, 1.0, 0.0).astype(BF)

        scale = 1.0 / total
        own_cols = dot_nt(one_hot(side, n), grad).astype(BF)
        own_rows = dot(one_hot(rows, d), grad).astype(BF)
        nr_ref[...] = DECAY * r_ref[...] + ((1.0 - DECAY) * scale * scale) * dot(own_cols, grad)
        nl_ref[...] = DECAY * l_ref[...] + ((1.0 - DECAY) * scale * scale) * dot_nt(own_rows, grad)
        part = dot(lr_ref[...].astype(BF), grad).astype(BF)
        new = w_ref[...] - (MAT_RATE * scale) * dot(part, rr_ref[...].astype(BF))
        nw_ref[...] = new
        copy_ref[...] = new.astype(BF)

    ins = [w, left, right, left_root, right_root, *pieces]
    outs = [sds((d, n), F32), sds((rows, d), F32), sds((side, n), F32), sds((rows, n), F32), sds((rows, n), BF)]
    return run(
        kernel,
        (1,),
        ins,
        fulls(ins),
        outs,
        fulls(outs),
        idx,
        name,
        2 * rows * n * (2 * d + n) + 4 * rows * d * n,
    )


def body(
    tokens,
    cotangent,
    doc_lengths,
    outer_norms,
    attn_norm,
    ffn_norm,
    w_qkv,
    left_qkv,
    right_qkv,
    left_root_qkv,
    right_root_qkv,
    w_out,
    left_out,
    right_out,
    left_root_out,
    right_root_out,
    w_up,
    left_up,
    right_up,
    left_root_up,
    right_root_up,
    w_down,
    left_down,
    right_down,
    left_root_down,
    right_root_down,
):
    row_count = tokens.shape[0]
    n_dp, n_mp = lax.axis_size("dp"), lax.axis_size("mp")
    fine = n_dp // WAYS
    total = row_count * n_dp
    dp_at, mp_at = lax.axis_index("dp"), lax.axis_index("mp")
    idx = jnp.stack([dp_at // fine, mp_at, dp_at]).astype(jnp.int32)
    hw = w_qkv.shape[2] // 3

    def swap(x, axis, size, k):
        return lax.ppermute(x, axis, [(i, i ^ k) for i in range(size)])

    def dp(x, k):
        return swap(x, "dp", n_dp, k * fine)

    def mp(x, k):
        return swap(x, "mp", n_mp, k)

    def fine_rows(x):
        k = 1
        while k < fine:
            got = swap(x, "dp", n_dp, k)
            x = jnp.where((dp_at & k) == 0, jnp.concatenate([x, got], 0), jnp.concatenate([got, x], 0))
            k *= 2
        return x

    def fine_sum(x):
        k = 1
        while k < fine:
            x = x + swap(x, "dp", n_dp, k)
            k *= 2
        return x

    def gather8(own):
        parts = {0: own}
        for k in (2, 4, 6):
            parts[k] = dp(own, k)
        parts[1] = dp(own, 1)
        for k in (2, 4, 6):
            parts[k ^ 1] = dp(parts[k], 1)
        return [parts[k] for k in range(WAYS)]

    def gather4(own):
        far = mp(own, 2)
        return [own, mp(own, 1), far, mp(far, 1)]

    def scatter4(send, keep):
        got = mp(send, 1)
        return keep, got, mp((keep[1] + got[1].astype(F32)).astype(BF), 2)

    def scatter8(send, keep):
        part = keep + dp(send, 1).astype(F32)
        low = part.astype(BF)
        total_own = part[0]
        for i in range(1, WAYS // 2):
            total_own = total_own + dp(low[i], 2 * i).astype(F32)
        return fine_sum(total_own.astype(BF))

    out_rows = fine_rows(w_out[0].astype(BF))
    first = jnp.concatenate(
        [fine_rows(w_qkv[0].astype(BF)), pack_rows(out_rows, 3 * hw)], axis=0
    )
    first = gather8(first)
    up = gather8(fine_rows(w_up[0].astype(BF)))
    down = gather8(fine_rows(w_down[0].astype(BF)))
    attn_all = lax.all_gather(attn_norm, "mp")

    ends = jnp.cumsum(doc_lengths[0])
    places = jnp.arange(row_count, dtype=jnp.int32)
    start = jnp.max(jnp.where(ends[None, :] <= places[:, None], ends[None, :], 0), axis=1, keepdims=True)
    start = start.astype(jnp.int32)
    hat, _ = normalize(tokens.astype(F32))
    a_low = (hat * outer_norms[0] + outer_norms[1]).astype(BF)

    q, k, v, wq, wo = project(a_low, first, hw, idx)
    o, probs = attend(start, q, k, v, idx)
    wo_all = gather4(wo)
    o_all = gather4(o)
    hidden, c_low = outproj(attn_all, outer_norms, tokens, o_all, wo_all, idx)
    u, dw, stats, wu, wd = ffn_up(c_low, cotangent, ffn_norm, up, down, idx)
    stats = lax.all_gather(stats, "mp")
    w_low, du, dc_send, dc_keep, ffn_grads = ffn_mid(u, dw, stats, ffn_norm, wu, idx)
    dc = scatter4(dc_send, dc_keep)
    down_own = scatter8(*weight_grad(w_low, cotangent, idx, "grad_down"))
    up_own = scatter8(*weight_grad(c_low, du, idx, "grad_up"))
    bo = scatter4(*rel_matmul(w_low, wd, False, idx, "ffn_out"))
    dh, outer_late, attn_grads, *rest = shard_back(*dc, hidden, cotangent, attn_all, outer_norms, o_all, wo_all, idx)
    do, (go_send, go_keep) = rest[:n_mp], rest[n_mp:]
    do = [do[0]] + [mp(do[k], k) for k in range(1, n_mp)]
    go = scatter4(go_send, go_keep)
    grad_out_part = go[0][0] + go[1][0].astype(F32) + go[2].astype(F32)
    dqkv = attend_back(q, k, v, probs, do, idx)
    qkv_own = scatter8(*weight_grad(a_low, dqkv, idx, "grad_qkv", grad_out_part))
    da = scatter4(*rel_matmul(dqkv, wq, True, idx, "grad_a"))
    gt, outer_early = shard_end(*da, tokens, outer_norms, dh, idx)
    grad_tokens = spread_rows(gather4(gt), idx, "spread_tokens")
    h_own = lax.dynamic_slice_in_dim(hidden, mp_at * BLK, BLK, 0)
    out_own = (h_own + bo[0][0] + bo[1][0].astype(F32) + bo[2].astype(F32)).astype(BF)
    block_out = spread_rows(gather4(out_own), idx, "spread_out")

    outer_grads, attn_grads = lax.psum((jnp.concatenate([outer_early, outer_late], 0), attn_grads), "mp")
    attn_own = lax.dynamic_index_in_dim(attn_grads, mp_at, 0, False)
    vec = jnp.concatenate(
        [outer_grads.reshape(-1), attn_own.reshape(-1), ffn_grads.reshape(-1)]
    )
    size = vec.shape[0]
    vec = jnp.pad(vec, (0, -size % 1024)).reshape(-1, 128)
    step = 1
    while step < n_dp:
        vec = vec + swap(vec, "dp", n_dp, step)
        step *= 2
    vec = vec.reshape(-1)
    cut = outer_grads.size
    cut2 = cut + attn_own.size
    outer_grads = vec[:cut].reshape(outer_grads.shape)
    attn_grads = vec[cut:cut2].reshape(attn_own.shape)
    ffn_grads = vec[cut2:size].reshape(ffn_grads.shape)

    factor = VEC_RATE / math.sqrt(total)
    unit_factor = UNIT_RATE / math.sqrt(total)

    def update(pieces, w, left, right, left_root, right_root, packed, name):
        return precondition(
            pieces, w[0], left[0], right[0], left_root[0], right_root[0], total, packed, idx, name
        )

    down_pieces, up_pieces, qkv_pieces = gather8(down_own), gather8(up_own), gather8(qkv_own)
    down_res = update(down_pieces, w_down, left_down, right_down, left_root_down, right_root_down, None, "update_down")
    up_res = update(up_pieces, w_up, left_up, right_up, left_root_up, right_root_up, None, "update_up")
    out_res = update(qkv_pieces, w_out, left_out, right_out, left_root_out, right_root_out, "tail", "update_out")
    qkv_res = update(qkv_pieces, w_qkv, left_qkv, right_qkv, left_root_qkv, right_root_qkv, "head", "update_qkv")
    return (
        block_out,
        grad_tokens,
        outer_grads,
        attn_grads,
        ffn_grads,
        outer_norms - factor * outer_grads,
        attn_norm - factor * attn_grads,
        ffn_norm - unit_factor * ffn_grads,
        *(x[None] for x in qkv_res),
        *(x[None] for x in out_res),
        *(x[None] for x in up_res),
        *(x[None] for x in down_res),
    )


def solution(mesh):
    rows = P("dp", None)
    mats = (P("mp", "dp", None),) * 4 + (P("mp", None, None),)
    res = (P("mp", None, None),) + (P("mp", "dp", None),) * 4
    cols = P(None, "mp")
    return jax.shard_map(
        body,
        mesh=mesh,
        in_specs=(rows, rows, rows, P(), cols, cols) + mats * 4,
        out_specs=(rows, rows, P(), cols, cols, P(), cols, cols) + res * 4,
        check_vma=False,
    )
```

time: 795 us -> 332 us (0.42)
  waiting for transfers between devices: 422 us -> 71.1 us
  blocking collectives: 143 us -> 21.4 us
  matrix products: 108 us -> 0 us
  starting transfers between devices: 0.5 us -> 91.3 us
  Pallas kernels: 0 us -> 87.9 us
  other arithmetic: 73.4 us -> 21.2 us
  between operations: 16.4 us -> 1.4 us
  local copies, waits for them, and re-layouts: 22.3 us -> 36.3 us
    psum x4 -> x0, waiting for transfers between devices: 422 us -> none  [the longest x1 189 us: body(): lax.psum((grad_qkv, grad_out, grad_up, grad_down, attn_grads, ffn_grads,...]
    dot_general x34 -> x0, matrix products: 108 us -> none  [the longest x1 11.2 us: body(): jnp.einsum('qhe,khe->hqk', grad_att_low, value_rows, preferred_element_ty...]
    ppermute x0 -> x80, starting transfers between devices: none -> 91.3 us  [swap(): return lax.ppermute(x, axis, [(i, i ^ k) for i in range(size)])]
    pallas_call x0 -> x19, Pallas kernels: none -> 87.9 us  [run(): pl.pallas_call(kernel, grid_spec=pltpu.PrefetchScalarGridSpec(num_scalar_...]
    ppermute x0 -> x80, waiting for transfers between devices: none -> 71.1 us  [swap(): return lax.ppermute(x, axis, [(i, i ^ k) for i in range(size)])]
    psum x7 -> x1, blocking collectives: 77.4 us -> 10.7 us  [body(): lax.psum((jnp.concatenate([outer_early, outer_late], 0), attn_grads), 'mp')]
    all_gather x2, blocking collectives: 65.7 us -> 10.7 us  [the longest x1 5.59 us: body(): stats = lax.all_gather(stats, 'mp')]
    reduce_sum x11 -> x2, other arithmetic: 30.9 us -> 2.3 us  [rowsum(): return jnp.sum(x, -1, keepdims=True)]
  transfers between devices with their start and end apart: 6 -> 80, of which waited for: 4 -> 23; matrix products, arithmetic and copies ran while one was open for 6% -> 8% of each run, Pallas kernels for 0% -> 20%
where the time goes in v1:
time: 332 us; the launch traced here: 331 us
  starting transfers between devices  91.3 us (28%)
  Pallas kernels  87.9 us (26%)
  waiting for transfers between devices  71.1 us (21%)
  local copies, waits for them, and re-layouts  36.3 us (11%)
  blocking collectives  21.4 us (6%)
  other arithmetic  21.2 us (6%)
    ppermute x80, starting transfers between devices, swap(): return lax.ppermute(x, axis, [(i, i ^ k) for i in range(size)])  91.3 us
    pallas_call x19, Pallas kernels, run(): pl.pallas_call(kernel, grid_spec=pltpu.PrefetchScalarGridSpec(num_scalar_...  87.9 us
    ppermute x80, waiting for transfers between devices, swap(): return lax.ppermute(x, axis, [(i, i ^ k) for i in range(size)])  71.1 us
    unnamed x163, local copies, waits for them, and re-layouts  30.5 us
    psum x1, blocking collectives, body(): lax.psum((jnp.concatenate([outer_early, outer_late], 0), attn_grads), 'mp')  10.7 us
  transfers between devices with their start and end apart: 80, of which 23 were waited for; matrix products, arithmetic and copies ran while one was open for 8% of the time, Pallas kernels for 20%

profile of v1, /device:TPU:0, one launch (start us, length us, event | category | flops | bytes accessed | tf_op | source)
XLA Modules:
  0.0 330.5 jit_solution(9380743179114750641)
XLA Ops:
  2.8 3.0 collective-permute-start.1
  5.9 2.6 collective-permute-start.3
  16.2 4.7 %collective-permute-done.3.refs_4_ = bf16[128,576]{1,0:T(8,128)(2,1)S(1)} collective-permute-done((bf16[128,576]{1,0:T(8,128)(2,1)S(1)}, bf16[128,576]{1,0:T(8,128)(2,1)S(1)}, u32[]{:S(2)}, u32[]{:S(2)}) %collective-permute-start.3) | collective-permute-done | bytes 147488 | tf_op jit(solution)/shard_map/ppermute | solution.py:648
  23.4 3.1 collective-permute-start.16
  31.0 2.8 project.1
  34.9 8.7 %attend.1 = (bf16[1024,192]{1,0:T(8,128)(2,1)S(1)}, bf16[3,1024,1024]{2,1,0:T(8,128)(2,1)}) custom-call(s32[3]{0:T(128)S(1)} %pad_add_fusion.idx, s32[1024,1]{1,0:T(8,128)S(1)} %copy.61.start_ref, bf16[1024,192]{1,0:T(8,128)(2,1)S(1)} %get-tuple-element.88.q_ref, bf16[1024,192]{1,0:T(8,128)(2,1)S(1)} %get-tuple-element.89.k_ref, ...), custom_call_target="tpu_custom_call" | custom-call | flops 3221225472 | bytes 7868416 | tf_op jit(solution)/shard_map/attend/pallas_call | solution.py:36
  46.5 2.3 collective-permute-start.23
  50.9 3.5 %collective-permute-start.13 = (bf16[96,768]{1,0:T(8,128)(2,1)}, bf16[96,768]{1,0:T(8,128)(2,1)S(1)}, u32[]{:S(2)}, u32[]{:S(2)}) collective-permute-start(bf16[96,768]{1,0:T(8,128)(2,1)} %bitcast_convert_fusion.1.refs_0_), channel_id=1, source_target_pairs={{0,4},{4,0},{8,12},{12,8},{16,20},{20,16},{24,28},{28,24},{1,5},{5... | collective-permute-start | bytes 442376 | tf_op jit(solution)/shard_map/ppermute | solution.py:648
  54.4 4.8 %collective-permute-done.23.refs_12_ = bf16[96,768]{1,0:T(8,128)(2,1)S(1)} collective-permute-done((bf16[96,768]{1,0:T(8,128)(2,1)S(1)}, bf16[96,768]{1,0:T(8,128)(2,1)S(1)}, u32[]{:S(2)}, u32[]{:S(2)}) %collective-permute-start.23) | collective-permute-done | bytes 147488 | tf_op jit(solution)/shard_map/ppermute | solution.py:648
  61.6 4.0 %collective-permute-done.20.refs_9_ = bf16[96,768]{1,0:T(8,128)(2,1)S(1)} collective-permute-done((bf16[96,768]{1,0:T(8,128)(2,1)S(1)}, bf16[96,768]{1,0:T(8,128)(2,1)S(1)}, u32[]{:S(2)}, u32[]{:S(2)}) %collective-permute-start.20) | collective-permute-done | bytes 147488 | tf_op jit(solution)/shard_map/ppermute | solution.py:648
  65.9 5.0 %collective-permute-done.15.refs_3_ = bf16[96,768]{1,0:T(8,128)(2,1)S(1)} collective-permute-done((bf16[96,768]{1,0:T(8,128)(2,1)}, bf16[96,768]{1,0:T(8,128)(2,1)S(1)}, u32[]{:S(2)}, u32[]{:S(2)}) %collective-permute-start.15) | collective-permute-done | bytes 147488 | tf_op jit(solution)/shard_map/ppermute | solution.py:648
  75.3 5.2 %all-gather.2.an_ref = f32[4,2,192]{2,1,0:T(2,128)S(1)} all-gather(f32[1,2,192]{2,1,0:T(2,128)S(1)} %bitcast.147), channel_id=2, replica_groups=mesh['dp'=8,'mp'=4] {'mp'}, dimensions={0}, use_global_device_ids=true | all-gather | bytes 7680 | tf_op jit(solution)/shard_map/all_gather | solution.py:703
  80.5 6.8 %outproj.1 = (f32[1024,768]{1,0:T(8,128)}, bf16[1024,768]{1,0:T(8,128)(2,1)S(1)}) custom-call(s32[3]{0:T(128)S(1)} %pad_add_fusion.idx, f32[4,2,192]{2,1,0:T(2,128)S(1)} %all-gather.2.an_ref, f32[4,768]{1,0:T(4,128)S(1)} %copy-done.46, bf16[1024,768]{1,0:T(8,128)(2,1)} %tok_ref.3, bf16[1024,192]{1,0:T(8,128)(2,1)S(1)} %get-tuple-element.91.refs_0_, ...), custom_call_target="tpu_custom_call" | custom-call | flops 1207959552 | bytes 9062400 | tf_op jit(solution)/shard_map/outproj/pallas_call | solution.py:36
  88.5 7.4 %ffn_up.1 = (f32[1024,768]{1,0:T(8,128)}, f32[1024,768]{1,0:T(8,128)}, f32[8,1024]{1,0:T(8,128)S(1)}, bf16[768,768]{1,0:T(8,128)(2,1)S(1)}, bf16[768,768]{1,0:T(8,128)(2,1)S(1)}) custom-call(s32[3]{0:T(128)S(1)} %pad_add_fusion.idx, bf16[1024,768]{1,0:T(8,128)(2,1)} %copy-done.51, bf16[1024,768]{1,0:T(8,128)(2,1)} %y_ref.1, f32[2,768]{1,0:T(2,128)S(1)} %copy-done.50, ...), custom_call_target="tpu_custom_call" | custom-call | flops 2415919104 | bytes 14194688 | tf_op jit(solution)/shard_map/ffn_up/pallas_call | solution.py:36
  96.9 5.6 %all-gather.1 = f32[32,1024]{1,0:T(8,128)S(1)} all-gather(f32[8,1024]{1,0:T(8,128)S(1)} %get-tuple-element.97), channel_id=3, replica_groups=mesh['dp'=8,'mp'=4] {'mp'}, dimensions={0}, use_global_device_ids=true | all-gather | bytes 163840 | tf_op jit(solution)/shard_map/all_gather | solution.py:718
  102.5 8.9 %ffn_mid.1 = (bf16[1024,768]{1,0:T(8,128)(2,1)S(1)}, bf16[1024,768]{1,0:T(8,128)(2,1)S(1)}, bf16[2,256,768]{2,1,0:T(8,128)(2,1)}, f32[2,256,768]{2,1,0:T(8,128)}, f32[2,768]{1,0:T(2,128)S(1)}) custom-call(s32[3]{0:T(128)S(1)} %pad_add_fusion.idx, f32[1024,768]{1,0:T(8,128)} %get-tuple-element.95.u_ref, f32[1024,768]{1,0:T(8,128)} %get-tuple-element.96.dw_ref, ...), custom_call_target="tpu_custom_call" | custom-call | flops 1207959552 | bytes 13119488 | tf_op jit(solution)/shard_map/ffn_mid/pallas_call | solution.py:36
  112.5 3.5 %grad_down.1 = (bf16[4,96,768]{2,1,0:T(8,128)(2,1)}, f32[4,96,768]{2,1,0:T(8,128)S(1)}) custom-call(s32[3]{0:T(128)S(1)} %pad_add_fusion.idx, bf16[1024,768]{1,0:T(8,128)(2,1)S(1)} %get-tuple-element.99.x_ref, bf16[1024,768]{1,0:T(8,128)(2,1)S(1)} %copy-done.12), custom_call_target="tpu_custom_call" | custom-call | flops 1207959552 | bytes 4915200 | tf_op jit(solution)/shard_map/grad_down/pallas_call | solution.py:36
  121.7 3.5 %grad_up.1 = (bf16[4,96,768]{2,1,0:T(8,128)(2,1)}, f32[4,96,768]{2,1,0:T(8,128)S(1)}) custom-call(s32[3]{0:T(128)S(1)} %pad_add_fusion.idx, bf16[1024,768]{1,0:T(8,128)(2,1)S(1)} %copy-done.52, bf16[1024,768]{1,0:T(8,128)(2,1)S(1)} %copy-done.56), custom_call_target="tpu_custom_call" | custom-call | flops 1207959552 | bytes 4915200 | tf_op jit(solution)/shard_map/grad_up/pallas_call | solution.py:36
  129.2 2.7 ffn_out.1
  138.2 2.1 collective-permute-start.70
  140.3 5.4 %collective-permute-done.58 = bf16[4,96,768]{2,1,0:T(8,128)(2,1)} collective-permute-done((bf16[4,96,768]{2,1,0:T(8,128)(2,1)}, bf16[4,96,768]{2,1,0:T(8,128)(2,1)}, u32[]{:S(2)}, u32[]{:S(2)}) %collective-permute-start.58) | collective-permute-done | bytes 589856 | tf_op jit(solution)/shard_map/ppermute | solution.py:648
  147.1 4.8 %shard_back.1 = (f32[256,768]{1,0:T(8,128)S(1)}, f32[2,768]{1,0:T(2,128)S(1)}, f32[4,2,192]{2,1,0:T(2,128)S(1)}, bf16[256,192]{1,0:T(8,128)(2,1)S(1)}, bf16[256,...) custom-call(s32[3]{0:T(128)S(1)} %pad_add_fusion.idx, ...), custom_call_target="tpu_custom_call" | custom-call | flops 603979776 | bytes 13203456 | tf_op jit(solution)/shard_map/shard_back/pallas_call | solution.py:36
  153.8 3.0 collective-permute-start.71
  158.2 2.6 collective-permute-start.72
  162.4 10.7 %attend_back.1.x_ref.y_ref = bf16[1024,576]{1,0:T(8,128)(2,1)S(1)} custom-call(s32[3]{0:T(128)S(1)} %pad_add_fusion.idx, bf16[1024,192]{1,0:T(8,128)(2,1)S(1)} %copy-done.64, bf16[1024,192]{1,0:T(8,128)(2,1)S(1)} %copy-done.66, bf16[1024,192]{1,0:T(8,128)(2,1)S(1)} %copy-done.68, bf16[3,1024,1024]{2,1,0:T(8,128)(2,1)} %get-tuple-element.103.p_ref, ...), custom_call_target="tpu_custom_call" | custom-call | flops 6442450944 | bytes 9043968 | tf_op jit(solution)/shard_map/attend_back/pallas_call | solution.py:36
  173.1 3.0 grad_a.1
  179.7 9.5 %collective-permute-done.60 = bf16[96,768]{1,0:T(8,128)(2,1)S(1)} collective-permute-done((bf16[96,768]{1,0:T(8,128)(2,1)S(1)}, bf16[96,768]{1,0:T(8,128)(2,1)S(1)}, u32[]{:S(2)}, u32[]{:S(2)}) %collective-permute-start.60) | collective-permute-done | bytes 147488 | tf_op jit(solution)/shard_map/ppermute | solution.py:648
  189.2 4.5 %collective-permute-start.76 = (bf16[96,768]{1,0:T(8,128)(2,1)S(1)}, bf16[96,768]{1,0:T(8,128)(2,1)S(1)}, u32[]{:S(2)}, u32[]{:S(2)}) collective-permute-start(bf16[96,768]{1,0:T(8,128)(2,1)S(1)} %fusion.19.refs_0_), channel_id=1, source_target_pairs={{0,16},{4,20},{8,24},{12,28},{16,0},{20,4},{24,8},{28,12},{1,17},{... | collective-permute-start | bytes 442376 | tf_op jit(solution)/shard_map/ppermute | solution.py:648
  199.1 5.7 %collective-permute-done.76.refs_4_ = bf16[96,768]{1,0:T(8,128)(2,1)S(1)} collective-permute-done((bf16[96,768]{1,0:T(8,128)(2,1)S(1)}, bf16[96,768]{1,0:T(8,128)(2,1)S(1)}, u32[]{:S(2)}, u32[]{:S(2)}) %collective-permute-start.76) | collective-permute-done | bytes 147488 | tf_op jit(solution)/shard_map/ppermute | solution.py:648
  217.4 3.7 %update_down.1 = (f32[768,768]{1,0:T(8,128)}, f32[96,768]{1,0:T(8,128)}, f32[96,768]{1,0:T(8,128)}, f32[96,768]{1,0:T(8,128)}, bf16[96,768]{1,0:T(8,128)(2,1)}) custom-call(s32[3]{0:T(128)S(1)} %pad_add_fusion.idx, f32[96,768]{1,0:T(8,128)S(1)} %bitcast.129, f32[96,768]{1,0:T(8,128)S(1)} %bitcast.133, f32[96,768]{1,0:T(8,128)S(1)} %bitcast.134, ...), custom_call_target="tpu_custom_call" | custom-call | flops 566231040 | bytes 8110080 | tf_op jit(solution)/shard_map/update_down/pallas_call | solution.py:36
  221.7 2.7 grad_qkv.1
  226.3 2.2 copy.62
  232.8 3.0 shard_end.1
  235.8 10.7 %all-reduce.1 = (f32[4,2,192]{2,1,0:T(2,128)S(1)}, f32[3072]{0:T(1024)S(1)}) all-reduce(f32[4,2,192]{2,1,0:T(2,128)S(1)} %get-tuple-element.117, f32[3072]{0:T(1024)S(1)} %reshape.139), channel_id=1, replica_groups=mesh['dp'=8,'mp'=4] {'mp'}, use_global_device_ids=true, to_apply=%region_5.6 | all-reduce | flops 4608 | bytes 36864 | tf_op jit(solution)/shard_map/psum | solution.py:738
  256.0 2.1 copy.63
  258.2 2.5 fusion.27
  269.5 4.9 %update_up.1 = (f32[768,768]{1,0:T(8,128)}, f32[96,768]{1,0:T(8,128)}, f32[96,768]{1,0:T(8,128)}, f32[96,768]{1,0:T(8,128)}, bf16[96,768]{1,0:T(8,128)(2,1)}) custom-call(s32[3]{0:T(128)S(1)} %pad_add_fusion.idx, f32[96,768]{1,0:T(8,128)S(1)} %bitcast.130, f32[96,768]{1,0:T(8,128)S(1)} %bitcast.136, f32[96,768]{1,0:T(8,128)S(1)} %bitcast.137, ...), custom_call_target="tpu_custom_call" | custom-call | flops 566231040 | bytes 8110080 | tf_op jit(solution)/shard_map/update_up/pallas_call | solution.py:36
  274.4 2.3 spread_out.1
  278.2 3.9 %collective-permute-done.44 = f32[40,128]{1,0:T(8,128)S(1)} collective-permute-done((f32[40,128]{1,0:T(8,128)S(1)}, f32[40,128]{1,0:T(8,128)S(1)}, u32[]{:S(2)}, u32[]{:S(2)}) %collective-permute-start.44) | collective-permute-done | bytes 20512 | tf_op jit(solution)/shard_map/ppermute | solution.py:648
  284.5 2.6 collective-permute-start.54
  289.3 3.5 %collective-permute-done.52.refs_2_ = bf16[128,576]{1,0:T(8,128)(2,1)S(1)} collective-permute-done((bf16[128,576]{1,0:T(8,128)(2,1)S(1)}, bf16[128,576]{1,0:T(8,128)(2,1)S(1)}, u32[]{:S(2)}, u32[]{:S(2)}) %collective-permute-start.52) | collective-permute-done | bytes 147488 | tf_op jit(solution)/shard_map/ppermute | solution.py:648
  293.4 6.1 %collective-permute-done.54.refs_4_ = bf16[128,576]{1,0:T(8,128)(2,1)S(1)} collective-permute-done((bf16[128,576]{1,0:T(8,128)(2,1)S(1)}, bf16[128,576]{1,0:T(8,128)(2,1)S(1)}, u32[]{:S(2)}, u32[]{:S(2)}) %collective-permute-start.54) | collective-permute-done | bytes 147488 | tf_op jit(solution)/shard_map/ppermute | solution.py:648
  302.7 3.9 %collective-permute-done.53.refs_3_ = bf16[128,576]{1,0:T(8,128)(2,1)S(1)} collective-permute-done((bf16[128,576]{1,0:T(8,128)(2,1)S(1)}, bf16[128,576]{1,0:T(8,128)(2,1)S(1)}, u32[]{:S(2)}, u32[]{:S(2)}) %collective-permute-start.53) | collective-permute-done | bytes 147488 | tf_op jit(solution)/shard_map/ppermute | solution.py:648
  306.6 3.0 collective-permute-done.55.refs_5_
  314.3 2.8 update_qkv.1
  318.3 2.9 copy.64
  324.8 2.2 update_out.1
  326.9 3.6 %spread_tokens.1 = bf16[1024,768]{1,0:T(8,128)(2,1)} custom-call(s32[3]{0:T(128)S(1)} %pad_add_fusion.idx, bf16[256,768]{1,0:T(8,128)(2,1)} %get-tuple-element.114.refs_0_, bf16[256,768]{1,0:T(8,128)(2,1)} %collective-permute-done.39.refs_1_, bf16[256,768]{1,0:T(8,128)(2,1)} %collective-permute-done.40.refs_2_, bf16[256,768]{1,0:T(8,128)(2,1)} %collective-permute-done.41.refs_3_), custom_call_target="tpu_custom_call" | custom-call | bytes 3145728 | tf_op jit(solution)/shard_map/spread_tokens/pallas_call | solution.py:36
  (349 shorter events, 121.1 us)
Async XLA Ops:
  2.8 12.9 %collective-permute-start.1 = (bf16[128,576]{1,0:T(8,128)(2,1)S(1)}, bf16[128,576]{1,0:T(8,128)(2,1)S(1)}, u32[]{:S(2)}, u32[]{:S(2)}) collective-permute-start(bf16[128,576]{1,0:T(8,128)(2,1)S(1)} %maximum_maximum_fusion.refs_0_), channel_id=1, source_target_pairs={{0,8},{4,12},{8,0},{12,4},{16,24},{20,28},{24,16},{28,20},{1,9},{5... | collective-permute-start | bytes 442376 | tf_op jit(solution)/shard_map/ppermute | solution.py:648
  5.9 15.1 %collective-permute-start.3 = (bf16[128,576]{1,0:T(8,128)(2,1)S(1)}, bf16[128,576]{1,0:T(8,128)(2,1)S(1)}, u32[]{:S(2)}, u32[]{:S(2)}) collective-permute-start(bf16[128,576]{1,0:T(8,128)(2,1)S(1)} %maximum_maximum_fusion.refs_0_), channel_id=1, source_target_pairs={{0,16},{4,20},{8,24},{12,28},{16,0},{20,4},{24,8},{28,12},{1,17},{... | collective-permute-start | bytes 442376 | tf_op jit(solution)/shard_map/ppermute | solution.py:648
  8.4 14.0 %collective-permute-start.5 = (bf16[128,576]{1,0:T(8,128)(2,1)S(1)}, bf16[128,576]{1,0:T(8,128)(2,1)S(1)}, u32[]{:S(2)}, u32[]{:S(2)}) collective-permute-start(bf16[128,576]{1,0:T(8,128)(2,1)S(1)} %maximum_maximum_fusion.refs_0_), channel_id=1, source_target_pairs={{0,24},{4,28},{8,16},{12,20},{16,8},{20,12},{24,0},{28,4},{1,25},{... | collective-permute-start | bytes 442376 | tf_op jit(solution)/shard_map/ppermute | solution.py:648
  8.4 14.9 %collective-permute-start = (bf16[128,576]{1,0:T(8,128)(2,1)S(1)}, bf16[128,576]{1,0:T(8,128)(2,1)S(1)}, u32[]{:S(2)}, u32[]{:S(2)}) collective-permute-start(bf16[128,576]{1,0:T(8,128)(2,1)S(1)} %maximum_maximum_fusion.refs_0_), channel_id=1, source_target_pairs={{0,4},{4,0},{8,12},{12,8},{16,20},{20,16},{24,28},{28,24},{1,5},{5... | collective-permute-start | bytes 442376 | tf_op jit(solution)/shard_map/ppermute | solution.py:648
  11.8 34.1 %collective-permute-start.14 = (bf16[96,768]{1,0:T(8,128)(2,1)}, bf16[96,768]{1,0:T(8,128)(2,1)}, u32[]{:S(2)}, u32[]{:S(2)}) collective-permute-start(bf16[96,768]{1,0:T(8,128)(2,1)} %bitcast_convert_fusion.1.refs_0_), channel_id=1, source_target_pairs={{0,8},{4,12},{8,0},{12,4},{16,24},{20,28},{24,16},{28,20},{1,9},{5... | collective-permute-start | bytes 442376 | tf_op jit(solution)/shard_map/ppermute | solution.py:648
  23.4 23.1 %collective-permute-start.16 = (bf16[96,768]{1,0:T(8,128)(2,1)}, bf16[96,768]{1,0:T(8,128)(2,1)S(1)}, u32[]{:S(2)}, u32[]{:S(2)}) collective-permute-start(bf16[96,768]{1,0:T(8,128)(2,1)} %bitcast_convert_fusion.1.refs_0_), channel_id=1, source_target_pairs={{0,16},{4,20},{8,24},{12,28},{16,0},{20,4},{24,8},{28,12},{1,17},{... | collective-permute-start | bytes 442376 | tf_op jit(solution)/shard_map/ppermute | solution.py:648
  26.5 22.3 %collective-permute-start.18 = (bf16[96,768]{1,0:T(8,128)(2,1)}, bf16[96,768]{1,0:T(8,128)(2,1)S(1)}, u32[]{:S(2)}, u32[]{:S(2)}) collective-permute-start(bf16[96,768]{1,0:T(8,128)(2,1)} %bitcast_convert_fusion.1.refs_0_), channel_id=1, source_target_pairs={{0,24},{4,28},{8,16},{12,20},{16,8},{20,12},{24,0},{28,4},{1,25},{... | collective-permute-start | bytes 442376 | tf_op jit(solution)/shard_map/ppermute | solution.py:648
  43.6 15.7 %collective-permute-start.8 = (bf16[1024,192]{1,0:T(8,128)(2,1)S(1)}, bf16[1024,192]{1,0:T(8,128)(2,1)S(1)}, u32[]{:S(2)}, u32[]{:S(2)}) collective-permute-start(bf16[1024,192]{1,0:T(8,128)(2,1)S(1)} %get-tuple-element.91.refs_0_), channel_id=1, source_target_pairs={{0,2},{1,3},{2,0},{3,1},{4,6},{5,7},{6,4},{7,5},{8,10},{9,11},{10,... | collective-permute-start | bytes 1179656 | tf_op jit(solution)/shard_map/ppermute | solution.py:648
  45.9 15.7 %collective-permute-start.11 = (bf16[192,768]{1,0:T(8,128)(2,1)S(1)}, bf16[192,768]{1,0:T(8,128)(2,1)S(1)}, u32[]{:S(2)}, u32[]{:S(2)}) collective-permute-start(bf16[192,768]{1,0:T(8,128)(2,1)S(1)} %get-tuple-element.92.refs_4_), channel_id=1, source_target_pairs={{0,2},{1,3},{2,0},{3,1},{4,6},{5,7},{6,4},{7,5},{8,10},{9,11},{10,... | collective-permute-start | bytes 884744 | tf_op jit(solution)/shard_map/ppermute | solution.py:648
  46.5 12.8 %collective-permute-start.23 = (bf16[96,768]{1,0:T(8,128)(2,1)S(1)}, bf16[96,768]{1,0:T(8,128)(2,1)S(1)}, u32[]{:S(2)}, u32[]{:S(2)}) collective-permute-start(bf16[96,768]{1,0:T(8,128)(2,1)S(1)} %bitcast_convert_fusion.refs_8_), channel_id=1, source_target_pairs={{0,16},{4,20},{8,24},{12,28},{16,0},{20,4},{24,8},{28,12},{1,17},{... | collective-permute-start | bytes 442376 | tf_op jit(solution)/shard_map/ppermute | solution.py:648
  59.2 13.7 %collective-permute-start.7 = (bf16[1024,192]{1,0:T(8,128)(2,1)S(1)}, bf16[1024,192]{1,0:T(8,128)(2,1)S(1)}, u32[]{:S(2)}, u32[]{:S(2)}) collective-permute-start(bf16[1024,192]{1,0:T(8,128)(2,1)S(1)} %get-tuple-element.91.refs_0_), channel_id=1, source_target_pairs={{0,1},{1,0},{2,3},{3,2},{4,5},{5,4},{6,7},{7,6},{8,9},{9,8},{10,11... | collective-permute-start | bytes 1179656 | tf_op jit(solution)/shard_map/ppermute | solution.py:648
  59.3 15.8 %collective-permute-start.9 = (bf16[1024,192]{1,0:T(8,128)(2,1)S(1)}, bf16[1024,192]{1,0:T(8,128)(2,1)S(1)}, u32[]{:S(2)}, u32[]{:S(2)}) collective-permute-start(bf16[1024,192]{1,0:T(8,128)(2,1)S(1)} %collective-permute-done.8.refs_2_), channel_id=1, source_target_pairs={{0,1},{1,0},{2,3},{3,2},{4,5},{5,4},{6,7},{7,6},{8,9},{9,8},{10,11... | collective-permute-start | bytes 1179656 | tf_op jit(solution)/shard_map/ppermute | solution.py:648
  70.9 17.5 %collective-permute-start.17 = (bf16[96,768]{1,0:T(8,128)(2,1)S(1)}, bf16[96,768]{1,0:T(8,128)(2,1)S(1)}, u32[]{:S(2)}, u32[]{:S(2)}) collective-permute-start(bf16[96,768]{1,0:T(8,128)(2,1)S(1)} %collective-permute-done.16.refs_4_), channel_id=1, source_target_pairs={{0,4},{4,0},{8,12},{12,8},{16,20},{20,16},{24,28},{28,24},{1,5},{5... | collective-permute-start | bytes 442376 | tf_op jit(solution)/shard_map/ppermute | solution.py:648
  71.3 17.2 %collective-permute-start.19 = (bf16[96,768]{1,0:T(8,128)(2,1)S(1)}, bf16[96,768]{1,0:T(8,128)(2,1)S(1)}, u32[]{:S(2)}, u32[]{:S(2)}) collective-permute-start(bf16[96,768]{1,0:T(8,128)(2,1)S(1)} %collective-permute-done.18.refs_6_), channel_id=1, source_target_pairs={{0,4},{4,0},{8,12},{12,8},{16,20},{20,16},{24,28},{28,24},{1,5},{5... | collective-permute-start | bytes 442376 | tf_op jit(solution)/shard_map/ppermute | solution.py:648
  73.0 15.5 %collective-permute-start.22 = (bf16[96,768]{1,0:T(8,128)(2,1)S(1)}, bf16[96,768]{1,0:T(8,128)(2,1)S(1)}, u32[]{:S(2)}, u32[]{:S(2)}) collective-permute-start(bf16[96,768]{1,0:T(8,128)(2,1)S(1)} %collective-permute-done.21.refs_10_), channel_id=1, source_target_pairs={{0,4},{4,0},{8,12},{12,8},{16,20},{20,16},{24,28},{28,24},{1,5},{5... | collective-permute-start | bytes 442376 | tf_op jit(solution)/shard_map/ppermute | solution.py:648
  73.3 15.2 %collective-permute-start.24 = (bf16[96,768]{1,0:T(8,128)(2,1)S(1)}, bf16[96,768]{1,0:T(8,128)(2,1)S(1)}, u32[]{:S(2)}, u32[]{:S(2)}) collective-permute-start(bf16[96,768]{1,0:T(8,128)(2,1)S(1)} %collective-permute-done.23.refs_12_), channel_id=1, source_target_pairs={{0,4},{4,0},{8,12},{12,8},{16,20},{20,16},{24,28},{28,24},{1,5},{5... | collective-permute-start | bytes 442376 | tf_op jit(solution)/shard_map/ppermute | solution.py:648
  75.0 13.5 %collective-permute-start.26 = (bf16[96,768]{1,0:T(8,128)(2,1)S(1)}, bf16[96,768]{1,0:T(8,128)(2,1)S(1)}, u32[]{:S(2)}, u32[]{:S(2)}) collective-permute-start(bf16[96,768]{1,0:T(8,128)(2,1)S(1)} %collective-permute-done.25.refs_14_), channel_id=1, source_target_pairs={{0,4},{4,0},{8,12},{12,8},{16,20},{20,16},{24,28},{28,24},{1,5},{5... | collective-permute-start | bytes 442376 | tf_op jit(solution)/shard_map/ppermute | solution.py:648
  117.1 16.5 %collective-permute-start.69 = (bf16[4,96,768]{2,1,0:T(8,128)(2,1)}, bf16[4,96,768]{2,1,0:T(8,128)(2,1)}, u32[]{:S(2)}, u32[]{:S(2)}) collective-permute-start(bf16[4,96,768]{2,1,0:T(8,128)(2,1)} %get-tuple-element.142), channel_id=1, source_target_pairs={{0,4},{4,0},{8,12},{12,8},{16,20},{20,16},{24,28},{28,24},{1,5},{5... | collective-permute-start | bytes 1769480 | tf_op jit(solution)/shard_map/ppermute | solution.py:648
  118.8 16.1 %collective-permute-start.32 = (bf16[2,256,768]{2,1,0:T(8,128)(2,1)}, bf16[2,256,768]{2,1,0:T(8,128)(2,1)}, u32[]{:S(2)}, u32[]{:S(2)}) collective-permute-start(bf16[2,256,768]{2,1,0:T(8,128)(2,1)} %get-tuple-element.105), channel_id=1, source_target_pairs={{0,1},{1,0},{2,3},{3,2},{4,5},{5,4},{6,7},{7,6},{8,9},{9,8},{10,11... | collective-permute-start | bytes 2359304 | tf_op jit(solution)/shard_map/ppermute | solution.py:648
  126.2 19.4 %collective-permute-start.58 = (bf16[4,96,768]{2,1,0:T(8,128)(2,1)}, bf16[4,96,768]{2,1,0:T(8,128)(2,1)}, u32[]{:S(2)}, u32[]{:S(2)}) collective-permute-start(bf16[4,96,768]{2,1,0:T(8,128)(2,1)} %get-tuple-element.135), channel_id=1, source_target_pairs={{0,4},{4,0},{8,12},{12,8},{16,20},{20,16},{24,28},{28,24},{1,5},{5... | collective-permute-start | bytes 1769480 | tf_op jit(solution)/shard_map/ppermute | solution.py:648
  131.9 61.9 %collective-permute-start.27 = (bf16[2,256,768]{2,1,0:T(8,128)(2,1)S(1)}, bf16[2,256,768]{2,1,0:T(8,128)(2,1)}, u32[]{:S(2)}, u32[]{:S(2)}) collective-permute-start(bf16[2,256,768]{2,1,0:T(8,128)(2,1)S(1)} %get-tuple-element.102), channel_id=1, source_target_pairs={{0,1},{1,0},{2,3},{3,2},{4,5},{5,4},{6,7},{7,6},{8,9},{9,8},{10,11... | collective-permute-start | bytes 2359304 | tf_op jit(solution)/shard_map/ppermute | solution.py:648
  138.2 38.0 %collective-permute-start.70 = (bf16[96,768]{1,0:T(8,128)(2,1)S(1)}, bf16[96,768]{1,0:T(8,128)(2,1)S(1)}, u32[]{:S(2)}, u32[]{:S(2)}) collective-permute-start(bf16[96,768]{1,0:T(8,128)(2,1)S(1)} %get-tuple-element.273), channel_id=1, source_target_pairs={{0,8},{4,12},{8,0},{12,4},{16,24},{20,28},{24,16},{28,20},{1,9},{5... | collective-permute-start | bytes 442376 | tf_op jit(solution)/shard_map/ppermute | solution.py:648
  153.8 23.5 %collective-permute-start.71 = (bf16[96,768]{1,0:T(8,128)(2,1)S(1)}, bf16[96,768]{1,0:T(8,128)(2,1)S(1)}, u32[]{:S(2)}, u32[]{:S(2)}) collective-permute-start(bf16[96,768]{1,0:T(8,128)(2,1)S(1)} %get-tuple-element.275), channel_id=1, source_target_pairs={{0,16},{4,20},{8,24},{12,28},{16,0},{20,4},{24,8},{28,12},{1,17},{... | collective-permute-start | bytes 442376 | tf_op jit(solution)/shard_map/ppermute | solution.py:648
  158.2 20.8 %collective-permute-start.72 = (bf16[96,768]{1,0:T(8,128)(2,1)S(1)}, bf16[96,768]{1,0:T(8,128)(2,1)S(1)}, u32[]{:S(2)}, u32[]{:S(2)}) collective-permute-start(bf16[96,768]{1,0:T(8,128)(2,1)S(1)} %get-tuple-element.274), channel_id=1, source_target_pairs={{0,24},{4,28},{8,16},{12,20},{16,8},{20,12},{24,0},{28,4},{1,25},{... | collective-permute-start | bytes 442376 | tf_op jit(solution)/shard_map/ppermute | solution.py:648
  160.8 18.2 %collective-permute-start.59 = (bf16[96,768]{1,0:T(8,128)(2,1)S(1)}, bf16[96,768]{1,0:T(8,128)(2,1)S(1)}, u32[]{:S(2)}, u32[]{:S(2)}) collective-permute-start(bf16[96,768]{1,0:T(8,128)(2,1)S(1)} %get-tuple-element.276), channel_id=1, source_target_pairs={{0,8},{4,12},{8,0},{12,4},{16,24},{20,28},{24,16},{28,20},{1,9},{5... | collective-permute-start | bytes 442376 | tf_op jit(solution)/shard_map/ppermute | solution.py:648
  176.1 13.1 %collective-permute-start.60 = (bf16[96,768]{1,0:T(8,128)(2,1)S(1)}, bf16[96,768]{1,0:T(8,128)(2,1)S(1)}, u32[]{:S(2)}, u32[]{:S(2)}) collective-permute-start(bf16[96,768]{1,0:T(8,128)(2,1)S(1)} %get-tuple-element.278), channel_id=1, source_target_pairs={{0,16},{4,20},{8,24},{12,28},{16,0},{20,4},{24,8},{28,12},{1,17},{... | collective-permute-start | bytes 442376 | tf_op jit(solution)/shard_map/ppermute | solution.py:648
  179.1 27.7 %collective-permute-start.45 = (bf16[2,192,768]{2,1,0:T(8,128)(2,1)S(1)}, bf16[2,192,768]{2,1,0:T(8,128)(2,1)S(1)}, u32[]{:S(2)}, u32[]{:S(2)}) collective-permute-start(bf16[2,192,768]{2,1,0:T(8,128)(2,1)S(1)} %get-tuple-element.120), channel_id=1, source_target_pairs={{0,1},{1,0},{2,3},{3,2},{4,5},{5,4},{6,7},{7,6},{8,9},{9,8},{10,11... | collective-permute-start | bytes 1769480 | tf_op jit(solution)/shard_map/ppermute | solution.py:648
  179.1 29.5 %collective-permute-start.37 = (bf16[2,256,768]{2,1,0:T(8,128)(2,1)S(1)}, bf16[2,256,768]{2,1,0:T(8,128)(2,1)S(1)}, u32[]{:S(2)}, u32[]{:S(2)}) collective-permute-start(bf16[2,256,768]{2,1,0:T(8,128)(2,1)S(1)} %get-tuple-element.112), channel_id=1, source_target_pairs={{0,1},{1,0},{2,3},{3,2},{4,5},{5,4},{6,7},{7,6},{8,9},{9,8},{10,11... | collective-permute-start | bytes 2359304 | tf_op jit(solution)/shard_map/ppermute | solution.py:648
  189.2 15.5 %collective-permute-start.76 = (bf16[96,768]{1,0:T(8,128)(2,1)S(1)}, bf16[96,768]{1,0:T(8,128)(2,1)S(1)}, u32[]{:S(2)}, u32[]{:S(2)}) collective-permute-start(bf16[96,768]{1,0:T(8,128)(2,1)S(1)} %fusion.19.refs_0_), channel_id=1, source_target_pairs={{0,16},{4,20},{8,24},{12,28},{16,0},{20,4},{24,8},{28,12},{1,17},{... | collective-permute-start | bytes 442376 | tf_op jit(solution)/shard_map/ppermute | solution.py:648
  193.8 12.7 %collective-permute-start.78 = (bf16[96,768]{1,0:T(8,128)(2,1)S(1)}, bf16[96,768]{1,0:T(8,128)(2,1)S(1)}, u32[]{:S(2)}, u32[]{:S(2)}) collective-permute-start(bf16[96,768]{1,0:T(8,128)(2,1)S(1)} %fusion.19.refs_0_), channel_id=1, source_target_pairs={{0,24},{4,28},{8,16},{12,20},{16,8},{20,12},{24,0},{28,4},{1,25},{... | collective-permute-start | bytes 442376 | tf_op jit(solution)/shard_map/ppermute | solution.py:648
  197.3 13.6 %collective-permute-start.73 = (bf16[96,768]{1,0:T(8,128)(2,1)S(1)}, bf16[96,768]{1,0:T(8,128)(2,1)S(1)}, u32[]{:S(2)}, u32[]{:S(2)}) collective-permute-start(bf16[96,768]{1,0:T(8,128)(2,1)S(1)} %fusion.19.refs_0_), channel_id=1, source_target_pairs={{0,4},{4,0},{8,12},{12,8},{16,20},{20,16},{24,28},{28,24},{1,5},{5... | collective-permute-start | bytes 442376 | tf_op jit(solution)/shard_map/ppermute | solution.py:648
  208.6 12.5 %collective-permute-start.46 = (bf16[192,768]{1,0:T(8,128)(2,1)S(1)}, bf16[192,768]{1,0:T(8,128)(2,1)S(1)}, u32[]{:S(2)}, u32[]{:S(2)}) collective-permute-start(bf16[192,768]{1,0:T(8,128)(2,1)S(1)} %fusion.15), channel_id=1, source_target_pairs={{0,2},{1,3},{2,0},{3,1},{4,6},{5,7},{6,4},{7,5},{8,10},{9,11},{10,... | collective-permute-start | bytes 884744 | tf_op jit(solution)/shard_map/ppermute | solution.py:648
  210.9 41.0 %collective-permute-start.63 = (bf16[96,768]{1,0:T(8,128)(2,1)S(1)}, bf16[96,768]{1,0:T(8,128)(2,1)S(1)}, u32[]{:S(2)}, u32[]{:S(2)}) collective-permute-start(bf16[96,768]{1,0:T(8,128)(2,1)S(1)} %fusion.23.refs_0_), channel_id=1, source_target_pairs={{0,8},{4,12},{8,0},{12,4},{16,24},{20,28},{24,16},{28,20},{1,9},{5... | collective-permute-start | bytes 442376 | tf_op jit(solution)/shard_map/ppermute | solution.py:648
  212.3 40.0 %collective-permute-start.65 = (bf16[96,768]{1,0:T(8,128)(2,1)S(1)}, bf16[96,768]{1,0:T(8,128)(2,1)}, u32[]{:S(2)}, u32[]{:S(2)}) collective-permute-start(bf16[96,768]{1,0:T(8,128)(2,1)S(1)} %fusion.23.refs_0_), channel_id=1, source_target_pairs={{0,16},{4,20},{8,24},{12,28},{16,0},{20,4},{24,8},{28,12},{1,17},{... | collective-permute-start | bytes 442376 | tf_op jit(solution)/shard_map/ppermute | solution.py:648
  214.2 39.8 %collective-permute-start.67 = (bf16[96,768]{1,0:T(8,128)(2,1)S(1)}, bf16[96,768]{1,0:T(8,128)(2,1)}, u32[]{:S(2)}, u32[]{:S(2)}) collective-permute-start(bf16[96,768]{1,0:T(8,128)(2,1)S(1)} %fusion.23.refs_0_), channel_id=1, source_target_pairs={{0,24},{4,28},{8,16},{12,20},{16,8},{20,12},{24,0},{28,4},{1,25},{... | collective-permute-start | bytes 442376 | tf_op jit(solution)/shard_map/ppermute | solution.py:648
  215.7 12.8 %collective-permute-start.38 = (bf16[256,768]{1,0:T(8,128)(2,1)}, bf16[256,768]{1,0:T(8,128)(2,1)}, u32[]{:S(2)}, u32[]{:S(2)}) collective-permute-start(bf16[256,768]{1,0:T(8,128)(2,1)} %fusion.10), channel_id=1, source_target_pairs={{0,2},{1,3},{2,0},{3,1},{4,6},{5,7},{6,4},{7,5},{8,10},{9,11},{10,... | collective-permute-start | bytes 1179656 | tf_op jit(solution)/shard_map/ppermute | solution.py:648
  221.1 25.5 %collective-permute-start.28 = (bf16[256,768]{1,0:T(8,128)(2,1)}, bf16[256,768]{1,0:T(8,128)(2,1)}, u32[]{:S(2)}, u32[]{:S(2)}) collective-permute-start(bf16[256,768]{1,0:T(8,128)(2,1)} %fusion.8), channel_id=1, source_target_pairs={{0,2},{1,3},{2,0},{3,1},{4,6},{5,7},{6,4},{7,5},{8,10},{9,11},{10,... | collective-permute-start | bytes 1179656 | tf_op jit(solution)/shard_map/ppermute | solution.py:648
  228.5 25.9 %collective-permute-start.47 = (bf16[4,128,576]{1,2,0:T(8,128)(2,1)}, bf16[4,128,576]{1,2,0:T(8,128)(2,1)}, u32[]{:S(2)}, u32[]{:S(2)}) collective-permute-start(bf16[4,128,576]{1,2,0:T(8,128)(2,1)} %copy.62), channel_id=1, source_target_pairs={{0,4},{4,0},{8,12},{12,8},{16,20},{20,16},{24,28},{28,24},{1,5},{5... | collective-permute-start | bytes 1769480 | tf_op jit(solution)/shard_map/ppermute | solution.py:648
  260.6 13.8 %collective-permute-start.31 = (bf16[256,768]{1,0:T(8,128)(2,1)S(1)}, bf16[256,768]{1,0:T(8,128)(2,1)S(1)}, u32[]{:S(2)}, u32[]{:S(2)}) collective-permute-start(bf16[256,768]{1,0:T(8,128)(2,1)S(1)} %collective-permute-done.30.refs_2_), channel_id=1, source_target_pairs={{0,1},{1,0},{2,3},{3,2},{4,5},{5,4},{6,7},{7,6},{8,9},{9,8},{10,11... | collective-permute-start | bytes 1179656 | tf_op jit(solution)/shard_map/ppermute | solution.py:648
  263.5 18.8 %collective-permute-start.48 = (bf16[128,576]{1,0:T(8,128)(2,1)}, bf16[128,576]{1,0:T(8,128)(2,1)}, u32[]{:S(2)}, u32[]{:S(2)}) collective-permute-start(bf16[128,576]{1,0:T(8,128)(2,1)} %get-tuple-element.270), channel_id=1, source_target_pairs={{0,8},{4,12},{8,0},{12,4},{16,24},{20,28},{24,16},{28,20},{1,9},{5... | collective-permute-start | bytes 442376 | tf_op jit(solution)/shard_map/ppermute | solution.py:648
  265.1 17.2 %collective-permute-start.49 = (bf16[128,576]{1,0:T(8,128)(2,1)}, bf16[128,576]{1,0:T(8,128)(2,1)}, u32[]{:S(2)}, u32[]{:S(2)}) collective-permute-start(bf16[128,576]{1,0:T(8,128)(2,1)} %get-tuple-element.272), channel_id=1, source_target_pairs={{0,16},{4,20},{8,24},{12,28},{16,0},{20,4},{24,8},{28,12},{1,17},{... | collective-permute-start | bytes 442376 | tf_op jit(solution)/shard_map/ppermute | solution.py:648
  266.3 16.0 %collective-permute-start.50 = (bf16[128,576]{1,0:T(8,128)(2,1)}, bf16[128,576]{1,0:T(8,128)(2,1)}, u32[]{:S(2)}, u32[]{:S(2)}) collective-permute-start(bf16[128,576]{1,0:T(8,128)(2,1)} %get-tuple-element.271), channel_id=1, source_target_pairs={{0,24},{4,28},{8,16},{12,20},{16,8},{20,12},{24,0},{28,4},{1,25},{... | collective-permute-start | bytes 442376 | tf_op jit(solution)/shard_map/ppermute | solution.py:648
  268.1 14.0 %collective-permute-start.44 = (f32[40,128]{1,0:T(8,128)S(1)}, f32[40,128]{1,0:T(8,128)S(1)}, u32[]{:S(2)}, u32[]{:S(2)}) collective-permute-start(f32[40,128]{1,0:T(8,128)S(1)} %fusion.30), channel_id=1, source_target_pairs={{0,16},{4,20},{8,24},{12,28},{16,0},{20,4},{24,8},{28,12},{1,17},{... | collective-permute-start | bytes 61448 | tf_op jit(solution)/shard_map/ppermute | solution.py:648
  282.1 44.8 %collective-permute-start.39 = (bf16[256,768]{1,0:T(8,128)(2,1)}, bf16[256,768]{1,0:T(8,128)(2,1)}, u32[]{:S(2)}, u32[]{:S(2)}) collective-permute-start(bf16[256,768]{1,0:T(8,128)(2,1)} %get-tuple-element.114.refs_0_), channel_id=1, source_target_pairs={{0,1},{1,0},{2,3},{3,2},{4,5},{5,4},{6,7},{7,6},{8,9},{9,8},{10,11... | collective-permute-start | bytes 1179656 | tf_op jit(solution)/shard_map/ppermute | solution.py:648
  284.5 15.0 %collective-permute-start.54 = (bf16[128,576]{1,0:T(8,128)(2,1)S(1)}, bf16[128,576]{1,0:T(8,128)(2,1)S(1)}, u32[]{:S(2)}, u32[]{:S(2)}) collective-permute-start(bf16[128,576]{1,0:T(8,128)(2,1)S(1)} %fusion.14.refs_0_), channel_id=1, source_target_pairs={{0,16},{4,20},{8,24},{12,28},{16,0},{20,4},{24,8},{28,12},{1,17},{... | collective-permute-start | bytes 442376 | tf_op jit(solution)/shard_map/ppermute | solution.py:648
  287.0 13.1 %collective-permute-start.56 = (bf16[128,576]{1,0:T(8,128)(2,1)S(1)}, bf16[128,576]{1,0:T(8,128)(2,1)S(1)}, u32[]{:S(2)}, u32[]{:S(2)}) collective-permute-start(bf16[128,576]{1,0:T(8,128)(2,1)S(1)} %fusion.14.refs_0_), channel_id=1, source_target_pairs={{0,24},{4,28},{8,16},{12,20},{16,8},{20,12},{24,0},{28,4},{1,25},{... | collective-permute-start | bytes 442376 | tf_op jit(solution)/shard_map/ppermute | solution.py:648
  288.6 12.9 %collective-permute-start.51 = (bf16[128,576]{1,0:T(8,128)(2,1)S(1)}, bf16[128,576]{1,0:T(8,128)(2,1)S(1)}, u32[]{:S(2)}, u32[]{:S(2)}) collective-permute-start(bf16[128,576]{1,0:T(8,128)(2,1)S(1)} %fusion.14.refs_0_), channel_id=1, source_target_pairs={{0,4},{4,0},{8,12},{12,8},{16,20},{20,16},{24,28},{28,24},{1,5},{5... | collective-permute-start | bytes 442376 | tf_op jit(solution)/shard_map/ppermute | solution.py:648
  292.8 34.1 %collective-permute-start.41 = (bf16[256,768]{1,0:T(8,128)(2,1)}, bf16[256,768]{1,0:T(8,128)(2,1)}, u32[]{:S(2)}, u32[]{:S(2)}) collective-permute-start(bf16[256,768]{1,0:T(8,128)(2,1)} %collective-permute-done.40.refs_2_), channel_id=1, source_target_pairs={{0,1},{1,0},{2,3},{3,2},{4,5},{5,4},{6,7},{7,6},{8,9},{9,8},{10,11... | collective-permute-start | bytes 1179656 | tf_op jit(solution)/shard_map/ppermute | solution.py:648
  (113 other events, 1101.2 us)

commit v2 on v1

v2 whole, which is shorter than its diff:
```python
import math

import jax
import jax.numpy as jnp
from jax import lax
from jax.experimental import pallas as pl
from jax.experimental.pallas import tpu as pltpu
from jax.sharding import PartitionSpec as P

HD = 64
EPS = 1e-05
DECAY = 0.5
MAT_RATE = 0.5
VEC_RATE = 0.05
UNIT_RATE = 0.3
GELU_A = math.sqrt(2.0 / math.pi)
GELU_B = 0.044715
BF = jnp.bfloat16
F32 = jnp.float32
VMEM = 22 * 1024 * 1024
WAYS = 8
RATE = 4e8
TICK = 5
BLK = 256
ORDER = (0, 4, 2, 6)


def full(shape):
    return pl.BlockSpec(shape, lambda *args: (0,) * len(shape))


def fulls(arrays):
    return [full(x.shape) for x in arrays]


def run(kernel, grid, ins, in_specs, outs, out_specs, idx, name, micros, scratch=(), after=(), hbm=()):
    count, kernel_in = len(ins), kernel
    ins = [pltpu.with_memory_space_constraint(x, pltpu.HBM) if i in hbm else x for i, x in enumerate(ins)]

    def kernel(idx, *refs):
        kernel_in(idx, *refs[:count], *refs[count + len(after) :])

    return pl.pallas_call(
        kernel,
        grid_spec=pltpu.PrefetchScalarGridSpec(
            num_scalar_prefetch=1,
            grid=grid,
            in_specs=list(in_specs) + [pl.BlockSpec(memory_space=pl.ANY)] * len(after),
            out_specs=out_specs,
            scratch_shapes=list(scratch),
        ),
        out_shape=outs,
        compiler_params=pltpu.CompilerParams(vmem_limit_bytes=VMEM),
        cost_estimate=pl.CostEstimate(flops=int(micros * RATE), bytes_accessed=1024, transcendentals=0),
        name=name,
    )(idx, *ins, *after)


def sds(shape, dtype):
    return jax.ShapeDtypeStruct(shape, dtype)


def near(shape, dtype):
    return pltpu.VMEM(shape, dtype)


def far(shape, dtype):
    return pltpu.HBM(shape, dtype)


def dot(x, y):
    return jnp.dot(x, y, preferred_element_type=F32)


def dot_nt(x, y):
    return lax.dot_general(x, y, (((1,), (1,)), ((), ())), preferred_element_type=F32)


def dot_tn(x, y):
    return lax.dot_general(x, y, (((0,), (0,)), ((), ())), preferred_element_type=F32)


def rowsum(x):
    return jnp.sum(x, -1, keepdims=True)


def normalize(x):
    n = x.shape[-1]
    off = x - rowsum(x) / n
    r = lax.rsqrt(rowsum(off * off) / n + EPS)
    return off * r, r


def gelu_parts(u):
    t = jnp.tanh(GELU_A * (u + GELU_B * (u * u * u)))
    return 0.5 * u * (1.0 + t), t


def unpack_rows(side, wide):
    groups = wide // side.shape[1]
    rows = side.shape[0] // groups
    return jnp.concatenate([side[i * rows : (i + 1) * rows] for i in range(groups)], axis=1)


def pack_rows(block, groups):
    n = block.shape[1] // groups
    return jnp.concatenate([block[:, i * n : (i + 1) * n] for i in range(groups)], axis=0)


def project_kernel(idx, a_ref, an_ref, *refs):
    pieces = refs[:WAYS]
    q_ref, k_ref, v_ref, wq_ref, wo_ref, scr = refs[WAYS:]
    rows = wq_ref.shape[0] // WAYS
    orows = scr.shape[0] // WAYS
    hw = q_ref.shape[1]

    @pl.when(pl.program_id(0) == 0)
    def _():
        for k in range(WAYS):
            j = jnp.bitwise_xor(idx[0], k)
            wq_ref[pl.ds(pl.multiple_of(j * rows, rows), rows), :] = pieces[k][:, : 3 * hw]
            tail = pieces[k][:, 3 * hw :].astype(F32)
            scr[pl.ds(pl.multiple_of(j * orows, orows), orows), :] = unpack_rows(tail, wo_ref.shape[1])
        wo_ref[:hw, :] = scr[...].astype(BF)
        norm = jnp.concatenate([an_ref[0:1, :], an_ref[1:2, :]], axis=1)
        high = norm.astype(BF).astype(F32)
        row = jnp.concatenate([high, norm - high], axis=1)
        pad = wo_ref.shape[0] - hw
        at = lax.broadcasted_iota(jnp.int32, (pad, row.shape[1]), 0)
        wo_ref[hw:, :] = jnp.where(at == 0, row, 0.0).astype(BF)

    res = dot(a_ref[...], wq_ref[...]).astype(BF)
    q_ref[...] = res[:, :hw] * BF(HD ** (-0.5))
    k_ref[...] = res[:, hw : 2 * hw]
    v_ref[...] = res[:, 2 * hw :]


def project(a, norm, pieces, hw, idx):
    rows, d = a.shape
    n = 3 * hw
    blk = lambda w: pl.BlockSpec((BLK, w), lambda s, i: (s, 0))
    return run(
        project_kernel,
        (rows // BLK,),
        [a, norm, *pieces],
        [blk(d), full(norm.shape)] + fulls(pieces),
        [far((rows, hw), BF)] * 3 + [far((d, n), BF), far((hw + 16, d), BF)],
        [blk(hw)] * 3 + [full((d, n)), full((hw + 16, d))],
        idx,
        "project",
        40,
        [pltpu.VMEM((hw, d), F32)],
    )


def attend_kernel(idx, start_ref, q_ref, k_ref, v_ref, o_ref, p_ref):
    h = pl.program_id(0)
    rows, hw = q_ref.shape
    lane = (lax.broadcasted_iota(jnp.int32, (1, hw), 1) // HD) == h
    for i in range(rows // BLK):
        lo, hi = i * BLK, (i + 1) * BLK
        qb = jnp.where(lane, q_ref[lo:hi, :], BF(0))
        s = dot_nt(qb, k_ref[:hi, :])
        kpos = lax.broadcasted_iota(jnp.int32, (BLK, hi), 1)
        qpos = lo + lax.broadcasted_iota(jnp.int32, (BLK, hi), 0)
        s = jnp.where((kpos >= start_ref[lo:hi, :]) & (kpos <= qpos), s, -1e30)
        p = jnp.exp(s - jnp.max(s, -1, keepdims=True))
        p = (p * (1.0 / rowsum(p))).astype(BF)
        p_ref[0, lo:hi, :hi] = p
        ob = dot(p, v_ref[:hi, :]).astype(BF)
        o_ref[lo:hi, :] = jnp.where(lane, ob, o_ref[lo:hi, :])


def attend(start, q, k, v, idx, after=()):
    rows, hw = q.shape
    heads = hw // HD
    return run(
        attend_kernel,
        (heads,),
        [start, q, k, v],
        fulls([start, q, k, v]),
        [far((rows, hw), BF), far((heads, rows, rows), BF)],
        [full((rows, hw)), pl.BlockSpec((1, rows, rows), lambda s, i: (s, 0, 0))],
        idx,
        "attend",
        10,
        after=after,
        hbm=(1, 2, 3),
    )


def wide_norm(o_refs):
    parts = [x[...].astype(F32) for x in o_refs]
    n = sum(x.shape[-1] for x in parts)
    mean = sum(rowsum(x) for x in parts) / n
    parts = [x - mean for x in parts]
    r = lax.rsqrt(sum(rowsum(x * x) for x in parts) / n + EPS)
    return [x * r for x in parts], r


def unpack_norm(w_ref):
    hw = w_ref.shape[0] - 16
    row = w_ref[hw:, :].astype(F32)[0:1, :]
    gain, bias, gain_low, bias_low = (row[:, i * hw : (i + 1) * hw] for i in range(4))
    return gain + gain_low, bias + bias_low


def outproj_kernel(idx, on_ref, tok_ref, *refs):
    g = (len(refs) - 2) // 2
    o_refs, w_refs = refs[:g], refs[g : 2 * g]
    h_ref, c_ref = refs[2 * g :]
    hats, _ = wide_norm(o_refs)
    acc = tok_ref[...].astype(F32)
    for k in range(g):
        gain, bias = unpack_norm(w_refs[k])
        y = (hats[k] * gain + bias).astype(BF)
        acc = acc + dot(y, w_refs[k][: gain.shape[1], :])
    h_ref[...] = acc
    hat, _ = normalize(acc)
    c_ref[...] = (hat * on_ref[2:3, :] + on_ref[3:4, :]).astype(BF)


def outproj(on, tok, o, w, idx, after=()):
    rows, d = tok.shape
    hw = o[0].shape[1]
    blk = lambda n: pl.BlockSpec((BLK, n), lambda s, i: (s, 0))
    return run(
        outproj_kernel,
        (rows // BLK,),
        [on, tok, *o, *w],
        fulls([on]) + [blk(d)] + [blk(hw)] * len(o) + fulls(w),
        [far((rows, d), F32), near((rows, d), BF)],
        [blk(d), blk(d)],
        idx,
        "outproj",
        0,
        after=after,
        hbm=range(1, 2 + 2 * len(o)),
    )


def ffn_up_kernel(idx, c_ref, e_ref, fn_ref, *refs):
    ups, downs = refs[:2], refs[2:6]
    u_ref, dw_ref, st_ref, wu_ref, wd_ref = refs[6:]
    rows = ups[0].shape[1]

    @pl.when(pl.program_id(0) == 0)
    def _():
        for i, k in enumerate(ORDER):
            for odd in range(2):
                j = jnp.bitwise_xor(idx[0], k + odd)
                at = pl.ds(pl.multiple_of(j * rows, rows), rows)
                wu_ref[at, :] = ups[odd][i]
                wd_ref[at, :] = downs[i][odd]

    u = dot(c_ref[...], wu_ref[...])
    u_ref[...] = u
    z, _ = gelu_parts(u)
    mean = rowsum(z) / z.shape[-1]
    z = z - mean
    dw = dot_nt(e_ref[...], wd_ref[...])
    dw_ref[...] = dw
    eg = dw * fn_ref[0:1, :]
    stats = [mean, rowsum(z * z), rowsum(eg), rowsum(eg * z)]
    place = lax.broadcasted_iota(jnp.int32, (BLK, 128), 1)
    tile = jnp.zeros((BLK, 128), F32)
    for i, x in enumerate(stats):
        tile = jnp.where(place == i, x, tile)
    st_ref[...] = tile.T[:8, :]


def ffn_up(c, e, fn, pieces, idx):
    rows, d = c.shape
    fl = fn.shape[1]
    rblk = lambda n: pl.BlockSpec((BLK, n), lambda s, i: (s, 0))
    return run(
        ffn_up_kernel,
        (rows // BLK,),
        [c, e, fn, *pieces],
        [rblk(d), rblk(d), full(fn.shape)] + fulls(pieces),
        [near((rows, fl), F32), near((rows, fl), F32), sds((8, rows), F32), near((d, fl), BF), far((fl, d), BF)],
        [rblk(fl), rblk(fl), pl.BlockSpec((8, BLK), lambda s, i: (0, s)), full((d, fl)), full((fl, d))],
        idx,
        "ffn_up",
        7.5,
        hbm=(1,) + tuple(range(3, 9)),
    )


def rel_of(s):
    return jnp.where(s < 2, 2 * s + 1, 2 * s - 4)


def rel_block(s, i):
    return jnp.bitwise_xor(rel_of(s), i[1])


def rel_spec(n):
    return pl.BlockSpec((BLK, n), lambda s, i: (rel_block(s, i), 0))


SEND_SPEC = lambda n: pl.BlockSpec((1, BLK, n), lambda s, i: (jnp.minimum(s, 1), 0, 0))
KEEP_SPEC = lambda n: pl.BlockSpec((1, BLK, n), lambda s, i: (jnp.maximum(s - 2, 0), 0, 0))


def put_rel(send_ref, keep_ref, value):
    @pl.when(pl.program_id(0) < 2)
    def _():
        send_ref[0] = value.astype(BF)

    @pl.when(pl.program_id(0) >= 2)
    def _():
        keep_ref[0] = value


def ffn_mid_kernel(idx, u_ref, dw_ref, st_ref, fn_ref, wu_ref, w_ref, du_ref, send_ref, keep_ref, fg_ref):
    g = st_ref.shape[0]
    fl = u_ref.shape[1]
    n = g * fl
    st = [st_ref[k] for k in range(g)]
    mean = sum(x[0:1] for x in st) / g
    gap = [x[0:1] - mean for x in st]
    spread = sum(x[1:2] + fl * (gp * gp) for x, gp in zip(st, gap)) / n
    r = lax.rsqrt(spread + EPS)
    s_plain = sum(x[2:3] for x in st) / n
    s_norm = r * (sum(x[3:4] + gp * x[2:3] for x, gp in zip(st, gap)) / n)
    cols = jnp.concatenate([mean, r, s_plain, s_norm, jnp.zeros((124, BLK), F32)], axis=0).T
    mean, r, s_plain, s_norm = (cols[:, i : i + 1] for i in range(4))
    u = u_ref[...]
    z, t = gelu_parts(u)
    hat = (z - mean) * r
    w_ref[...] = (hat * fn_ref[0:1, :] + fn_ref[1:2, :]).astype(BF)
    dw = dw_ref[...]
    dz = r * (dw * fn_ref[0:1, :] - s_plain - hat * s_norm)
    slope = 0.5 * (1.0 + t) + 0.5 * u * (1.0 - t * t) * (GELU_A * (1.0 + (3.0 * GELU_B) * (u * u)))
    du = (dz * slope).astype(BF)
    du_ref[...] = du
    put_rel(send_ref, keep_ref, dot_nt(du, wu_ref[...]))
    grads = jnp.concatenate([jnp.sum(dw * hat, 0, keepdims=True), jnp.sum(dw, 0, keepdims=True)], axis=0)

    @pl.when(pl.program_id(0) == 0)
    def _():
        fg_ref[...] = grads

    @pl.when(pl.program_id(0) > 0)
    def _():
        fg_ref[...] += grads


def ffn_mid(u, dw, st, fn, wu, idx):
    rows, fl = u.shape
    d = wu.shape[0]
    return run(
        ffn_mid_kernel,
        (rows // BLK,),
        [u, dw, st, fn, wu],
        [rel_spec(fl), rel_spec(fl), pl.BlockSpec((st.shape[0], 8, BLK), lambda s, i: (0, 0, rel_block(s, i)))]
        + fulls([fn, wu]),
        [far((rows, fl), BF), far((rows, fl), BF), sds((2, BLK, d), BF), far((2, BLK, d), F32), sds((2, fl), F32)],
        [rel_spec(fl), rel_spec(fl), SEND_SPEC(d), KEEP_SPEC(d), full((2, fl))],
        idx,
        "ffn_mid",
        6.5,
    )


def ffn_out(x, w, idx, after):
    rows, depth = x.shape
    d = w.shape[1]

    def kernel(idx, x_ref, w_ref, send_ref, keep_ref):
        put_rel(send_ref, keep_ref, dot(x_ref[...], w_ref[...]))

    return run(
        kernel,
        (rows // BLK,),
        [x, w],
        [rel_spec(depth), full(w.shape)],
        [sds((2, BLK, d), BF), far((2, BLK, d), F32)],
        [SEND_SPEC(d), KEEP_SPEC(d)],
        idx,
        "ffn_out",
        0,
        (),
        after,
        (0, 1),
    )


def put_blocks(scr, send_ref, keep_ref, first, step):
    for i, k in enumerate(ORDER):
        for odd, dest in enumerate((keep_ref, send_ref)):
            j = jnp.bitwise_xor(first, k + odd)
            value = scr[pl.ds(pl.multiple_of(j * step, step), step), :]
            dest[i, :, : value.shape[1]] = value.astype(dest.dtype)


def weight_grad(x, y, idx, name, after=()):
    rows, d = x.shape
    n = y.shape[1]
    step = d // WAYS
    steps = d // BLK

    def kernel(idx, x_ref, y_ref, send_ref, keep_ref, scr):
        s = pl.program_id(0)
        scr[pl.ds(pl.multiple_of(s * BLK, BLK), BLK), :] = dot_tn(x_ref[...], y_ref[...])

        @pl.when(s == steps - 1)
        def _():
            put_blocks(scr, send_ref, keep_ref, idx[0], step)

    return run(
        kernel,
        (steps,),
        [x, y],
        [pl.BlockSpec((rows, BLK), lambda s, i: (0, s)), full(y.shape)],
        [sds((WAYS // 2, step, n), BF), far((WAYS // 2, step, n), F32)],
        [full((WAYS // 2, step, n))] * 2,
        idx,
        name,
        3.5,
        [pltpu.VMEM((d, n), F32)],
        after,
    )


def qkv_back(a, dqkv, wq, go, idx, after=()):
    rows, d = a.shape
    n = dqkv.shape[1]
    step = d // WAYS
    hw = go[2].shape[0]
    groups = d // hw
    orows = hw // WAYS

    def kernel(idx, a_ref, d_ref, w_ref, go0_ref, go1_ref, go2_ref, gs_ref, gk_ref, send_ref, keep_ref, scr, go_ref):
        go_ref[...] = go0_ref[0] + go1_ref[0].astype(F32) + go2_ref[...].astype(F32)
        for s in range(d // BLK):
            scr[s * BLK : (s + 1) * BLK, :] = dot_tn(a_ref[:, s * BLK : (s + 1) * BLK], d_ref[...])
        put_blocks(scr, gs_ref, gk_ref, idx[0], step)
        for i, k in enumerate(ORDER):
            for odd, dest in enumerate((gk_ref, gs_ref)):
                j = jnp.bitwise_xor(idx[0], k + odd)
                tail = pack_rows(go_ref[pl.ds(pl.multiple_of(j * orows, orows), orows), :], groups)
                dest[i, :, n:] = tail.astype(dest.dtype)
        for k in range(4):
            j = jnp.bitwise_xor(idx[1], k)
            dest = send_ref if k % 2 else keep_ref
            value = dot_nt(d_ref[pl.ds(pl.multiple_of(j * BLK, BLK), BLK), :], w_ref[...])
            dest[k // 2] = value.astype(dest.dtype)

    ins = [a, dqkv, wq, *go]
    lead = pl.BlockSpec((1, hw, d), lambda s, i: (0, 0, 0))
    half = (WAYS // 2, step, d)
    part = (2, BLK, d)
    outs = [sds(half, BF), far(half, F32), sds(part, BF), far(part, F32)]
    return run(
        kernel, (1,), ins, fulls(ins[:3]) + [lead, lead, full(go[2].shape)], outs, fulls(outs), idx, "qkv_back", 5.5,
        [pltpu.VMEM((d, n), F32), pltpu.VMEM((hw, d), F32)],
        after=after,
        hbm=(0, 2, 3),
    )


def shard_back_kernel(idx, dc0_ref, dc1_ref, dc2_ref, h_ref, e_ref, on_ref, *refs):
    g = 4
    o_refs, w_refs = refs[:g], refs[g : 2 * g]
    dh_ref, ol_ref, ag_ref, *do_refs = refs[2 * g :]
    do_refs, (gs_ref, gk_ref) = do_refs[:g], do_refs[g:]
    dc = dc0_ref[0] + dc1_ref[0].astype(F32) + dc2_ref[...].astype(F32)
    hat, r = normalize(h_ref[...])
    wgt = dc * on_ref[2:3, :]
    n = dc.shape[-1]
    dh = e_ref[...].astype(F32) + r * (wgt - rowsum(wgt) / n - hat * (rowsum(wgt * hat) / n))
    dh_ref[...] = dh
    ol_ref[...] = jnp.concatenate([jnp.sum(dc * hat, 0, keepdims=True), jnp.sum(dc, 0, keepdims=True)], axis=0)
    dhb = dh.astype(BF)
    hats, r = wide_norm(o_refs)
    norms = [unpack_norm(w_refs[k]) for k in range(g)]
    dys = [dot_nt(dhb, w_refs[k][: norms[k][0].shape[1], :]) for k in range(g)]
    wgts = [dys[k] * norms[k][0] for k in range(g)]
    s_plain = sum(rowsum(x) for x in wgts) / n
    s_norm = sum(rowsum(x * y) for x, y in zip(wgts, hats)) / n
    for k in range(g):
        do_refs[k][...] = (r * (wgts[k] - s_plain - hats[k] * s_norm)).astype(BF)
        ag_ref[jnp.bitwise_xor(idx[1], k)] = jnp.concatenate(
            [jnp.sum(dys[k] * hats[k], 0, keepdims=True), jnp.sum(dys[k], 0, keepdims=True)], axis=0
        )
    for k in range(g):
        y = (hats[k] * norms[k][0] + norms[k][1]).astype(BF)
        dest = gs_ref if k % 2 else gk_ref
        dest[k // 2] = dot_tn(y, dhb).astype(dest.dtype)


def shard_back(dc_keep, dc_one, dc_two, h, e, on, o, w, idx, after):
    rows, d = h.shape
    g = len(o)
    hw = o[0].shape[1]
    mine = lambda n: pl.BlockSpec((BLK, n), lambda s, i: (i[1], 0))
    lead = pl.BlockSpec((1, BLK, d), lambda s, i: (0, 0, 0))
    ins = [dc_keep, dc_one, dc_two, h, e, on, *o, *w]
    return run(
        shard_back_kernel,
        (1,),
        ins,
        [lead, lead, full((BLK, d)), mine(d), mine(d)] + fulls([on]) + [mine(hw)] * g + fulls(w),
        [far((BLK, d), F32), sds((2, d), F32), sds((g, 2, hw), F32)]
        + [sds((BLK, hw), BF)] * g
        + [sds((2, hw, d), BF), far((2, hw, d), F32)],
        [full((BLK, d)), full((2, d)), full((g, 2, hw))]
        + [full((BLK, hw))] * g
        + [full((2, hw, d))] * 2,
        idx,
        "shard_back",
        0,
        after=after,
        hbm=(0, 1, 2, 3, 4) + tuple(range(6, 6 + 2 * g)),
    )


def attend_back_kernel(idx, q_ref, k_ref, v_ref, p_ref, *refs):
    d_refs = refs[:4]
    out_ref, do_scr, dq_scr, dk_scr, dv_scr = refs[4:]
    h = pl.program_id(0)
    rows, hw = q_ref.shape

    @pl.when(h == 0)
    def _():
        for k in range(4):
            j = jnp.bitwise_xor(idx[1], k)
            do_scr[pl.ds(pl.multiple_of(j * BLK, BLK), BLK), :] = d_refs[k][...]
        dk_scr[...] = jnp.zeros_like(dk_scr)
        dv_scr[...] = jnp.zeros_like(dv_scr)
        dq_scr[...] = jnp.zeros_like(dq_scr)

    lane = (lax.broadcasted_iota(jnp.int32, (1, hw), 1) // HD) == h
    for i in range(rows // BLK):
        lo, hi = i * BLK, (i + 1) * BLK
        dob = jnp.where(lane, do_scr[lo:hi, :], BF(0))
        qb = jnp.where(lane, q_ref[lo:hi, :], BF(0))
        pb = p_ref[0, lo:hi, :hi]
        p = pb.astype(F32)
        dp = dot_nt(dob, v_ref[:hi, :])
        ds = (p * (dp - rowsum(p * dp))).astype(BF)
        dq_scr[lo:hi, :] = jnp.where(lane, dot(ds, k_ref[:hi, :]), dq_scr[lo:hi, :])
        dk_scr[:hi, :] += dot_tn(ds, qb)
        dv_scr[:hi, :] += dot_tn(pb, dob)

    @pl.when(h == pl.num_programs(0) - 1)
    def _():
        out_ref[...] = jnp.concatenate([dq_scr[...] * HD ** (-0.5), dk_scr[...], dv_scr[...]], axis=1).astype(BF)


def attend_back(q, k, v, p, do, idx, after):
    rows, hw = q.shape
    heads = hw // HD
    return run(
        attend_back_kernel,
        (heads,),
        [q, k, v, p, *do],
        fulls([q, k, v]) + [pl.BlockSpec((1, rows, rows), lambda s, i: (s, 0, 0))] + fulls(do),
        [sds((rows, 3 * hw), BF)],
        [full((rows, 3 * hw))],
        idx,
        "attend_back",
        11,
        [pltpu.VMEM((rows, hw), BF)] + [pltpu.VMEM((rows, hw), F32)] * 3,
        after=after,
        hbm=range(8),
    )[0]


def shard_end_kernel(idx, da0_ref, da1_ref, da2_ref, tok_ref, on_ref, dh_ref, gt_ref, oe_ref):
    da = da0_ref[0] + da1_ref[0].astype(F32) + da2_ref[...].astype(F32)
    hat, r = normalize(tok_ref[...].astype(F32))
    wgt = da * on_ref[0:1, :]
    n = da.shape[-1]
    grad = r * (wgt - rowsum(wgt) / n - hat * (rowsum(wgt * hat) / n))
    gt_ref[...] = (dh_ref[...] + grad).astype(BF)
    oe_ref[...] = jnp.concatenate([jnp.sum(da * hat, 0, keepdims=True), jnp.sum(da, 0, keepdims=True)], axis=0)


def shard_end(da_keep, da_one, da_two, tok, on, dh, idx, after=()):
    d = tok.shape[1]
    lead = pl.BlockSpec((1, BLK, d), lambda s, i: (0, 0, 0))
    return run(
        shard_end_kernel,
        (1,),
        [da_keep, da_one, da_two, tok, on, dh],
        [lead, lead, full((BLK, d)), pl.BlockSpec((BLK, d), lambda s, i: (i[1], 0)), full(on.shape), full((BLK, d))],
        [sds((BLK, d), BF), sds((2, d), F32)],
        [full((BLK, d)), full((2, d))],
        idx,
        "shard_end",
        0,
        after=after,
    )


def spread_rows(parts, idx, name, after=()):
    rows, d = parts[0].shape

    def kernel(idx, *refs):
        for k, part in enumerate(refs[:-1]):
            at = pl.ds(pl.multiple_of(jnp.bitwise_xor(idx[1], k) * rows, rows), rows)
            refs[-1][at, :] = part[...]

    out = (rows * len(parts), d)
    return run(kernel, (1,), parts, fulls(parts), [far(out, BF)], [full(out)], idx, name, 2, (), after)[0]


def far_sum(keep, got, idx, after=(), tick=TICK):
    rows, d = keep.shape[1:]

    def kernel(idx, keep_ref, got_ref, out_ref):
        out_ref[...] = (keep_ref[0] + got_ref[0].astype(F32)).astype(BF)

    second = pl.BlockSpec((1, rows, d), lambda s, i: (1, 0, 0))
    out = [sds((rows, d), BF)]
    return run(kernel, (1,), [keep, got], [second] * 2, out, fulls(out), idx, "far_sum", tick, (), after)[0]


def fold(keep, got, idx, after=(), tick=TICK):
    count, rows, d = keep.shape
    half = count // 2

    def kernel(idx, keep_ref, got_ref, stay_ref, send_ref):
        stay_ref[...] = keep_ref[:half] + got_ref[:half].astype(F32)
        send = (keep_ref[half:] + got_ref[half:].astype(F32)).astype(BF)
        send_ref[...] = send if half > 1 else send[0]

    outs = [sds((half, rows, d), F32), sds((half, rows, d) if half > 1 else (rows, d), BF)]
    return run(kernel, (1,), [keep, got], fulls([keep, got]), outs, fulls(outs), idx, "fold", tick, (), after)


def close(own, got, idx, after=(), vec=None):
    rows, d = got[0].shape

    def kernel(idx, own_ref, *refs):
        out_ref = refs[-1]
        total = own_ref[...].reshape(rows, d)
        for ref in refs[: len(got)]:
            total = total + ref[...].astype(F32)
        out_ref[:rows, :] = total.astype(BF)
        if vec is not None:
            x = refs[len(got)][...]
            high = x.astype(BF).astype(F32)
            out_ref[rows:, :] = jnp.concatenate([high, x - high], axis=0).astype(BF)

    ins = [own, *got] + ([] if vec is None else [vec])
    out = [sds((rows if vec is None else rows + 2 * vec.shape[0], d), BF)]
    return run(kernel, (1,), ins, fulls(ins), out, fulls(out), idx, "close", TICK, (), after)[0]


def join(parts, idx, after=()):
    shapes = [x.shape if len(x.shape) == 3 else (1, *x.shape) for x in parts]

    def kernel(idx, *refs):
        at = 0
        for ref, shape in zip(refs, shapes):
            refs[-1][at : at + shape[0]] = ref[...].reshape(shape)
            at += shape[0]

    out = [sds((sum(x[0] for x in shapes), *shapes[0][1:]), BF)]
    return run(kernel, (1,), parts, fulls(parts), out, fulls(out), idx, "join", 2 * TICK, (), after)[0]


def block_end(h, keep, got, last, idx, after=()):
    rows, d = last.shape

    def kernel(idx, h_ref, keep_ref, got_ref, last_ref, out_ref):
        total = h_ref[...] + keep_ref[0] + got_ref[0].astype(F32) + last_ref[...].astype(F32)
        out_ref[...] = total.astype(BF)

    lead = pl.BlockSpec((1, rows, d), lambda s, i: (0, 0, 0))
    mine = pl.BlockSpec((rows, d), lambda s, i: (i[1], 0))
    ins = [h, keep, got, last]
    out = [sds((rows, d), BF)]
    return run(
        kernel, (1,), ins, [mine, lead, lead, full((rows, d))], out, fulls(out), idx, "block_end", TICK, (), after, (0,)
    )[0]


def vec_add(x, y, idx, after=()):
    def kernel(idx, x_ref, y_ref, out_ref):
        out_ref[...] = x_ref[...] + y_ref[...]

    out = [sds(x.shape, F32)]
    return run(kernel, (1,), [x, y], fulls([x, y]), out, fulls(out), idx, "vec_add", TICK, (), after)[0]


def one_hot(place, count, width):
    at = lax.broadcasted_iota(jnp.int32, (count, width), 1)
    want = place * count + lax.broadcasted_iota(jnp.int32, (count, width), 0)
    return jnp.where(at == want, 1.0, 0.0).astype(BF)


def precondition(idx, ins, outs, scr, total, flip):
    w_ref, l_ref, r_ref, lr_ref, rr_ref = ins
    g_ref, nl_ref, nr_ref, nw_ref, copy_ref = outs
    d, n = scr.shape
    rows, side = w_ref.shape[0], r_ref.shape[0]
    whole = scr[...]
    g_ref[...] = whole.T if flip else whole
    grad = whole.astype(BF)
    scale = 1.0 / total
    own_cols = dot_nt(one_hot(idx[2], side, n), grad).astype(BF)
    own_rows = dot(one_hot(idx[2], rows, d), grad).astype(BF)
    nr_ref[...] = DECAY * r_ref[...] + ((1.0 - DECAY) * scale * scale) * dot(own_cols, grad)
    nl_ref[...] = DECAY * l_ref[...] + ((1.0 - DECAY) * scale * scale) * dot_nt(own_rows, grad)
    part = dot(lr_ref[...].astype(BF), grad).astype(BF)
    new = w_ref[...] - (MAT_RATE * scale) * dot(part, rr_ref[...].astype(BF))
    nw_ref[...] = new
    copy_ref[...] = new.astype(BF)


def update_outs(mats):
    w, left, right = mats[:3]
    (rows, n), d, side = w.shape, left.shape[1], right.shape[0]
    flip = n % 128 != 0
    outs = [sds((n, d) if flip else (d, n), F32), sds((rows, d), F32), sds((side, n), F32)]
    return outs + [sds((rows, n), F32), sds((rows, n), BF)], flip, pltpu.VMEM((d, n), F32)


def update_one(mats, near_blocks, far_blocks, total, idx, name, after=()):
    outs, flip, scr = update_outs(mats)
    step = mats[1].shape[1] // WAYS

    def kernel(idx, *refs):
        ins, (even, odd), rest = refs[:5], refs[5:7], refs[7:]
        for i, k in enumerate(ORDER):
            for far_one, blocks in enumerate((even, odd)):
                j = jnp.bitwise_xor(idx[0], k + far_one)
                rest[5][pl.ds(pl.multiple_of(j * step, step), step), :] = blocks[i].astype(F32)
        precondition(idx, ins, rest[:5], rest[5], total, flip)

    ins = [*mats, near_blocks, far_blocks]
    res = run(kernel, (1,), ins, fulls(ins), outs, fulls(outs), idx, name, 4, [scr], after, range(7))
    return [res[0].T if flip else res[0], *res[1:]]


def update_pair(mats, mats2, near_blocks, far_blocks, params, rates, total, idx, name, after=()):
    outs, flip, scr = update_outs(mats)
    outs2, flip2, scr2 = update_outs(mats2)
    step, n = mats[1].shape[1] // WAYS, mats[0].shape[1]
    step2, n2 = mats2[1].shape[1] // WAYS, mats2[0].shape[1]
    half = params.shape[0]

    def kernel(idx, *refs):
        ins, ins2, (even, odd), par_ref, rest = refs[:5], refs[5:10], refs[10:12], refs[12], refs[13:]
        sums = 0.0
        for i, k in enumerate(ORDER):
            for far_one, blocks in enumerate((even, odd)):
                j = jnp.bitwise_xor(idx[0], k + far_one)
                block = blocks[i].astype(F32)
                rest[-2][pl.ds(pl.multiple_of(j * step, step), step), :] = block[:step, :n]
                rest[-1][pl.ds(pl.multiple_of(j * step2, step2), step2), :] = unpack_rows(block[:step, n:], n2)
                sums = sums + (block[step : step + half] + block[step + half :])
        at = lax.broadcasted_iota(jnp.int32, sums.shape, 0) * sums.shape[1]
        at = at + lax.broadcasted_iota(jnp.int32, sums.shape, 1)
        slow, fast, border = rates
        rest[10][...] = sums
        rest[11][...] = par_ref[...] - jnp.where(at < border, slow, fast) * sums
        precondition(idx, ins2, rest[5:10], rest[-1], total, flip2)
        precondition(idx, ins, rest[:5], rest[-2], total, flip)

    all_outs = outs + outs2 + [sds(params.shape, F32)] * 2
    ins = [*mats, *mats2, near_blocks, far_blocks, params]
    res = run(kernel, (1,), ins, fulls(ins), all_outs, fulls(all_outs), idx, name, 6, [scr, scr2], after, range(13))
    res = list(res)
    res[0] = res[0].T if flip else res[0]
    res[5] = res[5].T if flip2 else res[5]
    return res[:5], res[5:10], res[10], res[11]


def body(
    tokens,
    cotangent,
    doc_lengths,
    outer_norms,
    attn_norm,
    ffn_norm,
    w_qkv,
    left_qkv,
    right_qkv,
    left_root_qkv,
    right_root_qkv,
    w_out,
    left_out,
    right_out,
    left_root_out,
    right_root_out,
    w_up,
    left_up,
    right_up,
    left_root_up,
    right_root_up,
    w_down,
    left_down,
    right_down,
    left_root_down,
    right_root_down,
):
    row_count = tokens.shape[0]
    n_dp, n_mp = lax.axis_size("dp"), lax.axis_size("mp")
    fine = n_dp // WAYS
    total = row_count * n_dp
    dp_at, mp_at = lax.axis_index("dp"), lax.axis_index("mp")
    idx = jnp.stack([dp_at // fine, mp_at, dp_at]).astype(jnp.int32)
    hw = w_qkv.shape[2] // 3

    def swap(x, axis, size, k):
        return lax.ppermute(x, axis, [(i, i ^ k) for i in range(size)])

    def dp(x, k):
        return swap(x, "dp", n_dp, k * fine)

    def mp(x, k):
        return swap(x, "mp", n_mp, k)

    def fine_rows(x):
        k = 1
        while k < fine:
            got = swap(x, "dp", n_dp, k)
            x = jnp.where((dp_at & k) == 0, jnp.concatenate([x, got], 0), jnp.concatenate([got, x], 0))
            k *= 2
        return x

    def fine_sum(x):
        k = 1
        while k < fine:
            x = x + swap(x, "dp", n_dp, k)
            k *= 2
        return x

    def gather8(own, *early):
        parts = {0: own}
        for k in (2, 4, 6):
            parts[k] = dp(own, k)
        parts[1] = dp(own, 1)
        for k in (2, 4, 6):
            parts[k ^ 1] = dp(after(parts[k], *early) if early else parts[k], 1)
        return [parts[k] for k in range(WAYS)]

    def gather4(own):
        far = mp(own, 2)
        return [own, mp(own, 1), far, mp(far, 1)]

    def scatter4(send, keep):
        got = mp(send, 1)
        return keep, got, mp((keep[1] + got[1].astype(F32)).astype(BF), 2)

    def gather8_halves(own):
        two = jnp.stack([own, dp(own, 4)])
        four = jnp.concatenate([two, dp(two, 2)])
        return four, dp(four, 1)

    def after(x, *deps):
        return lax.optimization_barrier((x, *deps))[0]

    out_rows = fine_rows(w_out[0].astype(BF))
    groups = tokens.shape[1] // hw
    first = jnp.concatenate([fine_rows(w_qkv[0].astype(BF)), pack_rows(out_rows, groups)], axis=1)
    up_own = fine_rows(w_up[0].astype(BF))
    down_own = fine_rows(w_down[0].astype(BF))
    down_two = jnp.stack([down_own, dp(down_own, 1)])
    first = gather8(first, down_two)

    ends = jnp.cumsum(doc_lengths[0])
    places = jnp.arange(row_count, dtype=jnp.int32)
    start = jnp.max(jnp.where(ends[None, :] <= places[:, None], ends[None, :], 0), axis=1, keepdims=True)
    start = start.astype(jnp.int32)
    hat, _ = normalize(tokens.astype(F32))
    a_low = (hat * outer_norms[0] + outer_norms[1]).astype(BF)

    up_go = after(up_own, first[2], first[4], first[6], down_two)
    up_z = [dp(up_go, k) for k in ORDER[1:]]
    q, k, v, wq, wo = project(a_low, attn_norm, first, hw, idx)
    wo_far = mp(wo, 2)
    o, probs = attend(start, q, k, v, idx)
    o, *up_z = lax.optimization_barrier((o, *up_z))
    up_four = jnp.stack([up_own, *up_z])
    o, wo, wo_far, up_four = lax.optimization_barrier((o, wo, wo_far, up_four))
    o_far = mp(o, 2)
    up_x = dp(up_four, 1)
    down_go = after(down_two, up_four)
    down_z = [dp(down_go, k) for k in ORDER[1:]]
    o_near, wo_near, wo_last = mp(after(o, o_far), 1), mp(after(wo, o_far), 1), mp(after(wo_far, o_far), 1)
    o_all = [o, o_near, o_far, mp(o_far, 1)]
    wo_all = [wo, wo_near, wo_far, wo_last]
    hidden, c_low = outproj(outer_norms, tokens, o_all, wo_all, idx, [up_x])
    u, dw, stats, wu, wd = ffn_up(c_low, cotangent, ffn_norm, [up_four, up_x, down_two, *down_z], idx)
    stats = lax.all_gather(stats, "mp")
    w_low, du, dc_send, dc_keep, ffn_grads = ffn_mid(u, dw, stats, ffn_norm, wu, idx)
    dc_got = mp(dc_send, 1)
    dc_sum = far_sum(dc_keep, dc_got, idx)
    down_send, down_keep = weight_grad(w_low, cotangent, idx, "grad_down", [dc_sum])
    down_x = dp(down_send, 1)
    up_send, up_keep = weight_grad(c_low, du, idx, "grad_up", [down_send])
    up_x2 = dp(after(up_send, down_send), 1)
    dh, outer_late, attn_grads, *rest = shard_back(
        dc_keep, dc_got, mp(dc_sum, 2), hidden, cotangent, outer_norms, o_all, wo_all, idx, [up_send]
    )
    do, (go_send, go_keep) = rest[:n_mp], rest[n_mp:]
    do = [do[0]] + [mp(do[k], k) for k in range(1, n_mp)]
    go_got = mp(go_send, 1)
    down_t, down_low = fold(down_keep, down_x, idx, [do[1]], 0)
    go_sum = far_sum(go_keep, go_got, idx, [down_low], 0)
    dqkv = attend_back(q, k, v, probs, do, idx, [go_sum])
    down_z1 = dp(down_low, 2)
    go_far = mp(go_sum, 2)
    down_t, down_low = fold(down_t, down_z1, idx, [dqkv])
    up_t, up_low = fold(up_keep, up_x2, idx, [down_low])
    qkv_send, qkv_keep, da_send, da_keep = qkv_back(a_low, dqkv, wq, [go_keep, go_got, go_far], idx, [up_low])

    down_z2, up_z1 = dp(down_low, 4), dp(up_low, 2)
    qkv_x = dp(qkv_send, 1)
    da_got = mp(da_send, 1)
    da_sum = far_sum(da_keep, da_got, idx)
    da_far = mp(da_sum, 2)
    down_done = fine_sum(close(down_t, [down_z2], idx, [da_sum]))
    down_r4 = dp(down_done, 4)
    up_t, up_low = fold(up_t, up_z1, idx, [down_done])
    up_z2 = dp(up_low, 4)
    bo_send, bo_keep = ffn_out(w_low, wd, idx, [up_low])
    bo_got = mp(bo_send, 1)
    qkv_t, qkv_low = fold(qkv_keep, qkv_x, idx, [bo_send], 0)
    qkv_z1 = dp(qkv_low, 2)
    gt, outer_early = shard_end(da_keep, da_got, da_far, tokens, outer_norms, dh, idx, [qkv_low])
    gt_far = mp(gt, 2)
    lanes = outer_late.shape[1]
    vec = jnp.concatenate([outer_early, outer_late, attn_grads.reshape(-1, lanes)])
    vec_got = mp(vec, 1)
    down_two = join([down_done, down_r4], idx, [gt])
    down_r2 = dp(down_two, 2)
    up_done = fine_sum(close(up_t, [up_z2], idx, [down_two]))
    up_r4 = dp(up_done, 4)
    vec = vec_add(vec, vec_got, idx, [up_done])
    vec_got = mp(vec, 2)
    bo_sum = far_sum(bo_keep, bo_got, idx, [vec])
    bo_far = mp(bo_sum, 2)
    qkv_t, qkv_low = fold(qkv_t, qkv_z1, idx, [bo_sum])
    qkv_z2 = dp(qkv_low, 4)
    out_own = block_end(hidden, bo_keep, bo_got, bo_far, idx, [qkv_low])
    out_far = mp(out_own, 2)
    gt_far = after(gt_far, out_own)
    gt_all = [gt, mp(after(gt, gt_far), 1), gt_far, mp(gt_far, 1)]
    down_four = join([down_two, down_r2], idx, [out_own])
    down_other = dp(down_four, 1)
    vec = vec_add(vec, vec_got, idx, [down_four])
    up_two = join([up_done, up_r4], idx, [vec])
    up_r2 = dp(up_two, 2)
    grad_tokens = spread_rows(gt_all, idx, "spread_tokens", [up_two])
    attn_own = lax.dynamic_index_in_dim(vec[4:].reshape(attn_grads.shape), mp_at, 0, False)

    def flat(*parts):
        x = jnp.concatenate([p.reshape(-1) for p in parts])
        return jnp.pad(x, (0, WAYS * lanes - x.shape[0])).reshape(WAYS, lanes)

    vec = fine_sum(flat(vec[:4], attn_own, ffn_grads))
    cut = outer_norms.size
    cut2 = cut + attn_norm.size
    size = cut2 + ffn_norm.size
    params = flat(outer_norms, attn_norm, ffn_norm)
    rates = (VEC_RATE / math.sqrt(total), UNIT_RATE / math.sqrt(total), cut2)

    qkv_own = close(qkv_t, [qkv_z2], idx, [grad_tokens], None if fine > 1 else vec)
    if fine > 1:
        high = vec.astype(BF)
        qkv_own = jnp.concatenate([fine_sum(qkv_own), high, (vec - high.astype(F32)).astype(BF)])
    qkv_z = [dp(qkv_own, k) for k in ORDER[1:]]
    up_four = join([up_two, up_r2], idx, [qkv_own])
    up_other = dp(up_four, 1)
    down_mats = [x[0] for x in (w_down, left_down, right_down, left_root_down, right_root_down)]
    down_res = update_one(down_mats, down_four, down_other, total, idx, "update_down", [up_four])
    qkv_four = join([qkv_own, *qkv_z], idx, [down_res[3]])
    qkv_other = dp(qkv_four, 1)
    out_far = after(out_far, qkv_four)
    out_all = [out_own, mp(after(out_own, out_far), 1), out_far, mp(out_far, 1)]
    block_out = spread_rows(out_all, idx, "spread_out", [qkv_four])

    def mats(*arrays):
        return [x[0] for x in arrays]

    up_mats = mats(w_up, left_up, right_up, left_root_up, right_root_up)
    up_res = update_one(up_mats, up_four, up_other, total, idx, "update_up", [block_out])
    qkv_res, out_res, vec, new_vec = update_pair(
        mats(w_qkv, left_qkv, right_qkv, left_root_qkv, right_root_qkv),
        mats(w_out, left_out, right_out, left_root_out, right_root_out),
        qkv_four,
        qkv_other,
        params,
        rates,
        total,
        idx,
        "update_qkv",
        [up_res[3]],
    )

    def cut_up(x):
        x = x.reshape(-1)
        return (
            x[:cut].reshape(outer_norms.shape),
            x[cut:cut2].reshape(attn_norm.shape),
            x[cut2:size].reshape(ffn_norm.shape),
        )

    return (
        block_out,
        grad_tokens,
        *cut_up(vec),
        *cut_up(new_vec),
        *(x[None] for x in qkv_res),
        *(x[None] for x in out_res),
        *(x[None] for x in up_res),
        *(x[None] for x in down_res),
    )


def solution(mesh):
    rows = P("dp", None)
    mats = (P("mp", "dp", None),) * 4 + (P("mp", None, None),)
    res = (P("mp", None, None),) + (P("mp", "dp", None),) * 4
    cols = P(None, "mp")
    return jax.shard_map(
        body,
        mesh=mesh,
        in_specs=(rows, rows, rows, P(), cols, cols) + mats * 4,
        out_specs=(rows, rows, P(), cols, cols, P(), cols, cols) + res * 4,
        check_vma=False,
    )
```

time: 332 us -> 275 us (0.83)
  Pallas kernels: 87.9 us -> 118 us
  starting transfers between devices: 91.3 us -> 66.4 us
  waiting for transfers between devices: 71.1 us -> 52.6 us
  blocking collectives: 21.4 us -> 5.59 us
  local copies, waits for them, and re-layouts: 36.3 us -> 22.1 us
  other arithmetic: 21.2 us -> 8.03 us
    pallas_call x19 -> x38, Pallas kernels: 87.9 us -> 118 us  [run(): pl.pallas_call(kernel, grid_spec=pltpu.PrefetchScalarGridSpec(num_scalar_...]
    ppermute x80 -> x59, starting transfers between devices: 91.3 us -> 66.4 us  [swap(): return lax.ppermute(x, axis, [(i, i ^ k) for i in range(size)])]
    ppermute x80 -> x59, waiting for transfers between devices: 71.1 us -> 52.6 us  [swap(): return lax.ppermute(x, axis, [(i, i ^ k) for i in range(size)])]
    unnamed x163 -> x114, local copies, waits for them, and re-layouts: 30.5 us -> 16.2 us
    convert_element_type x13 -> x2, other arithmetic: 13.9 us -> 1.83 us  [the longest x1 1.09 us: body(): down_own = fine_rows(w_down[0].astype(BF))]
    psum x1 -> x0, blocking collectives: 10.7 us -> none  [body(): lax.psum((jnp.concatenate([outer_early, outer_late], 0), attn_grads), 'mp')]
    all_gather x1 -> x0, blocking collectives: 5.15 us -> none  [body(): attn_all = lax.all_gather(attn_norm, 'mp')]
  transfers between devices with their start and end apart: 80 -> 59, of which waited for: 23 -> 18; matrix products, arithmetic and copies ran while one was open for 8% -> 3% of each run, Pallas kernels for 20% -> 32%
where the time goes in v2:
time: 275 us; the launch traced here: 274 us
  Pallas kernels  118 us (43%)
  starting transfers between devices  66.4 us (24%)
  waiting for transfers between devices  52.6 us (19%)
  local copies, waits for them, and re-layouts  22.1 us (8%)
  other arithmetic  8.03 us (3%)
  blocking collectives  5.59 us (2%)
    pallas_call x38, Pallas kernels, run(): pl.pallas_call(kernel, grid_spec=pltpu.PrefetchScalarGridSpec(num_scalar_...  118 us
    ppermute x59, starting transfers between devices, swap(): return lax.ppermute(x, axis, [(i, i ^ k) for i in range(size)])  66.4 us
    ppermute x59, waiting for transfers between devices, swap(): return lax.ppermute(x, axis, [(i, i ^ k) for i in range(size)])  52.6 us
    unnamed x114, local copies, waits for them, and re-layouts  16.2 us
    all_gather x1, blocking collectives, body(): stats = lax.all_gather(stats, 'mp')  5.59 us
  transfers between devices with their start and end apart: 59, of which 18 were waited for; matrix products, arithmetic and copies ran while one was open for 3% of the time, Pallas kernels for 32%

profile of v2, /device:TPU:0, one launch (start us, length us, event | category | flops | bytes accessed | tf_op | source)
XLA Modules:
  0.0 274.2 jit_solution(10182731433333250149)
XLA Ops:
  2.8 3.0 %collective-permute-start = (bf16[96,768]{1,0:T(8,128)(2,1)S(1)}, bf16[96,768]{1,0:T(8,128)(2,1)S(1)}, u32[]{:S(2)}, u32[]{:S(2)}) collective-permute-start(bf16[96,768]{1,0:T(8,128)(2,1)S(1)} %maximum_maximum_fusion.refs_2_), channel_id=1, source_target_pairs={{0,4},{4,0},{8,12},{12,8},{16,20},{20,16},{24,28},{28,24},{1,5},{5... | collective-permute-start | bytes 442376 | tf_op jit(solution)/shard_map/ppermute | solution.py:812
  5.8 1.6 collective-permute-start.1
  7.4 2.6 collective-permute-start.4
  12.5 1.7 convert_reduce_fusion
  17.5 1.7 collective-permute-start.3
  19.2 2.1 collective-permute-done.4.refs_6_
  23.7 1.7 collective-permute-start.8
  26.6 1.6 collective-permute-start.10
  28.3 4.1 %project.1 = (bf16[1024,192]{1,0:T(8,128)(2,1)}, bf16[1024,192]{1,0:T(8,128)(2,1)}, bf16[1024,192]{1,0:T(8,128)(2,1)}, bf16[768,576]{1,0:T(8,128)(2,1)}, bf16[208,768]{1,0:T(8,128)(2,1)}) custom-call(s32[3]{0:T(128)S(1)} %pad_add_fusion.idx, bf16[1024,768]{1,0:T(8,128)(2,1)S(1)} %fusion.5.refs_0_, f32[2,192]{1,0:T(2,128)S(1)} %copy-done.21, ...), custom_call_target="tpu_custom_call" | custom-call | flops 16000000000 | bytes 1024 | tf_op jit(solution)/shard_map/project/pallas_call | solution.py:43
  33.9 10.2 %attend.1 = (bf16[1024,192]{1,0:T(8,128)(2,1)}, bf16[3,1024,1024]{2,1,0:T(8,128)(2,1)}) custom-call(s32[3]{0:T(128)S(1)} %pad_add_fusion.idx, s32[1024,1]{1,0:T(8,128)S(1)} %copy.55.refs_0_, bf16[1024,192]{1,0:T(8,128)(2,1)} %get-tuple-element.126.refs_1_.refs_0_, bf16[1024,192]{1,0:T(8,128)(2,1)} %get-tuple-element.127.refs_2_.refs_1_, ...), custom_call_target="tpu_custom_call" | custom-call | flops 4000000000 | bytes 1024 | tf_op jit(solution)/shard_map/attend/pallas_call | solution.py:43
  46.3 8.9 %collective-permute-done.12.refs_4_.refs_8_ = bf16[1024,192]{1,0:T(8,128)(2,1)S(1)} collective-permute-done((bf16[1024,192]{1,0:T(8,128)(2,1)}, bf16[1024,192]{1,0:T(8,128)(2,1)S(1)}, u32[]{:S(2)}, u32[]{:S(2)}) %collective-permute-start.12) | collective-permute-done | bytes 393248 | tf_op jit(solution)/shard_map/ppermute | solution.py:812
  56.8 3.1 %collective-permute-start.18 = (bf16[2,96,768]{2,1,0:T(8,128)(2,1)S(1)}, bf16[2,96,768]{2,1,0:T(8,128)(2,1)S(1)}, u32[]{:S(2)}, u32[]{:S(2)}) collective-permute-start(bf16[2,96,768]{2,1,0:T(8,128)(2,1)S(1)} %copy-done.49), channel_id=1, source_target_pairs={{0,16},{4,20},{8,24},{12,28},{16,0},{20,4},{24,8},{28,12},{1,17},{... | collective-permute-start | bytes 884744 | tf_op jit(solution)/shard_map/ppermute | solution.py:812
  63.2 7.9 %outproj.1 = (f32[1024,768]{1,0:T(8,128)}, bf16[1024,768]{1,0:T(8,128)(2,1)S(1)}) custom-call(s32[3]{0:T(128)S(1)} %pad_add_fusion.idx, f32[4,768]{1,0:T(4,128)S(1)} %copy-done.18, bf16[1024,768]{1,0:T(8,128)(2,1)} %refs_3_.3, bf16[1024,192]{1,0:T(8,128)(2,1)} %get-tuple-element.137.refs_2_.refs_6_, bf16[1024,192]{1,0:T(8,128)(2,1)} %copy-done.39, ...), custom_call_target="tpu_custom_call" | custom-call | bytes 1024 | tf_op jit(solution)/shard_map/outproj/pallas_call | solution.py:43
  71.1 4.2 %collective-permute-done.18.refs_6_ = bf16[2,96,768]{2,1,0:T(8,128)(2,1)S(1)} collective-permute-done((bf16[2,96,768]{2,1,0:T(8,128)(2,1)S(1)}, bf16[2,96,768]{2,1,0:T(8,128)(2,1)S(1)}, u32[]{:S(2)}, u32[]{:S(2)}) %collective-permute-start.18) | collective-permute-done | bytes 294944 | tf_op jit(solution)/shard_map/ppermute | solution.py:812
  75.3 5.1 %collective-permute-done.20.refs_8_ = bf16[2,96,768]{2,1,0:T(8,128)(2,1)S(1)} collective-permute-done((bf16[2,96,768]{2,1,0:T(8,128)(2,1)S(1)}, bf16[2,96,768]{2,1,0:T(8,128)(2,1)S(1)}, u32[]{:S(2)}, u32[]{:S(2)}) %collective-permute-start.20) | collective-permute-done | bytes 294944 | tf_op jit(solution)/shard_map/ppermute | solution.py:812
  81.1 7.3 %ffn_up.1 = (f32[1024,768]{1,0:T(8,128)S(1)}, f32[1024,768]{1,0:T(8,128)S(1)}, f32[8,1024]{1,0:T(8,128)S(1)}, bf16[768,768]{1,0:T(8,128)(2,1)S(1)}, bf16[768,768]{1,0:T(8,128)(2,1)}) custom-call(s32[3]{0:T(128)S(1)} %pad_add_fusion.idx, bf16[1024,768]{1,0:T(8,128)(2,1)S(1)} %get-tuple-element.144.refs_0_, bf16[1024,768]{1,0:T(8,128)(2,1)} %refs_4_.2, ...), custom_call_target="tpu_custom_call" | custom-call | flops 3000000000 | bytes 1024 | tf_op jit(solution)/shard_map/ffn_up/pallas_call | solution.py:43
  88.4 5.6 %all-gather = f32[32,1024]{1,0:T(8,128)S(1)} all-gather(f32[8,1024]{1,0:T(8,128)S(1)} %get-tuple-element.148), channel_id=2, replica_groups=mesh['dp'=8,'mp'=4] {'mp'}, dimensions={0}, use_global_device_ids=true | all-gather | bytes 163840 | tf_op jit(solution)/shard_map/all_gather | solution.py:892
  94.0 7.7 %ffn_mid.1 = (bf16[1024,768]{1,0:T(8,128)(2,1)}, bf16[1024,768]{1,0:T(8,128)(2,1)}, bf16[2,256,768]{2,1,0:T(8,128)(2,1)S(1)}, f32[2,256,768]{2,1,0:T(8,128)}, f32[2,768]{1,0:T(2,128)S(1)}) custom-call(s32[3]{0:T(128)S(1)} %pad_add_fusion.idx, f32[1024,768]{1,0:T(8,128)S(1)} %get-tuple-element.146.refs_0_, f32[1024,768]{1,0:T(8,128)S(1)} %get-tuple-element.147.refs_1_, ...), custom_call_target="tpu_custom_call" | custom-call | flops 2600000000 | bytes 1024 | tf_op jit(solution)/shard_map/ffn_mid/pallas_call | solution.py:43
  102.0 1.9 collective-permute-done.21.refs_1_
  104.0 1.7 copy-done.4
  107.6 3.8 %grad_down.1 = (bf16[4,96,768]{2,1,0:T(8,128)(2,1)S(1)}, f32[4,96,768]{2,1,0:T(8,128)}) custom-call(s32[3]{0:T(128)S(1)} %pad_add_fusion.idx, bf16[1024,768]{1,0:T(8,128)(2,1)S(1)} %copy-done.6, bf16[1024,768]{1,0:T(8,128)(2,1)S(1)} %copy-done.3, bf16[256,768]{1,0:T(8,128)(2,1)S(1)} %far_sum.4.refs_2_), custom_call_target="tpu_custom_call" | custom-call | flops 1400000000 | bytes 1024 | tf_op jit(solution)/shard_map/grad_down/pallas_call | solution.py:43
  112.9 3.7 %grad_up.1 = (bf16[4,96,768]{2,1,0:T(8,128)(2,1)S(1)}, f32[4,96,768]{2,1,0:T(8,128)}) custom-call(s32[3]{0:T(128)S(1)} %pad_add_fusion.idx, bf16[1024,768]{1,0:T(8,128)(2,1)S(1)} %get-tuple-element.144.refs_0_, bf16[1024,768]{1,0:T(8,128)(2,1)S(1)} %copy-done.30, bf16[4,96,768]{2,1,0:T(8,128)(2,1)S(1)} %get-tuple-element.155.refs_2_), custom_call_target="tpu_custom_call" | custom-call | flops 1400000000 | bytes 1024 | tf_op jit(solution)/shard_map/grad_up/pallas_call | solution.py:43
  118.5 5.5 %shard_back.1 = (f32[256,768]{1,0:T(8,128)}, f32[2,768]{1,0:T(2,128)S(1)}, f32[4,2,192]{2,1,0:T(2,128)S(1)}, bf16[256,192]{1,0:T(8,128)(2,1)S(1)}, bf16[256,192]...) custom-call(s32[3]{0:T(128)S(1)} %pad_add_fusion.idx, ...), custom_call_target="tpu_custom_call" | custom-call | bytes 1024 | tf_op jit(solution)/shard_map/shard_back/pallas_call | solution.py:43
  129.1 5.8 %collective-permute-start.26 = (bf16[2,96,768]{2,1,0:T(8,128)(2,1)S(1)}, bf16[2,96,768]{2,1,0:T(8,128)(2,1)S(1)}, u32[]{:S(2)}, u32[]{:S(2)}) collective-permute-start(bf16[2,96,768]{2,1,0:T(8,128)(2,1)S(1)} %get-tuple-element.162.refs_2_), channel_id=1, source_target_pairs={{0,8},{4,12},{8,0},{12,4},{16,24},{20,28},{24,16},{28,20},{1,9},{5... | collective-permute-start | bytes 884744 | tf_op jit(solution)/shard_map/ppermute | solution.py:812
  136.7 11.4 %attend_back.1.refs_2_.refs_1_ = bf16[1024,576]{1,0:T(8,128)(2,1)S(1)} custom-call(s32[3]{0:T(128)S(1)} %pad_add_fusion.idx, bf16[1024,192]{1,0:T(8,128)(2,1)} %get-tuple-element.126.refs_1_.refs_0_, bf16[1024,192]{1,0:T(8,128)(2,1)} %get-tuple-element.127.refs_2_.refs_1_, bf16[1024,192]{1,0:T(8,128)(2,1)} %get-tuple-element.128.refs_3_.refs_2_, ...), custom_call_target="tpu_custom_call" | custom-call | flops 4400000000 | bytes 1024 | tf_op jit(solution)/shard_map/attend_back/pallas_call | solution.py:43
  150.9 6.9 %qkv_back.1 = (bf16[4,96,768]{2,1,0:T(8,128)(2,1)}, f32[4,96,768]{2,1,0:T(8,128)}, bf16[2,256,768]{2,1,0:T(8,128)(2,1)S(1)}, f32[2,256,768]{2,1,0:T(8,128)}) custom-call(s32[3]{0:T(128)S(1)} %pad_add_fusion.idx, bf16[1024,768]{1,0:T(8,128)(2,1)} %copy-done.5, bf16[1024,576]{1,0:T(8,128)(2,1)S(1)} %attend_back.1.refs_2_.refs_1_, ...), custom_call_target="tpu_custom_call" | custom-call | flops 2200000000 | bytes 1024 | tf_op jit(solution)/shard_map/qkv_back/pallas_call | solution.py:43
  158.6 4.9 %collective-permute-start.30 = (bf16[2,96,768]{2,1,0:T(8,128)(2,1)S(1)}, bf16[2,96,768]{2,1,0:T(8,128)(2,1)}, u32[]{:S(2)}, u32[]{:S(2)}) collective-permute-start(bf16[2,96,768]{2,1,0:T(8,128)(2,1)S(1)} %get-tuple-element.171.refs_6_), channel_id=1, source_target_pairs={{0,8},{4,12},{8,0},{12,4},{16,24},{20,28},{24,16},{28,20},{1,9},{5... | collective-permute-start | bytes 884744 | tf_op jit(solution)/shard_map/ppermute | solution.py:812
  163.5 1.7 collective-permute-start.31
  168.5 4.3 %collective-permute-done.31.refs_1_ = bf16[96,768]{1,0:T(8,128)(2,1)S(1)} collective-permute-done((bf16[96,768]{1,0:T(8,128)(2,1)S(1)}, bf16[96,768]{1,0:T(8,128)(2,1)S(1)}, u32[]{:S(2)}, u32[]{:S(2)}) %collective-permute-start.31) | collective-permute-done | bytes 147488 | tf_op jit(solution)/shard_map/ppermute | solution.py:812
  173.4 3.4 %collective-permute-start.39 = (bf16[96,768]{1,0:T(8,128)(2,1)S(1)}, bf16[96,768]{1,0:T(8,128)(2,1)S(1)}, u32[]{:S(2)}, u32[]{:S(2)}) collective-permute-start(bf16[96,768]{1,0:T(8,128)(2,1)S(1)} %close.3.refs_2_.refs_0_), channel_id=1, source_target_pairs={{0,16},{4,20},{8,24},{12,28},{16,0},{20,4},{24,8},{28,12},{1,17},{... | collective-permute-start | bytes 442376 | tf_op jit(solution)/shard_map/ppermute | solution.py:812
  176.8 1.6 fold.9
  178.9 5.5 %ffn_out.1 = (bf16[2,256,768]{2,1,0:T(8,128)(2,1)S(1)}, f32[2,256,768]{2,1,0:T(8,128)}) custom-call(s32[3]{0:T(128)S(1)} %pad_add_fusion.idx, bf16[1024,768]{1,0:T(8,128)(2,1)} %get-tuple-element.150.refs_0_, bf16[768,768]{1,0:T(8,128)(2,1)} %get-tuple-element.151.refs_1_, bf16[96,768]{1,0:T(8,128)(2,1)S(1)} %get-tuple-element.176.refs_2_), custom_call_target="tpu_custom_call" | custom-call | bytes 1024 | tf_op jit(solution)/shard_map/ffn_out/pallas_call | solution.py:43
  185.1 3.4 %collective-permute-start.41 = (bf16[2,96,768]{2,1,0:T(8,128)(2,1)S(1)}, bf16[2,96,768]{2,1,0:T(8,128)(2,1)}, u32[]{:S(2)}, u32[]{:S(2)}) collective-permute-start(bf16[2,96,768]{2,1,0:T(8,128)(2,1)S(1)} %get-tuple-element.182.refs_6_), channel_id=1, source_target_pairs={{0,8},{4,12},{8,0},{12,4},{16,24},{20,28},{24,16},{28,20},{1,9},{5... | collective-permute-start | bytes 884744 | tf_op jit(solution)/shard_map/ppermute | solution.py:812
  195.1 1.6 collective-permute-start.46
  198.2 2.2 fold.11
  200.4 5.6 %collective-permute-done.40.refs_3_ = bf16[256,768]{1,0:T(8,128)(2,1)S(1)} collective-permute-done((bf16[256,768]{1,0:T(8,128)(2,1)S(1)}, bf16[256,768]{1,0:T(8,128)(2,1)S(1)}, u32[]{:S(2)}, u32[]{:S(2)}) %collective-permute-start.40) | collective-permute-done | bytes 393248 | tf_op jit(solution)/shard_map/ppermute | solution.py:812
  206.4 1.9 block_end.1.refs_2_.refs_0_
  208.8 1.5 join.6.refs_2_.refs_5_
  210.3 4.6 %collective-permute-done.44.refs_1_ = f32[6,768]{1,0:T(8,128)S(1)} collective-permute-done((f32[6,768]{1,0:T(8,128)S(1)}, f32[6,768]{1,0:T(8,128)S(1)}, u32[]{:S(2)}, u32[]{:S(2)}) %collective-permute-start.44) | collective-permute-done | bytes 18464 | tf_op jit(solution)/shard_map/ppermute | solution.py:812
  219.4 1.8 spread_tokens.1.refs_3_
  226.9 1.6 collective-permute-start.52
  230.1 3.5 %collective-permute-done.53.refs_6_ = bf16[4,96,768]{2,1,0:T(8,128)(2,1)S(1)} collective-permute-done((bf16[4,96,768]{2,1,0:T(8,128)(2,1)S(1)}, bf16[4,96,768]{2,1,0:T(8,128)(2,1)S(1)}, u32[]{:S(2)}, u32[]{:S(2)}) %collective-permute-start.53) | collective-permute-done | bytes 589856 | tf_op jit(solution)/shard_map/ppermute | solution.py:812
  234.4 5.4 %update_down.1 = (f32[768,768]{1,0:T(8,128)}, f32[96,768]{1,0:T(8,128)}, f32[96,768]{1,0:T(8,128)}, f32[96,768]{1,0:T(8,128)}, bf16[96,768]{1,0:T(8,128)(2,1)}) custom-call(s32[3]{0:T(128)S(1)} %pad_add_fusion.idx, f32[96,768]{1,0:T(8,128)} %bitcast.64, f32[96,768]{1,0:T(8,128)} %bitcast.77, f32[96,768]{1,0:T(8,128)} %bitcast.78, f32[96,768]{1,0:T(8,128)} %bitcast.79, ...), custom_call_target="tpu_custom_call" | custom-call | flops 1600000000 | bytes 1024 | tf_op jit(solution)/shard_map/update_down/pallas_call | solution.py:43
  245.0 1.8 spread_out.1.refs_7_
  246.8 3.1 %collective-permute-done.58.refs_6_ = bf16[4,96,768]{2,1,0:T(8,128)(2,1)S(1)} collective-permute-done((bf16[4,96,768]{2,1,0:T(8,128)(2,1)S(1)}, bf16[4,96,768]{2,1,0:T(8,128)(2,1)S(1)}, u32[]{:S(2)}, u32[]{:S(2)}) %collective-permute-start.58) | collective-permute-done | bytes 589856 | tf_op jit(solution)/shard_map/ppermute | solution.py:812
  252.1 5.4 %update_up.1 = (f32[768,768]{1,0:T(8,128)}, f32[96,768]{1,0:T(8,128)}, f32[96,768]{1,0:T(8,128)}, f32[96,768]{1,0:T(8,128)}, bf16[96,768]{1,0:T(8,128)(2,1)}) custom-call(s32[3]{0:T(128)S(1)} %pad_add_fusion.idx, f32[96,768]{1,0:T(8,128)} %bitcast.60, f32[96,768]{1,0:T(8,128)} %bitcast.61, f32[96,768]{1,0:T(8,128)} %bitcast.62, f32[96,768]{1,0:T(8,128)} %bitcast.63, ...), custom_call_target="tpu_custom_call" | custom-call | flops 1600000000 | bytes 1024 | tf_op jit(solution)/shard_map/update_up/pallas_call | solution.py:43
  257.5 5.1 %collective-permute-done.57.refs_11_ = bf16[4,112,768]{2,1,0:T(8,128)(2,1)} collective-permute-done((bf16[4,112,768]{2,1,0:T(8,128)(2,1)S(1)}, bf16[4,112,768]{2,1,0:T(8,128)(2,1)}, u32[]{:S(2)}, u32[]{:S(2)}) %collective-permute-start.57) | collective-permute-done | bytes 688160 | tf_op jit(solution)/shard_map/ppermute | solution.py:812
  263.5 7.0 %update_qkv.1 = (f32[576,768]{1,0:T(8,128)}, f32[96,768]{1,0:T(8,128)}, f32[72,576]{1,0:T(8,128)}, f32[96,576]{1,0:T(8,128)}, bf16[96,576]{1,0:T(8,128)(2,1)}, /...) custom-call(s32[3]{0:T(128)S(1)} %pad_add_fusion.idx, ...), custom_call_target="tpu_custom_call" | custom-call | flops 2400000000 | bytes 1024 | tf_op jit(solution)/shard_map/update_qkv/pallas_call | solution.py:43
  (269 shorter events, 75.3 us)
Async XLA Ops:
  2.8 22.6 %collective-permute-start = (bf16[96,768]{1,0:T(8,128)(2,1)S(1)}, bf16[96,768]{1,0:T(8,128)(2,1)S(1)}, u32[]{:S(2)}, u32[]{:S(2)}) collective-permute-start(bf16[96,768]{1,0:T(8,128)(2,1)S(1)} %maximum_maximum_fusion.refs_2_), channel_id=1, source_target_pairs={{0,4},{4,0},{8,12},{12,8},{16,20},{20,16},{24,28},{28,24},{1,5},{5... | collective-permute-start | bytes 442376 | tf_op jit(solution)/shard_map/ppermute | solution.py:812
  5.8 11.6 %collective-permute-start.1 = (bf16[96,768]{1,0:T(8,128)(2,1)S(1)}, bf16[96,768]{1,0:T(8,128)(2,1)S(1)}, u32[]{:S(2)}, u32[]{:S(2)}) collective-permute-start(bf16[96,768]{1,0:T(8,128)(2,1)S(1)} %maximum_maximum_fusion.refs_2_), channel_id=1, source_target_pairs={{0,8},{4,12},{8,0},{12,4},{16,24},{20,28},{24,16},{28,20},{1,9},{5... | collective-permute-start | bytes 442376 | tf_op jit(solution)/shard_map/ppermute | solution.py:812
  7.4 13.9 %collective-permute-start.4 = (bf16[96,768]{1,0:T(8,128)(2,1)S(1)}, bf16[96,768]{1,0:T(8,128)(2,1)S(1)}, u32[]{:S(2)}, u32[]{:S(2)}) collective-permute-start(bf16[96,768]{1,0:T(8,128)(2,1)S(1)} %maximum_maximum_fusion.refs_2_), channel_id=1, source_target_pairs={{0,16},{4,20},{8,24},{12,28},{16,0},{20,4},{24,8},{28,12},{1,17},{... | collective-permute-start | bytes 442376 | tf_op jit(solution)/shard_map/ppermute | solution.py:812
  10.0 11.8 %collective-permute-start.6 = (bf16[96,768]{1,0:T(8,128)(2,1)S(1)}, bf16[96,768]{1,0:T(8,128)(2,1)S(1)}, u32[]{:S(2)}, u32[]{:S(2)}) collective-permute-start(bf16[96,768]{1,0:T(8,128)(2,1)S(1)} %maximum_maximum_fusion.refs_2_), channel_id=1, source_target_pairs={{0,24},{4,28},{8,16},{12,20},{16,8},{20,12},{24,0},{28,4},{1,25},{... | collective-permute-start | bytes 442376 | tf_op jit(solution)/shard_map/ppermute | solution.py:812
  17.5 9.1 %collective-permute-start.3 = (bf16[96,768]{1,0:T(8,128)(2,1)S(1)}, bf16[96,768]{1,0:T(8,128)(2,1)S(1)}, u32[]{:S(2)}, u32[]{:S(2)}) collective-permute-start(bf16[96,768]{1,0:T(8,128)(2,1)S(1)} %collective-permute-done.1.refs_4_), channel_id=1, source_target_pairs={{0,4},{4,0},{8,12},{12,8},{16,20},{20,16},{24,28},{28,24},{1,5},{5... | collective-permute-start | bytes 442376 | tf_op jit(solution)/shard_map/ppermute | solution.py:812
  21.3 6.8 %collective-permute-start.5 = (bf16[96,768]{1,0:T(8,128)(2,1)S(1)}, bf16[96,768]{1,0:T(8,128)(2,1)S(1)}, u32[]{:S(2)}, u32[]{:S(2)}) collective-permute-start(bf16[96,768]{1,0:T(8,128)(2,1)S(1)} %collective-permute-done.4.refs_6_), channel_id=1, source_target_pairs={{0,4},{4,0},{8,12},{12,8},{16,20},{20,16},{24,28},{28,24},{1,5},{5... | collective-permute-start | bytes 442376 | tf_op jit(solution)/shard_map/ppermute | solution.py:812
  21.8 6.4 %collective-permute-start.7 = (bf16[96,768]{1,0:T(8,128)(2,1)S(1)}, bf16[96,768]{1,0:T(8,128)(2,1)S(1)}, u32[]{:S(2)}, u32[]{:S(2)}) collective-permute-start(bf16[96,768]{1,0:T(8,128)(2,1)S(1)} %collective-permute-done.6.refs_8_), channel_id=1, source_target_pairs={{0,4},{4,0},{8,12},{12,8},{16,20},{20,16},{24,28},{28,24},{1,5},{5... | collective-permute-start | bytes 442376 | tf_op jit(solution)/shard_map/ppermute | solution.py:812
  23.7 20.4 %collective-permute-start.8 = (bf16[96,768]{1,0:T(8,128)(2,1)}, bf16[96,768]{1,0:T(8,128)(2,1)S(1)}, u32[]{:S(2)}, u32[]{:S(2)}) collective-permute-start(bf16[96,768]{1,0:T(8,128)(2,1)} %get-tuple-element.130), channel_id=1, source_target_pairs={{0,16},{4,20},{8,24},{12,28},{16,0},{20,4},{24,8},{28,12},{1,17},{... | collective-permute-start | bytes 442376 | tf_op jit(solution)/shard_map/ppermute | solution.py:812
  25.4 18.7 %collective-permute-start.9 = (bf16[96,768]{1,0:T(8,128)(2,1)}, bf16[96,768]{1,0:T(8,128)(2,1)S(1)}, u32[]{:S(2)}, u32[]{:S(2)}) collective-permute-start(bf16[96,768]{1,0:T(8,128)(2,1)} %get-tuple-element.130), channel_id=1, source_target_pairs={{0,8},{4,12},{8,0},{12,4},{16,24},{20,28},{24,16},{28,20},{1,9},{5... | collective-permute-start | bytes 442376 | tf_op jit(solution)/shard_map/ppermute | solution.py:812
  26.6 17.5 %collective-permute-start.10 = (bf16[96,768]{1,0:T(8,128)(2,1)}, bf16[96,768]{1,0:T(8,128)(2,1)S(1)}, u32[]{:S(2)}, u32[]{:S(2)}) collective-permute-start(bf16[96,768]{1,0:T(8,128)(2,1)} %get-tuple-element.130), channel_id=1, source_target_pairs={{0,24},{4,28},{8,16},{12,20},{16,8},{20,12},{24,0},{28,4},{1,25},{... | collective-permute-start | bytes 442376 | tf_op jit(solution)/shard_map/ppermute | solution.py:812
  32.3 11.9 %collective-permute-start.11 = (bf16[208,768]{1,0:T(8,128)(2,1)}, bf16[208,768]{1,0:T(8,128)(2,1)S(1)}, u32[]{:S(2)}, u32[]{:S(2)}) collective-permute-start(bf16[208,768]{1,0:T(8,128)(2,1)} %get-tuple-element.139.refs_6_.refs_10_), channel_id=1, source_target_pairs={{0,2},{1,3},{2,0},{3,1},{4,6},{5,7},{6,4},{7,5},{8,10},{9,11},{10,... | collective-permute-start | bytes 958472 | tf_op jit(solution)/shard_map/ppermute | solution.py:812
  44.2 11.0 %collective-permute-start.12 = (bf16[1024,192]{1,0:T(8,128)(2,1)}, bf16[1024,192]{1,0:T(8,128)(2,1)S(1)}, u32[]{:S(2)}, u32[]{:S(2)}) collective-permute-start(bf16[1024,192]{1,0:T(8,128)(2,1)} %get-tuple-element.137.refs_2_.refs_6_), channel_id=1, source_target_pairs={{0,2},{1,3},{2,0},{3,1},{4,6},{5,7},{6,4},{7,5},{8,10},{9,11},{10,... | collective-permute-start | bytes 1179656 | tf_op jit(solution)/shard_map/ppermute | solution.py:812
  44.8 12.0 %collective-permute-start.17 = (bf16[4,96,768]{2,1,0:T(8,128)(2,1)S(1)}, bf16[4,96,768]{2,1,0:T(8,128)(2,1)S(1)}, u32[]{:S(2)}, u32[]{:S(2)}) collective-permute-start(bf16[4,96,768]{2,1,0:T(8,128)(2,1)S(1)} %pad_maximum_fusion.refs_3_), channel_id=1, source_target_pairs={{0,4},{4,0},{8,12},{12,8},{16,20},{20,16},{24,28},{28,24},{1,5},{5... | collective-permute-start | bytes 1769480 | tf_op jit(solution)/shard_map/ppermute | solution.py:812
  55.2 5.9 %collective-permute-start.16 = (bf16[208,768]{1,0:T(8,128)(2,1)S(1)}, bf16[208,768]{1,0:T(8,128)(2,1)S(1)}, u32[]{:S(2)}, u32[]{:S(2)}) collective-permute-start(bf16[208,768]{1,0:T(8,128)(2,1)S(1)} %collective-permute-done.11.refs_8_.refs_12_), channel_id=1, source_target_pairs={{0,1},{1,0},{2,3},{3,2},{4,5},{5,4},{6,7},{7,6},{8,9},{9,8},{10,11... | collective-permute-start | bytes 958472 | tf_op jit(solution)/shard_map/ppermute | solution.py:812
  56.8 18.5 %collective-permute-start.18 = (bf16[2,96,768]{2,1,0:T(8,128)(2,1)S(1)}, bf16[2,96,768]{2,1,0:T(8,128)(2,1)S(1)}, u32[]{:S(2)}, u32[]{:S(2)}) collective-permute-start(bf16[2,96,768]{2,1,0:T(8,128)(2,1)S(1)} %copy-done.49), channel_id=1, source_target_pairs={{0,16},{4,20},{8,24},{12,28},{16,0},{20,4},{24,8},{28,12},{1,17},{... | collective-permute-start | bytes 884744 | tf_op jit(solution)/shard_map/ppermute | solution.py:812
  59.9 15.4 %collective-permute-start.19 = (bf16[2,96,768]{2,1,0:T(8,128)(2,1)S(1)}, bf16[2,96,768]{2,1,0:T(8,128)(2,1)S(1)}, u32[]{:S(2)}, u32[]{:S(2)}) collective-permute-start(bf16[2,96,768]{2,1,0:T(8,128)(2,1)S(1)} %copy-done.49), channel_id=1, source_target_pairs={{0,8},{4,12},{8,0},{12,4},{16,24},{20,28},{24,16},{28,20},{1,9},{5... | collective-permute-start | bytes 884744 | tf_op jit(solution)/shard_map/ppermute | solution.py:812
  61.1 19.3 %collective-permute-start.20 = (bf16[2,96,768]{2,1,0:T(8,128)(2,1)S(1)}, bf16[2,96,768]{2,1,0:T(8,128)(2,1)S(1)}, u32[]{:S(2)}, u32[]{:S(2)}) collective-permute-start(bf16[2,96,768]{2,1,0:T(8,128)(2,1)S(1)} %copy-done.49), channel_id=1, source_target_pairs={{0,24},{4,28},{8,16},{12,20},{16,8},{20,12},{24,0},{28,4},{1,25},{... | collective-permute-start | bytes 884744 | tf_op jit(solution)/shard_map/ppermute | solution.py:812
  106.3 11.4 %collective-permute-start.24 = (bf16[256,768]{1,0:T(8,128)(2,1)S(1)}, bf16[256,768]{1,0:T(8,128)(2,1)S(1)}, u32[]{:S(2)}, u32[]{:S(2)}) collective-permute-start(bf16[256,768]{1,0:T(8,128)(2,1)S(1)} %far_sum.4.refs_2_), channel_id=1, source_target_pairs={{0,2},{1,3},{2,0},{3,1},{4,6},{5,7},{6,4},{7,5},{8,10},{9,11},{10,... | collective-permute-start | bytes 1179656 | tf_op jit(solution)/shard_map/ppermute | solution.py:812
  111.4 17.0 %collective-permute-start.23 = (bf16[4,96,768]{2,1,0:T(8,128)(2,1)S(1)}, bf16[4,96,768]{2,1,0:T(8,128)(2,1)S(1)}, u32[]{:S(2)}, u32[]{:S(2)}) collective-permute-start(bf16[4,96,768]{2,1,0:T(8,128)(2,1)S(1)} %get-tuple-element.155.refs_2_), channel_id=1, source_target_pairs={{0,4},{4,0},{8,12},{12,8},{16,20},{20,16},{24,28},{28,24},{1,5},{5... | collective-permute-start | bytes 1769480 | tf_op jit(solution)/shard_map/ppermute | solution.py:812
  124.7 10.2 %collective-permute-start.29 = (bf16[2,192,768]{2,1,0:T(8,128)(2,1)S(1)}, bf16[2,192,768]{2,1,0:T(8,128)(2,1)S(1)}, u32[]{:S(2)}, u32[]{:S(2)}) collective-permute-start(bf16[2,192,768]{2,1,0:T(8,128)(2,1)S(1)} %get-tuple-element.168), channel_id=1, source_target_pairs={{0,1},{1,0},{2,3},{3,2},{4,5},{5,4},{6,7},{7,6},{8,9},{9,8},{10,11... | collective-permute-start | bytes 1769480 | tf_op jit(solution)/shard_map/ppermute | solution.py:812
  125.2 10.8 %collective-permute-start.27 = (bf16[256,192]{1,0:T(8,128)(2,1)S(1)}, bf16[256,192]{1,0:T(8,128)(2,1)S(1)}, u32[]{:S(2)}, u32[]{:S(2)}) collective-permute-start(bf16[256,192]{1,0:T(8,128)(2,1)S(1)} %get-tuple-element.165), channel_id=1, source_target_pairs={{0,2},{1,3},{2,0},{3,1},{4,6},{5,7},{6,4},{7,5},{8,10},{9,11},{10,... | collective-permute-start | bytes 294920 | tf_op jit(solution)/shard_map/ppermute | solution.py:812
  126.0 10.1 %collective-permute-start.28 = (bf16[256,192]{1,0:T(8,128)(2,1)S(1)}, bf16[256,192]{1,0:T(8,128)(2,1)S(1)}, u32[]{:S(2)}, u32[]{:S(2)}) collective-permute-start(bf16[256,192]{1,0:T(8,128)(2,1)S(1)} %get-tuple-element.166), channel_id=1, source_target_pairs={{0,3},{1,2},{2,1},{3,0},{4,7},{5,6},{6,5},{7,4},{8,11},{9,10},{10,... | collective-permute-start | bytes 294920 | tf_op jit(solution)/shard_map/ppermute | solution.py:812
  126.9 21.9 %collective-permute-start.22 = (bf16[4,96,768]{2,1,0:T(8,128)(2,1)S(1)}, bf16[4,96,768]{2,1,0:T(8,128)(2,1)S(1)}, u32[]{:S(2)}, u32[]{:S(2)}) collective-permute-start(bf16[4,96,768]{2,1,0:T(8,128)(2,1)S(1)} %get-tuple-element.158.refs_14_), channel_id=1, source_target_pairs={{0,4},{4,0},{8,12},{12,8},{16,20},{20,16},{24,28},{28,24},{1,5},{5... | collective-permute-start | bytes 1769480 | tf_op jit(solution)/shard_map/ppermute | solution.py:812
  129.1 19.1 %collective-permute-start.26 = (bf16[2,96,768]{2,1,0:T(8,128)(2,1)S(1)}, bf16[2,96,768]{2,1,0:T(8,128)(2,1)S(1)}, u32[]{:S(2)}, u32[]{:S(2)}) collective-permute-start(bf16[2,96,768]{2,1,0:T(8,128)(2,1)S(1)} %get-tuple-element.162.refs_2_), channel_id=1, source_target_pairs={{0,8},{4,12},{8,0},{12,4},{16,24},{20,28},{24,16},{28,20},{1,9},{5... | collective-permute-start | bytes 884744 | tf_op jit(solution)/shard_map/ppermute | solution.py:812
  135.5 15.5 %collective-permute-start.32 = (bf16[192,768]{1,0:T(8,128)(2,1)S(1)}, bf16[192,768]{1,0:T(8,128)(2,1)S(1)}, u32[]{:S(2)}, u32[]{:S(2)}) collective-permute-start(bf16[192,768]{1,0:T(8,128)(2,1)S(1)} %far_sum.5.refs_8_), channel_id=1, source_target_pairs={{0,2},{1,3},{2,0},{3,1},{4,6},{5,7},{6,4},{7,5},{8,10},{9,11},{10,... | collective-permute-start | bytes 884744 | tf_op jit(solution)/shard_map/ppermute | solution.py:812
  157.8 7.4 %collective-permute-start.33 = (bf16[2,256,768]{2,1,0:T(8,128)(2,1)S(1)}, bf16[2,256,768]{2,1,0:T(8,128)(2,1)S(1)}, u32[]{:S(2)}, u32[]{:S(2)}) collective-permute-start(bf16[2,256,768]{2,1,0:T(8,128)(2,1)S(1)} %get-tuple-element.175), channel_id=1, source_target_pairs={{0,1},{1,0},{2,3},{3,2},{4,5},{5,4},{6,7},{7,6},{8,9},{9,8},{10,11... | collective-permute-start | bytes 2359304 | tf_op jit(solution)/shard_map/ppermute | solution.py:812
  157.8 26.6 %collective-permute-start.36 = (bf16[4,96,768]{2,1,0:T(8,128)(2,1)}, bf16[4,96,768]{2,1,0:T(8,128)(2,1)S(1)}, u32[]{:S(2)}, u32[]{:S(2)}) collective-permute-start(bf16[4,96,768]{2,1,0:T(8,128)(2,1)} %get-tuple-element.181), channel_id=1, source_target_pairs={{0,4},{4,0},{8,12},{12,8},{16,20},{20,16},{24,28},{28,24},{1,5},{5... | collective-permute-start | bytes 1769480 | tf_op jit(solution)/shard_map/ppermute | solution.py:812
  158.6 18.3 %collective-permute-start.30 = (bf16[2,96,768]{2,1,0:T(8,128)(2,1)S(1)}, bf16[2,96,768]{2,1,0:T(8,128)(2,1)}, u32[]{:S(2)}, u32[]{:S(2)}) collective-permute-start(bf16[2,96,768]{2,1,0:T(8,128)(2,1)S(1)} %get-tuple-element.171.refs_6_), channel_id=1, source_target_pairs={{0,8},{4,12},{8,0},{12,4},{16,24},{20,28},{24,16},{28,20},{1,9},{5... | collective-permute-start | bytes 884744 | tf_op jit(solution)/shard_map/ppermute | solution.py:812
  163.5 9.3 %collective-permute-start.31 = (bf16[96,768]{1,0:T(8,128)(2,1)S(1)}, bf16[96,768]{1,0:T(8,128)(2,1)S(1)}, u32[]{:S(2)}, u32[]{:S(2)}) collective-permute-start(bf16[96,768]{1,0:T(8,128)(2,1)S(1)} %get-tuple-element.169.refs_2_), channel_id=1, source_target_pairs={{0,16},{4,20},{8,24},{12,28},{16,0},{20,4},{24,8},{28,12},{1,17},{... | collective-permute-start | bytes 442376 | tf_op jit(solution)/shard_map/ppermute | solution.py:812
  168.0 20.5 %collective-permute-start.35 = (bf16[256,768]{1,0:T(8,128)(2,1)}, bf16[256,768]{1,0:T(8,128)(2,1)S(1)}, u32[]{:S(2)}, u32[]{:S(2)}) collective-permute-start(bf16[256,768]{1,0:T(8,128)(2,1)} %far_sum.6.refs_2_), channel_id=1, source_target_pairs={{0,2},{1,3},{2,0},{3,1},{4,6},{5,7},{6,4},{7,5},{8,10},{9,11},{10,... | collective-permute-start | bytes 1179656 | tf_op jit(solution)/shard_map/ppermute | solution.py:812
  173.4 16.7 %collective-permute-start.39 = (bf16[96,768]{1,0:T(8,128)(2,1)S(1)}, bf16[96,768]{1,0:T(8,128)(2,1)S(1)}, u32[]{:S(2)}, u32[]{:S(2)}) collective-permute-start(bf16[96,768]{1,0:T(8,128)(2,1)S(1)} %close.3.refs_2_.refs_0_), channel_id=1, source_target_pairs={{0,16},{4,20},{8,24},{12,28},{16,0},{20,4},{24,8},{28,12},{1,17},{... | collective-permute-start | bytes 442376 | tf_op jit(solution)/shard_map/ppermute | solution.py:812
  178.4 12.9 %collective-permute-start.38 = (bf16[96,768]{1,0:T(8,128)(2,1)S(1)}, bf16[96,768]{1,0:T(8,128)(2,1)S(1)}, u32[]{:S(2)}, u32[]{:S(2)}) collective-permute-start(bf16[96,768]{1,0:T(8,128)(2,1)S(1)} %get-tuple-element.176.refs_2_), channel_id=1, source_target_pairs={{0,16},{4,20},{8,24},{12,28},{16,0},{20,4},{24,8},{28,12},{1,17},{... | collective-permute-start | bytes 442376 | tf_op jit(solution)/shard_map/ppermute | solution.py:812
  184.4 8.1 %collective-permute-start.34 = (bf16[2,256,768]{2,1,0:T(8,128)(2,1)S(1)}, bf16[2,256,768]{2,1,0:T(8,128)(2,1)S(1)}, u32[]{:S(2)}, u32[]{:S(2)}) collective-permute-start(bf16[2,256,768]{2,1,0:T(8,128)(2,1)S(1)} %get-tuple-element.178.refs_2_), channel_id=1, source_target_pairs={{0,1},{1,0},{2,3},{3,2},{4,5},{5,4},{6,7},{7,6},{8,9},{9,8},{10,11... | collective-permute-start | bytes 2359304 | tf_op jit(solution)/shard_map/ppermute | solution.py:812
  185.1 12.6 %collective-permute-start.41 = (bf16[2,96,768]{2,1,0:T(8,128)(2,1)S(1)}, bf16[2,96,768]{2,1,0:T(8,128)(2,1)}, u32[]{:S(2)}, u32[]{:S(2)}) collective-permute-start(bf16[2,96,768]{2,1,0:T(8,128)(2,1)S(1)} %get-tuple-element.182.refs_6_), channel_id=1, source_target_pairs={{0,8},{4,12},{8,0},{12,4},{16,24},{20,28},{24,16},{28,20},{1,9},{5... | collective-permute-start | bytes 884744 | tf_op jit(solution)/shard_map/ppermute | solution.py:812
  194.0 12.0 %collective-permute-start.40 = (bf16[256,768]{1,0:T(8,128)(2,1)S(1)}, bf16[256,768]{1,0:T(8,128)(2,1)S(1)}, u32[]{:S(2)}, u32[]{:S(2)}) collective-permute-start(bf16[256,768]{1,0:T(8,128)(2,1)S(1)} %far_sum.7.refs_2_), channel_id=1, source_target_pairs={{0,2},{1,3},{2,0},{3,1},{4,6},{5,7},{6,4},{7,5},{8,10},{9,11},{10,... | collective-permute-start | bytes 1179656 | tf_op jit(solution)/shard_map/ppermute | solution.py:812
  194.5 13.8 %collective-permute-start.45 = (bf16[2,96,768]{2,1,0:T(8,128)(2,1)}, bf16[2,96,768]{2,1,0:T(8,128)(2,1)S(1)}, u32[]{:S(2)}, u32[]{:S(2)}) collective-permute-start(bf16[2,96,768]{2,1,0:T(8,128)(2,1)} %join.5.refs_2_.refs_0_), channel_id=1, source_target_pairs={{0,8},{4,12},{8,0},{12,4},{16,24},{20,28},{24,16},{28,20},{1,9},{5... | collective-permute-start | bytes 884744 | tf_op jit(solution)/shard_map/ppermute | solution.py:812
  195.1 20.4 %collective-permute-start.46 = (bf16[256,768]{1,0:T(8,128)(2,1)S(1)}, bf16[256,768]{1,0:T(8,128)(2,1)S(1)}, u32[]{:S(2)}, u32[]{:S(2)}) collective-permute-start(bf16[256,768]{1,0:T(8,128)(2,1)S(1)} %get-tuple-element.193.refs_2_.refs_0_), channel_id=1, source_target_pairs={{0,2},{1,3},{2,0},{3,1},{4,6},{5,7},{6,4},{7,5},{8,10},{9,11},{10,... | collective-permute-start | bytes 1179656 | tf_op jit(solution)/shard_map/ppermute | solution.py:812
  196.7 19.6 %collective-permute-start.49 = (bf16[96,768]{1,0:T(8,128)(2,1)S(1)}, bf16[96,768]{1,0:T(8,128)(2,1)}, u32[]{:S(2)}, u32[]{:S(2)}) collective-permute-start(bf16[96,768]{1,0:T(8,128)(2,1)S(1)} %close.4.refs_2_.refs_0_), channel_id=1, source_target_pairs={{0,16},{4,20},{8,24},{12,28},{16,0},{20,4},{24,8},{28,12},{1,17},{... | collective-permute-start | bytes 442376 | tf_op jit(solution)/shard_map/ppermute | solution.py:812
  197.7 17.2 %collective-permute-start.44 = (f32[6,768]{1,0:T(8,128)S(1)}, f32[6,768]{1,0:T(8,128)S(1)}, u32[]{:S(2)}, u32[]{:S(2)}) collective-permute-start(f32[6,768]{1,0:T(8,128)S(1)} %vec_add.2.refs_2_.refs_0_), channel_id=1, source_target_pairs={{0,2},{1,3},{2,0},{3,1},{4,6},{5,7},{6,4},{7,5},{8,10},{9,11},{10,... | collective-permute-start | bytes 55304 | tf_op jit(solution)/shard_map/ppermute | solution.py:812
  206.0 15.2 %collective-permute-start.43 = (bf16[96,768]{1,0:T(8,128)(2,1)}, bf16[96,768]{1,0:T(8,128)(2,1)}, u32[]{:S(2)}, u32[]{:S(2)}) collective-permute-start(bf16[96,768]{1,0:T(8,128)(2,1)} %get-tuple-element.189.refs_4_), channel_id=1, source_target_pairs={{0,16},{4,20},{8,24},{12,28},{16,0},{20,4},{24,8},{28,12},{1,17},{... | collective-permute-start | bytes 442376 | tf_op jit(solution)/shard_map/ppermute | solution.py:812
  208.3 34.4 %collective-permute-start.42 = (bf16[256,768]{1,0:T(8,128)(2,1)S(1)}, bf16[256,768]{1,0:T(8,128)(2,1)S(1)}, u32[]{:S(2)}, u32[]{:S(2)}) collective-permute-start(bf16[256,768]{1,0:T(8,128)(2,1)S(1)} %block_end.1.refs_2_.refs_0_), channel_id=1, source_target_pairs={{0,2},{1,3},{2,0},{3,1},{4,6},{5,7},{6,4},{7,5},{8,10},{9,11},{10,... | collective-permute-start | bytes 1179656 | tf_op jit(solution)/shard_map/ppermute | solution.py:812
  217.8 9.1 %collective-permute-start.54 = (bf16[2,96,768]{2,1,0:T(8,128)(2,1)S(1)}, bf16[2,96,768]{2,1,0:T(8,128)(2,1)}, u32[]{:S(2)}, u32[]{:S(2)}) collective-permute-start(bf16[2,96,768]{2,1,0:T(8,128)(2,1)S(1)} %join.7.refs_4_.refs_0_), channel_id=1, source_target_pairs={{0,8},{4,12},{8,0},{12,4},{16,24},{20,28},{24,16},{28,20},{1,9},{5... | collective-permute-start | bytes 884744 | tf_op jit(solution)/shard_map/ppermute | solution.py:812
  218.5 15.0 %collective-permute-start.53 = (bf16[4,96,768]{2,1,0:T(8,128)(2,1)S(1)}, bf16[4,96,768]{2,1,0:T(8,128)(2,1)S(1)}, u32[]{:S(2)}, u32[]{:S(2)}) collective-permute-start(bf16[4,96,768]{2,1,0:T(8,128)(2,1)S(1)} %join.6.refs_2_.refs_5_), channel_id=1, source_target_pairs={{0,4},{4,0},{8,12},{12,8},{16,20},{20,16},{24,28},{28,24},{1,5},{5... | collective-permute-start | bytes 1769480 | tf_op jit(solution)/shard_map/ppermute | solution.py:812
  224.1 15.7 %collective-permute-start.50 = (bf16[112,768]{1,0:T(8,128)(2,1)S(1)}, bf16[112,768]{1,0:T(8,128)(2,1)S(1)}, u32[]{:S(2)}, u32[]{:S(2)}) collective-permute-start(bf16[112,768]{1,0:T(8,128)(2,1)S(1)} %close.5.refs_2_.refs_0_), channel_id=1, source_target_pairs={{0,16},{4,20},{8,24},{12,28},{16,0},{20,4},{24,8},{28,12},{1,17},{... | collective-permute-start | bytes 516104 | tf_op jit(solution)/shard_map/ppermute | solution.py:812
  225.2 14.6 %collective-permute-start.51 = (bf16[112,768]{1,0:T(8,128)(2,1)S(1)}, bf16[112,768]{1,0:T(8,128)(2,1)S(1)}, u32[]{:S(2)}, u32[]{:S(2)}) collective-permute-start(bf16[112,768]{1,0:T(8,128)(2,1)S(1)} %close.5.refs_2_.refs_0_), channel_id=1, source_target_pairs={{0,8},{4,12},{8,0},{12,4},{16,24},{20,28},{24,16},{28,20},{1,9},{5... | collective-permute-start | bytes 516104 | tf_op jit(solution)/shard_map/ppermute | solution.py:812
  226.9 12.9 %collective-permute-start.52 = (bf16[112,768]{1,0:T(8,128)(2,1)S(1)}, bf16[112,768]{1,0:T(8,128)(2,1)S(1)}, u32[]{:S(2)}, u32[]{:S(2)}) collective-permute-start(bf16[112,768]{1,0:T(8,128)(2,1)S(1)} %close.5.refs_2_.refs_0_), channel_id=1, source_target_pairs={{0,24},{4,28},{8,16},{12,20},{16,8},{20,12},{24,0},{28,4},{1,25},{... | collective-permute-start | bytes 516104 | tf_op jit(solution)/shard_map/ppermute | solution.py:812
  233.6 16.3 %collective-permute-start.58 = (bf16[4,96,768]{2,1,0:T(8,128)(2,1)S(1)}, bf16[4,96,768]{2,1,0:T(8,128)(2,1)S(1)}, u32[]{:S(2)}, u32[]{:S(2)}) collective-permute-start(bf16[4,96,768]{2,1,0:T(8,128)(2,1)S(1)} %join.8.refs_7_.refs_5_), channel_id=1, source_target_pairs={{0,4},{4,0},{8,12},{12,8},{16,20},{20,16},{24,28},{28,24},{1,5},{5... | collective-permute-start | bytes 1769480 | tf_op jit(solution)/shard_map/ppermute | solution.py:812
  241.4 21.1 %collective-permute-start.57 = (bf16[4,112,768]{2,1,0:T(8,128)(2,1)S(1)}, bf16[4,112,768]{2,1,0:T(8,128)(2,1)}, u32[]{:S(2)}, u32[]{:S(2)}) collective-permute-start(bf16[4,112,768]{2,1,0:T(8,128)(2,1)S(1)} %join.9.refs_4_.refs_10_), channel_id=1, source_target_pairs={{0,4},{4,0},{8,12},{12,8},{16,20},{20,16},{24,28},{28,24},{1,5},{5... | collective-permute-start | bytes 2064392 | tf_op jit(solution)/shard_map/ppermute | solution.py:812
  (68 other events, 427.1 us)

commit v3 on v2

--- a/solution.py
+++ b/solution.py
@@ -235,13 +235,13 @@
         "outproj",
         0,
         after=after,
-        hbm=range(1, 2 + 2 * len(o)),
+        hbm=(1,),
     )
 
 
 def ffn_up_kernel(idx, c_ref, e_ref, fn_ref, *refs):
-    ups, downs = refs[:2], refs[2:6]
-    u_ref, dw_ref, st_ref, wu_ref, wd_ref = refs[6:]
+    ups, downs = refs[:2], refs[2:4]
+    u_ref, dw_ref, st_ref, wu_ref, wd_ref = refs[4:]
     rows = ups[0].shape[1]
 
     @pl.when(pl.program_id(0) == 0)
@@ -251,7 +251,7 @@
                 j = jnp.bitwise_xor(idx[0], k + odd)
                 at = pl.ds(pl.multiple_of(j * rows, rows), rows)
                 wu_ref[at, :] = ups[odd][i]
-                wd_ref[at, :] = downs[i][odd]
+                wd_ref[at, :] = downs[i // 2][i % 2 * 2 + odd]
 
     u = dot(c_ref[...], wu_ref[...])
     u_ref[...] = u
@@ -283,7 +283,7 @@
         idx,
         "ffn_up",
         7.5,
-        hbm=(1,) + tuple(range(3, 9)),
+        hbm=(1,),
     )
 
 
@@ -300,20 +300,24 @@
 
 
 SEND_SPEC = lambda n: pl.BlockSpec((1, BLK, n), lambda s, i: (jnp.minimum(s, 1), 0, 0))
-KEEP_SPEC = lambda n: pl.BlockSpec((1, BLK, n), lambda s, i: (jnp.maximum(s - 2, 0), 0, 0))
-
-
-def put_rel(send_ref, keep_ref, value):
+KEEP_SPEC = lambda n: full((BLK, n))
+
+
+def put_rel(send_ref, keep_ref, last_ref, value):
     @pl.when(pl.program_id(0) < 2)
     def _():
         send_ref[0] = value.astype(BF)
 
-    @pl.when(pl.program_id(0) >= 2)
+    @pl.when(pl.program_id(0) == 2)
     def _():
-        keep_ref[0] = value
-
-
-def ffn_mid_kernel(idx, u_ref, dw_ref, st_ref, fn_ref, wu_ref, w_ref, du_ref, send_ref, keep_ref, fg_ref):
+        keep_ref[...] = value
+
+    @pl.when(pl.program_id(0) == 3)
+    def _():
+        last_ref[...] = value
+
+
+def ffn_mid_kernel(idx, u_ref, dw_ref, st_ref, fn_ref, wu_ref, w_ref, du_ref, send_ref, keep_ref, last_ref, fg_ref):
     g = st_ref.shape[0]
     fl = u_ref.shape[1]
     n = g * fl
@@ -335,7 +339,7 @@
     slope = 0.5 * (1.0 + t) + 0.5 * u * (1.0 - t * t) * (GELU_A * (1.0 + (3.0 * GELU_B) * (u * u)))
     du = (dz * slope).astype(BF)
     du_ref[...] = du
-    put_rel(send_ref, keep_ref, dot_nt(du, wu_ref[...]))
+    put_rel(send_ref, keep_ref, last_ref, dot_nt(du, wu_ref[...]))
     grads = jnp.concatenate([jnp.sum(dw * hat, 0, keepdims=True), jnp.sum(dw, 0, keepdims=True)], axis=0)
 
     @pl.when(pl.program_id(0) == 0)
@@ -356,8 +360,8 @@
         [u, dw, st, fn, wu],
         [rel_spec(fl), rel_spec(fl), pl.BlockSpec((st.shape[0], 8, BLK), lambda s, i: (0, 0, rel_block(s, i)))]
         + fulls([fn, wu]),
-        [far((rows, fl), BF), far((rows, fl), BF), sds((2, BLK, d), BF), far((2, BLK, d), F32), sds((2, fl), F32)],
-        [rel_spec(fl), rel_spec(fl), SEND_SPEC(d), KEEP_SPEC(d), full((2, fl))],
+        [far((rows, fl), BF), far((rows, fl), BF), sds((2, BLK, d), BF), far((BLK, d), F32), sds((BLK, d), F32), sds((2, fl), F32)],
+        [rel_spec(fl), rel_spec(fl), SEND_SPEC(d), KEEP_SPEC(d), KEEP_SPEC(d), full((2, fl))],
         idx,
         "ffn_mid",
         6.5,
@@ -368,16 +372,16 @@
     rows, depth = x.shape
     d = w.shape[1]
 
-    def kernel(idx, x_ref, w_ref, send_ref, keep_ref):
-        put_rel(send_ref, keep_ref, dot(x_ref[...], w_ref[...]))
+    def kernel(idx, x_ref, w_ref, send_ref, keep_ref, last_ref):
+        put_rel(send_ref, keep_ref, last_ref, dot(x_ref[...], w_ref[...]))
 
     return run(
         kernel,
         (rows // BLK,),
         [x, w],
         [rel_spec(depth), full(w.shape)],
-        [sds((2, BLK, d), BF), far((2, BLK, d), F32)],
-        [SEND_SPEC(d), KEEP_SPEC(d)],
+        [sds((2, BLK, d), BF), far((BLK, d), F32), sds((BLK, d), F32)],
+        [SEND_SPEC(d), KEEP_SPEC(d), KEEP_SPEC(d)],
         idx,
         "ffn_out",
         0,
@@ -432,8 +436,8 @@
     groups = d // hw
     orows = hw // WAYS
 
-    def kernel(idx, a_ref, d_ref, w_ref, go0_ref, go1_ref, go2_ref, gs_ref, gk_ref, send_ref, keep_ref, scr, go_ref):
-        go_ref[...] = go0_ref[0] + go1_ref[0].astype(F32) + go2_ref[...].astype(F32)
+    def kernel(idx, a_ref, d_ref, w_ref, go0_ref, go1_ref, go2_ref, gs_ref, gk_ref, send_ref, keep_ref, last_ref, scr, go_ref):
+        go_ref[...] = go0_ref[...] + go1_ref[0].astype(F32) + go2_ref[...].astype(F32)
         for s in range(d // BLK):
             scr[s * BLK : (s + 1) * BLK, :] = dot_tn(a_ref[:, s * BLK : (s + 1) * BLK], d_ref[...])
         put_blocks(scr, gs_ref, gk_ref, idx[0], step)
@@ -444,17 +448,19 @@
                 dest[i, :, n:] = tail.astype(dest.dtype)
         for k in range(4):
             j = jnp.bitwise_xor(idx[1], k)
-            dest = send_ref if k % 2 else keep_ref
             value = dot_nt(d_ref[pl.ds(pl.multiple_of(j * BLK, BLK), BLK), :], w_ref[...])
-            dest[k // 2] = value.astype(dest.dtype)
+            if k % 2:
+                send_ref[k // 2] = value.astype(BF)
+            else:
+                (last_ref if k else keep_ref)[...] = value
 
     ins = [a, dqkv, wq, *go]
     lead = pl.BlockSpec((1, hw, d), lambda s, i: (0, 0, 0))
     half = (WAYS // 2, step, d)
     part = (2, BLK, d)
-    outs = [sds(half, BF), far(half, F32), sds(part, BF), far(part, F32)]
-    return run(
-        kernel, (1,), ins, fulls(ins[:3]) + [lead, lead, full(go[2].shape)], outs, fulls(outs), idx, "qkv_back", 5.5,
+    outs = [sds(half, BF), far(half, F32), sds(part, BF), far(part[1:], F32), sds(part[1:], F32)]
+    return run(
+        kernel, (1,), ins, fulls(ins[:4]) + [lead, full(go[2].shape)], outs, fulls(outs), idx, "qkv_back", 5.5,
         [pltpu.VMEM((d, n), F32), pltpu.VMEM((hw, d), F32)],
         after=after,
         hbm=(0, 2, 3),
@@ -465,8 +471,8 @@
     g = 4
     o_refs, w_refs = refs[:g], refs[g : 2 * g]
     dh_ref, ol_ref, ag_ref, *do_refs = refs[2 * g :]
-    do_refs, (gs_ref, gk_ref) = do_refs[:g], do_refs[g:]
-    dc = dc0_ref[0] + dc1_ref[0].astype(F32) + dc2_ref[...].astype(F32)
+    do_refs, (gs_ref, gk_ref, gl_ref) = do_refs[:g], do_refs[g:]
+    dc = dc0_ref[...] + dc1_ref[0].astype(F32) + dc2_ref[...].astype(F32)
     hat, r = normalize(h_ref[...])
     wgt = dc * on_ref[2:3, :]
     n = dc.shape[-1]
@@ -487,8 +493,11 @@
         )
     for k in range(g):
         y = (hats[k] * norms[k][0] + norms[k][1]).astype(BF)
-        dest = gs_ref if k % 2 else gk_ref
-        dest[k // 2] = dot_tn(y, dhb).astype(dest.dtype)
+        value = dot_tn(y, dhb)
+        if k % 2:
+            gs_ref[k // 2] = value.astype(BF)
+        else:
+            (gl_ref if k else gk_ref)[...] = value
 
 
 def shard_back(dc_keep, dc_one, dc_two, h, e, on, o, w, idx, after):
@@ -502,18 +511,18 @@
         shard_back_kernel,
         (1,),
         ins,
-        [lead, lead, full((BLK, d)), mine(d), mine(d)] + fulls([on]) + [mine(hw)] * g + fulls(w),
+        [full((BLK, d)), lead, full((BLK, d)), mine(d), mine(d)] + fulls([on]) + [mine(hw)] * g + fulls(w),
         [far((BLK, d), F32), sds((2, d), F32), sds((g, 2, hw), F32)]
         + [sds((BLK, hw), BF)] * g
-        + [sds((2, hw, d), BF), far((2, hw, d), F32)],
+        + [sds((2, hw, d), BF), far((hw, d), F32), sds((hw, d), F32)],
         [full((BLK, d)), full((2, d)), full((g, 2, hw))]
         + [full((BLK, hw))] * g
-        + [full((2, hw, d))] * 2,
+        + [full((2, hw, d)), full((hw, d)), full((hw, d))],
         idx,
         "shard_back",
         0,
         after=after,
-        hbm=(0, 1, 2, 3, 4) + tuple(range(6, 6 + 2 * g)),
+        hbm=(0, 3, 4) + tuple(range(6, 6 + 2 * g)),
     )
 
 
@@ -565,12 +574,12 @@
         11,
         [pltpu.VMEM((rows, hw), BF)] + [pltpu.VMEM((rows, hw), F32)] * 3,
         after=after,
-        hbm=range(8),
+        hbm=range(4),
     )[0]
 
 
 def shard_end_kernel(idx, da0_ref, da1_ref, da2_ref, tok_ref, on_ref, dh_ref, gt_ref, oe_ref):
-    da = da0_ref[0] + da1_ref[0].astype(F32) + da2_ref[...].astype(F32)
+    da = da0_ref[...] + da1_ref[0].astype(F32) + da2_ref[...].astype(F32)
     hat, r = normalize(tok_ref[...].astype(F32))
     wgt = da * on_ref[0:1, :]
     n = da.shape[-1]
@@ -586,7 +595,7 @@
         shard_end_kernel,
         (1,),
         [da_keep, da_one, da_two, tok, on, dh],
-        [lead, lead, full((BLK, d)), pl.BlockSpec((BLK, d), lambda s, i: (i[1], 0)), full(on.shape), full((BLK, d))],
+        [full((BLK, d)), lead, full((BLK, d)), pl.BlockSpec((BLK, d), lambda s, i: (i[1], 0)), full(on.shape), full((BLK, d))],
         [sds((BLK, d), BF), sds((2, d), F32)],
         [full((BLK, d)), full((2, d))],
         idx,
@@ -600,23 +609,24 @@
     rows, d = parts[0].shape
 
     def kernel(idx, *refs):
-        for k, part in enumerate(refs[:-1]):
+        for k, part in enumerate(refs[:-2]):
             at = pl.ds(pl.multiple_of(jnp.bitwise_xor(idx[1], k) * rows, rows), rows)
-            refs[-1][at, :] = part[...]
-
-    out = (rows * len(parts), d)
-    return run(kernel, (1,), parts, fulls(parts), [far(out, BF)], [full(out)], idx, name, 2, (), after)[0]
-
-
-def far_sum(keep, got, idx, after=(), tick=TICK):
-    rows, d = keep.shape[1:]
-
-    def kernel(idx, keep_ref, got_ref, out_ref):
-        out_ref[...] = (keep_ref[0] + got_ref[0].astype(F32)).astype(BF)
+            refs[-2][at, :] = part[...]
+        refs[-1][...] = jnp.zeros(refs[-1].shape, F32)
+
+    outs = [sds((rows * len(parts), d), BF), sds((8, 128), F32)]
+    return run(kernel, (1,), parts, fulls(parts), outs, fulls(outs), idx, name, 2, (), after)
+
+
+def far_sum(last, got, idx, after=(), tick=TICK):
+    rows, d = last.shape
+
+    def kernel(idx, last_ref, got_ref, out_ref):
+        out_ref[...] = (last_ref[...] + got_ref[0].astype(F32)).astype(BF)
 
     second = pl.BlockSpec((1, rows, d), lambda s, i: (1, 0, 0))
     out = [sds((rows, d), BF)]
-    return run(kernel, (1,), [keep, got], [second] * 2, out, fulls(out), idx, "far_sum", tick, (), after)[0]
+    return run(kernel, (1,), [last, got], [full((rows, d)), second], out, fulls(out), idx, "far_sum", tick, (), after)[0]
 
 
 def fold(keep, got, idx, after=(), tick=TICK):
@@ -629,7 +639,7 @@
         send_ref[...] = send if half > 1 else send[0]
 
     outs = [sds((half, rows, d), F32), sds((half, rows, d) if half > 1 else (rows, d), BF)]
-    return run(kernel, (1,), [keep, got], fulls([keep, got]), outs, fulls(outs), idx, "fold", tick, (), after)
+    return run(kernel, (1,), [keep, got], fulls([keep, got]), outs, fulls(outs), idx, "fold", tick, (), after, (0,) if half > 1 else ())
 
 
 def close(own, got, idx, after=(), vec=None):
@@ -668,15 +678,16 @@
     rows, d = last.shape
 
     def kernel(idx, h_ref, keep_ref, got_ref, last_ref, out_ref):
-        total = h_ref[...] + keep_ref[0] + got_ref[0].astype(F32) + last_ref[...].astype(F32)
+        total = h_ref[...] + keep_ref[...] + got_ref[0].astype(F32) + last_ref[...].astype(F32)
         out_ref[...] = total.astype(BF)
 
     lead = pl.BlockSpec((1, rows, d), lambda s, i: (0, 0, 0))
     mine = pl.BlockSpec((rows, d), lambda s, i: (i[1], 0))
+    own = full((rows, d))
     ins = [h, keep, got, last]
     out = [sds((rows, d), BF)]
     return run(
-        kernel, (1,), ins, [mine, lead, lead, full((rows, d))], out, fulls(out), idx, "block_end", TICK, (), after, (0,)
+        kernel, (1,), ins, [mine, own, lead, own], out, fulls(out), idx, "block_end", TICK, (), after, (0,)
     )[0]
 
 
@@ -730,23 +741,26 @@
         for i, k in enumerate(ORDER):
             for far_one, blocks in enumerate((even, odd)):
                 j = jnp.bitwise_xor(idx[0], k + far_one)
-                rest[5][pl.ds(pl.multiple_of(j * step, step), step), :] = blocks[i].astype(F32)
-        precondition(idx, ins, rest[:5], rest[5], total, flip)
+                rest[6][pl.ds(pl.multiple_of(j * step, step), step), :] = blocks[i].astype(F32)
+        precondition(idx, ins, rest[:5], rest[6], total, flip)
+        rest[5][...] = jnp.zeros(rest[5].shape, F32)
 
     ins = [*mats, near_blocks, far_blocks]
-    res = run(kernel, (1,), ins, fulls(ins), outs, fulls(outs), idx, name, 4, [scr], after, range(7))
+    outs = outs + [sds((8, 128), F32)]
+    res = run(kernel, (1,), ins, fulls(ins), outs, fulls(outs), idx, name, 4, [scr], after, range(5))
     return [res[0].T if flip else res[0], *res[1:]]
 
 
-def update_pair(mats, mats2, near_blocks, far_blocks, params, rates, total, idx, name, after=()):
+def update_pair(mats, mats2, near_blocks, far_blocks, norms, rates, total, idx, name, after=()):
     outs, flip, scr = update_outs(mats)
     outs2, flip2, scr2 = update_outs(mats2)
     step, n = mats[1].shape[1] // WAYS, mats[0].shape[1]
     step2, n2 = mats2[1].shape[1] // WAYS, mats2[0].shape[1]
-    half = params.shape[0]
+    half = (near_blocks.shape[1] - step) // 2
+    wide = norms[1].shape[1]
 
     def kernel(idx, *refs):
-        ins, ins2, (even, odd), par_ref, rest = refs[:5], refs[5:10], refs[10:12], refs[12], refs[13:]
+        ins, ins2, (even, odd), norm_refs, rest = refs[:5], refs[5:10], refs[10:12], refs[12:15], refs[15:]
         sums = 0.0
         for i, k in enumerate(ORDER):
             for far_one, blocks in enumerate((even, odd)):
@@ -755,21 +769,20 @@
                 rest[-2][pl.ds(pl.multiple_of(j * step, step), step), :] = block[:step, :n]
                 rest[-1][pl.ds(pl.multiple_of(j * step2, step2), step2), :] = unpack_rows(block[:step, n:], n2)
                 sums = sums + (block[step : step + half] + block[step + half :])
-        at = lax.broadcasted_iota(jnp.int32, sums.shape, 0) * sums.shape[1]
-        at = at + lax.broadcasted_iota(jnp.int32, sums.shape, 1)
-        slow, fast, border = rates
-        rest[10][...] = sums
-        rest[11][...] = par_ref[...] - jnp.where(at < border, slow, fast) * sums
+        grads = [sums[:4], jnp.concatenate([sums[4:5, :wide], sums[4:5, wide : 2 * wide]], axis=0), sums[5:7]]
+        for i, (grad, rate) in enumerate(zip(grads, (rates[0], rates[0], rates[1]))):
+            rest[10 + i][...] = grad
+            rest[13 + i][...] = norm_refs[i][...] - rate * grad
         precondition(idx, ins2, rest[5:10], rest[-1], total, flip2)
         precondition(idx, ins, rest[:5], rest[-2], total, flip)
 
-    all_outs = outs + outs2 + [sds(params.shape, F32)] * 2
-    ins = [*mats, *mats2, near_blocks, far_blocks, params]
-    res = run(kernel, (1,), ins, fulls(ins), all_outs, fulls(all_outs), idx, name, 6, [scr, scr2], after, range(13))
+    all_outs = outs + outs2 + [sds(x.shape, F32) for x in [*norms, *norms]]
+    ins = [*mats, *mats2, near_blocks, far_blocks, *norms]
+    res = run(kernel, (1,), ins, fulls(ins), all_outs, fulls(all_outs), idx, name, 6, [scr, scr2], after, range(10))
     res = list(res)
     res[0] = res[0].T if flip else res[0]
     res[5] = res[5].T if flip2 else res[5]
-    return res[:5], res[5:10], res[10], res[11]
+    return res[:5], res[5:10], res[10:]
 
 
 def body(
@@ -874,6 +887,7 @@
 
     up_go = after(up_own, first[2], first[4], first[6], down_two)
     up_z = [dp(up_go, k) for k in ORDER[1:]]
+    down_z2 = dp(after(down_two, up_go), 4)
     q, k, v, wq, wo = project(a_low, attn_norm, first, hw, idx)
     wo_far = mp(wo, 2)
     o, probs = attend(start, q, k, v, idx)
@@ -882,17 +896,18 @@
     o, wo, wo_far, up_four = lax.optimization_barrier((o, wo, wo_far, up_four))
     o_far = mp(o, 2)
     up_x = dp(up_four, 1)
-    down_go = after(down_two, up_four)
-    down_z = [dp(down_go, k) for k in ORDER[1:]]
-    o_near, wo_near, wo_last = mp(after(o, o_far), 1), mp(after(wo, o_far), 1), mp(after(wo_far, o_far), 1)
+    wo_near, wo_last = mp(after(wo, up_four), 1), mp(wo_far, 1)
+    down_four = join([down_two, down_z2], idx, [up_four, wo_near, wo_last])
+    down_z1 = dp(down_four, 2)
+    o_near = mp(after(o, o_far), 1)
     o_all = [o, o_near, o_far, mp(o_far, 1)]
     wo_all = [wo, wo_near, wo_far, wo_last]
     hidden, c_low = outproj(outer_norms, tokens, o_all, wo_all, idx, [up_x])
-    u, dw, stats, wu, wd = ffn_up(c_low, cotangent, ffn_norm, [up_four, up_x, down_two, *down_z], idx)
+    u, dw, stats, wu, wd = ffn_up(c_low, cotangent, ffn_norm, [up_four, up_x, down_four, down_z1], idx)
     stats = lax.all_gather(stats, "mp")
-    w_low, du, dc_send, dc_keep, ffn_grads = ffn_mid(u, dw, stats, ffn_norm, wu, idx)
+    w_low, du, dc_send, dc_keep, dc_last, ffn_grads = ffn_mid(u, dw, stats, ffn_norm, wu, idx)
     dc_got = mp(dc_send, 1)
-    dc_sum = far_sum(dc_keep, dc_got, idx)
+    dc_sum = far_sum(dc_last, dc_got, idx)
     down_send, down_keep = weight_grad(w_low, cotangent, idx, "grad_down", [dc_sum])
     down_x = dp(down_send, 1)
     up_send, up_keep = weight_grad(c_low, du, idx, "grad_up", [down_send])
@@ -900,32 +915,36 @@
     dh, outer_late, attn_grads, *rest = shard_back(
         dc_keep, dc_got, mp(dc_sum, 2), hidden, cotangent, outer_norms, o_all, wo_all, idx, [up_send]
     )
-    do, (go_send, go_keep) = rest[:n_mp], rest[n_mp:]
+    do, (go_send, go_keep, go_last) = rest[:n_mp], rest[n_mp:]
     do = [do[0]] + [mp(do[k], k) for k in range(1, n_mp)]
     go_got = mp(go_send, 1)
-    down_t, down_low = fold(down_keep, down_x, idx, [do[1]], 0)
-    go_sum = far_sum(go_keep, go_got, idx, [down_low], 0)
+    bo_send, bo_keep, bo_last = ffn_out(w_low, wd, idx, [do[1]])
+    bo_got = mp(bo_send, 1)
+    down_t, down_low = fold(down_keep, down_x, idx, [bo_send], 0)
+    go_sum = far_sum(go_last, go_got, idx, [down_low], 0)
     dqkv = attend_back(q, k, v, probs, do, idx, [go_sum])
     down_z1 = dp(down_low, 2)
     go_far = mp(go_sum, 2)
     down_t, down_low = fold(down_t, down_z1, idx, [dqkv])
     up_t, up_low = fold(up_keep, up_x2, idx, [down_low])
-    qkv_send, qkv_keep, da_send, da_keep = qkv_back(a_low, dqkv, wq, [go_keep, go_got, go_far], idx, [up_low])
+    bo_sum = far_sum(bo_last, bo_got, idx, [up_low])
+    bo_far = mp(bo_sum, 2)
+    qkv_send, qkv_keep, da_send, da_keep, da_last = qkv_back(a_low, dqkv, wq, [go_keep, go_got, go_far], idx, [bo_sum])
 
     down_z2, up_z1 = dp(down_low, 4), dp(up_low, 2)
     qkv_x = dp(qkv_send, 1)
     da_got = mp(da_send, 1)
-    da_sum = far_sum(da_keep, da_got, idx)
+    da_sum = far_sum(da_last, da_got, idx)
     da_far = mp(da_sum, 2)
     down_done = fine_sum(close(down_t, [down_z2], idx, [da_sum]))
     down_r4 = dp(down_done, 4)
     up_t, up_low = fold(up_t, up_z1, idx, [down_done])
     up_z2 = dp(up_low, 4)
-    bo_send, bo_keep = ffn_out(w_low, wd, idx, [up_low])
-    bo_got = mp(bo_send, 1)
-    qkv_t, qkv_low = fold(qkv_keep, qkv_x, idx, [bo_send], 0)
+    qkv_t, qkv_low = fold(qkv_keep, qkv_x, idx, [up_low], 0)
     qkv_z1 = dp(qkv_low, 2)
-    gt, outer_early = shard_end(da_keep, da_got, da_far, tokens, outer_norms, dh, idx, [qkv_low])
+    out_own = block_end(hidden, bo_keep, bo_got, bo_far, idx, [qkv_low])
+    out_far = mp(out_own, 2)
+    gt, outer_early = shard_end(da_keep, da_got, da_far, tokens, outer_norms, dh, idx, [out_own])
     gt_far = mp(gt, 2)
     lanes = outer_late.shape[1]
     vec = jnp.concatenate([outer_early, outer_late, attn_grads.reshape(-1, lanes)])
@@ -934,36 +953,26 @@
     down_r2 = dp(down_two, 2)
     up_done = fine_sum(close(up_t, [up_z2], idx, [down_two]))
     up_r4 = dp(up_done, 4)
-    vec = vec_add(vec, vec_got, idx, [up_done])
-    vec_got = mp(vec, 2)
-    bo_sum = far_sum(bo_keep, bo_got, idx, [vec])
-    bo_far = mp(bo_sum, 2)
-    qkv_t, qkv_low = fold(qkv_t, qkv_z1, idx, [bo_sum])
+    qkv_t, qkv_low = fold(qkv_t, qkv_z1, idx, [up_done])
     qkv_z2 = dp(qkv_low, 4)
-    out_own = block_end(hidden, bo_keep, bo_got, bo_far, idx, [qkv_low])
-    out_far = mp(out_own, 2)
-    gt_far = after(gt_far, out_own)
+    gt_far = after(gt_far, qkv_low)
     gt_all = [gt, mp(after(gt, gt_far), 1), gt_far, mp(gt_far, 1)]
-    down_four = join([down_two, down_r2], idx, [out_own])
+    down_four = join([down_two, down_r2], idx, [qkv_low])
     down_other = dp(down_four, 1)
     vec = vec_add(vec, vec_got, idx, [down_four])
+    vec_got = mp(vec, 2)
     up_two = join([up_done, up_r4], idx, [vec])
+    vec = vec_add(vec, vec_got, idx, [up_two])
     up_r2 = dp(up_two, 2)
-    grad_tokens = spread_rows(gt_all, idx, "spread_tokens", [up_two])
-    attn_own = lax.dynamic_index_in_dim(vec[4:].reshape(attn_grads.shape), mp_at, 0, False)
-
-    def flat(*parts):
-        x = jnp.concatenate([p.reshape(-1) for p in parts])
-        return jnp.pad(x, (0, WAYS * lanes - x.shape[0])).reshape(WAYS, lanes)
-
-    vec = fine_sum(flat(vec[:4], attn_own, ffn_grads))
-    cut = outer_norms.size
-    cut2 = cut + attn_norm.size
-    size = cut2 + ffn_norm.size
-    params = flat(outer_norms, attn_norm, ffn_norm)
-    rates = (VEC_RATE / math.sqrt(total), UNIT_RATE / math.sqrt(total), cut2)
-
-    qkv_own = close(qkv_t, [qkv_z2], idx, [grad_tokens], None if fine > 1 else vec)
+    grad_tokens, token = spread_rows(gt_all, idx, "spread_tokens", [vec])
+    out_far = after(out_far, vec)
+    out_all = [out_own, mp(after(out_own, out_far), 1), out_far, mp(out_far, 1)]
+    block_out, token = spread_rows(out_all, idx, "spread_out", [token])
+    attn_own = lax.dynamic_slice_in_dim(vec[4:].reshape(n_mp, -1), mp_at, 1, 0)
+    attn_own = jnp.pad(attn_own, ((0, 0), (0, lanes - attn_own.shape[1])))
+    vec = jnp.concatenate([vec[:4], attn_own, ffn_grads, jnp.zeros((1, lanes), F32)])
+    vec = fine_sum(vec)
+    qkv_own = close(qkv_t, [qkv_z2], idx, [token], None if fine > 1 else vec)
     if fine > 1:
         high = vec.astype(BF)
         qkv_own = jnp.concatenate([fine_sum(qkv_own), high, (vec - high.astype(F32)).astype(BF)])
@@ -971,44 +980,31 @@
     up_four = join([up_two, up_r2], idx, [qkv_own])
     up_other = dp(up_four, 1)
     down_mats = [x[0] for x in (w_down, left_down, right_down, left_root_down, right_root_down)]
-    down_res = update_one(down_mats, down_four, down_other, total, idx, "update_down", [up_four])
-    qkv_four = join([qkv_own, *qkv_z], idx, [down_res[3]])
+    *down_res, token = update_one(down_mats, down_four, down_other, total, idx, "update_down", [up_four])
+    qkv_four = join([qkv_own, *qkv_z], idx, [token])
     qkv_other = dp(qkv_four, 1)
-    out_far = after(out_far, qkv_four)
-    out_all = [out_own, mp(after(out_own, out_far), 1), out_far, mp(out_far, 1)]
-    block_out = spread_rows(out_all, idx, "spread_out", [qkv_four])
-
     def mats(*arrays):
         return [x[0] for x in arrays]
 
     up_mats = mats(w_up, left_up, right_up, left_root_up, right_root_up)
-    up_res = update_one(up_mats, up_four, up_other, total, idx, "update_up", [block_out])
-    qkv_res, out_res, vec, new_vec = update_pair(
+    *up_res, token = update_one(up_mats, up_four, up_other, total, idx, "update_up", [qkv_four])
+    qkv_res, out_res, vecs = update_pair(
         mats(w_qkv, left_qkv, right_qkv, left_root_qkv, right_root_qkv),
         mats(w_out, left_out, right_out, left_root_out, right_root_out),
         qkv_four,
         qkv_other,
-        params,
-        rates,
+        [outer_norms, attn_norm, ffn_norm],
+        (VEC_RATE / math.sqrt(total), UNIT_RATE / math.sqrt(total)),
         total,
         idx,
         "update_qkv",
-        [up_res[3]],
-    )
-
-    def cut_up(x):
-        x = x.reshape(-1)
-        return (
-            x[:cut].reshape(outer_norms.shape),
-            x[cut:cut2].reshape(attn_norm.shape),
-            x[cut2:size].reshape(ffn_norm.shape),
-        )
+        [token],
+    )
 
     return (
         block_out,
         grad_tokens,
-        *cut_up(vec),
-        *cut_up(new_vec),
+        *vecs,
         *(x[None] for x in qkv_res),
         *(x[None] for x in out_res),
         *(x[None] for x in up_res),

time: 275 us -> 254 us (0.924)
  local copies, waits for them, and re-layouts: 22.1 us -> 4.26 us
  Pallas kernels: 118 us -> 114 us
    unnamed x114 -> x66, local copies, waits for them, and re-layouts: 16.2 us -> 2.96 us
    pallas_call x38 -> x39, Pallas kernels: 118 us -> 114 us  [run(): pl.pallas_call(kernel, grid_spec=pltpu.PrefetchScalarGridSpec(num_scalar_...]
    ppermute x59 -> x58, starting transfers between devices: 66.4 us -> 65.8 us  [swap(): return lax.ppermute(x, axis, [(i, i ^ k) for i in range(size)])]
    ppermute x59 -> x58, waiting for transfers between devices: 52.6 us -> 53.1 us  [swap(): return lax.ppermute(x, axis, [(i, i ^ k) for i in range(size)])]
  transfers between devices with their start and end apart: 59 -> 58, of which waited for: 18 -> 19; matrix products, arithmetic and copies ran while one was open for 3% -> 3% of each run, Pallas kernels for 32% -> 34%
where the time goes in v3:
time: 254 us; the launch traced here: 253 us
  Pallas kernels  114 us (45%)
  starting transfers between devices  65.8 us (26%)
  waiting for transfers between devices  53.1 us (21%)
  other arithmetic  9.03 us (4%)
  blocking collectives  5.59 us (2%)
  local copies, waits for them, and re-layouts  4.26 us (2%)
    pallas_call x39, Pallas kernels, run(): pl.pallas_call(kernel, grid_spec=pltpu.PrefetchScalarGridSpec(num_scalar_...  114 us
    ppermute x58, starting transfers between devices, swap(): return lax.ppermute(x, axis, [(i, i ^ k) for i in range(size)])  65.8 us
    ppermute x58, waiting for transfers between devices, swap(): return lax.ppermute(x, axis, [(i, i ^ k) for i in range(size)])  53.1 us
    all_gather x1, blocking collectives, body(): stats = lax.all_gather(stats, 'mp')  5.59 us
  transfers between devices with their start and end apart: 58, of which 19 were waited for; matrix products, arithmetic and copies ran while one was open for 3% of the time, Pallas kernels for 34%

profile of v3, /device:TPU:0, one launch (start us, length us, event | category | flops | bytes accessed | tf_op | source)
XLA Modules:
  0.0 253.0 jit_solution(8853042803731257427)
XLA Ops:
  2.8 3.0 %collective-permute-start = (bf16[96,768]{1,0:T(8,128)(2,1)S(1)}, bf16[96,768]{1,0:T(8,128)(2,1)S(1)}, u32[]{:S(2)}, u32[]{:S(2)}) collective-permute-start(bf16[96,768]{1,0:T(8,128)(2,1)S(1)} %maximum_maximum_fusion.refs_2_), channel_id=1, source_target_pairs={{0,4},{4,0},{8,12},{12,8},{16,20},{20,16},{24,28},{28,24},{1,5},{5... | collective-permute-start | bytes 442376 | tf_op jit(solution)/shard_map/ppermute | solution.py:825
  5.8 1.6 collective-permute-start.1
  7.4 2.6 %collective-permute-start.4 = (bf16[96,768]{1,0:T(8,128)(2,1)S(1)}, bf16[96,768]{1,0:T(8,128)(2,1)}, u32[]{:S(2)}, u32[]{:S(2)}) collective-permute-start(bf16[96,768]{1,0:T(8,128)(2,1)S(1)} %maximum_maximum_fusion.refs_2_), channel_id=1, source_target_pairs={{0,16},{4,20},{8,24},{12,28},{16,0},{20,4},{24,8},{28,12},{1,17},{... | collective-permute-start | bytes 442376 | tf_op jit(solution)/shard_map/ppermute | solution.py:825
  10.2 1.8 fusion.10
  13.1 1.7 convert_reduce_fusion
  23.8 1.7 collective-permute-start.8
  26.7 2.5 collective-permute-start.10
  29.2 4.9 %project.1 = (bf16[1024,192]{1,0:T(8,128)(2,1)}, bf16[1024,192]{1,0:T(8,128)(2,1)}, bf16[1024,192]{1,0:T(8,128)(2,1)}, bf16[768,576]{1,0:T(8,128)(2,1)}, bf16[208,768]{1,0:T(8,128)(2,1)}) custom-call(s32[3]{0:T(128)S(1)} %pad_add_fusion.idx, bf16[1024,768]{1,0:T(8,128)(2,1)S(1)} %fusion.5.refs_0_, f32[2,192]{1,0:T(2,128)S(1)} %copy-done.21, ...), custom_call_target="tpu_custom_call" | custom-call | flops 16000000000 | bytes 1024 | tf_op jit(solution)/shard_map/project/pallas_call | solution.py:43
  35.6 10.2 %attend.1 = (bf16[1024,192]{1,0:T(8,128)(2,1)}, bf16[3,1024,1024]{2,1,0:T(8,128)(2,1)}) custom-call(s32[3]{0:T(128)S(1)} %pad_add_fusion.idx, s32[1024,1]{1,0:T(8,128)S(1)} %copy.55.refs_0_, bf16[1024,192]{1,0:T(8,128)(2,1)} %get-tuple-element.139.refs_1_.refs_0_, bf16[1024,192]{1,0:T(8,128)(2,1)} %get-tuple-element.140.refs_2_.refs_1_, ...), custom_call_target="tpu_custom_call" | custom-call | flops 4000000000 | bytes 1024 | tf_op jit(solution)/shard_map/attend/pallas_call | solution.py:43
  46.5 1.6 collective-permute-start.18
  50.1 12.6 %collective-permute-done.18.refs_1_ = bf16[2,96,768]{2,1,0:T(8,128)(2,1)S(1)} collective-permute-done((bf16[2,96,768]{2,1,0:T(8,128)(2,1)S(1)}, bf16[2,96,768]{2,1,0:T(8,128)(2,1)S(1)}, u32[]{:S(2)}, u32[]{:S(2)}) %collective-permute-start.18) | collective-permute-done | bytes 294944 | tf_op jit(solution)/shard_map/ppermute | solution.py:825
  66.2 7.1 %outproj.1 = (f32[1024,768]{1,0:T(8,128)}, bf16[1024,768]{1,0:T(8,128)(2,1)S(1)}) custom-call(s32[3]{0:T(128)S(1)} %pad_add_fusion.idx, f32[4,768]{1,0:T(4,128)S(1)} %copy-done.15, bf16[1024,768]{1,0:T(8,128)(2,1)} %refs_3_.3, bf16[1024,192]{1,0:T(8,128)(2,1)S(1)} %copy-done.2, bf16[1024,192]{1,0:T(8,128)(2,1)S(1)} %collective-permute-done.13.refs_3_.refs_7_, ...), custom_call_target="tpu_custom_call" | custom-call | bytes 1024 | tf_op jit(solution)/shard_map/outproj/pallas_call | solution.py:43
  73.3 4.6 %collective-permute-done.19.refs_6_ = bf16[4,96,768]{2,1,0:T(8,128)(2,1)S(1)} collective-permute-done((bf16[4,96,768]{2,1,0:T(8,128)(2,1)S(1)}, bf16[4,96,768]{2,1,0:T(8,128)(2,1)S(1)}, u32[]{:S(2)}, u32[]{:S(2)}) %collective-permute-start.19) | collective-permute-done | bytes 589856 | tf_op jit(solution)/shard_map/ppermute | solution.py:825
  77.9 6.6 %ffn_up.1 = (f32[1024,768]{1,0:T(8,128)S(1)}, f32[1024,768]{1,0:T(8,128)S(1)}, f32[8,1024]{1,0:T(8,128)S(1)}, bf16[768,768]{1,0:T(8,128)(2,1)S(1)}, bf16[768,768]{1,0:T(8,128)(2,1)}) custom-call(s32[3]{0:T(128)S(1)} %pad_add_fusion.idx, bf16[1024,768]{1,0:T(8,128)(2,1)S(1)} %get-tuple-element.156.refs_0_, bf16[1024,768]{1,0:T(8,128)(2,1)} %refs_4_.2, ...), custom_call_target="tpu_custom_call" | custom-call | flops 3000000000 | bytes 1024 | tf_op jit(solution)/shard_map/ffn_up/pallas_call | solution.py:43
  84.4 5.6 %all-gather = f32[32,1024]{1,0:T(8,128)S(1)} all-gather(f32[8,1024]{1,0:T(8,128)S(1)} %get-tuple-element.160), channel_id=2, replica_groups=mesh['dp'=8,'mp'=4] {'mp'}, dimensions={0}, use_global_device_ids=true | all-gather | bytes 163840 | tf_op jit(solution)/shard_map/all_gather | solution.py:907
  90.0 7.7 %ffn_mid.1 = (bf16[1024,768]{1,0:T(8,128)(2,1)}, bf16[1024,768]{1,0:T(8,128)(2,1)}, bf16[2,256,768]{2,1,0:T(8,128)(2,1)S(1)}, f32[256,768]{1,0:T(8,128)}, f32[256,768]{1,0:T(8,128)S(1)}, /*index=5*/f32[2,768]{1,0:T(2,128)S(1)}) custom-call(s32[3]{0:T(128)S(1)} %pad_add_fusion.idx, f32[1024,768]{1,0:T(8,128)S(1)} %get-tuple-element.158.refs_0_, ...), custom_call_target="tpu_custom_call" | custom-call | flops 2600000000 | bytes 1024 | tf_op jit(solution)/shard_map/ffn_mid/pallas_call | solution.py:43
  98.1 1.9 collective-permute-done.20.refs_1_
  101.9 3.7 %grad_down.1 = (bf16[4,96,768]{2,1,0:T(8,128)(2,1)S(1)}, f32[4,96,768]{2,1,0:T(8,128)}) custom-call(s32[3]{0:T(128)S(1)} %pad_add_fusion.idx, bf16[1024,768]{1,0:T(8,128)(2,1)S(1)} %copy-done.7, bf16[1024,768]{1,0:T(8,128)(2,1)S(1)} %copy-done.8, bf16[256,768]{1,0:T(8,128)(2,1)S(1)} %far_sum.4.refs_2_), custom_call_target="tpu_custom_call" | custom-call | flops 1400000000 | bytes 1024 | tf_op jit(solution)/shard_map/grad_down/pallas_call | solution.py:43
  107.1 3.7 %grad_up.1 = (bf16[4,96,768]{2,1,0:T(8,128)(2,1)S(1)}, f32[4,96,768]{2,1,0:T(8,128)}) custom-call(s32[3]{0:T(128)S(1)} %pad_add_fusion.idx, bf16[1024,768]{1,0:T(8,128)(2,1)S(1)} %get-tuple-element.156.refs_0_, bf16[1024,768]{1,0:T(8,128)(2,1)S(1)} %copy-done.22, bf16[4,96,768]{2,1,0:T(8,128)(2,1)S(1)} %get-tuple-element.168.refs_2_), custom_call_target="tpu_custom_call" | custom-call | flops 1400000000 | bytes 1024 | tf_op jit(solution)/shard_map/grad_up/pallas_call | solution.py:43
  112.1 5.1 %shard_back.1 = (f32[256,768]{1,0:T(8,128)}, f32[2,768]{1,0:T(2,128)S(1)}, f32[4,2,192]{2,1,0:T(2,128)S(1)}, bf16[256,192]{1,0:T(8,128)(2,1)S(1)}, bf16[256,192]...) custom-call(s32[3]{0:T(128)S(1)} %pad_add_fusion.idx, ...), custom_call_target="tpu_custom_call" | custom-call | bytes 1024 | tf_op jit(solution)/shard_map/shard_back/pallas_call | solution.py:43
  120.8 5.5 %ffn_out.1 = (bf16[2,256,768]{2,1,0:T(8,128)(2,1)S(1)}, f32[256,768]{1,0:T(8,128)}, f32[256,768]{1,0:T(8,128)S(1)}) custom-call(s32[3]{0:T(128)S(1)} %pad_add_fusion.idx, bf16[1024,768]{1,0:T(8,128)(2,1)} %get-tuple-element.162.refs_0_, bf16[768,768]{1,0:T(8,128)(2,1)} %get-tuple-element.163.refs_1_, bf16[256,192]{1,0:T(8,128)(2,1)S(1)} %collective-permute-done.22.refs_2_.refs_5_), custom_call_target="tpu_custom_call" | custom-call | bytes 1024 | tf_op jit(solution)/shard_map/ffn_out/pallas_call | solution.py:43
  126.5 2.0 fold.6
  130.2 11.3 %attend_back.1.refs_2_.refs_1_ = bf16[1024,576]{1,0:T(8,128)(2,1)S(1)} custom-call(s32[3]{0:T(128)S(1)} %pad_add_fusion.idx, bf16[1024,192]{1,0:T(8,128)(2,1)} %get-tuple-element.139.refs_1_.refs_0_, bf16[1024,192]{1,0:T(8,128)(2,1)} %get-tuple-element.140.refs_2_.refs_1_, bf16[1024,192]{1,0:T(8,128)(2,1)} %get-tuple-element.141.refs_3_.refs_2_, ...), custom_call_target="tpu_custom_call" | custom-call | flops 4400000000 | bytes 1024 | tf_op jit(solution)/shard_map/attend_back/pallas_call | solution.py:43
  142.1 2.0 fold.8
  144.9 6.6 %qkv_back.1 = (bf16[4,96,768]{2,1,0:T(8,128)(2,1)}, f32[4,96,768]{2,1,0:T(8,128)}, bf16[2,256,768]{2,1,0:T(8,128)(2,1)S(1)}, f32[256,768]{1,0:T(8,128)}, f32[256,768]{1,0:T(8,128)S(1)}) custom-call(s32[3]{0:T(128)S(1)} %pad_add_fusion.idx, bf16[1024,768]{1,0:T(8,128)(2,1)} %copy-done.6, bf16[1024,576]{1,0:T(8,128)(2,1)S(1)} %attend_back.1.refs_2_.refs_1_, ...), custom_call_target="tpu_custom_call" | custom-call | flops 2200000000 | bytes 1024 | tf_op jit(solution)/shard_map/qkv_back/pallas_call | solution.py:43
  153.2 1.6 collective-permute-start.33
  154.7 2.1 collective-permute-start.34
  156.8 1.5 collective-permute-start.30
  160.7 4.0 %collective-permute-done.34.refs_1_ = bf16[96,768]{1,0:T(8,128)(2,1)S(1)} collective-permute-done((bf16[96,768]{1,0:T(8,128)(2,1)S(1)}, bf16[96,768]{1,0:T(8,128)(2,1)S(1)}, u32[]{:S(2)}, u32[]{:S(2)}) %collective-permute-start.34) | collective-permute-done | bytes 147488 | tf_op jit(solution)/shard_map/ppermute | solution.py:825
  165.3 3.4 %collective-permute-start.39 = (bf16[96,768]{1,0:T(8,128)(2,1)S(1)}, bf16[96,768]{1,0:T(8,128)(2,1)S(1)}, u32[]{:S(2)}, u32[]{:S(2)}) collective-permute-start(bf16[96,768]{1,0:T(8,128)(2,1)S(1)} %close.3.refs_2_.refs_0_), channel_id=1, source_target_pairs={{0,16},{4,20},{8,24},{12,28},{16,0},{20,4},{24,8},{28,12},{1,17},{... | collective-permute-start | bytes 442376 | tf_op jit(solution)/shard_map/ppermute | solution.py:825
  169.9 1.9 fold.10
  171.8 3.5 %collective-permute-start.41 = (bf16[2,96,768]{2,1,0:T(8,128)(2,1)S(1)}, bf16[2,96,768]{2,1,0:T(8,128)(2,1)S(1)}, u32[]{:S(2)}, u32[]{:S(2)}) collective-permute-start(bf16[2,96,768]{2,1,0:T(8,128)(2,1)S(1)} %get-tuple-element.196.refs_4_), channel_id=1, source_target_pairs={{0,8},{4,12},{8,0},{12,4},{16,24},{20,28},{24,16},{28,20},{1,9},{5... | collective-permute-start | bytes 884744 | tf_op jit(solution)/shard_map/ppermute | solution.py:825
  175.3 2.1 block_end.1.refs_6_.refs_0_
  177.5 1.6 collective-permute-start.36
  182.8 1.7 collective-permute-done.41.refs_1_
  184.5 4.4 %collective-permute-start.44 = (bf16[96,768]{1,0:T(8,128)(2,1)S(1)}, bf16[96,768]{1,0:T(8,128)(2,1)S(1)}, u32[]{:S(2)}, u32[]{:S(2)}) collective-permute-start(bf16[96,768]{1,0:T(8,128)(2,1)S(1)} %close.4.refs_2_.refs_0_), channel_id=1, source_target_pairs={{0,16},{4,20},{8,24},{12,28},{16,0},{20,4},{24,8},{28,12},{1,17},{... | collective-permute-start | bytes 442376 | tf_op jit(solution)/shard_map/ppermute | solution.py:825
  189.6 4.4 %collective-permute-done.40.refs_1_ = bf16[2,96,768]{2,1,0:T(8,128)(2,1)S(1)} collective-permute-done((bf16[2,96,768]{2,1,0:T(8,128)(2,1)S(1)}, bf16[2,96,768]{2,1,0:T(8,128)(2,1)S(1)}, u32[]{:S(2)}, u32[]{:S(2)}) %collective-permute-start.40) | collective-permute-done | bytes 294944 | tf_op jit(solution)/shard_map/ppermute | solution.py:825
  194.0 2.8 %collective-permute-start.50 = (bf16[96,768]{1,0:T(8,128)(2,1)S(1)}, bf16[96,768]{1,0:T(8,128)(2,1)S(1)}, u32[]{:S(2)}, u32[]{:S(2)}) collective-permute-start(bf16[96,768]{1,0:T(8,128)(2,1)S(1)} %get-tuple-element.205.refs_2_), channel_id=1, source_target_pairs={{0,16},{4,20},{8,24},{12,28},{16,0},{20,4},{24,8},{28,12},{1,17},{... | collective-permute-start | bytes 442376 | tf_op jit(solution)/shard_map/ppermute | solution.py:825
  204.7 2.5 collective-permute-start.55
  207.1 1.8 spread_tokens.1
  208.9 2.9 %spread_out.1 = (bf16[1024,768]{1,0:T(8,128)(2,1)}, f32[8,128]{1,0:T(8,128)S(1)}) custom-call(s32[3]{0:T(128)S(1)} %pad_add_fusion.idx, bf16[256,768]{1,0:T(8,128)(2,1)S(1)} %block_end.1.refs_6_.refs_0_, bf16[256,768]{1,0:T(8,128)(2,1)} %collective-permute-done.45.refs_1_, bf16[256,768]{1,0:T(8,128)(2,1)S(1)} %collective-permute-done.36.refs_2_, ...), custom_call_target="tpu_custom_call" | custom-call | flops 800000000 | bytes 1024 | tf_op jit(solution)/shard_map/spread_out/pallas_call | solution.py:43
  212.6 4.3 %collective-permute-start.53 = (bf16[112,768]{1,0:T(8,128)(2,1)S(1)}, bf16[112,768]{1,0:T(8,128)(2,1)S(1)}, u32[]{:S(2)}, u32[]{:S(2)}) collective-permute-start(bf16[112,768]{1,0:T(8,128)(2,1)S(1)} %close.5.refs_2_.refs_0_), channel_id=1, source_target_pairs={{0,24},{4,28},{8,16},{12,20},{16,8},{20,12},{24,0},{28,4},{1,25},{... | collective-permute-start | bytes 516104 | tf_op jit(solution)/shard_map/ppermute | solution.py:825
  218.4 5.1 %update_down.1 = (f32[768,768]{1,0:T(8,128)}, f32[96,768]{1,0:T(8,128)}, f32[96,768]{1,0:T(8,128)}, f32[96,768]{1,0:T(8,128)}, bf16[96,768]{1,0:T(8,128)(2,1)}, /*index=5*/f32[8,128]{1,0:T(8,128)S(1)}) custom-call(s32[3]{0:T(128)S(1)} %pad_add_fusion.idx, f32[96,768]{1,0:T(8,128)} %bitcast.58, f32[96,768]{1,0:T(8,128)} %bitcast.71, f32[96,768]{1,0:T(8,128)} %bitcast.72, ...), custom_call_target="tpu_custom_call" | custom-call | flops 1600000000 | bytes 1024 | tf_op jit(solution)/shard_map/update_down/pallas_call | solution.py:43
  223.9 2.5 collective-permute-done.53.refs_3_
  227.6 6.2 %collective-permute-done.57.refs_6_ = bf16[4,96,768]{2,1,0:T(8,128)(2,1)S(1)} collective-permute-done((bf16[4,96,768]{2,1,0:T(8,128)(2,1)S(1)}, bf16[4,96,768]{2,1,0:T(8,128)(2,1)S(1)}, u32[]{:S(2)}, u32[]{:S(2)}) %collective-permute-start.57) | collective-permute-done | bytes 589856 | tf_op jit(solution)/shard_map/ppermute | solution.py:825
  233.8 5.1 %update_up.1 = (f32[768,768]{1,0:T(8,128)}, f32[96,768]{1,0:T(8,128)}, f32[96,768]{1,0:T(8,128)}, f32[96,768]{1,0:T(8,128)}, bf16[96,768]{1,0:T(8,128)(2,1)}, /*index=5*/f32[8,128]{1,0:T(8,128)S(1)}) custom-call(s32[3]{0:T(128)S(1)} %pad_add_fusion.idx, f32[96,768]{1,0:T(8,128)} %bitcast.59, f32[96,768]{1,0:T(8,128)} %bitcast.74, f32[96,768]{1,0:T(8,128)} %bitcast.75, ...), custom_call_target="tpu_custom_call" | custom-call | flops 1600000000 | bytes 1024 | tf_op jit(solution)/shard_map/update_up/pallas_call | solution.py:43
  238.9 7.2 %collective-permute-done.56.refs_11_ = bf16[4,112,768]{2,1,0:T(8,128)(2,1)S(1)} collective-permute-done((bf16[4,112,768]{2,1,0:T(8,128)(2,1)S(1)}, bf16[4,112,768]{2,1,0:T(8,128)(2,1)S(1)}, u32[]{:S(2)}, u32[]{:S(2)}) %collective-permute-start.56) | collective-permute-done | bytes 688160 | tf_op jit(solution)/shard_map/ppermute | solution.py:825
  246.1 6.7 %update_qkv.1 = (f32[576,768]{1,0:T(8,128)}, f32[96,768]{1,0:T(8,128)}, f32[72,576]{1,0:T(8,128)}, f32[96,576]{1,0:T(8,128)}, bf16[96,576]{1,0:T(8,128)(2,1)}, /...) custom-call(s32[3]{0:T(128)S(1)} %pad_add_fusion.idx, ...), custom_call_target="tpu_custom_call" | custom-call | flops 2400000000 | bytes 1024 | tf_op jit(solution)/shard_map/update_qkv/pallas_call | solution.py:43
  (200 shorter events, 54.6 us)
Async XLA Ops:
  2.8 22.7 %collective-permute-start = (bf16[96,768]{1,0:T(8,128)(2,1)S(1)}, bf16[96,768]{1,0:T(8,128)(2,1)S(1)}, u32[]{:S(2)}, u32[]{:S(2)}) collective-permute-start(bf16[96,768]{1,0:T(8,128)(2,1)S(1)} %maximum_maximum_fusion.refs_2_), channel_id=1, source_target_pairs={{0,4},{4,0},{8,12},{12,8},{16,20},{20,16},{24,28},{28,24},{1,5},{5... | collective-permute-start | bytes 442376 | tf_op jit(solution)/shard_map/ppermute | solution.py:825
  5.8 12.7 %collective-permute-start.1 = (bf16[96,768]{1,0:T(8,128)(2,1)S(1)}, bf16[96,768]{1,0:T(8,128)(2,1)}, u32[]{:S(2)}, u32[]{:S(2)}) collective-permute-start(bf16[96,768]{1,0:T(8,128)(2,1)S(1)} %maximum_maximum_fusion.refs_2_), channel_id=1, source_target_pairs={{0,8},{4,12},{8,0},{12,4},{16,24},{20,28},{24,16},{28,20},{1,9},{5... | collective-permute-start | bytes 442376 | tf_op jit(solution)/shard_map/ppermute | solution.py:825
  7.4 14.0 %collective-permute-start.4 = (bf16[96,768]{1,0:T(8,128)(2,1)S(1)}, bf16[96,768]{1,0:T(8,128)(2,1)}, u32[]{:S(2)}, u32[]{:S(2)}) collective-permute-start(bf16[96,768]{1,0:T(8,128)(2,1)S(1)} %maximum_maximum_fusion.refs_2_), channel_id=1, source_target_pairs={{0,16},{4,20},{8,24},{12,28},{16,0},{20,4},{24,8},{28,12},{1,17},{... | collective-permute-start | bytes 442376 | tf_op jit(solution)/shard_map/ppermute | solution.py:825
  10.0 11.9 %collective-permute-start.6 = (bf16[96,768]{1,0:T(8,128)(2,1)S(1)}, bf16[96,768]{1,0:T(8,128)(2,1)}, u32[]{:S(2)}, u32[]{:S(2)}) collective-permute-start(bf16[96,768]{1,0:T(8,128)(2,1)S(1)} %maximum_maximum_fusion.refs_2_), channel_id=1, source_target_pairs={{0,24},{4,28},{8,16},{12,20},{16,8},{20,12},{24,0},{28,4},{1,25},{... | collective-permute-start | bytes 442376 | tf_op jit(solution)/shard_map/ppermute | solution.py:825
  18.5 8.2 %collective-permute-start.3 = (bf16[96,768]{1,0:T(8,128)(2,1)}, bf16[96,768]{1,0:T(8,128)(2,1)S(1)}, u32[]{:S(2)}, u32[]{:S(2)}) collective-permute-start(bf16[96,768]{1,0:T(8,128)(2,1)} %collective-permute-done.1.refs_4_), channel_id=1, source_target_pairs={{0,4},{4,0},{8,12},{12,8},{16,20},{20,16},{24,28},{28,24},{1,5},{5... | collective-permute-start | bytes 442376 | tf_op jit(solution)/shard_map/ppermute | solution.py:825
  21.4 7.8 %collective-permute-start.5 = (bf16[96,768]{1,0:T(8,128)(2,1)}, bf16[96,768]{1,0:T(8,128)(2,1)S(1)}, u32[]{:S(2)}, u32[]{:S(2)}) collective-permute-start(bf16[96,768]{1,0:T(8,128)(2,1)} %collective-permute-done.4.refs_6_), channel_id=1, source_target_pairs={{0,4},{4,0},{8,12},{12,8},{16,20},{20,16},{24,28},{28,24},{1,5},{5... | collective-permute-start | bytes 442376 | tf_op jit(solution)/shard_map/ppermute | solution.py:825
  21.9 7.2 %collective-permute-start.7 = (bf16[96,768]{1,0:T(8,128)(2,1)}, bf16[96,768]{1,0:T(8,128)(2,1)S(1)}, u32[]{:S(2)}, u32[]{:S(2)}) collective-permute-start(bf16[96,768]{1,0:T(8,128)(2,1)} %collective-permute-done.6.refs_8_), channel_id=1, source_target_pairs={{0,4},{4,0},{8,12},{12,8},{16,20},{20,16},{24,28},{28,24},{1,5},{5... | collective-permute-start | bytes 442376 | tf_op jit(solution)/shard_map/ppermute | solution.py:825
  23.8 21.9 %collective-permute-start.8 = (bf16[96,768]{1,0:T(8,128)(2,1)}, bf16[96,768]{1,0:T(8,128)(2,1)S(1)}, u32[]{:S(2)}, u32[]{:S(2)}) collective-permute-start(bf16[96,768]{1,0:T(8,128)(2,1)} %get-tuple-element.143), channel_id=1, source_target_pairs={{0,16},{4,20},{8,24},{12,28},{16,0},{20,4},{24,8},{28,12},{1,17},{... | collective-permute-start | bytes 442376 | tf_op jit(solution)/shard_map/ppermute | solution.py:825
  25.5 20.3 %collective-permute-start.9 = (bf16[96,768]{1,0:T(8,128)(2,1)}, bf16[96,768]{1,0:T(8,128)(2,1)S(1)}, u32[]{:S(2)}, u32[]{:S(2)}) collective-permute-start(bf16[96,768]{1,0:T(8,128)(2,1)} %get-tuple-element.143), channel_id=1, source_target_pairs={{0,8},{4,12},{8,0},{12,4},{16,24},{20,28},{24,16},{28,20},{1,9},{5... | collective-permute-start | bytes 442376 | tf_op jit(solution)/shard_map/ppermute | solution.py:825
  26.7 19.1 %collective-permute-start.10 = (bf16[96,768]{1,0:T(8,128)(2,1)}, bf16[96,768]{1,0:T(8,128)(2,1)S(1)}, u32[]{:S(2)}, u32[]{:S(2)}) collective-permute-start(bf16[96,768]{1,0:T(8,128)(2,1)} %get-tuple-element.143), channel_id=1, source_target_pairs={{0,24},{4,28},{8,16},{12,20},{16,8},{20,12},{24,0},{28,4},{1,25},{... | collective-permute-start | bytes 442376 | tf_op jit(solution)/shard_map/ppermute | solution.py:825
  34.1 11.8 %collective-permute-start.11 = (bf16[208,768]{1,0:T(8,128)(2,1)}, bf16[208,768]{1,0:T(8,128)(2,1)S(1)}, u32[]{:S(2)}, u32[]{:S(2)}) collective-permute-start(bf16[208,768]{1,0:T(8,128)(2,1)} %get-tuple-element.153.refs_6_.refs_10_), channel_id=1, source_target_pairs={{0,2},{1,3},{2,0},{3,1},{4,6},{5,7},{6,4},{7,5},{8,10},{9,11},{10,... | collective-permute-start | bytes 958472 | tf_op jit(solution)/shard_map/ppermute | solution.py:825
  45.9 16.8 %collective-permute-start.15 = (bf16[208,768]{1,0:T(8,128)(2,1)S(1)}, bf16[208,768]{1,0:T(8,128)(2,1)S(1)}, u32[]{:S(2)}, u32[]{:S(2)}) collective-permute-start(bf16[208,768]{1,0:T(8,128)(2,1)S(1)} %copy-done.9), channel_id=1, source_target_pairs={{0,1},{1,0},{2,3},{3,2},{4,5},{5,4},{6,7},{7,6},{8,9},{9,8},{10,11... | collective-permute-start | bytes 958472 | tf_op jit(solution)/shard_map/ppermute | solution.py:825
  46.0 16.7 %collective-permute-start.16 = (bf16[208,768]{1,0:T(8,128)(2,1)S(1)}, bf16[208,768]{1,0:T(8,128)(2,1)S(1)}, u32[]{:S(2)}, u32[]{:S(2)}) collective-permute-start(bf16[208,768]{1,0:T(8,128)(2,1)S(1)} %collective-permute-done.11.refs_8_.refs_12_), channel_id=1, source_target_pairs={{0,1},{1,0},{2,3},{3,2},{4,5},{5,4},{6,7},{7,6},{8,9},{9,8},{10,11... | collective-permute-start | bytes 958472 | tf_op jit(solution)/shard_map/ppermute | solution.py:825
  46.5 16.2 %collective-permute-start.18 = (bf16[2,96,768]{2,1,0:T(8,128)(2,1)S(1)}, bf16[2,96,768]{2,1,0:T(8,128)(2,1)S(1)}, u32[]{:S(2)}, u32[]{:S(2)}) collective-permute-start(bf16[2,96,768]{2,1,0:T(8,128)(2,1)S(1)} %pad_maximum_fusion.1.refs_0_), channel_id=1, source_target_pairs={{0,16},{4,20},{8,24},{12,28},{16,0},{20,4},{24,8},{28,12},{1,17},{... | collective-permute-start | bytes 884744 | tf_op jit(solution)/shard_map/ppermute | solution.py:825
  48.1 15.9 %collective-permute-start.17 = (bf16[4,96,768]{2,1,0:T(8,128)(2,1)S(1)}, bf16[4,96,768]{2,1,0:T(8,128)(2,1)S(1)}, u32[]{:S(2)}, u32[]{:S(2)}) collective-permute-start(bf16[4,96,768]{2,1,0:T(8,128)(2,1)S(1)} %pad_maximum_fusion.refs_2_.refs_3_), channel_id=1, source_target_pairs={{0,4},{4,0},{8,12},{12,8},{16,20},{20,16},{24,28},{28,24},{1,5},{5... | collective-permute-start | bytes 1769480 | tf_op jit(solution)/shard_map/ppermute | solution.py:825
  49.6 13.8 %collective-permute-start.12 = (bf16[1024,192]{1,0:T(8,128)(2,1)}, bf16[1024,192]{1,0:T(8,128)(2,1)S(1)}, u32[]{:S(2)}, u32[]{:S(2)}) collective-permute-start(bf16[1024,192]{1,0:T(8,128)(2,1)} %get-tuple-element.150.refs_2_.refs_6_), channel_id=1, source_target_pairs={{0,2},{1,3},{2,0},{3,1},{4,6},{5,7},{6,4},{7,5},{8,10},{9,11},{10,... | collective-permute-start | bytes 1179656 | tf_op jit(solution)/shard_map/ppermute | solution.py:825
  63.3 14.5 %collective-permute-start.19 = (bf16[4,96,768]{2,1,0:T(8,128)(2,1)S(1)}, bf16[4,96,768]{2,1,0:T(8,128)(2,1)S(1)}, u32[]{:S(2)}, u32[]{:S(2)}) collective-permute-start(bf16[4,96,768]{2,1,0:T(8,128)(2,1)S(1)} %join.6.refs_5_), channel_id=1, source_target_pairs={{0,8},{4,12},{8,0},{12,4},{16,24},{20,28},{24,16},{28,20},{1,9},{5... | collective-permute-start | bytes 1769480 | tf_op jit(solution)/shard_map/ppermute | solution.py:825
  100.7 11.4 %collective-permute-start.21 = (bf16[256,768]{1,0:T(8,128)(2,1)S(1)}, bf16[256,768]{1,0:T(8,128)(2,1)S(1)}, u32[]{:S(2)}, u32[]{:S(2)}) collective-permute-start(bf16[256,768]{1,0:T(8,128)(2,1)S(1)} %far_sum.4.refs_2_), channel_id=1, source_target_pairs={{0,2},{1,3},{2,0},{3,1},{4,6},{5,7},{6,4},{7,5},{8,10},{9,11},{10,... | collective-permute-start | bytes 1179656 | tf_op jit(solution)/shard_map/ppermute | solution.py:825
  105.6 20.8 %collective-permute-start.25 = (bf16[4,96,768]{2,1,0:T(8,128)(2,1)S(1)}, bf16[4,96,768]{2,1,0:T(8,128)(2,1)S(1)}, u32[]{:S(2)}, u32[]{:S(2)}) collective-permute-start(bf16[4,96,768]{2,1,0:T(8,128)(2,1)S(1)} %get-tuple-element.168.refs_2_), channel_id=1, source_target_pairs={{0,4},{4,0},{8,12},{12,8},{16,20},{20,16},{24,28},{28,24},{1,5},{5... | collective-permute-start | bytes 1769480 | tf_op jit(solution)/shard_map/ppermute | solution.py:825
  117.1 11.3 %collective-permute-start.29 = (bf16[2,192,768]{2,1,0:T(8,128)(2,1)S(1)}, bf16[2,192,768]{2,1,0:T(8,128)(2,1)S(1)}, u32[]{:S(2)}, u32[]{:S(2)}) collective-permute-start(bf16[2,192,768]{2,1,0:T(8,128)(2,1)S(1)} %get-tuple-element.184), channel_id=1, source_target_pairs={{0,1},{1,0},{2,3},{3,2},{4,5},{5,4},{6,7},{7,6},{8,9},{9,8},{10,11... | collective-permute-start | bytes 1769480 | tf_op jit(solution)/shard_map/ppermute | solution.py:825
  117.7 12.0 %collective-permute-start.27 = (bf16[256,192]{1,0:T(8,128)(2,1)S(1)}, bf16[256,192]{1,0:T(8,128)(2,1)S(1)}, u32[]{:S(2)}, u32[]{:S(2)}) collective-permute-start(bf16[256,192]{1,0:T(8,128)(2,1)S(1)} %get-tuple-element.181), channel_id=1, source_target_pairs={{0,2},{1,3},{2,0},{3,1},{4,6},{5,7},{6,4},{7,5},{8,10},{9,11},{10,... | collective-permute-start | bytes 294920 | tf_op jit(solution)/shard_map/ppermute | solution.py:825
  118.1 12.1 %collective-permute-start.28 = (bf16[256,192]{1,0:T(8,128)(2,1)S(1)}, bf16[256,192]{1,0:T(8,128)(2,1)S(1)}, u32[]{:S(2)}, u32[]{:S(2)}) collective-permute-start(bf16[256,192]{1,0:T(8,128)(2,1)S(1)} %get-tuple-element.182), channel_id=1, source_target_pairs={{0,3},{1,2},{2,1},{3,0},{4,7},{5,6},{6,5},{7,4},{8,11},{9,10},{10,... | collective-permute-start | bytes 294920 | tf_op jit(solution)/shard_map/ppermute | solution.py:825
  119.3 22.8 %collective-permute-start.24 = (bf16[4,96,768]{2,1,0:T(8,128)(2,1)S(1)}, bf16[4,96,768]{2,1,0:T(8,128)(2,1)S(1)}, u32[]{:S(2)}, u32[]{:S(2)}) collective-permute-start(bf16[4,96,768]{2,1,0:T(8,128)(2,1)S(1)} %get-tuple-element.175.refs_14_), channel_id=1, source_target_pairs={{0,4},{4,0},{8,12},{12,8},{16,20},{20,16},{24,28},{28,24},{1,5},{5... | collective-permute-start | bytes 1769480 | tf_op jit(solution)/shard_map/ppermute | solution.py:825
  126.4 17.8 %collective-permute-start.23 = (bf16[2,256,768]{2,1,0:T(8,128)(2,1)S(1)}, bf16[2,256,768]{2,1,0:T(8,128)(2,1)S(1)}, u32[]{:S(2)}, u32[]{:S(2)}) collective-permute-start(bf16[2,256,768]{2,1,0:T(8,128)(2,1)S(1)} %get-tuple-element.172.refs_2_), channel_id=1, source_target_pairs={{0,1},{1,0},{2,3},{3,2},{4,5},{5,4},{6,7},{7,6},{8,9},{9,8},{10,11... | collective-permute-start | bytes 2359304 | tf_op jit(solution)/shard_map/ppermute | solution.py:825
  128.5 13.0 %collective-permute-start.26 = (bf16[2,96,768]{2,1,0:T(8,128)(2,1)S(1)}, bf16[2,96,768]{2,1,0:T(8,128)(2,1)S(1)}, u32[]{:S(2)}, u32[]{:S(2)}) collective-permute-start(bf16[2,96,768]{2,1,0:T(8,128)(2,1)S(1)} %get-tuple-element.178.refs_2_), channel_id=1, source_target_pairs={{0,8},{4,12},{8,0},{12,4},{16,24},{20,28},{24,16},{28,20},{1,9},{5... | collective-permute-start | bytes 884744 | tf_op jit(solution)/shard_map/ppermute | solution.py:825
  129.7 15.3 %collective-permute-start.31 = (bf16[192,768]{1,0:T(8,128)(2,1)S(1)}, bf16[192,768]{1,0:T(8,128)(2,1)S(1)}, u32[]{:S(2)}, u32[]{:S(2)}) collective-permute-start(bf16[192,768]{1,0:T(8,128)(2,1)S(1)} %far_sum.5.refs_8_), channel_id=1, source_target_pairs={{0,2},{1,3},{2,0},{3,1},{4,6},{5,7},{6,4},{7,5},{8,10},{9,11},{10,... | collective-permute-start | bytes 884744 | tf_op jit(solution)/shard_map/ppermute | solution.py:825
  152.5 17.4 %collective-permute-start.32 = (bf16[4,96,768]{2,1,0:T(8,128)(2,1)}, bf16[4,96,768]{2,1,0:T(8,128)(2,1)S(1)}, u32[]{:S(2)}, u32[]{:S(2)}) collective-permute-start(bf16[4,96,768]{2,1,0:T(8,128)(2,1)} %get-tuple-element.190), channel_id=1, source_target_pairs={{0,4},{4,0},{8,12},{12,8},{16,20},{20,16},{24,28},{28,24},{1,5},{5... | collective-permute-start | bytes 1769480 | tf_op jit(solution)/shard_map/ppermute | solution.py:825
  153.2 15.6 %collective-permute-start.33 = (bf16[2,96,768]{2,1,0:T(8,128)(2,1)}, bf16[2,96,768]{2,1,0:T(8,128)(2,1)S(1)}, u32[]{:S(2)}, u32[]{:S(2)}) collective-permute-start(bf16[2,96,768]{2,1,0:T(8,128)(2,1)} %copy-done.19), channel_id=1, source_target_pairs={{0,8},{4,12},{8,0},{12,4},{16,24},{20,28},{24,16},{28,20},{1,9},{5... | collective-permute-start | bytes 884744 | tf_op jit(solution)/shard_map/ppermute | solution.py:825
  154.7 10.0 %collective-permute-start.34 = (bf16[96,768]{1,0:T(8,128)(2,1)S(1)}, bf16[96,768]{1,0:T(8,128)(2,1)S(1)}, u32[]{:S(2)}, u32[]{:S(2)}) collective-permute-start(bf16[96,768]{1,0:T(8,128)(2,1)S(1)} %get-tuple-element.185.refs_2_), channel_id=1, source_target_pairs={{0,16},{4,20},{8,24},{12,28},{16,0},{20,4},{24,8},{28,12},{1,17},{... | collective-permute-start | bytes 442376 | tf_op jit(solution)/shard_map/ppermute | solution.py:825
  156.8 18.5 %collective-permute-start.30 = (bf16[256,768]{1,0:T(8,128)(2,1)S(1)}, bf16[256,768]{1,0:T(8,128)(2,1)S(1)}, u32[]{:S(2)}, u32[]{:S(2)}) collective-permute-start(bf16[256,768]{1,0:T(8,128)(2,1)S(1)} %far_sum.6.refs_6_), channel_id=1, source_target_pairs={{0,2},{1,3},{2,0},{3,1},{4,6},{5,7},{6,4},{7,5},{8,10},{9,11},{10,... | collective-permute-start | bytes 1179656 | tf_op jit(solution)/shard_map/ppermute | solution.py:825
  160.1 18.9 %collective-permute-start.37 = (bf16[256,768]{1,0:T(8,128)(2,1)S(1)}, bf16[256,768]{1,0:T(8,128)(2,1)S(1)}, u32[]{:S(2)}, u32[]{:S(2)}) collective-permute-start(bf16[256,768]{1,0:T(8,128)(2,1)S(1)} %far_sum.7.refs_2_), channel_id=1, source_target_pairs={{0,2},{1,3},{2,0},{3,1},{4,6},{5,7},{6,4},{7,5},{8,10},{9,11},{10,... | collective-permute-start | bytes 1179656 | tf_op jit(solution)/shard_map/ppermute | solution.py:825
  165.3 15.1 %collective-permute-start.39 = (bf16[96,768]{1,0:T(8,128)(2,1)S(1)}, bf16[96,768]{1,0:T(8,128)(2,1)S(1)}, u32[]{:S(2)}, u32[]{:S(2)}) collective-permute-start(bf16[96,768]{1,0:T(8,128)(2,1)S(1)} %close.3.refs_2_.refs_0_), channel_id=1, source_target_pairs={{0,16},{4,20},{8,24},{12,28},{16,0},{20,4},{24,8},{28,12},{1,17},{... | collective-permute-start | bytes 442376 | tf_op jit(solution)/shard_map/ppermute | solution.py:825
  169.4 12.4 %collective-permute-start.42 = (bf16[96,768]{1,0:T(8,128)(2,1)S(1)}, bf16[96,768]{1,0:T(8,128)(2,1)S(1)}, u32[]{:S(2)}, u32[]{:S(2)}) collective-permute-start(bf16[96,768]{1,0:T(8,128)(2,1)S(1)} %get-tuple-element.195.refs_2_), channel_id=1, source_target_pairs={{0,16},{4,20},{8,24},{12,28},{16,0},{20,4},{24,8},{28,12},{1,17},{... | collective-permute-start | bytes 442376 | tf_op jit(solution)/shard_map/ppermute | solution.py:825
  171.8 12.8 %collective-permute-start.41 = (bf16[2,96,768]{2,1,0:T(8,128)(2,1)S(1)}, bf16[2,96,768]{2,1,0:T(8,128)(2,1)S(1)}, u32[]{:S(2)}, u32[]{:S(2)}) collective-permute-start(bf16[2,96,768]{2,1,0:T(8,128)(2,1)S(1)} %get-tuple-element.196.refs_4_), channel_id=1, source_target_pairs={{0,8},{4,12},{8,0},{12,4},{16,24},{20,28},{24,16},{28,20},{1,9},{5... | collective-permute-start | bytes 884744 | tf_op jit(solution)/shard_map/ppermute | solution.py:825
  177.5 24.9 %collective-permute-start.36 = (bf16[256,768]{1,0:T(8,128)(2,1)S(1)}, bf16[256,768]{1,0:T(8,128)(2,1)S(1)}, u32[]{:S(2)}, u32[]{:S(2)}) collective-permute-start(bf16[256,768]{1,0:T(8,128)(2,1)S(1)} %block_end.1.refs_6_.refs_0_), channel_id=1, source_target_pairs={{0,2},{1,3},{2,0},{3,1},{4,6},{5,7},{6,4},{7,5},{8,10},{9,11},{10,... | collective-permute-start | bytes 1179656 | tf_op jit(solution)/shard_map/ppermute | solution.py:825
  180.4 17.0 %collective-permute-start.38 = (f32[6,768]{1,0:T(8,128)S(1)}, f32[6,768]{1,0:T(8,128)S(1)}, u32[]{:S(2)}, u32[]{:S(2)}) collective-permute-start(f32[6,768]{1,0:T(8,128)S(1)} %pad_maximum_fusion.2.refs_0_), channel_id=1, source_target_pairs={{0,1},{1,0},{2,3},{3,2},{4,5},{5,4},{6,7},{7,6},{8,9},{9,8},{10,11... | collective-permute-start | bytes 55304 | tf_op jit(solution)/shard_map/ppermute | solution.py:825
  180.4 19.6 %collective-permute-start.47 = (bf16[256,768]{1,0:T(8,128)(2,1)S(1)}, bf16[256,768]{1,0:T(8,128)(2,1)S(1)}, u32[]{:S(2)}, u32[]{:S(2)}) collective-permute-start(bf16[256,768]{1,0:T(8,128)(2,1)S(1)} %get-tuple-element.209.refs_2_.refs_0_), channel_id=1, source_target_pairs={{0,2},{1,3},{2,0},{3,1},{4,6},{5,7},{6,4},{7,5},{8,10},{9,11},{10,... | collective-permute-start | bytes 1179656 | tf_op jit(solution)/shard_map/ppermute | solution.py:825
  181.8 12.2 %collective-permute-start.40 = (bf16[2,96,768]{2,1,0:T(8,128)(2,1)S(1)}, bf16[2,96,768]{2,1,0:T(8,128)(2,1)S(1)}, u32[]{:S(2)}, u32[]{:S(2)}) collective-permute-start(bf16[2,96,768]{2,1,0:T(8,128)(2,1)S(1)} %join.7.refs_2_.refs_0_), channel_id=1, source_target_pairs={{0,8},{4,12},{8,0},{12,4},{16,24},{20,28},{24,16},{28,20},{1,9},{5... | collective-permute-start | bytes 884744 | tf_op jit(solution)/shard_map/ppermute | solution.py:825
  184.5 14.9 %collective-permute-start.44 = (bf16[96,768]{1,0:T(8,128)(2,1)S(1)}, bf16[96,768]{1,0:T(8,128)(2,1)S(1)}, u32[]{:S(2)}, u32[]{:S(2)}) collective-permute-start(bf16[96,768]{1,0:T(8,128)(2,1)S(1)} %close.4.refs_2_.refs_0_), channel_id=1, source_target_pairs={{0,16},{4,20},{8,24},{12,28},{16,0},{20,4},{24,8},{28,12},{1,17},{... | collective-permute-start | bytes 442376 | tf_op jit(solution)/shard_map/ppermute | solution.py:825
  194.0 17.8 %collective-permute-start.50 = (bf16[96,768]{1,0:T(8,128)(2,1)S(1)}, bf16[96,768]{1,0:T(8,128)(2,1)S(1)}, u32[]{:S(2)}, u32[]{:S(2)}) collective-permute-start(bf16[96,768]{1,0:T(8,128)(2,1)S(1)} %get-tuple-element.205.refs_2_), channel_id=1, source_target_pairs={{0,16},{4,20},{8,24},{12,28},{16,0},{20,4},{24,8},{28,12},{1,17},{... | collective-permute-start | bytes 442376 | tf_op jit(solution)/shard_map/ppermute | solution.py:825
  202.4 6.6 %collective-permute-start.46 = (bf16[256,768]{1,0:T(8,128)(2,1)S(1)}, bf16[256,768]{1,0:T(8,128)(2,1)}, u32[]{:S(2)}, u32[]{:S(2)}) collective-permute-start(bf16[256,768]{1,0:T(8,128)(2,1)S(1)} %collective-permute-done.36.refs_2_), channel_id=1, source_target_pairs={{0,1},{1,0},{2,3},{3,2},{4,5},{5,4},{6,7},{7,6},{8,9},{9,8},{10,11... | collective-permute-start | bytes 1179656 | tf_op jit(solution)/shard_map/ppermute | solution.py:825
  203.1 15.3 %collective-permute-start.54 = (bf16[4,96,768]{2,1,0:T(8,128)(2,1)S(1)}, bf16[4,96,768]{2,1,0:T(8,128)(2,1)S(1)}, u32[]{:S(2)}, u32[]{:S(2)}) collective-permute-start(bf16[4,96,768]{2,1,0:T(8,128)(2,1)S(1)} %join.8.refs_2_.refs_5_), channel_id=1, source_target_pairs={{0,4},{4,0},{8,12},{12,8},{16,20},{20,16},{24,28},{28,24},{1,5},{5... | collective-permute-start | bytes 1769480 | tf_op jit(solution)/shard_map/ppermute | solution.py:825
  204.7 12.2 %collective-permute-start.55 = (bf16[2,96,768]{2,1,0:T(8,128)(2,1)}, bf16[2,96,768]{2,1,0:T(8,128)(2,1)S(1)}, u32[]{:S(2)}, u32[]{:S(2)}) collective-permute-start(bf16[2,96,768]{2,1,0:T(8,128)(2,1)} %copy-done.17), channel_id=1, source_target_pairs={{0,8},{4,12},{8,0},{12,4},{16,24},{20,28},{24,16},{28,20},{1,9},{5... | collective-permute-start | bytes 884744 | tf_op jit(solution)/shard_map/ppermute | solution.py:825
  212.4 11.5 %collective-permute-start.51 = (bf16[112,768]{1,0:T(8,128)(2,1)S(1)}, bf16[112,768]{1,0:T(8,128)(2,1)S(1)}, u32[]{:S(2)}, u32[]{:S(2)}) collective-permute-start(bf16[112,768]{1,0:T(8,128)(2,1)S(1)} %close.5.refs_2_.refs_0_), channel_id=1, source_target_pairs={{0,16},{4,20},{8,24},{12,28},{16,0},{20,4},{24,8},{28,12},{1,17},{... | collective-permute-start | bytes 516104 | tf_op jit(solution)/shard_map/ppermute | solution.py:825
  212.5 11.4 %collective-permute-start.52 = (bf16[112,768]{1,0:T(8,128)(2,1)S(1)}, bf16[112,768]{1,0:T(8,128)(2,1)S(1)}, u32[]{:S(2)}, u32[]{:S(2)}) collective-permute-start(bf16[112,768]{1,0:T(8,128)(2,1)S(1)} %close.5.refs_2_.refs_0_), channel_id=1, source_target_pairs={{0,8},{4,12},{8,0},{12,4},{16,24},{20,28},{24,16},{28,20},{1,9},{5... | collective-permute-start | bytes 516104 | tf_op jit(solution)/shard_map/ppermute | solution.py:825
  212.6 13.8 %collective-permute-start.53 = (bf16[112,768]{1,0:T(8,128)(2,1)S(1)}, bf16[112,768]{1,0:T(8,128)(2,1)S(1)}, u32[]{:S(2)}, u32[]{:S(2)}) collective-permute-start(bf16[112,768]{1,0:T(8,128)(2,1)S(1)} %close.5.refs_2_.refs_0_), channel_id=1, source_target_pairs={{0,24},{4,28},{8,16},{12,20},{16,8},{20,12},{24,0},{28,4},{1,25},{... | collective-permute-start | bytes 516104 | tf_op jit(solution)/shard_map/ppermute | solution.py:825
  217.5 16.3 %collective-permute-start.57 = (bf16[4,96,768]{2,1,0:T(8,128)(2,1)S(1)}, bf16[4,96,768]{2,1,0:T(8,128)(2,1)S(1)}, u32[]{:S(2)}, u32[]{:S(2)}) collective-permute-start(bf16[4,96,768]{2,1,0:T(8,128)(2,1)S(1)} %join.10.refs_7_.refs_5_), channel_id=1, source_target_pairs={{0,4},{4,0},{8,12},{12,8},{16,20},{20,16},{24,28},{28,24},{1,5},{5... | collective-permute-start | bytes 1769480 | tf_op jit(solution)/shard_map/ppermute | solution.py:825
  227.0 19.2 %collective-permute-start.56 = (bf16[4,112,768]{2,1,0:T(8,128)(2,1)S(1)}, bf16[4,112,768]{2,1,0:T(8,128)(2,1)S(1)}, u32[]{:S(2)}, u32[]{:S(2)}) collective-permute-start(bf16[4,112,768]{2,1,0:T(8,128)(2,1)S(1)} %join.11.refs_7_.refs_10_), channel_id=1, source_target_pairs={{0,4},{4,0},{8,12},{12,8},{16,20},{20,16},{24,28},{28,24},{1,5},{5... | collective-permute-start | bytes 2064392 | tf_op jit(solution)/shard_map/ppermute | solution.py:825
  (43 other events, 273.9 us)

commit v4 on v3

--- a/solution.py
+++ b/solution.py
@@ -460,7 +460,7 @@
     part = (2, BLK, d)
     outs = [sds(half, BF), far(half, F32), sds(part, BF), far(part[1:], F32), sds(part[1:], F32)]
     return run(
-        kernel, (1,), ins, fulls(ins[:4]) + [lead, full(go[2].shape)], outs, fulls(outs), idx, "qkv_back", 5.5,
+        kernel, (1,), ins, fulls(ins[:4]) + [lead, full(go[2].shape)], outs, fulls(outs), idx, "qkv_back", 40,
         [pltpu.VMEM((d, n), F32), pltpu.VMEM((hw, d), F32)],
         after=after,
         hbm=(0, 2, 3),
@@ -615,7 +615,7 @@
         refs[-1][...] = jnp.zeros(refs[-1].shape, F32)
 
     outs = [sds((rows * len(parts), d), BF), sds((8, 128), F32)]
-    return run(kernel, (1,), parts, fulls(parts), outs, fulls(outs), idx, name, 2, (), after)
+    return run(kernel, (1,), parts, fulls(parts), outs, fulls(outs), idx, name, 0, (), after)
 
 
 def far_sum(last, got, idx, after=(), tick=TICK):
@@ -642,7 +642,7 @@
     return run(kernel, (1,), [keep, got], fulls([keep, got]), outs, fulls(outs), idx, "fold", tick, (), after, (0,) if half > 1 else ())
 
 
-def close(own, got, idx, after=(), vec=None):
+def close(own, got, idx, after=(), vec=None, tick=TICK):
     rows, d = got[0].shape
 
     def kernel(idx, own_ref, *refs):
@@ -658,10 +658,10 @@
 
     ins = [own, *got] + ([] if vec is None else [vec])
     out = [sds((rows if vec is None else rows + 2 * vec.shape[0], d), BF)]
-    return run(kernel, (1,), ins, fulls(ins), out, fulls(out), idx, "close", TICK, (), after)[0]
-
-
-def join(parts, idx, after=()):
+    return run(kernel, (1,), ins, fulls(ins), out, fulls(out), idx, "close", tick, (), after)[0]
+
+
+def join(parts, idx, after=(), tick=2 * TICK):
     shapes = [x.shape if len(x.shape) == 3 else (1, *x.shape) for x in parts]
 
     def kernel(idx, *refs):
@@ -671,7 +671,7 @@
             at += shape[0]
 
     out = [sds((sum(x[0] for x in shapes), *shapes[0][1:]), BF)]
-    return run(kernel, (1,), parts, fulls(parts), out, fulls(out), idx, "join", 2 * TICK, (), after)[0]
+    return run(kernel, (1,), parts, fulls(parts), out, fulls(out), idx, "join", tick, (), after)[0]
 
 
 def block_end(h, keep, got, last, idx, after=()):
@@ -691,12 +691,12 @@
     )[0]
 
 
-def vec_add(x, y, idx, after=()):
+def vec_add(x, y, idx, after=(), tick=TICK):
     def kernel(idx, x_ref, y_ref, out_ref):
         out_ref[...] = x_ref[...] + y_ref[...]
 
     out = [sds(x.shape, F32)]
-    return run(kernel, (1,), [x, y], fulls([x, y]), out, fulls(out), idx, "vec_add", TICK, (), after)[0]
+    return run(kernel, (1,), [x, y], fulls([x, y]), out, fulls(out), idx, "vec_add", tick, (), after)[0]
 
 
 def one_hot(place, count, width):
@@ -732,7 +732,7 @@
     return outs + [sds((rows, n), F32), sds((rows, n), BF)], flip, pltpu.VMEM((d, n), F32)
 
 
-def update_one(mats, near_blocks, far_blocks, total, idx, name, after=()):
+def update_one(mats, near_blocks, far_blocks, total, idx, name, after=(), tick=0):
     outs, flip, scr = update_outs(mats)
     step = mats[1].shape[1] // WAYS
 
@@ -747,7 +747,7 @@
 
     ins = [*mats, near_blocks, far_blocks]
     outs = outs + [sds((8, 128), F32)]
-    res = run(kernel, (1,), ins, fulls(ins), outs, fulls(outs), idx, name, 4, [scr], after, range(5))
+    res = run(kernel, (1,), ins, fulls(ins), outs, fulls(outs), idx, name, tick, [scr], after, range(5))
     return [res[0].T if flip else res[0], *res[1:]]
 
 
@@ -919,60 +919,56 @@
     do = [do[0]] + [mp(do[k], k) for k in range(1, n_mp)]
     go_got = mp(go_send, 1)
     bo_send, bo_keep, bo_last = ffn_out(w_low, wd, idx, [do[1]])
-    bo_got = mp(bo_send, 1)
     down_t, down_low = fold(down_keep, down_x, idx, [bo_send], 0)
     go_sum = far_sum(go_last, go_got, idx, [down_low], 0)
     dqkv = attend_back(q, k, v, probs, do, idx, [go_sum])
     down_z1 = dp(down_low, 2)
     go_far = mp(go_sum, 2)
+    bo_got = mp(after(bo_send, dqkv), 1)
     down_t, down_low = fold(down_t, down_z1, idx, [dqkv])
     up_t, up_low = fold(up_keep, up_x2, idx, [down_low])
-    bo_sum = far_sum(bo_last, bo_got, idx, [up_low])
-    bo_far = mp(bo_sum, 2)
-    qkv_send, qkv_keep, da_send, da_keep, da_last = qkv_back(a_low, dqkv, wq, [go_keep, go_got, go_far], idx, [bo_sum])
+    qkv_send, qkv_keep, da_send, da_keep, da_last = qkv_back(
+        a_low, dqkv, wq, [go_keep, go_got, go_far], idx, [up_low]
+    )
 
     down_z2, up_z1 = dp(down_low, 4), dp(up_low, 2)
     qkv_x = dp(qkv_send, 1)
     da_got = mp(da_send, 1)
-    da_sum = far_sum(da_last, da_got, idx)
+    bo_sum = far_sum(bo_last, bo_got, idx, [qkv_send], 0)
+    bo_far = mp(bo_sum, 2)
+    da_sum = far_sum(da_last, da_got, idx, [bo_sum])
     da_far = mp(da_sum, 2)
     down_done = fine_sum(close(down_t, [down_z2], idx, [da_sum]))
     down_r4 = dp(down_done, 4)
-    up_t, up_low = fold(up_t, up_z1, idx, [down_done])
+    qkv_t, qkv_low = fold(qkv_keep, qkv_x, idx, [down_done], 0)
+    qkv_z1 = dp(qkv_low, 2)
+    up_t, up_low = fold(up_t, up_z1, idx, [qkv_low])
     up_z2 = dp(up_low, 4)
-    qkv_t, qkv_low = fold(qkv_keep, qkv_x, idx, [up_low], 0)
-    qkv_z1 = dp(qkv_low, 2)
-    out_own = block_end(hidden, bo_keep, bo_got, bo_far, idx, [qkv_low])
+    down_two = join([down_done, down_r4], idx, [up_low])
+    down_r2 = dp(down_two, 2)
+    out_own = block_end(hidden, bo_keep, bo_got, bo_far, idx, [down_two])
     out_far = mp(out_own, 2)
     gt, outer_early = shard_end(da_keep, da_got, da_far, tokens, outer_norms, dh, idx, [out_own])
     gt_far = mp(gt, 2)
     lanes = outer_late.shape[1]
     vec = jnp.concatenate([outer_early, outer_late, attn_grads.reshape(-1, lanes)])
     vec_got = mp(vec, 1)
-    down_two = join([down_done, down_r4], idx, [gt])
-    down_r2 = dp(down_two, 2)
-    up_done = fine_sum(close(up_t, [up_z2], idx, [down_two]))
+    up_done = fine_sum(close(up_t, [up_z2], idx, [gt]))
     up_r4 = dp(up_done, 4)
     qkv_t, qkv_low = fold(qkv_t, qkv_z1, idx, [up_done])
     qkv_z2 = dp(qkv_low, 4)
-    gt_far = after(gt_far, qkv_low)
-    gt_all = [gt, mp(after(gt, gt_far), 1), gt_far, mp(gt_far, 1)]
-    down_four = join([down_two, down_r2], idx, [qkv_low])
+    vec = vec_add(vec, vec_got, idx, [qkv_low])
+    vec_got = mp(vec, 2)
+    down_four = join([down_two, down_r2], idx, [vec])
     down_other = dp(down_four, 1)
-    vec = vec_add(vec, vec_got, idx, [down_four])
-    vec_got = mp(vec, 2)
-    up_two = join([up_done, up_r4], idx, [vec])
+    up_two = join([up_done, up_r4], idx, [down_four, gt_far, out_far])
+    up_r2 = dp(up_two, 2)
     vec = vec_add(vec, vec_got, idx, [up_two])
-    up_r2 = dp(up_two, 2)
-    grad_tokens, token = spread_rows(gt_all, idx, "spread_tokens", [vec])
-    out_far = after(out_far, vec)
-    out_all = [out_own, mp(after(out_own, out_far), 1), out_far, mp(out_far, 1)]
-    block_out, token = spread_rows(out_all, idx, "spread_out", [token])
     attn_own = lax.dynamic_slice_in_dim(vec[4:].reshape(n_mp, -1), mp_at, 1, 0)
     attn_own = jnp.pad(attn_own, ((0, 0), (0, lanes - attn_own.shape[1])))
     vec = jnp.concatenate([vec[:4], attn_own, ffn_grads, jnp.zeros((1, lanes), F32)])
     vec = fine_sum(vec)
-    qkv_own = close(qkv_t, [qkv_z2], idx, [token], None if fine > 1 else vec)
+    qkv_own = close(qkv_t, [qkv_z2], idx, [up_two], None if fine > 1 else vec)
     if fine > 1:
         high = vec.astype(BF)
         qkv_own = jnp.concatenate([fine_sum(qkv_own), high, (vec - high.astype(F32)).astype(BF)])
@@ -981,13 +977,19 @@
     up_other = dp(up_four, 1)
     down_mats = [x[0] for x in (w_down, left_down, right_down, left_root_down, right_root_down)]
     *down_res, token = update_one(down_mats, down_four, down_other, total, idx, "update_down", [up_four])
-    qkv_four = join([qkv_own, *qkv_z], idx, [token])
+    qkv_four = join([qkv_own, *qkv_z], idx, [token], 10)
     qkv_other = dp(qkv_four, 1)
+
     def mats(*arrays):
         return [x[0] for x in arrays]
 
     up_mats = mats(w_up, left_up, right_up, left_root_up, right_root_up)
-    *up_res, token = update_one(up_mats, up_four, up_other, total, idx, "update_up", [qkv_four])
+    *up_res, token = update_one(up_mats, up_four, up_other, total, idx, "update_up", [qkv_four], 0)
+    gt_far, out_far = after(gt_far, token), after(out_far, token)
+    gt_all = [gt, mp(after(gt, gt_far), 1), gt_far, mp(gt_far, 1)]
+    grad_tokens, token = spread_rows(gt_all, idx, "spread_tokens", [token])
+    out_all = [out_own, mp(after(out_own, out_far), 1), out_far, mp(out_far, 1)]
+    block_out, token = spread_rows(out_all, idx, "spread_out", [token])
     qkv_res, out_res, vecs = update_pair(
         mats(w_qkv, left_qkv, right_qkv, left_root_qkv, right_root_qkv),
         mats(w_out, left_out, right_out, left_root_out, right_root_out),

time: 254 us -> 243 us (0.957)
  starting transfers between devices: 65.8 us -> 56 us
    ppermute x58, starting transfers between devices: 65.8 us -> 56 us  [swap(): return lax.ppermute(x, axis, [(i, i ^ k) for i in range(size)])]
  transfers between devices with their start and end apart: 58 -> 58, of which waited for: 19 -> 23; matrix products, arithmetic and copies ran while one was open for 3% -> 3% of each run, Pallas kernels for 34% -> 38%
where the time goes in v4:
time: 243 us
  Pallas kernels  113 us (47%)
  starting transfers between devices  56 us (23%)
  waiting for transfers between devices  53.3 us (22%)
  other arithmetic  6.65 us (3%)
  local copies, waits for them, and re-layouts  6.39 us (3%)
  blocking collectives  5.59 us (2%)
    pallas_call x39, Pallas kernels, run(): pl.pallas_call(kernel, grid_spec=pltpu.PrefetchScalarGridSpec(num_scalar_...  113 us
    ppermute x58, starting transfers between devices, swap(): return lax.ppermute(x, axis, [(i, i ^ k) for i in range(size)])  56 us
    ppermute x58, waiting for transfers between devices, swap(): return lax.ppermute(x, axis, [(i, i ^ k) for i in range(size)])  53.3 us
    all_gather x1, blocking collectives, body(): stats = lax.all_gather(stats, 'mp')  5.59 us
  transfers between devices with their start and end apart: 58, of which 23 were waited for; matrix products, arithmetic and copies ran while one was open for 3% of the time, Pallas kernels for 38%

profile of v4, /device:TPU:0, one launch (start us, length us, event | category | flops | bytes accessed | tf_op | source)
XLA Modules:
  0.0 242.7 jit_solution(16929130002648620332)
XLA Ops:
  2.8 3.0 %collective-permute-start = (bf16[96,768]{1,0:T(8,128)(2,1)S(1)}, bf16[96,768]{1,0:T(8,128)(2,1)S(1)}, u32[]{:S(2)}, u32[]{:S(2)}) collective-permute-start(bf16[96,768]{1,0:T(8,128)(2,1)S(1)} %maximum_maximum_fusion.refs_2_), channel_id=1, source_target_pairs={{0,4},{4,0},{8,12},{12,8},{16,20},{20,16},{24,28},{28,24},{1,5},{5... | collective-permute-start | bytes 442376 | tf_op jit(solution)/shard_map/ppermute | solution.py:825
  5.8 1.6 collective-permute-start.1
  7.4 2.6 %collective-permute-start.4 = (bf16[96,768]{1,0:T(8,128)(2,1)S(1)}, bf16[96,768]{1,0:T(8,128)(2,1)}, u32[]{:S(2)}, u32[]{:S(2)}) collective-permute-start(bf16[96,768]{1,0:T(8,128)(2,1)S(1)} %maximum_maximum_fusion.refs_2_), channel_id=1, source_target_pairs={{0,16},{4,20},{8,24},{12,28},{16,0},{20,4},{24,8},{28,12},{1,17},{... | collective-permute-start | bytes 442376 | tf_op jit(solution)/shard_map/ppermute | solution.py:825
  12.5 1.7 convert_reduce_fusion
  17.6 3.8 %collective-permute-done.4.refs_6_ = bf16[96,768]{1,0:T(8,128)(2,1)} collective-permute-done((bf16[96,768]{1,0:T(8,128)(2,1)S(1)}, bf16[96,768]{1,0:T(8,128)(2,1)}, u32[]{:S(2)}, u32[]{:S(2)}) %collective-permute-start.4) | collective-permute-done | bytes 147488 | tf_op jit(solution)/shard_map/ppermute | solution.py:825
  23.8 1.7 collective-permute-start.8
  28.3 4.8 %project.1 = (bf16[1024,192]{1,0:T(8,128)(2,1)}, bf16[1024,192]{1,0:T(8,128)(2,1)}, bf16[1024,192]{1,0:T(8,128)(2,1)}, bf16[768,576]{1,0:T(8,128)(2,1)}, bf16[208,768]{1,0:T(8,128)(2,1)}) custom-call(s32[3]{0:T(128)S(1)} %pad_add_fusion.idx, bf16[1024,768]{1,0:T(8,128)(2,1)S(1)} %fusion.5.refs_0_, f32[2,192]{1,0:T(2,128)S(1)} %copy-done.24, ...), custom_call_target="tpu_custom_call" | custom-call | flops 16000000000 | bytes 1024 | tf_op jit(solution)/shard_map/project/pallas_call | solution.py:43
  34.7 10.1 %attend.1 = (bf16[1024,192]{1,0:T(8,128)(2,1)}, bf16[3,1024,1024]{2,1,0:T(8,128)(2,1)}) custom-call(s32[3]{0:T(128)S(1)} %pad_add_fusion.idx, s32[1024,1]{1,0:T(8,128)S(1)} %copy.55.refs_0_, bf16[1024,192]{1,0:T(8,128)(2,1)} %get-tuple-element.140.refs_1_.refs_0_, bf16[1024,192]{1,0:T(8,128)(2,1)} %get-tuple-element.141.refs_2_.refs_1_, ...), custom_call_target="tpu_custom_call" | custom-call | flops 4000000000 | bytes 1024 | tf_op jit(solution)/shard_map/attend/pallas_call | solution.py:43
  45.5 1.6 collective-permute-start.18
  48.2 13.5 %collective-permute-done.18.refs_1_ = bf16[2,96,768]{2,1,0:T(8,128)(2,1)S(1)} collective-permute-done((bf16[2,96,768]{2,1,0:T(8,128)(2,1)S(1)}, bf16[2,96,768]{2,1,0:T(8,128)(2,1)S(1)}, u32[]{:S(2)}, u32[]{:S(2)}) %collective-permute-start.18) | collective-permute-done | bytes 294944 | tf_op jit(solution)/shard_map/ppermute | solution.py:825
  65.2 7.1 %outproj.1 = (f32[1024,768]{1,0:T(8,128)}, bf16[1024,768]{1,0:T(8,128)(2,1)S(1)}) custom-call(s32[3]{0:T(128)S(1)} %pad_add_fusion.idx, f32[4,768]{1,0:T(4,128)S(1)} %copy-done.15, bf16[1024,768]{1,0:T(8,128)(2,1)} %refs_3_.3, bf16[1024,192]{1,0:T(8,128)(2,1)S(1)} %copy-done.2, bf16[1024,192]{1,0:T(8,128)(2,1)S(1)} %collective-permute-done.13.refs_3_.refs_7_, ...), custom_call_target="tpu_custom_call" | custom-call | bytes 1024 | tf_op jit(solution)/shard_map/outproj/pallas_call | solution.py:43
  72.3 5.0 %collective-permute-done.19.refs_6_ = bf16[4,96,768]{2,1,0:T(8,128)(2,1)S(1)} collective-permute-done((bf16[4,96,768]{2,1,0:T(8,128)(2,1)S(1)}, bf16[4,96,768]{2,1,0:T(8,128)(2,1)S(1)}, u32[]{:S(2)}, u32[]{:S(2)}) %collective-permute-start.19) | collective-permute-done | bytes 589856 | tf_op jit(solution)/shard_map/ppermute | solution.py:825
  77.4 6.6 %ffn_up.1 = (f32[1024,768]{1,0:T(8,128)S(1)}, f32[1024,768]{1,0:T(8,128)S(1)}, f32[8,1024]{1,0:T(8,128)S(1)}, bf16[768,768]{1,0:T(8,128)(2,1)S(1)}, bf16[768,768]{1,0:T(8,128)(2,1)}) custom-call(s32[3]{0:T(128)S(1)} %pad_add_fusion.idx, bf16[1024,768]{1,0:T(8,128)(2,1)S(1)} %get-tuple-element.157.refs_0_, bf16[1024,768]{1,0:T(8,128)(2,1)} %refs_4_.2, ...), custom_call_target="tpu_custom_call" | custom-call | flops 3000000000 | bytes 1024 | tf_op jit(solution)/shard_map/ffn_up/pallas_call | solution.py:43
  83.9 5.6 %all-gather = f32[32,1024]{1,0:T(8,128)S(1)} all-gather(f32[8,1024]{1,0:T(8,128)S(1)} %get-tuple-element.161), channel_id=2, replica_groups=mesh['dp'=8,'mp'=4] {'mp'}, dimensions={0}, use_global_device_ids=true | all-gather | bytes 163840 | tf_op jit(solution)/shard_map/all_gather | solution.py:907
  89.5 7.6 %ffn_mid.1 = (bf16[1024,768]{1,0:T(8,128)(2,1)}, bf16[1024,768]{1,0:T(8,128)(2,1)}, bf16[2,256,768]{2,1,0:T(8,128)(2,1)S(1)}, f32[256,768]{1,0:T(8,128)}, f32[256,768]{1,0:T(8,128)S(1)}, /*index=5*/f32[2,768]{1,0:T(2,128)S(1)}) custom-call(s32[3]{0:T(128)S(1)} %pad_add_fusion.idx, f32[1024,768]{1,0:T(8,128)S(1)} %get-tuple-element.159.refs_0_, ...), custom_call_target="tpu_custom_call" | custom-call | flops 2600000000 | bytes 1024 | tf_op jit(solution)/shard_map/ffn_mid/pallas_call | solution.py:43
  97.5 1.9 collective-permute-done.20.refs_1_
  101.3 3.7 %grad_down.1 = (bf16[4,96,768]{2,1,0:T(8,128)(2,1)S(1)}, f32[4,96,768]{2,1,0:T(8,128)}) custom-call(s32[3]{0:T(128)S(1)} %pad_add_fusion.idx, bf16[1024,768]{1,0:T(8,128)(2,1)S(1)} %copy-done.7, bf16[1024,768]{1,0:T(8,128)(2,1)S(1)} %copy-done.8, bf16[256,768]{1,0:T(8,128)(2,1)S(1)} %far_sum.4.refs_2_), custom_call_target="tpu_custom_call" | custom-call | flops 1400000000 | bytes 1024 | tf_op jit(solution)/shard_map/grad_down/pallas_call | solution.py:43
  105.5 3.7 %grad_up.1 = (bf16[4,96,768]{2,1,0:T(8,128)(2,1)S(1)}, f32[4,96,768]{2,1,0:T(8,128)}) custom-call(s32[3]{0:T(128)S(1)} %pad_add_fusion.idx, bf16[1024,768]{1,0:T(8,128)(2,1)S(1)} %get-tuple-element.157.refs_0_, bf16[1024,768]{1,0:T(8,128)(2,1)S(1)} %copy-done.26, bf16[4,96,768]{2,1,0:T(8,128)(2,1)S(1)} %get-tuple-element.169.refs_2_), custom_call_target="tpu_custom_call" | custom-call | flops 1400000000 | bytes 1024 | tf_op jit(solution)/shard_map/grad_up/pallas_call | solution.py:43
  109.2 2.3 collective-permute-done.21.refs_2_
  111.5 5.0 %shard_back.1 = (f32[256,768]{1,0:T(8,128)}, f32[2,768]{1,0:T(2,128)S(1)}, f32[4,2,192]{2,1,0:T(2,128)S(1)}, bf16[256,192]{1,0:T(8,128)(2,1)S(1)}, bf16[256,192]...) custom-call(s32[3]{0:T(128)S(1)} %pad_add_fusion.idx, ...), custom_call_target="tpu_custom_call" | custom-call | bytes 1024 | tf_op jit(solution)/shard_map/shard_back/pallas_call | solution.py:43
  119.8 5.5 %ffn_out.1 = (bf16[2,256,768]{2,1,0:T(8,128)(2,1)S(1)}, f32[256,768]{1,0:T(8,128)}, f32[256,768]{1,0:T(8,128)S(1)}) custom-call(s32[3]{0:T(128)S(1)} %pad_add_fusion.idx, bf16[1024,768]{1,0:T(8,128)(2,1)} %get-tuple-element.163.refs_0_, bf16[768,768]{1,0:T(8,128)(2,1)} %get-tuple-element.164.refs_1_, bf16[256,192]{1,0:T(8,128)(2,1)S(1)} %collective-permute-done.22.refs_2_.refs_5_), custom_call_target="tpu_custom_call" | custom-call | bytes 1024 | tf_op jit(solution)/shard_map/ffn_out/pallas_call | solution.py:43
  125.3 1.9 fold.6
  128.8 11.3 %attend_back.1.refs_2_.refs_1_ = bf16[1024,576]{1,0:T(8,128)(2,1)S(1)} custom-call(s32[3]{0:T(128)S(1)} %pad_add_fusion.idx, bf16[1024,192]{1,0:T(8,128)(2,1)} %get-tuple-element.140.refs_1_.refs_0_, bf16[1024,192]{1,0:T(8,128)(2,1)} %get-tuple-element.141.refs_2_.refs_1_, bf16[1024,192]{1,0:T(8,128)(2,1)} %get-tuple-element.142.refs_3_.refs_2_, ...), custom_call_target="tpu_custom_call" | custom-call | flops 4400000000 | bytes 1024 | tf_op jit(solution)/shard_map/attend_back/pallas_call | solution.py:43
  140.8 1.9 fold.8
  142.8 6.7 %qkv_back.1 = (bf16[4,96,768]{2,1,0:T(8,128)(2,1)}, f32[4,96,768]{2,1,0:T(8,128)}, bf16[2,256,768]{2,1,0:T(8,128)(2,1)}, f32[256,768]{1,0:T(8,128)}, f32[256,768]{1,0:T(8,128)S(1)}) custom-call(s32[3]{0:T(128)S(1)} %pad_add_fusion.idx, bf16[1024,768]{1,0:T(8,128)(2,1)} %copy-done.6, bf16[1024,576]{1,0:T(8,128)(2,1)S(1)} %attend_back.1.refs_2_.refs_1_, ...), custom_call_target="tpu_custom_call" | custom-call | flops 16000000000 | bytes 1024 | tf_op jit(solution)/shard_map/qkv_back/pallas_call | solution.py:43
  153.7 2.7 %collective-permute-start.32 = (bf16[96,768]{1,0:T(8,128)(2,1)}, bf16[96,768]{1,0:T(8,128)(2,1)S(1)}, u32[]{:S(2)}, u32[]{:S(2)}) collective-permute-start(bf16[96,768]{1,0:T(8,128)(2,1)} %copy-done.21), channel_id=1, source_target_pairs={{0,16},{4,20},{8,24},{12,28},{16,0},{20,4},{24,8},{28,12},{1,17},{... | collective-permute-start | bytes 442376 | tf_op jit(solution)/shard_map/ppermute | solution.py:825
  157.2 1.6 collective-permute-start.31
  160.0 3.6 %collective-permute-done.32.refs_1_ = bf16[96,768]{1,0:T(8,128)(2,1)S(1)} collective-permute-done((bf16[96,768]{1,0:T(8,128)(2,1)}, bf16[96,768]{1,0:T(8,128)(2,1)S(1)}, u32[]{:S(2)}, u32[]{:S(2)}) %collective-permute-start.32) | collective-permute-done | bytes 147488 | tf_op jit(solution)/shard_map/ppermute | solution.py:825
  164.8 1.6 collective-permute-done.36.refs_1_
  166.4 2.1 fold.9
  168.5 1.8 collective-permute-start.43
  170.9 1.8 collective-permute-start.38
  173.3 1.8 collective-permute-start.41
  175.2 2.1 block_end.1.refs_6_.refs_0_
  177.2 1.6 collective-permute-start.37
  181.5 3.5 %collective-permute-start.40 = (bf16[96,768]{1,0:T(8,128)(2,1)S(1)}, bf16[96,768]{1,0:T(8,128)(2,1)S(1)}, u32[]{:S(2)}, u32[]{:S(2)}) collective-permute-start(bf16[96,768]{1,0:T(8,128)(2,1)S(1)} %close.4.refs_2_.refs_0_), channel_id=1, source_target_pairs={{0,16},{4,20},{8,24},{12,28},{16,0},{20,4},{24,8},{28,12},{1,17},{... | collective-permute-start | bytes 442376 | tf_op jit(solution)/shard_map/ppermute | solution.py:825
  187.0 3.8 %collective-permute-done.41.refs_1_ = bf16[2,96,768]{2,1,0:T(8,128)(2,1)S(1)} collective-permute-done((bf16[2,96,768]{2,1,0:T(8,128)(2,1)S(1)}, bf16[2,96,768]{2,1,0:T(8,128)(2,1)S(1)}, u32[]{:S(2)}, u32[]{:S(2)}) %collective-permute-start.41) | collective-permute-done | bytes 294944 | tf_op jit(solution)/shard_map/ppermute | solution.py:825
  192.9 2.3 collective-permute-start.52
  201.4 1.6 collective-permute-start.50
  203.0 2.3 collective-permute-start.51
  207.1 2.0 collective-permute-done.52.refs_6_
  209.2 5.1 %update_down.1 = (f32[768,768]{1,0:T(8,128)}, f32[96,768]{1,0:T(8,128)}, f32[96,768]{1,0:T(8,128)}, f32[96,768]{1,0:T(8,128)}, bf16[96,768]{1,0:T(8,128)(2,1)}, /*index=5*/f32[8,128]{1,0:T(8,128)S(1)}) custom-call(s32[3]{0:T(128)S(1)} %pad_add_fusion.idx, f32[96,768]{1,0:T(8,128)} %bitcast.60, f32[96,768]{1,0:T(8,128)} %bitcast.62, f32[96,768]{1,0:T(8,128)} %bitcast.63, ...), custom_call_target="tpu_custom_call" | custom-call | bytes 1024 | tf_op jit(solution)/shard_map/update_down/pallas_call | solution.py:43
  217.3 5.2 %collective-permute-done.48.refs_6_ = bf16[4,96,768]{2,1,0:T(8,128)(2,1)S(1)} collective-permute-done((bf16[4,96,768]{2,1,0:T(8,128)(2,1)S(1)}, bf16[4,96,768]{2,1,0:T(8,128)(2,1)S(1)}, u32[]{:S(2)}, u32[]{:S(2)}) %collective-permute-start.48) | collective-permute-done | bytes 589856 | tf_op jit(solution)/shard_map/ppermute | solution.py:825
  222.6 5.1 %update_up.1 = (f32[768,768]{1,0:T(8,128)}, f32[96,768]{1,0:T(8,128)}, f32[96,768]{1,0:T(8,128)}, f32[96,768]{1,0:T(8,128)}, bf16[96,768]{1,0:T(8,128)(2,1)}, /*index=5*/f32[8,128]{1,0:T(8,128)S(1)}) custom-call(s32[3]{0:T(128)S(1)} %pad_add_fusion.idx, f32[96,768]{1,0:T(8,128)} %bitcast.61, f32[96,768]{1,0:T(8,128)} %bitcast.65, f32[96,768]{1,0:T(8,128)} %bitcast.66, ...), custom_call_target="tpu_custom_call" | custom-call | bytes 1024 | tf_op jit(solution)/shard_map/update_up/pallas_call | solution.py:43
  230.0 1.8 spread_tokens.1
  231.8 1.8 spread_out.1
  233.6 2.3 collective-permute-done.57.refs_11_
  235.9 6.7 %update_qkv.1 = (f32[576,768]{1,0:T(8,128)}, f32[96,768]{1,0:T(8,128)}, f32[72,576]{1,0:T(8,128)}, f32[96,576]{1,0:T(8,128)}, bf16[96,576]{1,0:T(8,128)(2,1)}, /...) custom-call(s32[3]{0:T(128)S(1)} %pad_add_fusion.idx, ...), custom_call_target="tpu_custom_call" | custom-call | flops 2400000000 | bytes 1024 | tf_op jit(solution)/shard_map/update_qkv/pallas_call | solution.py:43
  (212 shorter events, 56.7 us)
Async XLA Ops:
  2.8 22.7 %collective-permute-start = (bf16[96,768]{1,0:T(8,128)(2,1)S(1)}, bf16[96,768]{1,0:T(8,128)(2,1)S(1)}, u32[]{:S(2)}, u32[]{:S(2)}) collective-permute-start(bf16[96,768]{1,0:T(8,128)(2,1)S(1)} %maximum_maximum_fusion.refs_2_), channel_id=1, source_target_pairs={{0,4},{4,0},{8,12},{12,8},{16,20},{20,16},{24,28},{28,24},{1,5},{5... | collective-permute-start | bytes 442376 | tf_op jit(solution)/shard_map/ppermute | solution.py:825
  5.8 10.7 %collective-permute-start.1 = (bf16[96,768]{1,0:T(8,128)(2,1)S(1)}, bf16[96,768]{1,0:T(8,128)(2,1)}, u32[]{:S(2)}, u32[]{:S(2)}) collective-permute-start(bf16[96,768]{1,0:T(8,128)(2,1)S(1)} %maximum_maximum_fusion.refs_2_), channel_id=1, source_target_pairs={{0,8},{4,12},{8,0},{12,4},{16,24},{20,28},{24,16},{28,20},{1,9},{5... | collective-permute-start | bytes 442376 | tf_op jit(solution)/shard_map/ppermute | solution.py:825
  7.4 14.0 %collective-permute-start.4 = (bf16[96,768]{1,0:T(8,128)(2,1)S(1)}, bf16[96,768]{1,0:T(8,128)(2,1)}, u32[]{:S(2)}, u32[]{:S(2)}) collective-permute-start(bf16[96,768]{1,0:T(8,128)(2,1)S(1)} %maximum_maximum_fusion.refs_2_), channel_id=1, source_target_pairs={{0,16},{4,20},{8,24},{12,28},{16,0},{20,4},{24,8},{28,12},{1,17},{... | collective-permute-start | bytes 442376 | tf_op jit(solution)/shard_map/ppermute | solution.py:825
  10.0 11.9 %collective-permute-start.6 = (bf16[96,768]{1,0:T(8,128)(2,1)S(1)}, bf16[96,768]{1,0:T(8,128)(2,1)}, u32[]{:S(2)}, u32[]{:S(2)}) collective-permute-start(bf16[96,768]{1,0:T(8,128)(2,1)S(1)} %maximum_maximum_fusion.refs_2_), channel_id=1, source_target_pairs={{0,24},{4,28},{8,16},{12,20},{16,8},{20,12},{24,0},{28,4},{1,25},{... | collective-permute-start | bytes 442376 | tf_op jit(solution)/shard_map/ppermute | solution.py:825
  16.6 10.1 %collective-permute-start.3 = (bf16[96,768]{1,0:T(8,128)(2,1)}, bf16[96,768]{1,0:T(8,128)(2,1)S(1)}, u32[]{:S(2)}, u32[]{:S(2)}) collective-permute-start(bf16[96,768]{1,0:T(8,128)(2,1)} %collective-permute-done.1.refs_4_), channel_id=1, source_target_pairs={{0,4},{4,0},{8,12},{12,8},{16,20},{20,16},{24,28},{28,24},{1,5},{5... | collective-permute-start | bytes 442376 | tf_op jit(solution)/shard_map/ppermute | solution.py:825
  21.4 6.8 %collective-permute-start.5 = (bf16[96,768]{1,0:T(8,128)(2,1)}, bf16[96,768]{1,0:T(8,128)(2,1)S(1)}, u32[]{:S(2)}, u32[]{:S(2)}) collective-permute-start(bf16[96,768]{1,0:T(8,128)(2,1)} %collective-permute-done.4.refs_6_), channel_id=1, source_target_pairs={{0,4},{4,0},{8,12},{12,8},{16,20},{20,16},{24,28},{28,24},{1,5},{5... | collective-permute-start | bytes 442376 | tf_op jit(solution)/shard_map/ppermute | solution.py:825
  21.9 6.4 %collective-permute-start.7 = (bf16[96,768]{1,0:T(8,128)(2,1)}, bf16[96,768]{1,0:T(8,128)(2,1)S(1)}, u32[]{:S(2)}, u32[]{:S(2)}) collective-permute-start(bf16[96,768]{1,0:T(8,128)(2,1)} %collective-permute-done.6.refs_8_), channel_id=1, source_target_pairs={{0,4},{4,0},{8,12},{12,8},{16,20},{20,16},{24,28},{28,24},{1,5},{5... | collective-permute-start | bytes 442376 | tf_op jit(solution)/shard_map/ppermute | solution.py:825
  23.8 21.0 %collective-permute-start.8 = (bf16[96,768]{1,0:T(8,128)(2,1)S(1)}, bf16[96,768]{1,0:T(8,128)(2,1)S(1)}, u32[]{:S(2)}, u32[]{:S(2)}) collective-permute-start(bf16[96,768]{1,0:T(8,128)(2,1)S(1)} %get-tuple-element.144), channel_id=1, source_target_pairs={{0,16},{4,20},{8,24},{12,28},{16,0},{20,4},{24,8},{28,12},{1,17},{... | collective-permute-start | bytes 442376 | tf_op jit(solution)/shard_map/ppermute | solution.py:825
  25.5 19.3 %collective-permute-start.9 = (bf16[96,768]{1,0:T(8,128)(2,1)S(1)}, bf16[96,768]{1,0:T(8,128)(2,1)S(1)}, u32[]{:S(2)}, u32[]{:S(2)}) collective-permute-start(bf16[96,768]{1,0:T(8,128)(2,1)S(1)} %get-tuple-element.144), channel_id=1, source_target_pairs={{0,8},{4,12},{8,0},{12,4},{16,24},{20,28},{24,16},{28,20},{1,9},{5... | collective-permute-start | bytes 442376 | tf_op jit(solution)/shard_map/ppermute | solution.py:825
  26.7 18.2 %collective-permute-start.10 = (bf16[96,768]{1,0:T(8,128)(2,1)S(1)}, bf16[96,768]{1,0:T(8,128)(2,1)S(1)}, u32[]{:S(2)}, u32[]{:S(2)}) collective-permute-start(bf16[96,768]{1,0:T(8,128)(2,1)S(1)} %get-tuple-element.144), channel_id=1, source_target_pairs={{0,24},{4,28},{8,16},{12,20},{16,8},{20,12},{24,0},{28,4},{1,25},{... | collective-permute-start | bytes 442376 | tf_op jit(solution)/shard_map/ppermute | solution.py:825
  33.1 11.8 %collective-permute-start.11 = (bf16[208,768]{1,0:T(8,128)(2,1)}, bf16[208,768]{1,0:T(8,128)(2,1)S(1)}, u32[]{:S(2)}, u32[]{:S(2)}) collective-permute-start(bf16[208,768]{1,0:T(8,128)(2,1)} %get-tuple-element.154.refs_6_.refs_10_), channel_id=1, source_target_pairs={{0,2},{1,3},{2,0},{3,1},{4,6},{5,7},{6,4},{7,5},{8,10},{9,11},{10,... | collective-permute-start | bytes 958472 | tf_op jit(solution)/shard_map/ppermute | solution.py:825
  45.0 16.8 %collective-permute-start.15 = (bf16[208,768]{1,0:T(8,128)(2,1)S(1)}, bf16[208,768]{1,0:T(8,128)(2,1)S(1)}, u32[]{:S(2)}, u32[]{:S(2)}) collective-permute-start(bf16[208,768]{1,0:T(8,128)(2,1)S(1)} %copy-done.9), channel_id=1, source_target_pairs={{0,1},{1,0},{2,3},{3,2},{4,5},{5,4},{6,7},{7,6},{8,9},{9,8},{10,11... | collective-permute-start | bytes 958472 | tf_op jit(solution)/shard_map/ppermute | solution.py:825
  45.0 16.7 %collective-permute-start.16 = (bf16[208,768]{1,0:T(8,128)(2,1)S(1)}, bf16[208,768]{1,0:T(8,128)(2,1)S(1)}, u32[]{:S(2)}, u32[]{:S(2)}) collective-permute-start(bf16[208,768]{1,0:T(8,128)(2,1)S(1)} %collective-permute-done.11.refs_8_.refs_12_), channel_id=1, source_target_pairs={{0,1},{1,0},{2,3},{3,2},{4,5},{5,4},{6,7},{7,6},{8,9},{9,8},{10,11... | collective-permute-start | bytes 958472 | tf_op jit(solution)/shard_map/ppermute | solution.py:825
  45.5 16.2 %collective-permute-start.18 = (bf16[2,96,768]{2,1,0:T(8,128)(2,1)S(1)}, bf16[2,96,768]{2,1,0:T(8,128)(2,1)S(1)}, u32[]{:S(2)}, u32[]{:S(2)}) collective-permute-start(bf16[2,96,768]{2,1,0:T(8,128)(2,1)S(1)} %pad_maximum_fusion.1.refs_0_), channel_id=1, source_target_pairs={{0,16},{4,20},{8,24},{12,28},{16,0},{20,4},{24,8},{28,12},{1,17},{... | collective-permute-start | bytes 884744 | tf_op jit(solution)/shard_map/ppermute | solution.py:825
  47.1 15.9 %collective-permute-start.17 = (bf16[4,96,768]{2,1,0:T(8,128)(2,1)S(1)}, bf16[4,96,768]{2,1,0:T(8,128)(2,1)S(1)}, u32[]{:S(2)}, u32[]{:S(2)}) collective-permute-start(bf16[4,96,768]{2,1,0:T(8,128)(2,1)S(1)} %pad_maximum_fusion.refs_2_.refs_3_), channel_id=1, source_target_pairs={{0,4},{4,0},{8,12},{12,8},{16,20},{20,16},{24,28},{28,24},{1,5},{5... | collective-permute-start | bytes 1769480 | tf_op jit(solution)/shard_map/ppermute | solution.py:825
  47.7 14.7 %collective-permute-start.12 = (bf16[1024,192]{1,0:T(8,128)(2,1)}, bf16[1024,192]{1,0:T(8,128)(2,1)S(1)}, u32[]{:S(2)}, u32[]{:S(2)}) collective-permute-start(bf16[1024,192]{1,0:T(8,128)(2,1)} %get-tuple-element.151.refs_2_.refs_6_), channel_id=1, source_target_pairs={{0,2},{1,3},{2,0},{3,1},{4,6},{5,7},{6,4},{7,5},{8,10},{9,11},{10,... | collective-permute-start | bytes 1179656 | tf_op jit(solution)/shard_map/ppermute | solution.py:825
  62.4 15.0 %collective-permute-start.19 = (bf16[4,96,768]{2,1,0:T(8,128)(2,1)S(1)}, bf16[4,96,768]{2,1,0:T(8,128)(2,1)S(1)}, u32[]{:S(2)}, u32[]{:S(2)}) collective-permute-start(bf16[4,96,768]{2,1,0:T(8,128)(2,1)S(1)} %join.6.refs_5_), channel_id=1, source_target_pairs={{0,8},{4,12},{8,0},{12,4},{16,24},{20,28},{24,16},{28,20},{1,9},{5... | collective-permute-start | bytes 1769480 | tf_op jit(solution)/shard_map/ppermute | solution.py:825
  100.0 11.4 %collective-permute-start.21 = (bf16[256,768]{1,0:T(8,128)(2,1)S(1)}, bf16[256,768]{1,0:T(8,128)(2,1)S(1)}, u32[]{:S(2)}, u32[]{:S(2)}) collective-permute-start(bf16[256,768]{1,0:T(8,128)(2,1)S(1)} %far_sum.4.refs_2_), channel_id=1, source_target_pairs={{0,2},{1,3},{2,0},{3,1},{4,6},{5,7},{6,4},{7,5},{8,10},{9,11},{10,... | collective-permute-start | bytes 1179656 | tf_op jit(solution)/shard_map/ppermute | solution.py:825
  105.0 20.3 %collective-permute-start.26 = (bf16[4,96,768]{2,1,0:T(8,128)(2,1)S(1)}, bf16[4,96,768]{2,1,0:T(8,128)(2,1)S(1)}, u32[]{:S(2)}, u32[]{:S(2)}) collective-permute-start(bf16[4,96,768]{2,1,0:T(8,128)(2,1)S(1)} %get-tuple-element.169.refs_2_), channel_id=1, source_target_pairs={{0,4},{4,0},{8,12},{12,8},{16,20},{20,16},{24,28},{28,24},{1,5},{5... | collective-permute-start | bytes 1769480 | tf_op jit(solution)/shard_map/ppermute | solution.py:825
  117.1 10.5 %collective-permute-start.25 = (bf16[2,192,768]{2,1,0:T(8,128)(2,1)S(1)}, bf16[2,192,768]{2,1,0:T(8,128)(2,1)S(1)}, u32[]{:S(2)}, u32[]{:S(2)}) collective-permute-start(bf16[2,192,768]{2,1,0:T(8,128)(2,1)S(1)} %get-tuple-element.179), channel_id=1, source_target_pairs={{0,1},{1,0},{2,3},{3,2},{4,5},{5,4},{6,7},{7,6},{8,9},{9,8},{10,11... | collective-permute-start | bytes 1769480 | tf_op jit(solution)/shard_map/ppermute | solution.py:825
  117.6 11.2 %collective-permute-start.23 = (bf16[256,192]{1,0:T(8,128)(2,1)S(1)}, bf16[256,192]{1,0:T(8,128)(2,1)S(1)}, u32[]{:S(2)}, u32[]{:S(2)}) collective-permute-start(bf16[256,192]{1,0:T(8,128)(2,1)S(1)} %get-tuple-element.176), channel_id=1, source_target_pairs={{0,2},{1,3},{2,0},{3,1},{4,6},{5,7},{6,4},{7,5},{8,10},{9,11},{10,... | collective-permute-start | bytes 294920 | tf_op jit(solution)/shard_map/ppermute | solution.py:825
  118.1 10.7 %collective-permute-start.24 = (bf16[256,192]{1,0:T(8,128)(2,1)S(1)}, bf16[256,192]{1,0:T(8,128)(2,1)S(1)}, u32[]{:S(2)}, u32[]{:S(2)}) collective-permute-start(bf16[256,192]{1,0:T(8,128)(2,1)S(1)} %get-tuple-element.177), channel_id=1, source_target_pairs={{0,3},{1,2},{2,1},{3,0},{4,7},{5,6},{6,5},{7,4},{8,11},{9,10},{10,... | collective-permute-start | bytes 294920 | tf_op jit(solution)/shard_map/ppermute | solution.py:825
  119.3 21.5 %collective-permute-start.29 = (bf16[4,96,768]{2,1,0:T(8,128)(2,1)S(1)}, bf16[4,96,768]{2,1,0:T(8,128)(2,1)S(1)}, u32[]{:S(2)}, u32[]{:S(2)}) collective-permute-start(bf16[4,96,768]{2,1,0:T(8,128)(2,1)S(1)} %get-tuple-element.187.refs_14_), channel_id=1, source_target_pairs={{0,4},{4,0},{8,12},{12,8},{16,20},{20,16},{24,28},{28,24},{1,5},{5... | collective-permute-start | bytes 1769480 | tf_op jit(solution)/shard_map/ppermute | solution.py:825
  127.2 12.9 %collective-permute-start.30 = (bf16[2,96,768]{2,1,0:T(8,128)(2,1)S(1)}, bf16[2,96,768]{2,1,0:T(8,128)(2,1)S(1)}, u32[]{:S(2)}, u32[]{:S(2)}) collective-permute-start(bf16[2,96,768]{2,1,0:T(8,128)(2,1)S(1)} %get-tuple-element.181.refs_2_), channel_id=1, source_target_pairs={{0,8},{4,12},{8,0},{12,4},{16,24},{20,28},{24,16},{28,20},{1,9},{5... | collective-permute-start | bytes 884744 | tf_op jit(solution)/shard_map/ppermute | solution.py:825
  128.2 14.6 %collective-permute-start.28 = (bf16[192,768]{1,0:T(8,128)(2,1)S(1)}, bf16[192,768]{1,0:T(8,128)(2,1)S(1)}, u32[]{:S(2)}, u32[]{:S(2)}) collective-permute-start(bf16[192,768]{1,0:T(8,128)(2,1)S(1)} %far_sum.5.refs_8_), channel_id=1, source_target_pairs={{0,2},{1,3},{2,0},{3,1},{4,6},{5,7},{6,4},{7,5},{8,10},{9,11},{10,... | collective-permute-start | bytes 884744 | tf_op jit(solution)/shard_map/ppermute | solution.py:825
  140.1 16.5 %collective-permute-start.27 = (bf16[2,256,768]{2,1,0:T(8,128)(2,1)S(1)}, bf16[2,256,768]{2,1,0:T(8,128)(2,1)S(1)}, u32[]{:S(2)}, u32[]{:S(2)}) collective-permute-start(bf16[2,256,768]{2,1,0:T(8,128)(2,1)S(1)} %get-tuple-element.182.refs_2_), channel_id=1, source_target_pairs={{0,1},{1,0},{2,3},{3,2},{4,5},{5,4},{6,7},{7,6},{8,9},{9,8},{10,11... | collective-permute-start | bytes 2359304 | tf_op jit(solution)/shard_map/ppermute | solution.py:825
  150.4 8.4 %collective-permute-start.33 = (bf16[2,256,768]{2,1,0:T(8,128)(2,1)}, bf16[2,256,768]{2,1,0:T(8,128)(2,1)S(1)}, u32[]{:S(2)}, u32[]{:S(2)}) collective-permute-start(bf16[2,256,768]{2,1,0:T(8,128)(2,1)} %get-tuple-element.194), channel_id=1, source_target_pairs={{0,1},{1,0},{2,3},{3,2},{4,5},{5,4},{6,7},{7,6},{8,9},{9,8},{10,11... | collective-permute-start | bytes 2359304 | tf_op jit(solution)/shard_map/ppermute | solution.py:825
  150.9 15.6 %collective-permute-start.36 = (bf16[4,96,768]{2,1,0:T(8,128)(2,1)}, bf16[4,96,768]{2,1,0:T(8,128)(2,1)}, u32[]{:S(2)}, u32[]{:S(2)}) collective-permute-start(bf16[4,96,768]{2,1,0:T(8,128)(2,1)} %get-tuple-element.191.refs_2_), channel_id=1, source_target_pairs={{0,4},{4,0},{8,12},{12,8},{16,20},{20,16},{24,28},{28,24},{1,5},{5... | collective-permute-start | bytes 1769480 | tf_op jit(solution)/shard_map/ppermute | solution.py:825
  153.7 9.9 %collective-permute-start.32 = (bf16[96,768]{1,0:T(8,128)(2,1)}, bf16[96,768]{1,0:T(8,128)(2,1)S(1)}, u32[]{:S(2)}, u32[]{:S(2)}) collective-permute-start(bf16[96,768]{1,0:T(8,128)(2,1)} %copy-done.21), channel_id=1, source_target_pairs={{0,16},{4,20},{8,24},{12,28},{16,0},{20,4},{24,8},{28,12},{1,17},{... | collective-permute-start | bytes 442376 | tf_op jit(solution)/shard_map/ppermute | solution.py:825
  156.3 13.9 %collective-permute-start.35 = (bf16[2,96,768]{2,1,0:T(8,128)(2,1)S(1)}, bf16[2,96,768]{2,1,0:T(8,128)(2,1)S(1)}, u32[]{:S(2)}, u32[]{:S(2)}) collective-permute-start(bf16[2,96,768]{2,1,0:T(8,128)(2,1)S(1)} %get-tuple-element.190.refs_6_), channel_id=1, source_target_pairs={{0,8},{4,12},{8,0},{12,4},{16,24},{20,28},{24,16},{28,20},{1,9},{5... | collective-permute-start | bytes 884744 | tf_op jit(solution)/shard_map/ppermute | solution.py:825
  157.2 17.9 %collective-permute-start.31 = (bf16[256,768]{1,0:T(8,128)(2,1)S(1)}, bf16[256,768]{1,0:T(8,128)(2,1)S(1)}, u32[]{:S(2)}, u32[]{:S(2)}) collective-permute-start(bf16[256,768]{1,0:T(8,128)(2,1)S(1)} %far_sum.6.refs_2_), channel_id=1, source_target_pairs={{0,2},{1,3},{2,0},{3,1},{4,6},{5,7},{6,4},{7,5},{8,10},{9,11},{10,... | collective-permute-start | bytes 1179656 | tf_op jit(solution)/shard_map/ppermute | solution.py:825
  159.4 19.4 %collective-permute-start.39 = (bf16[256,768]{1,0:T(8,128)(2,1)S(1)}, bf16[256,768]{1,0:T(8,128)(2,1)S(1)}, u32[]{:S(2)}, u32[]{:S(2)}) collective-permute-start(bf16[256,768]{1,0:T(8,128)(2,1)S(1)} %far_sum.7.refs_2_), channel_id=1, source_target_pairs={{0,2},{1,3},{2,0},{3,1},{4,6},{5,7},{6,4},{7,5},{8,10},{9,11},{10,... | collective-permute-start | bytes 1179656 | tf_op jit(solution)/shard_map/ppermute | solution.py:825
  164.2 8.6 %collective-permute-start.34 = (bf16[96,768]{1,0:T(8,128)(2,1)S(1)}, bf16[96,768]{1,0:T(8,128)(2,1)S(1)}, u32[]{:S(2)}, u32[]{:S(2)}) collective-permute-start(bf16[96,768]{1,0:T(8,128)(2,1)S(1)} %close.3.refs_2_.refs_0_), channel_id=1, source_target_pairs={{0,16},{4,20},{8,24},{12,28},{16,0},{20,4},{24,8},{28,12},{1,17},{... | collective-permute-start | bytes 442376 | tf_op jit(solution)/shard_map/ppermute | solution.py:825
  168.5 16.5 %collective-permute-start.43 = (bf16[2,96,768]{2,1,0:T(8,128)(2,1)S(1)}, bf16[2,96,768]{2,1,0:T(8,128)(2,1)S(1)}, u32[]{:S(2)}, u32[]{:S(2)}) collective-permute-start(bf16[2,96,768]{2,1,0:T(8,128)(2,1)S(1)} %get-tuple-element.197.refs_2_), channel_id=1, source_target_pairs={{0,8},{4,12},{8,0},{12,4},{16,24},{20,28},{24,16},{28,20},{1,9},{5... | collective-permute-start | bytes 884744 | tf_op jit(solution)/shard_map/ppermute | solution.py:825
  170.9 10.0 %collective-permute-start.38 = (bf16[96,768]{1,0:T(8,128)(2,1)S(1)}, bf16[96,768]{1,0:T(8,128)(2,1)S(1)}, u32[]{:S(2)}, u32[]{:S(2)}) collective-permute-start(bf16[96,768]{1,0:T(8,128)(2,1)S(1)} %get-tuple-element.198.refs_2_), channel_id=1, source_target_pairs={{0,16},{4,20},{8,24},{12,28},{16,0},{20,4},{24,8},{28,12},{1,17},{... | collective-permute-start | bytes 442376 | tf_op jit(solution)/shard_map/ppermute | solution.py:825
  173.3 17.4 %collective-permute-start.41 = (bf16[2,96,768]{2,1,0:T(8,128)(2,1)S(1)}, bf16[2,96,768]{2,1,0:T(8,128)(2,1)S(1)}, u32[]{:S(2)}, u32[]{:S(2)}) collective-permute-start(bf16[2,96,768]{2,1,0:T(8,128)(2,1)S(1)} %join.7.refs_4_.refs_0_), channel_id=1, source_target_pairs={{0,8},{4,12},{8,0},{12,4},{16,24},{20,28},{24,16},{28,20},{1,9},{5... | collective-permute-start | bytes 884744 | tf_op jit(solution)/shard_map/ppermute | solution.py:825
  177.2 15.6 %collective-permute-start.37 = (bf16[256,768]{1,0:T(8,128)(2,1)S(1)}, bf16[256,768]{1,0:T(8,128)(2,1)S(1)}, u32[]{:S(2)}, u32[]{:S(2)}) collective-permute-start(bf16[256,768]{1,0:T(8,128)(2,1)S(1)} %block_end.1.refs_6_.refs_0_), channel_id=1, source_target_pairs={{0,2},{1,3},{2,0},{3,1},{4,6},{5,7},{6,4},{7,5},{8,10},{9,11},{10,... | collective-permute-start | bytes 1179656 | tf_op jit(solution)/shard_map/ppermute | solution.py:825
  180.1 15.3 %collective-permute-start.44 = (bf16[256,768]{1,0:T(8,128)(2,1)S(1)}, bf16[256,768]{1,0:T(8,128)(2,1)S(1)}, u32[]{:S(2)}, u32[]{:S(2)}) collective-permute-start(bf16[256,768]{1,0:T(8,128)(2,1)S(1)} %get-tuple-element.215.refs_2_.refs_0_), channel_id=1, source_target_pairs={{0,2},{1,3},{2,0},{3,1},{4,6},{5,7},{6,4},{7,5},{8,10},{9,11},{10,... | collective-permute-start | bytes 1179656 | tf_op jit(solution)/shard_map/ppermute | solution.py:825
  181.5 13.7 %collective-permute-start.40 = (bf16[96,768]{1,0:T(8,128)(2,1)S(1)}, bf16[96,768]{1,0:T(8,128)(2,1)S(1)}, u32[]{:S(2)}, u32[]{:S(2)}) collective-permute-start(bf16[96,768]{1,0:T(8,128)(2,1)S(1)} %close.4.refs_2_.refs_0_), channel_id=1, source_target_pairs={{0,16},{4,20},{8,24},{12,28},{16,0},{20,4},{24,8},{28,12},{1,17},{... | collective-permute-start | bytes 442376 | tf_op jit(solution)/shard_map/ppermute | solution.py:825
  186.4 12.0 %collective-permute-start.46 = (bf16[96,768]{1,0:T(8,128)(2,1)S(1)}, bf16[96,768]{1,0:T(8,128)(2,1)}, u32[]{:S(2)}, u32[]{:S(2)}) collective-permute-start(bf16[96,768]{1,0:T(8,128)(2,1)S(1)} %get-tuple-element.207.refs_2_), channel_id=1, source_target_pairs={{0,16},{4,20},{8,24},{12,28},{16,0},{20,4},{24,8},{28,12},{1,17},{... | collective-permute-start | bytes 442376 | tf_op jit(solution)/shard_map/ppermute | solution.py:825
  190.7 5.6 %collective-permute-start.47 = (f32[6,768]{1,0:T(8,128)S(1)}, f32[6,768]{1,0:T(8,128)S(1)}, u32[]{:S(2)}, u32[]{:S(2)}) collective-permute-start(f32[6,768]{1,0:T(8,128)S(1)} %vec_add.2.refs_2_.refs_0_), channel_id=1, source_target_pairs={{0,2},{1,3},{2,0},{3,1},{4,6},{5,7},{6,4},{7,5},{8,10},{9,11},{10,... | collective-permute-start | bytes 55304 | tf_op jit(solution)/shard_map/ppermute | solution.py:825
  192.9 16.3 %collective-permute-start.52 = (bf16[4,96,768]{2,1,0:T(8,128)(2,1)S(1)}, bf16[4,96,768]{2,1,0:T(8,128)(2,1)S(1)}, u32[]{:S(2)}, u32[]{:S(2)}) collective-permute-start(bf16[4,96,768]{2,1,0:T(8,128)(2,1)S(1)} %join.8.refs_2_.refs_5_), channel_id=1, source_target_pairs={{0,4},{4,0},{8,12},{12,8},{16,20},{20,16},{24,28},{28,24},{1,5},{5... | collective-permute-start | bytes 1769480 | tf_op jit(solution)/shard_map/ppermute | solution.py:825
  196.0 9.7 %collective-permute-start.45 = (bf16[2,96,768]{2,1,0:T(8,128)(2,1)S(1)}, bf16[2,96,768]{2,1,0:T(8,128)(2,1)S(1)}, u32[]{:S(2)}, u32[]{:S(2)}) collective-permute-start(bf16[2,96,768]{2,1,0:T(8,128)(2,1)S(1)} %join.9.refs_2_.refs_3_.refs_0_), channel_id=1, source_target_pairs={{0,8},{4,12},{8,0},{12,4},{16,24},{20,28},{24,16},{28,20},{1,9},{5... | collective-permute-start | bytes 884744 | tf_op jit(solution)/shard_map/ppermute | solution.py:825
  200.9 13.8 %collective-permute-start.49 = (bf16[112,768]{1,0:T(8,128)(2,1)S(1)}, bf16[112,768]{1,0:T(8,128)(2,1)S(1)}, u32[]{:S(2)}, u32[]{:S(2)}) collective-permute-start(bf16[112,768]{1,0:T(8,128)(2,1)S(1)} %close.5.refs_2_.refs_0_), channel_id=1, source_target_pairs={{0,16},{4,20},{8,24},{12,28},{16,0},{20,4},{24,8},{28,12},{1,17},{... | collective-permute-start | bytes 516104 | tf_op jit(solution)/shard_map/ppermute | solution.py:825
  201.4 14.3 %collective-permute-start.50 = (bf16[112,768]{1,0:T(8,128)(2,1)S(1)}, bf16[112,768]{1,0:T(8,128)(2,1)S(1)}, u32[]{:S(2)}, u32[]{:S(2)}) collective-permute-start(bf16[112,768]{1,0:T(8,128)(2,1)S(1)} %close.5.refs_2_.refs_0_), channel_id=1, source_target_pairs={{0,8},{4,12},{8,0},{12,4},{16,24},{20,28},{24,16},{28,20},{1,9},{5... | collective-permute-start | bytes 516104 | tf_op jit(solution)/shard_map/ppermute | solution.py:825
  203.0 12.7 %collective-permute-start.51 = (bf16[112,768]{1,0:T(8,128)(2,1)S(1)}, bf16[112,768]{1,0:T(8,128)(2,1)S(1)}, u32[]{:S(2)}, u32[]{:S(2)}) collective-permute-start(bf16[112,768]{1,0:T(8,128)(2,1)S(1)} %close.5.refs_2_.refs_0_), channel_id=1, source_target_pairs={{0,24},{4,28},{8,16},{12,20},{16,8},{20,12},{24,0},{28,4},{1,25},{... | collective-permute-start | bytes 516104 | tf_op jit(solution)/shard_map/ppermute | solution.py:825
  206.2 16.3 %collective-permute-start.48 = (bf16[4,96,768]{2,1,0:T(8,128)(2,1)S(1)}, bf16[4,96,768]{2,1,0:T(8,128)(2,1)S(1)}, u32[]{:S(2)}, u32[]{:S(2)}) collective-permute-start(bf16[4,96,768]{2,1,0:T(8,128)(2,1)S(1)} %join.10.refs_7_.refs_5_), channel_id=1, source_target_pairs={{0,4},{4,0},{8,12},{12,8},{16,20},{20,16},{24,28},{28,24},{1,5},{5... | collective-permute-start | bytes 1769480 | tf_op jit(solution)/shard_map/ppermute | solution.py:825
  216.2 19.6 %collective-permute-start.57 = (bf16[4,112,768]{2,1,0:T(8,128)(2,1)S(1)}, bf16[4,112,768]{2,1,0:T(8,128)(2,1)S(1)}, u32[]{:S(2)}, u32[]{:S(2)}) collective-permute-start(bf16[4,112,768]{2,1,0:T(8,128)(2,1)S(1)} %join.11.refs_7_.refs_10_), channel_id=1, source_target_pairs={{0,4},{4,0},{8,12},{12,8},{16,20},{20,16},{24,28},{28,24},{1,5},{5... | collective-permute-start | bytes 2064392 | tf_op jit(solution)/shard_map/ppermute | solution.py:825
  (49 other events, 272.2 us)

commit v5 on v4

--- a/solution.py
+++ b/solution.py
@@ -22,6 +22,7 @@
 RATE = 4e8
 TICK = 5
 BLK = 256
+WIDE = 512
 ORDER = (0, 4, 2, 6)
 
 
@@ -153,7 +154,7 @@
     )
 
 
-def attend_kernel(idx, start_ref, q_ref, k_ref, v_ref, o_ref, p_ref):
+def attend_kernel(idx, start_ref, q_ref, k_ref, v_ref, o_ref, *p_refs):
     h = pl.program_id(0)
     rows, hw = q_ref.shape
     lane = (lax.broadcasted_iota(jnp.int32, (1, hw), 1) // HD) == h
@@ -166,9 +167,17 @@
         s = jnp.where((kpos >= start_ref[lo:hi, :]) & (kpos <= qpos), s, -1e30)
         p = jnp.exp(s - jnp.max(s, -1, keepdims=True))
         p = (p * (1.0 / rowsum(p))).astype(BF)
-        p_ref[0, lo:hi, :hi] = p
+        p_refs[i][0] = p
         ob = dot(p, v_ref[:hi, :]).astype(BF)
         o_ref[lo:hi, :] = jnp.where(lane, ob, o_ref[lo:hi, :])
+
+
+def widths(rows):
+    return range(BLK, rows + BLK, BLK)
+
+
+def head_spec(width):
+    return pl.BlockSpec((1, BLK, width), lambda s, i: (s, 0, 0))
 
 
 def attend(start, q, k, v, idx, after=()):
@@ -179,8 +188,8 @@
         (heads,),
         [start, q, k, v],
         fulls([start, q, k, v]),
-        [far((rows, hw), BF), far((heads, rows, rows), BF)],
-        [full((rows, hw)), pl.BlockSpec((1, rows, rows), lambda s, i: (s, 0, 0))],
+        [far((rows, hw), BF)] + [far((heads, BLK, w), BF) for w in widths(rows)],
+        [full((rows, hw))] + [head_spec(w) for w in widths(rows)],
         idx,
         "attend",
         10,
@@ -223,10 +232,10 @@
 def outproj(on, tok, o, w, idx, after=()):
     rows, d = tok.shape
     hw = o[0].shape[1]
-    blk = lambda n: pl.BlockSpec((BLK, n), lambda s, i: (s, 0))
+    blk = lambda n: pl.BlockSpec((WIDE, n), lambda s, i: (s, 0))
     return run(
         outproj_kernel,
-        (rows // BLK,),
+        (rows // WIDE,),
         [on, tok, *o, *w],
         fulls([on]) + [blk(d)] + [blk(hw)] * len(o) + fulls(w),
         [far((rows, d), F32), near((rows, d), BF)],
@@ -241,7 +250,7 @@
 
 def ffn_up_kernel(idx, c_ref, e_ref, fn_ref, *refs):
     ups, downs = refs[:2], refs[2:4]
-    u_ref, dw_ref, st_ref, wu_ref, wd_ref = refs[4:]
+    z_ref, slope_ref, dw_ref, st_ref, wu_ref, wd_ref = refs[4:]
     rows = ups[0].shape[1]
 
     @pl.when(pl.program_id(0) == 0)
@@ -254,16 +263,17 @@
                 wd_ref[at, :] = downs[i // 2][i % 2 * 2 + odd]
 
     u = dot(c_ref[...], wu_ref[...])
-    u_ref[...] = u
-    z, _ = gelu_parts(u)
+    z, t = gelu_parts(u)
+    z_ref[...] = z
+    slope_ref[...] = 0.5 * (1.0 + t) + 0.5 * u * (1.0 - t * t) * (GELU_A * (1.0 + (3.0 * GELU_B) * (u * u)))
     mean = rowsum(z) / z.shape[-1]
     z = z - mean
     dw = dot_nt(e_ref[...], wd_ref[...])
     dw_ref[...] = dw
     eg = dw * fn_ref[0:1, :]
     stats = [mean, rowsum(z * z), rowsum(eg), rowsum(eg * z)]
-    place = lax.broadcasted_iota(jnp.int32, (BLK, 128), 1)
-    tile = jnp.zeros((BLK, 128), F32)
+    place = lax.broadcasted_iota(jnp.int32, (WIDE, 128), 1)
+    tile = jnp.zeros((WIDE, 128), F32)
     for i, x in enumerate(stats):
         tile = jnp.where(place == i, x, tile)
     st_ref[...] = tile.T[:8, :]
@@ -272,14 +282,14 @@
 def ffn_up(c, e, fn, pieces, idx):
     rows, d = c.shape
     fl = fn.shape[1]
-    rblk = lambda n: pl.BlockSpec((BLK, n), lambda s, i: (s, 0))
+    rblk = lambda n: pl.BlockSpec((WIDE, n), lambda s, i: (s, 0))
     return run(
         ffn_up_kernel,
-        (rows // BLK,),
+        (rows // WIDE,),
         [c, e, fn, *pieces],
         [rblk(d), rblk(d), full(fn.shape)] + fulls(pieces),
-        [near((rows, fl), F32), near((rows, fl), F32), sds((8, rows), F32), near((d, fl), BF), far((fl, d), BF)],
-        [rblk(fl), rblk(fl), pl.BlockSpec((8, BLK), lambda s, i: (0, s)), full((d, fl)), full((fl, d))],
+        [near((rows, fl), F32)] * 3 + [sds((8, rows), F32), near((d, fl), BF), far((fl, d), BF)],
+        [rblk(fl)] * 3 + [pl.BlockSpec((8, WIDE), lambda s, i: (0, s)), full((d, fl)), full((fl, d))],
         idx,
         "ffn_up",
         7.5,
@@ -317,9 +327,9 @@
         last_ref[...] = value
 
 
-def ffn_mid_kernel(idx, u_ref, dw_ref, st_ref, fn_ref, wu_ref, w_ref, du_ref, send_ref, keep_ref, last_ref, fg_ref):
+def ffn_mid_kernel(idx, z_ref, slope_ref, dw_ref, st_ref, fn_ref, wu_ref, w_ref, du_ref, send_ref, keep_ref, last_ref, fg_ref):
     g = st_ref.shape[0]
-    fl = u_ref.shape[1]
+    fl = z_ref.shape[1]
     n = g * fl
     st = [st_ref[k] for k in range(g)]
     mean = sum(x[0:1] for x in st) / g
@@ -330,14 +340,11 @@
     s_norm = r * (sum(x[3:4] + gp * x[2:3] for x, gp in zip(st, gap)) / n)
     cols = jnp.concatenate([mean, r, s_plain, s_norm, jnp.zeros((124, BLK), F32)], axis=0).T
     mean, r, s_plain, s_norm = (cols[:, i : i + 1] for i in range(4))
-    u = u_ref[...]
-    z, t = gelu_parts(u)
-    hat = (z - mean) * r
+    hat = (z_ref[...] - mean) * r
     w_ref[...] = (hat * fn_ref[0:1, :] + fn_ref[1:2, :]).astype(BF)
     dw = dw_ref[...]
     dz = r * (dw * fn_ref[0:1, :] - s_plain - hat * s_norm)
-    slope = 0.5 * (1.0 + t) + 0.5 * u * (1.0 - t * t) * (GELU_A * (1.0 + (3.0 * GELU_B) * (u * u)))
-    du = (dz * slope).astype(BF)
+    du = (dz * slope_ref[...]).astype(BF)
     du_ref[...] = du
     put_rel(send_ref, keep_ref, last_ref, dot_nt(du, wu_ref[...]))
     grads = jnp.concatenate([jnp.sum(dw * hat, 0, keepdims=True), jnp.sum(dw, 0, keepdims=True)], axis=0)
@@ -351,14 +358,14 @@
         fg_ref[...] += grads
 
 
-def ffn_mid(u, dw, st, fn, wu, idx):
-    rows, fl = u.shape
+def ffn_mid(z, slope, dw, st, fn, wu, idx):
+    rows, fl = z.shape
     d = wu.shape[0]
     return run(
         ffn_mid_kernel,
         (rows // BLK,),
-        [u, dw, st, fn, wu],
-        [rel_spec(fl), rel_spec(fl), pl.BlockSpec((st.shape[0], 8, BLK), lambda s, i: (0, 0, rel_block(s, i)))]
+        [z, slope, dw, st, fn, wu],
+        [rel_spec(fl)] * 3 + [pl.BlockSpec((st.shape[0], 8, BLK), lambda s, i: (0, 0, rel_block(s, i)))]
         + fulls([fn, wu]),
         [far((rows, fl), BF), far((rows, fl), BF), sds((2, BLK, d), BF), far((BLK, d), F32), sds((BLK, d), F32), sds((2, fl), F32)],
         [rel_spec(fl), rel_spec(fl), SEND_SPEC(d), KEEP_SPEC(d), KEEP_SPEC(d), full((2, fl))],
@@ -418,7 +425,7 @@
         (steps,),
         [x, y],
         [pl.BlockSpec((rows, BLK), lambda s, i: (0, s)), full(y.shape)],
-        [sds((WAYS // 2, step, n), BF), far((WAYS // 2, step, n), F32)],
+        [sds((WAYS // 2, step, n), BF), far((WAYS // 2, step, n), BF)],
         [full((WAYS // 2, step, n))] * 2,
         idx,
         name,
@@ -458,7 +465,7 @@
     lead = pl.BlockSpec((1, hw, d), lambda s, i: (0, 0, 0))
     half = (WAYS // 2, step, d)
     part = (2, BLK, d)
-    outs = [sds(half, BF), far(half, F32), sds(part, BF), far(part[1:], F32), sds(part[1:], F32)]
+    outs = [sds(half, BF), far(half, BF), sds(part, BF), far(part[1:], F32), sds(part[1:], F32)]
     return run(
         kernel, (1,), ins, fulls(ins[:4]) + [lead, full(go[2].shape)], outs, fulls(outs), idx, "qkv_back", 40,
         [pltpu.VMEM((d, n), F32), pltpu.VMEM((hw, d), F32)],
@@ -526,11 +533,12 @@
     )
 
 
-def attend_back_kernel(idx, q_ref, k_ref, v_ref, p_ref, *refs):
-    d_refs = refs[:4]
-    out_ref, do_scr, dq_scr, dk_scr, dv_scr = refs[4:]
+def attend_back_kernel(idx, q_ref, k_ref, v_ref, *refs):
     h = pl.program_id(0)
     rows, hw = q_ref.shape
+    count = rows // BLK
+    p_refs, d_refs = refs[:count], refs[count : count + 4]
+    out_ref, do_scr, dq_scr, dk_scr, dv_scr = refs[count + 4 :]
 
     @pl.when(h == 0)
     def _():
@@ -546,7 +554,7 @@
         lo, hi = i * BLK, (i + 1) * BLK
         dob = jnp.where(lane, do_scr[lo:hi, :], BF(0))
         qb = jnp.where(lane, q_ref[lo:hi, :], BF(0))
-        pb = p_ref[0, lo:hi, :hi]
+        pb = p_refs[i][0]
         p = pb.astype(F32)
         dp = dot_nt(dob, v_ref[:hi, :])
         ds = (p * (dp - rowsum(p * dp))).astype(BF)
@@ -565,8 +573,8 @@
     return run(
         attend_back_kernel,
         (heads,),
-        [q, k, v, p, *do],
-        fulls([q, k, v]) + [pl.BlockSpec((1, rows, rows), lambda s, i: (s, 0, 0))] + fulls(do),
+        [q, k, v, *p, *do],
+        fulls([q, k, v]) + [head_spec(w) for w in widths(rows)] + fulls(do),
         [sds((rows, 3 * hw), BF)],
         [full((rows, 3 * hw))],
         idx,
@@ -574,7 +582,7 @@
         11,
         [pltpu.VMEM((rows, hw), BF)] + [pltpu.VMEM((rows, hw), F32)] * 3,
         after=after,
-        hbm=range(4),
+        hbm=range(3 + len(p)),
     )[0]
 
 
@@ -634,8 +642,8 @@
     half = count // 2
 
     def kernel(idx, keep_ref, got_ref, stay_ref, send_ref):
-        stay_ref[...] = keep_ref[:half] + got_ref[:half].astype(F32)
-        send = (keep_ref[half:] + got_ref[half:].astype(F32)).astype(BF)
+        stay_ref[...] = keep_ref[:half].astype(F32) + got_ref[:half].astype(F32)
+        send = (keep_ref[half:].astype(F32) + got_ref[half:].astype(F32)).astype(BF)
         send_ref[...] = send if half > 1 else send[0]
 
     outs = [sds((half, rows, d), F32), sds((half, rows, d) if half > 1 else (rows, d), BF)]
@@ -697,6 +705,37 @@
 
     out = [sds(x.shape, F32)]
     return run(kernel, (1,), [x, y], fulls([x, y]), out, fulls(out), idx, "vec_add", tick, (), after)[0]
+
+
+def pack_weights(w, w2, groups, idx):
+    rows, n = w.shape
+
+    def kernel(idx, w_ref, w2_ref, out_ref):
+        out_ref[:, :n] = w_ref[...].astype(BF)
+        out_ref[:, n:] = pack_rows(w2_ref[...], groups).astype(BF)
+
+    out = [sds((rows, n + w2.shape[1] // groups), BF)]
+    return run(kernel, (1,), [w, w2], fulls([w, w2]), out, fulls(out), idx, "pack_weights", 1, hbm=(0, 1))[0]
+
+
+def cast_pair(x, y, idx):
+    def kernel(idx, x_ref, y_ref, x_out, y_out):
+        x_out[...] = x_ref[...].astype(BF)
+        y_out[...] = y_ref[...].astype(BF)
+
+    outs = [sds(x.shape, BF), sds(y.shape, BF)]
+    return run(kernel, (1,), [x, y], fulls([x, y]), outs, fulls(outs), idx, "cast_pair", 1, hbm=(0, 1))
+
+
+def warm(arrays, idx, after=()):
+    count = len(arrays)
+
+    def kernel(idx, *refs):
+        for x, y in zip(refs[:count], refs[count:]):
+            y[...] = x[...]
+
+    outs = [near(x.shape, x.dtype) for x in arrays]
+    return run(kernel, (1,), arrays, fulls(arrays), outs, fulls(outs), idx, "warm", 0, (), after, range(count))
 
 
 def one_hot(place, count, width):
@@ -778,7 +817,7 @@
 
     all_outs = outs + outs2 + [sds(x.shape, F32) for x in [*norms, *norms]]
     ins = [*mats, *mats2, near_blocks, far_blocks, *norms]
-    res = run(kernel, (1,), ins, fulls(ins), all_outs, fulls(all_outs), idx, name, 6, [scr, scr2], after, range(10))
+    res = run(kernel, (1,), ins, fulls(ins), all_outs, fulls(all_outs), idx, name, 6, [scr, scr2], after)
     res = list(res)
     res[0] = res[0].T if flip else res[0]
     res[5] = res[5].T if flip2 else res[5]
@@ -870,11 +909,13 @@
     def after(x, *deps):
         return lax.optimization_barrier((x, *deps))[0]
 
-    out_rows = fine_rows(w_out[0].astype(BF))
     groups = tokens.shape[1] // hw
-    first = jnp.concatenate([fine_rows(w_qkv[0].astype(BF)), pack_rows(out_rows, groups)], axis=1)
-    up_own = fine_rows(w_up[0].astype(BF))
-    down_own = fine_rows(w_down[0].astype(BF))
+    if fine == 1:
+        first = pack_weights(w_qkv[0], w_out[0], groups, idx)
+    else:
+        out_rows = fine_rows(w_out[0].astype(BF))
+        first = jnp.concatenate([fine_rows(w_qkv[0].astype(BF)), pack_rows(out_rows, groups)], axis=1)
+    up_own, down_own = (fine_rows(x) for x in cast_pair(w_up[0], w_down[0], idx))
     down_two = jnp.stack([down_own, dp(down_own, 1)])
     first = gather8(first, down_two)
 
@@ -890,22 +931,21 @@
     down_z2 = dp(after(down_two, up_go), 4)
     q, k, v, wq, wo = project(a_low, attn_norm, first, hw, idx)
     wo_far = mp(wo, 2)
-    o, probs = attend(start, q, k, v, idx)
+    o, *probs = attend(start, q, k, v, idx)
     o, *up_z = lax.optimization_barrier((o, *up_z))
-    up_four = jnp.stack([up_own, *up_z])
-    o, wo, wo_far, up_four = lax.optimization_barrier((o, wo, wo_far, up_four))
     o_far = mp(o, 2)
+    up_four = jnp.stack([up_own, *lax.optimization_barrier((*up_z, down_z2))[:-1]])
     up_x = dp(up_four, 1)
-    wo_near, wo_last = mp(after(wo, up_four), 1), mp(wo_far, 1)
+    wo_near, wo_last = mp(after(wo, up_four), 1), mp(after(wo_far, up_four), 1)
     down_four = join([down_two, down_z2], idx, [up_four, wo_near, wo_last])
     down_z1 = dp(down_four, 2)
     o_near = mp(after(o, o_far), 1)
     o_all = [o, o_near, o_far, mp(o_far, 1)]
     wo_all = [wo, wo_near, wo_far, wo_last]
     hidden, c_low = outproj(outer_norms, tokens, o_all, wo_all, idx, [up_x])
-    u, dw, stats, wu, wd = ffn_up(c_low, cotangent, ffn_norm, [up_four, up_x, down_four, down_z1], idx)
+    z, slope, dw, stats, wu, wd = ffn_up(c_low, cotangent, ffn_norm, [up_four, up_x, down_four, down_z1], idx)
     stats = lax.all_gather(stats, "mp")
-    w_low, du, dc_send, dc_keep, dc_last, ffn_grads = ffn_mid(u, dw, stats, ffn_norm, wu, idx)
+    w_low, du, dc_send, dc_keep, dc_last, ffn_grads = ffn_mid(z, slope, dw, stats, ffn_norm, wu, idx)
     dc_got = mp(dc_send, 1)
     dc_sum = far_sum(dc_last, dc_got, idx)
     down_send, down_keep = weight_grad(w_low, cotangent, idx, "grad_down", [dc_sum])
@@ -983,16 +1023,22 @@
     def mats(*arrays):
         return [x[0] for x in arrays]
 
+    ready = warm(
+        mats(w_qkv, left_qkv, right_qkv, left_root_qkv, right_root_qkv)
+        + mats(w_out, left_out, right_out, left_root_out, right_root_out),
+        idx,
+        [qkv_four],
+    )
     up_mats = mats(w_up, left_up, right_up, left_root_up, right_root_up)
-    *up_res, token = update_one(up_mats, up_four, up_other, total, idx, "update_up", [qkv_four], 0)
+    *up_res, token = update_one(up_mats, up_four, up_other, total, idx, "update_up", [ready[0]], 0)
     gt_far, out_far = after(gt_far, token), after(out_far, token)
     gt_all = [gt, mp(after(gt, gt_far), 1), gt_far, mp(gt_far, 1)]
     grad_tokens, token = spread_rows(gt_all, idx, "spread_tokens", [token])
     out_all = [out_own, mp(after(out_own, out_far), 1), out_far, mp(out_far, 1)]
     block_out, token = spread_rows(out_all, idx, "spread_out", [token])
     qkv_res, out_res, vecs = update_pair(
-        mats(w_qkv, left_qkv, right_qkv, left_root_qkv, right_root_qkv),
-        mats(w_out, left_out, right_out, left_root_out, right_root_out),
+        ready[:5],
+        ready[5:],
         qkv_four,
         qkv_other,
         [outer_norms, attn_norm, ffn_norm],

time: 243 us -> 239 us (0.984)
  other arithmetic: 6.65 us -> 2.05 us
  Pallas kernels: 113 us -> 117 us
  local copies, waits for them, and re-layouts: 6.39 us -> 2.42 us
    pallas_call x39 -> x42, Pallas kernels: 113 us -> 117 us  [run(): pl.pallas_call(kernel, grid_spec=pltpu.PrefetchScalarGridSpec(num_scalar_...]
    convert_element_type x4 -> x0, other arithmetic: 3.07 us -> none  [the longest x1 1.08 us: body(): down_own = fine_rows(w_down[0].astype(BF))]
  transfers between devices with their start and end apart: 58 -> 58, of which waited for: 23 -> 21; matrix products, arithmetic and copies ran while one was open for 3% -> 1% of each run, Pallas kernels for 38% -> 41%
where the time goes in v5:
time: 239 us; the launch traced here: 238 us
  Pallas kernels  117 us (49%)
  starting transfers between devices  55.9 us (23%)
  waiting for transfers between devices  53.4 us (22%)
  blocking collectives  5.59 us (2%)
  local copies, waits for them, and re-layouts  2.42 us (1%)
    pallas_call x42, Pallas kernels, run(): pl.pallas_call(kernel, grid_spec=pltpu.PrefetchScalarGridSpec(num_scalar_...  117 us
    ppermute x58, starting transfers between devices, swap(): return lax.ppermute(x, axis, [(i, i ^ k) for i in range(size)])  55.9 us
    ppermute x58, waiting for transfers between devices, swap(): return lax.ppermute(x, axis, [(i, i ^ k) for i in range(size)])  53.4 us
    all_gather x1, blocking collectives, body(): stats = lax.all_gather(stats, 'mp')  5.59 us
  transfers between devices with their start and end apart: 58, of which 21 were waited for; matrix products, arithmetic and copies ran while one was open for 1% of the time, Pallas kernels for 41%

profile of v5, /device:TPU:0, one launch (start us, length us, event | category | flops | bytes accessed | tf_op | source)
XLA Modules:
  0.0 238.4 jit_solution(13338432912725058787)
XLA Ops:
  0.8 2.4 pack_weights.1.refs_2_
  3.1 2.9 %collective-permute-start = (bf16[96,768]{1,0:T(8,128)(2,1)}, bf16[96,768]{1,0:T(8,128)(2,1)}, u32[]{:S(2)}, u32[]{:S(2)}) collective-permute-start(bf16[96,768]{1,0:T(8,128)(2,1)} %pack_weights.1.refs_2_), channel_id=1, source_target_pairs={{0,4},{4,0},{8,12},{12,8},{16,20},{20,16},{24,28},{28,24},{1,5},{5... | collective-permute-start | bytes 442376 | tf_op jit(solution)/shard_map/ppermute | solution.py:864
  7.6 2.6 %collective-permute-start.4 = (bf16[96,768]{1,0:T(8,128)(2,1)}, bf16[96,768]{1,0:T(8,128)(2,1)}, u32[]{:S(2)}, u32[]{:S(2)}) collective-permute-start(bf16[96,768]{1,0:T(8,128)(2,1)} %pack_weights.1.refs_2_), channel_id=1, source_target_pairs={{0,16},{4,20},{8,24},{12,28},{16,0},{20,4},{24,8},{28,12},{1,17},{... | collective-permute-start | bytes 442376 | tf_op jit(solution)/shard_map/ppermute | solution.py:864
  10.4 1.6 cast_pair.1
  13.4 3.9 %collective-permute-done.2 = bf16[96,768]{1,0:T(8,128)(2,1)S(1)} collective-permute-done((bf16[96,768]{1,0:T(8,128)(2,1)S(1)}, bf16[96,768]{1,0:T(8,128)(2,1)S(1)}, u32[]{:S(2)}, u32[]{:S(2)}) %collective-permute-start.2) | collective-permute-done | bytes 147488 | tf_op jit(solution)/shard_map/ppermute | solution.py:864
  17.7 4.1 %collective-permute-done.4.refs_6_ = bf16[96,768]{1,0:T(8,128)(2,1)} collective-permute-done((bf16[96,768]{1,0:T(8,128)(2,1)}, bf16[96,768]{1,0:T(8,128)(2,1)}, u32[]{:S(2)}, u32[]{:S(2)}) %collective-permute-start.4) | collective-permute-done | bytes 147488 | tf_op jit(solution)/shard_map/ppermute | solution.py:864
  25.0 1.7 collective-permute-start.8
  30.3 5.1 %project.1 = (bf16[1024,192]{1,0:T(8,128)(2,1)}, bf16[1024,192]{1,0:T(8,128)(2,1)}, bf16[1024,192]{1,0:T(8,128)(2,1)}, bf16[768,576]{1,0:T(8,128)(2,1)}, bf16[208,768]{1,0:T(8,128)(2,1)}) custom-call(s32[3]{0:T(128)S(1)} %pad_add_fusion.idx, bf16[1024,768]{1,0:T(8,128)(2,1)S(1)} %fusion.5.refs_0_, f32[2,192]{1,0:T(2,128)S(1)} %copy-done.23, ...), custom_call_target="tpu_custom_call" | custom-call | flops 16000000000 | bytes 1024 | tf_op jit(solution)/shard_map/project/pallas_call | solution.py:44
  37.0 9.8 %attend.1 = (bf16[1024,192]{1,0:T(8,128)(2,1)}, bf16[3,256,256]{2,1,0:T(8,128)(2,1)}, bf16[3,256,512]{2,1,0:T(8,128)(2,1)}, bf16[3,256,768]{2,1,0:T(8,128)(2,1)}, bf16[3,256,1024]{2,1,0:T(8,128)(2,1)}) custom-call(s32[3]{0:T(128)S(1)} %pad_add_fusion.idx, s32[1024,1]{1,0:T(8,128)S(1)} %copy.55.refs_0_, bf16[1024,192]{1,0:T(8,128)(2,1)} %get-tuple-element.157.refs_1_.refs_0_, ...), custom_call_target="tpu_custom_call" | custom-call | flops 4000000000 | bytes 1024 | tf_op jit(solution)/shard_map/attend/pallas_call | solution.py:44
  46.8 4.8 %collective-permute-done.14.refs_1_ = bf16[2,96,768]{2,1,0:T(8,128)(2,1)S(1)} collective-permute-done((bf16[2,96,768]{2,1,0:T(8,128)(2,1)S(1)}, bf16[2,96,768]{2,1,0:T(8,128)(2,1)S(1)}, u32[]{:S(2)}, u32[]{:S(2)}) %collective-permute-start.14) | collective-permute-done | bytes 294944 | tf_op jit(solution)/shard_map/ppermute | solution.py:864
  56.0 10.4 %collective-permute-done.11.refs_4_.refs_8_ = bf16[1024,192]{1,0:T(8,128)(2,1)S(1)} collective-permute-done((bf16[1024,192]{1,0:T(8,128)(2,1)}, bf16[1024,192]{1,0:T(8,128)(2,1)S(1)}, u32[]{:S(2)}, u32[]{:S(2)}) %collective-permute-start.11) | collective-permute-done | bytes 393248 | tf_op jit(solution)/shard_map/ppermute | solution.py:864
  66.9 1.9 collective-permute-done.18.refs_10_.refs_4_
  69.1 6.8 %outproj.1 = (f32[1024,768]{1,0:T(8,128)}, bf16[1024,768]{1,0:T(8,128)(2,1)S(1)}) custom-call(s32[3]{0:T(128)S(1)} %pad_add_fusion.idx, f32[4,768]{1,0:T(4,128)S(1)} %copy-done.15, bf16[1024,768]{1,0:T(8,128)(2,1)} %refs_3_.1, bf16[1024,192]{1,0:T(8,128)(2,1)S(1)} %copy-done.2, bf16[1024,192]{1,0:T(8,128)(2,1)S(1)} %collective-permute-done.12.refs_3_.refs_7_, ...), custom_call_target="tpu_custom_call" | custom-call | bytes 1024 | tf_op jit(solution)/shard_map/outproj/pallas_call | solution.py:44
  75.9 7.2 %ffn_up.1 = (f32[1024,768]{1,0:T(8,128)S(1)}, f32[1024,768]{1,0:T(8,128)S(1)}, f32[1024,768]{1,0:T(8,128)S(1)}, f32[8,1024]{1,0:T(8,128)S(1)}, bf16[768,768]{1,0:T(8,128)(2,1)S(1)}, /*index=5*/bf16[768,768]{1,0:T(8,128)(2,1)}) custom-call(s32[3]{0:T(128)S(1)} %pad_add_fusion.idx, bf16[1024,768]{1,0:T(8,128)(2,1)S(1)} %get-tuple-element.176.refs_0_, ...), custom_call_target="tpu_custom_call" | custom-call | flops 3000000000 | bytes 1024 | tf_op jit(solution)/shard_map/ffn_up/pallas_call | solution.py:44
  83.1 5.6 %all-gather = f32[32,1024]{1,0:T(8,128)S(1)} all-gather(f32[8,1024]{1,0:T(8,128)S(1)} %get-tuple-element.180), channel_id=2, replica_groups=mesh['dp'=8,'mp'=4] {'mp'}, dimensions={0}, use_global_device_ids=true | all-gather | bytes 163840 | tf_op jit(solution)/shard_map/all_gather | solution.py:947
  88.7 6.2 %ffn_mid.1 = (bf16[1024,768]{1,0:T(8,128)(2,1)}, bf16[1024,768]{1,0:T(8,128)(2,1)}, bf16[2,256,768]{2,1,0:T(8,128)(2,1)S(1)}, f32[256,768]{1,0:T(8,128)}, f32[256,768]{1,0:T(8,128)S(1)}, /*index=5*/f32[2,768]{1,0:T(2,128)S(1)}) custom-call(s32[3]{0:T(128)S(1)} %pad_add_fusion.idx, f32[1024,768]{1,0:T(8,128)S(1)} %get-tuple-element.177.refs_0_, ...), custom_call_target="tpu_custom_call" | custom-call | flops 2600000000 | bytes 1024 | tf_op jit(solution)/shard_map/ffn_mid/pallas_call | solution.py:44
  95.3 1.9 collective-permute-done.20.refs_1_
  97.8 1.6 collective-permute-start.21
  99.4 3.5 %grad_down.1 = (bf16[4,96,768]{2,1,0:T(8,128)(2,1)S(1)}, bf16[4,96,768]{2,1,0:T(8,128)(2,1)}) custom-call(s32[3]{0:T(128)S(1)} %pad_add_fusion.idx, bf16[1024,768]{1,0:T(8,128)(2,1)S(1)} %copy-done.7, bf16[1024,768]{1,0:T(8,128)(2,1)S(1)} %copy-done.8, bf16[256,768]{1,0:T(8,128)(2,1)S(1)} %far_sum.4.refs_2_), custom_call_target="tpu_custom_call" | custom-call | flops 1400000000 | bytes 1024 | tf_op jit(solution)/shard_map/grad_down/pallas_call | solution.py:44
  104.5 3.5 %grad_up.1 = (bf16[4,96,768]{2,1,0:T(8,128)(2,1)S(1)}, bf16[4,96,768]{2,1,0:T(8,128)(2,1)}) custom-call(s32[3]{0:T(128)S(1)} %pad_add_fusion.idx, bf16[1024,768]{1,0:T(8,128)(2,1)S(1)} %get-tuple-element.176.refs_0_, bf16[1024,768]{1,0:T(8,128)(2,1)S(1)} %copy-done.19, bf16[4,96,768]{2,1,0:T(8,128)(2,1)S(1)} %get-tuple-element.188.refs_2_), custom_call_target="tpu_custom_call" | custom-call | flops 1400000000 | bytes 1024 | tf_op jit(solution)/shard_map/grad_up/pallas_call | solution.py:44
  109.3 5.1 %shard_back.1 = (f32[256,768]{1,0:T(8,128)}, f32[2,768]{1,0:T(2,128)S(1)}, f32[4,2,192]{2,1,0:T(2,128)S(1)}, bf16[256,192]{1,0:T(8,128)(2,1)S(1)}, bf16[256,192]...) custom-call(s32[3]{0:T(128)S(1)} %pad_add_fusion.idx, ...), custom_call_target="tpu_custom_call" | custom-call | bytes 1024 | tf_op jit(solution)/shard_map/shard_back/pallas_call | solution.py:44
  118.1 5.5 %ffn_out.1 = (bf16[2,256,768]{2,1,0:T(8,128)(2,1)S(1)}, f32[256,768]{1,0:T(8,128)}, f32[256,768]{1,0:T(8,128)S(1)}) custom-call(s32[3]{0:T(128)S(1)} %pad_add_fusion.idx, bf16[1024,768]{1,0:T(8,128)(2,1)} %get-tuple-element.182.refs_0_, bf16[768,768]{1,0:T(8,128)(2,1)} %get-tuple-element.183.refs_1_, bf16[256,192]{1,0:T(8,128)(2,1)S(1)} %collective-permute-done.22.refs_2_.refs_8_), custom_call_target="tpu_custom_call" | custom-call | bytes 1024 | tf_op jit(solution)/shard_map/ffn_out/pallas_call | solution.py:44
  123.6 1.7 fold.6
  127.6 11.2 %attend_back.1.refs_2_.refs_1_ = bf16[1024,576]{1,0:T(8,128)(2,1)S(1)} custom-call(s32[3]{0:T(128)S(1)} %pad_add_fusion.idx, bf16[1024,192]{1,0:T(8,128)(2,1)} %get-tuple-element.157.refs_1_.refs_0_, bf16[1024,192]{1,0:T(8,128)(2,1)} %get-tuple-element.158.refs_2_.refs_1_, bf16[1024,192]{1,0:T(8,128)(2,1)} %get-tuple-element.159.refs_3_.refs_2_, ...), custom_call_target="tpu_custom_call" | custom-call | flops 4400000000 | bytes 1024 | tf_op jit(solution)/shard_map/attend_back/pallas_call | solution.py:44
  139.6 1.7 fold.8
  141.4 6.6 %qkv_back.1 = (bf16[4,96,768]{2,1,0:T(8,128)(2,1)}, bf16[4,96,768]{2,1,0:T(8,128)(2,1)}, bf16[2,256,768]{2,1,0:T(8,128)(2,1)}, f32[256,768]{1,0:T(8,128)}, f32[256,768]{1,0:T(8,128)S(1)}) custom-call(s32[3]{0:T(128)S(1)} %pad_add_fusion.idx, bf16[1024,768]{1,0:T(8,128)(2,1)} %copy-done.6, bf16[1024,576]{1,0:T(8,128)(2,1)S(1)} %attend_back.1.refs_2_.refs_1_, ...), custom_call_target="tpu_custom_call" | custom-call | flops 16000000000 | bytes 1024 | tf_op jit(solution)/shard_map/qkv_back/pallas_call | solution.py:44
  150.0 2.5 %collective-permute-start.32 = (bf16[96,768]{1,0:T(8,128)(2,1)}, bf16[96,768]{1,0:T(8,128)(2,1)S(1)}, u32[]{:S(2)}, u32[]{:S(2)}) collective-permute-start(bf16[96,768]{1,0:T(8,128)(2,1)} %copy-done.22), channel_id=1, source_target_pairs={{0,16},{4,20},{8,24},{12,28},{16,0},{20,4},{24,8},{28,12},{1,17},{... | collective-permute-start | bytes 442376 | tf_op jit(solution)/shard_map/ppermute | solution.py:864
  155.9 3.9 %collective-permute-done.32.refs_1_ = bf16[96,768]{1,0:T(8,128)(2,1)S(1)} collective-permute-done((bf16[96,768]{1,0:T(8,128)(2,1)}, bf16[96,768]{1,0:T(8,128)(2,1)S(1)}, u32[]{:S(2)}, u32[]{:S(2)}) %collective-permute-start.32) | collective-permute-done | bytes 147488 | tf_op jit(solution)/shard_map/ppermute | solution.py:864
  161.0 3.9 %collective-permute-done.36.refs_1_ = bf16[4,96,768]{2,1,0:T(8,128)(2,1)} collective-permute-done((bf16[4,96,768]{2,1,0:T(8,128)(2,1)}, bf16[4,96,768]{2,1,0:T(8,128)(2,1)}, u32[]{:S(2)}, u32[]{:S(2)}) %collective-permute-start.36) | collective-permute-done | bytes 589856 | tf_op jit(solution)/shard_map/ppermute | solution.py:864
  164.9 1.9 fold.9
  166.8 2.1 collective-permute-start.43
  170.7 2.1 collective-permute-start.41
  172.8 2.1 block_end.1.refs_6_.refs_0_
  180.1 3.4 %collective-permute-start.40 = (bf16[96,768]{1,0:T(8,128)(2,1)S(1)}, bf16[96,768]{1,0:T(8,128)(2,1)S(1)}, u32[]{:S(2)}, u32[]{:S(2)}) collective-permute-start(bf16[96,768]{1,0:T(8,128)(2,1)S(1)} %close.4.refs_2_.refs_0_), channel_id=1, source_target_pairs={{0,16},{4,20},{8,24},{12,28},{16,0},{20,4},{24,8},{28,12},{1,17},{... | collective-permute-start | bytes 442376 | tf_op jit(solution)/shard_map/ppermute | solution.py:864
  185.4 2.1 collective-permute-done.41.refs_1_
  188.7 1.9 collective-permute-start.52
  190.6 2.4 %collective-permute-done.44.refs_3_.refs_2_ = bf16[256,768]{1,0:T(8,128)(2,1)S(1)} collective-permute-done((bf16[256,768]{1,0:T(8,128)(2,1)S(1)}, bf16[256,768]{1,0:T(8,128)(2,1)S(1)}, u32[]{:S(2)}, u32[]{:S(2)}) %collective-permute-start.44) | collective-permute-done | bytes 393248 | tf_op jit(solution)/shard_map/ppermute | solution.py:864
  199.3 1.8 collective-permute-start.50
  201.1 1.9 collective-permute-start.51
  205.1 5.1 %update_down.1 = (f32[768,768]{1,0:T(8,128)}, f32[96,768]{1,0:T(8,128)}, f32[96,768]{1,0:T(8,128)}, f32[96,768]{1,0:T(8,128)}, bf16[96,768]{1,0:T(8,128)(2,1)}, /*index=5*/f32[8,128]{1,0:T(8,128)S(1)}) custom-call(s32[3]{0:T(128)S(1)} %pad_add_fusion.idx, f32[96,768]{1,0:T(8,128)} %bitcast.63, f32[96,768]{1,0:T(8,128)} %bitcast.64, f32[96,768]{1,0:T(8,128)} %bitcast.65, ...), custom_call_target="tpu_custom_call" | custom-call | bytes 1024 | tf_op jit(solution)/shard_map/update_down/pallas_call | solution.py:44
  210.2 2.3 collective-permute-done.49.refs_1_
  214.4 3.5 %warm.1 = (f32[96,576]{1,0:T(8,128)S(1)}, f32[96,768]{1,0:T(8,128)S(1)}, f32[72,576]{1,0:T(8,128)S(1)}, f32[96,768]{1,0:T(8,128)S(1)}, f32[576,576]{1,0:T(8,128)...) custom-call(s32[3]{0:T(128)S(1)} %pad_add_fusion.idx, ...), custom_call_target="tpu_custom_call" | custom-call | bytes 1024 | tf_op jit(solution)/shard_map/warm/pallas_call | solution.py:44
  217.9 3.0 %collective-permute-done.48.refs_6_ = bf16[4,96,768]{2,1,0:T(8,128)(2,1)S(1)} collective-permute-done((bf16[4,96,768]{2,1,0:T(8,128)(2,1)S(1)}, bf16[4,96,768]{2,1,0:T(8,128)(2,1)S(1)}, u32[]{:S(2)}, u32[]{:S(2)}) %collective-permute-start.48) | collective-permute-done | bytes 589856 | tf_op jit(solution)/shard_map/ppermute | solution.py:864
  220.9 5.1 %update_up.1 = (f32[768,768]{1,0:T(8,128)}, f32[96,768]{1,0:T(8,128)}, f32[96,768]{1,0:T(8,128)}, f32[96,768]{1,0:T(8,128)}, bf16[96,768]{1,0:T(8,128)(2,1)}, /*index=5*/f32[8,128]{1,0:T(8,128)S(1)}) custom-call(s32[3]{0:T(128)S(1)} %pad_add_fusion.idx, f32[96,768]{1,0:T(8,128)} %bitcast.68, f32[96,768]{1,0:T(8,128)} %bitcast.69, f32[96,768]{1,0:T(8,128)} %bitcast.70, ...), custom_call_target="tpu_custom_call" | custom-call | bytes 1024 | tf_op jit(solution)/shard_map/update_up/pallas_call | solution.py:44
  228.3 1.8 spread_tokens.1
  230.1 1.8 spread_out.1
  231.9 1.8 collective-permute-done.57.refs_11_
  233.7 4.5 %update_qkv.1 = (f32[576,768]{1,0:T(8,128)}, f32[96,768]{1,0:T(8,128)}, f32[72,576]{1,0:T(8,128)}, f32[96,576]{1,0:T(8,128)}, bf16[96,576]{1,0:T(8,128)(2,1)}, /...) custom-call(s32[3]{0:T(128)S(1)} %pad_add_fusion.idx, ...), custom_call_target="tpu_custom_call" | custom-call | flops 2400000000 | bytes 1024 | tf_op jit(solution)/shard_map/update_qkv/pallas_call | solution.py:44
  (197 shorter events, 56.4 us)
Async XLA Ops:
  3.1 23.6 %collective-permute-start = (bf16[96,768]{1,0:T(8,128)(2,1)}, bf16[96,768]{1,0:T(8,128)(2,1)}, u32[]{:S(2)}, u32[]{:S(2)}) collective-permute-start(bf16[96,768]{1,0:T(8,128)(2,1)} %pack_weights.1.refs_2_), channel_id=1, source_target_pairs={{0,4},{4,0},{8,12},{12,8},{16,20},{20,16},{24,28},{28,24},{1,5},{5... | collective-permute-start | bytes 442376 | tf_op jit(solution)/shard_map/ppermute | solution.py:864
  6.1 11.3 %collective-permute-start.1 = (bf16[96,768]{1,0:T(8,128)(2,1)}, bf16[96,768]{1,0:T(8,128)(2,1)}, u32[]{:S(2)}, u32[]{:S(2)}) collective-permute-start(bf16[96,768]{1,0:T(8,128)(2,1)} %pack_weights.1.refs_2_), channel_id=1, source_target_pairs={{0,8},{4,12},{8,0},{12,4},{16,24},{20,28},{24,16},{28,20},{1,9},{5... | collective-permute-start | bytes 442376 | tf_op jit(solution)/shard_map/ppermute | solution.py:864
  7.6 14.2 %collective-permute-start.4 = (bf16[96,768]{1,0:T(8,128)(2,1)}, bf16[96,768]{1,0:T(8,128)(2,1)}, u32[]{:S(2)}, u32[]{:S(2)}) collective-permute-start(bf16[96,768]{1,0:T(8,128)(2,1)} %pack_weights.1.refs_2_), channel_id=1, source_target_pairs={{0,16},{4,20},{8,24},{12,28},{16,0},{20,4},{24,8},{28,12},{1,17},{... | collective-permute-start | bytes 442376 | tf_op jit(solution)/shard_map/ppermute | solution.py:864
  10.2 12.2 %collective-permute-start.6 = (bf16[96,768]{1,0:T(8,128)(2,1)}, bf16[96,768]{1,0:T(8,128)(2,1)}, u32[]{:S(2)}, u32[]{:S(2)}) collective-permute-start(bf16[96,768]{1,0:T(8,128)(2,1)} %pack_weights.1.refs_2_), channel_id=1, source_target_pairs={{0,24},{4,28},{8,16},{12,20},{16,8},{20,12},{24,0},{28,4},{1,25},{... | collective-permute-start | bytes 442376 | tf_op jit(solution)/shard_map/ppermute | solution.py:864
  12.1 5.2 %collective-permute-start.2 = (bf16[96,768]{1,0:T(8,128)(2,1)S(1)}, bf16[96,768]{1,0:T(8,128)(2,1)S(1)}, u32[]{:S(2)}, u32[]{:S(2)}) collective-permute-start(bf16[96,768]{1,0:T(8,128)(2,1)S(1)} %get-tuple-element.153), channel_id=1, source_target_pairs={{0,4},{4,0},{8,12},{12,8},{16,20},{20,16},{24,28},{28,24},{1,5},{5... | collective-permute-start | bytes 442376 | tf_op jit(solution)/shard_map/ppermute | solution.py:864
  17.3 10.6 %collective-permute-start.3 = (bf16[96,768]{1,0:T(8,128)(2,1)}, bf16[96,768]{1,0:T(8,128)(2,1)}, u32[]{:S(2)}, u32[]{:S(2)}) collective-permute-start(bf16[96,768]{1,0:T(8,128)(2,1)} %collective-permute-done.1.refs_4_), channel_id=1, source_target_pairs={{0,4},{4,0},{8,12},{12,8},{16,20},{20,16},{24,28},{28,24},{1,5},{5... | collective-permute-start | bytes 442376 | tf_op jit(solution)/shard_map/ppermute | solution.py:864
  21.8 7.7 %collective-permute-start.5 = (bf16[96,768]{1,0:T(8,128)(2,1)}, bf16[96,768]{1,0:T(8,128)(2,1)}, u32[]{:S(2)}, u32[]{:S(2)}) collective-permute-start(bf16[96,768]{1,0:T(8,128)(2,1)} %collective-permute-done.4.refs_6_), channel_id=1, source_target_pairs={{0,4},{4,0},{8,12},{12,8},{16,20},{20,16},{24,28},{28,24},{1,5},{5... | collective-permute-start | bytes 442376 | tf_op jit(solution)/shard_map/ppermute | solution.py:864
  22.4 7.9 %collective-permute-start.7 = (bf16[96,768]{1,0:T(8,128)(2,1)}, bf16[96,768]{1,0:T(8,128)(2,1)}, u32[]{:S(2)}, u32[]{:S(2)}) collective-permute-start(bf16[96,768]{1,0:T(8,128)(2,1)} %collective-permute-done.6.refs_8_), channel_id=1, source_target_pairs={{0,4},{4,0},{8,12},{12,8},{16,20},{20,16},{24,28},{28,24},{1,5},{5... | collective-permute-start | bytes 442376 | tf_op jit(solution)/shard_map/ppermute | solution.py:864
  25.0 21.7 %collective-permute-start.8 = (bf16[96,768]{1,0:T(8,128)(2,1)}, bf16[96,768]{1,0:T(8,128)(2,1)S(1)}, u32[]{:S(2)}, u32[]{:S(2)}) collective-permute-start(bf16[96,768]{1,0:T(8,128)(2,1)} %copy-done.16), channel_id=1, source_target_pairs={{0,16},{4,20},{8,24},{12,28},{16,0},{20,4},{24,8},{28,12},{1,17},{... | collective-permute-start | bytes 442376 | tf_op jit(solution)/shard_map/ppermute | solution.py:864
  26.8 20.0 %collective-permute-start.9 = (bf16[96,768]{1,0:T(8,128)(2,1)}, bf16[96,768]{1,0:T(8,128)(2,1)S(1)}, u32[]{:S(2)}, u32[]{:S(2)}) collective-permute-start(bf16[96,768]{1,0:T(8,128)(2,1)} %copy-done.16), channel_id=1, source_target_pairs={{0,8},{4,12},{8,0},{12,4},{16,24},{20,28},{24,16},{28,20},{1,9},{5... | collective-permute-start | bytes 442376 | tf_op jit(solution)/shard_map/ppermute | solution.py:864
  27.9 18.9 %collective-permute-start.10 = (bf16[96,768]{1,0:T(8,128)(2,1)}, bf16[96,768]{1,0:T(8,128)(2,1)S(1)}, u32[]{:S(2)}, u32[]{:S(2)}) collective-permute-start(bf16[96,768]{1,0:T(8,128)(2,1)} %copy-done.16), channel_id=1, source_target_pairs={{0,24},{4,28},{8,16},{12,20},{16,8},{20,12},{24,0},{28,4},{1,25},{... | collective-permute-start | bytes 442376 | tf_op jit(solution)/shard_map/ppermute | solution.py:864
  29.5 22.0 %collective-permute-start.14 = (bf16[2,96,768]{2,1,0:T(8,128)(2,1)S(1)}, bf16[2,96,768]{2,1,0:T(8,128)(2,1)S(1)}, u32[]{:S(2)}, u32[]{:S(2)}) collective-permute-start(bf16[2,96,768]{2,1,0:T(8,128)(2,1)S(1)} %pad_maximum_fusion.1.refs_0_), channel_id=1, source_target_pairs={{0,16},{4,20},{8,24},{12,28},{16,0},{20,4},{24,8},{28,12},{1,17},{... | collective-permute-start | bytes 884744 | tf_op jit(solution)/shard_map/ppermute | solution.py:864
  35.4 16.3 %collective-permute-start.16 = (bf16[208,768]{1,0:T(8,128)(2,1)}, bf16[208,768]{1,0:T(8,128)(2,1)S(1)}, u32[]{:S(2)}, u32[]{:S(2)}) collective-permute-start(bf16[208,768]{1,0:T(8,128)(2,1)} %get-tuple-element.173.refs_6_.refs_10_), channel_id=1, source_target_pairs={{0,2},{1,3},{2,0},{3,1},{4,6},{5,7},{6,4},{7,5},{8,10},{9,11},{10,... | collective-permute-start | bytes 958472 | tf_op jit(solution)/shard_map/ppermute | solution.py:864
  51.7 3.6 %collective-permute-start.15 = (bf16[208,768]{1,0:T(8,128)(2,1)S(1)}, bf16[208,768]{1,0:T(8,128)(2,1)S(1)}, u32[]{:S(2)}, u32[]{:S(2)}) collective-permute-start(bf16[208,768]{1,0:T(8,128)(2,1)S(1)} %copy-done.9), channel_id=1, source_target_pairs={{0,1},{1,0},{2,3},{3,2},{4,5},{5,4},{6,7},{7,6},{8,9},{9,8},{10,11... | collective-permute-start | bytes 958472 | tf_op jit(solution)/shard_map/ppermute | solution.py:864
  52.2 14.1 %collective-permute-start.11 = (bf16[1024,192]{1,0:T(8,128)(2,1)}, bf16[1024,192]{1,0:T(8,128)(2,1)S(1)}, u32[]{:S(2)}, u32[]{:S(2)}) collective-permute-start(bf16[1024,192]{1,0:T(8,128)(2,1)} %get-tuple-element.164.refs_2_.refs_6_), channel_id=1, source_target_pairs={{0,2},{1,3},{2,0},{3,1},{4,6},{5,7},{6,4},{7,5},{8,10},{9,11},{10,... | collective-permute-start | bytes 1179656 | tf_op jit(solution)/shard_map/ppermute | solution.py:864
  53.8 15.0 %collective-permute-start.18 = (bf16[4,96,768]{2,1,0:T(8,128)(2,1)S(1)}, bf16[4,96,768]{2,1,0:T(8,128)(2,1)S(1)}, u32[]{:S(2)}, u32[]{:S(2)}) collective-permute-start(bf16[4,96,768]{2,1,0:T(8,128)(2,1)S(1)} %pad_maximum_fusion.refs_2_.refs_3_), channel_id=1, source_target_pairs={{0,4},{4,0},{8,12},{12,8},{16,20},{20,16},{24,28},{28,24},{1,5},{5... | collective-permute-start | bytes 1769480 | tf_op jit(solution)/shard_map/ppermute | solution.py:864
  55.9 20.0 %collective-permute-start.19 = (bf16[4,96,768]{2,1,0:T(8,128)(2,1)S(1)}, bf16[4,96,768]{2,1,0:T(8,128)(2,1)S(1)}, u32[]{:S(2)}, u32[]{:S(2)}) collective-permute-start(bf16[4,96,768]{2,1,0:T(8,128)(2,1)S(1)} %join.6.refs_5_), channel_id=1, source_target_pairs={{0,8},{4,12},{8,0},{12,4},{16,24},{20,28},{24,16},{28,20},{1,9},{5... | collective-permute-start | bytes 1769480 | tf_op jit(solution)/shard_map/ppermute | solution.py:864
  97.8 11.4 %collective-permute-start.21 = (bf16[256,768]{1,0:T(8,128)(2,1)S(1)}, bf16[256,768]{1,0:T(8,128)(2,1)S(1)}, u32[]{:S(2)}, u32[]{:S(2)}) collective-permute-start(bf16[256,768]{1,0:T(8,128)(2,1)S(1)} %far_sum.4.refs_2_), channel_id=1, source_target_pairs={{0,2},{1,3},{2,0},{3,1},{4,6},{5,7},{6,4},{7,5},{8,10},{9,11},{10,... | collective-permute-start | bytes 1179656 | tf_op jit(solution)/shard_map/ppermute | solution.py:864
  102.9 20.7 %collective-permute-start.26 = (bf16[4,96,768]{2,1,0:T(8,128)(2,1)S(1)}, bf16[4,96,768]{2,1,0:T(8,128)(2,1)S(1)}, u32[]{:S(2)}, u32[]{:S(2)}) collective-permute-start(bf16[4,96,768]{2,1,0:T(8,128)(2,1)S(1)} %get-tuple-element.188.refs_2_), channel_id=1, source_target_pairs={{0,4},{4,0},{8,12},{12,8},{16,20},{20,16},{24,28},{28,24},{1,5},{5... | collective-permute-start | bytes 1769480 | tf_op jit(solution)/shard_map/ppermute | solution.py:864
  114.4 11.1 %collective-permute-start.25 = (bf16[2,192,768]{2,1,0:T(8,128)(2,1)S(1)}, bf16[2,192,768]{2,1,0:T(8,128)(2,1)S(1)}, u32[]{:S(2)}, u32[]{:S(2)}) collective-permute-start(bf16[2,192,768]{2,1,0:T(8,128)(2,1)S(1)} %get-tuple-element.201), channel_id=1, source_target_pairs={{0,1},{1,0},{2,3},{3,2},{4,5},{5,4},{6,7},{7,6},{8,9},{9,8},{10,11... | collective-permute-start | bytes 1769480 | tf_op jit(solution)/shard_map/ppermute | solution.py:864
  114.9 12.7 %collective-permute-start.23 = (bf16[256,192]{1,0:T(8,128)(2,1)S(1)}, bf16[256,192]{1,0:T(8,128)(2,1)S(1)}, u32[]{:S(2)}, u32[]{:S(2)}) collective-permute-start(bf16[256,192]{1,0:T(8,128)(2,1)S(1)} %get-tuple-element.198), channel_id=1, source_target_pairs={{0,2},{1,3},{2,0},{3,1},{4,6},{5,7},{6,4},{7,5},{8,10},{9,11},{10,... | collective-permute-start | bytes 294920 | tf_op jit(solution)/shard_map/ppermute | solution.py:864
  116.4 11.2 %collective-permute-start.24 = (bf16[256,192]{1,0:T(8,128)(2,1)S(1)}, bf16[256,192]{1,0:T(8,128)(2,1)S(1)}, u32[]{:S(2)}, u32[]{:S(2)}) collective-permute-start(bf16[256,192]{1,0:T(8,128)(2,1)S(1)} %get-tuple-element.199), channel_id=1, source_target_pairs={{0,3},{1,2},{2,1},{3,0},{4,7},{5,6},{6,5},{7,4},{8,11},{9,10},{10,... | collective-permute-start | bytes 294920 | tf_op jit(solution)/shard_map/ppermute | solution.py:864
  116.6 23.0 %collective-permute-start.29 = (bf16[4,96,768]{2,1,0:T(8,128)(2,1)S(1)}, bf16[4,96,768]{2,1,0:T(8,128)(2,1)S(1)}, u32[]{:S(2)}, u32[]{:S(2)}) collective-permute-start(bf16[4,96,768]{2,1,0:T(8,128)(2,1)S(1)} %get-tuple-element.209.refs_14_), channel_id=1, source_target_pairs={{0,4},{4,0},{8,12},{12,8},{16,20},{20,16},{24,28},{28,24},{1,5},{5... | collective-permute-start | bytes 1769480 | tf_op jit(solution)/shard_map/ppermute | solution.py:864
  125.4 13.6 %collective-permute-start.30 = (bf16[2,96,768]{2,1,0:T(8,128)(2,1)S(1)}, bf16[2,96,768]{2,1,0:T(8,128)(2,1)S(1)}, u32[]{:S(2)}, u32[]{:S(2)}) collective-permute-start(bf16[2,96,768]{2,1,0:T(8,128)(2,1)S(1)} %get-tuple-element.203.refs_2_), channel_id=1, source_target_pairs={{0,8},{4,12},{8,0},{12,4},{16,24},{20,28},{24,16},{28,20},{1,9},{5... | collective-permute-start | bytes 884744 | tf_op jit(solution)/shard_map/ppermute | solution.py:864
  126.1 15.3 %collective-permute-start.28 = (bf16[192,768]{1,0:T(8,128)(2,1)S(1)}, bf16[192,768]{1,0:T(8,128)(2,1)S(1)}, u32[]{:S(2)}, u32[]{:S(2)}) collective-permute-start(bf16[192,768]{1,0:T(8,128)(2,1)S(1)} %far_sum.5.refs_11_), channel_id=1, source_target_pairs={{0,2},{1,3},{2,0},{3,1},{4,6},{5,7},{6,4},{7,5},{8,10},{9,11},{10,... | collective-permute-start | bytes 884744 | tf_op jit(solution)/shard_map/ppermute | solution.py:864
  138.9 13.7 %collective-permute-start.27 = (bf16[2,256,768]{2,1,0:T(8,128)(2,1)S(1)}, bf16[2,256,768]{2,1,0:T(8,128)(2,1)S(1)}, u32[]{:S(2)}, u32[]{:S(2)}) collective-permute-start(bf16[2,256,768]{2,1,0:T(8,128)(2,1)S(1)} %get-tuple-element.204.refs_2_), channel_id=1, source_target_pairs={{0,1},{1,0},{2,3},{3,2},{4,5},{5,4},{6,7},{7,6},{8,9},{9,8},{10,11... | collective-permute-start | bytes 2359304 | tf_op jit(solution)/shard_map/ppermute | solution.py:864
  148.9 4.9 %collective-permute-start.33 = (bf16[2,256,768]{2,1,0:T(8,128)(2,1)}, bf16[2,256,768]{2,1,0:T(8,128)(2,1)S(1)}, u32[]{:S(2)}, u32[]{:S(2)}) collective-permute-start(bf16[2,256,768]{2,1,0:T(8,128)(2,1)} %get-tuple-element.216), channel_id=1, source_target_pairs={{0,1},{1,0},{2,3},{3,2},{4,5},{5,4},{6,7},{7,6},{8,9},{9,8},{10,11... | collective-permute-start | bytes 2359304 | tf_op jit(solution)/shard_map/ppermute | solution.py:864
  149.3 15.6 %collective-permute-start.36 = (bf16[4,96,768]{2,1,0:T(8,128)(2,1)}, bf16[4,96,768]{2,1,0:T(8,128)(2,1)}, u32[]{:S(2)}, u32[]{:S(2)}) collective-permute-start(bf16[4,96,768]{2,1,0:T(8,128)(2,1)} %get-tuple-element.213.refs_2_), channel_id=1, source_target_pairs={{0,4},{4,0},{8,12},{12,8},{16,20},{20,16},{24,28},{28,24},{1,5},{5... | collective-permute-start | bytes 1769480 | tf_op jit(solution)/shard_map/ppermute | solution.py:864
  150.0 9.9 %collective-permute-start.32 = (bf16[96,768]{1,0:T(8,128)(2,1)}, bf16[96,768]{1,0:T(8,128)(2,1)S(1)}, u32[]{:S(2)}, u32[]{:S(2)}) collective-permute-start(bf16[96,768]{1,0:T(8,128)(2,1)} %copy-done.22), channel_id=1, source_target_pairs={{0,16},{4,20},{8,24},{12,28},{16,0},{20,4},{24,8},{28,12},{1,17},{... | collective-permute-start | bytes 442376 | tf_op jit(solution)/shard_map/ppermute | solution.py:864
  152.5 16.4 %collective-permute-start.35 = (bf16[2,96,768]{2,1,0:T(8,128)(2,1)}, bf16[2,96,768]{2,1,0:T(8,128)(2,1)S(1)}, u32[]{:S(2)}, u32[]{:S(2)}) collective-permute-start(bf16[2,96,768]{2,1,0:T(8,128)(2,1)} %copy-done.21), channel_id=1, source_target_pairs={{0,8},{4,12},{8,0},{12,4},{16,24},{20,28},{24,16},{28,20},{1,9},{5... | collective-permute-start | bytes 884744 | tf_op jit(solution)/shard_map/ppermute | solution.py:864
  153.2 19.6 %collective-permute-start.31 = (bf16[256,768]{1,0:T(8,128)(2,1)S(1)}, bf16[256,768]{1,0:T(8,128)(2,1)S(1)}, u32[]{:S(2)}, u32[]{:S(2)}) collective-permute-start(bf16[256,768]{1,0:T(8,128)(2,1)S(1)} %far_sum.6.refs_2_), channel_id=1, source_target_pairs={{0,2},{1,3},{2,0},{3,1},{4,6},{5,7},{6,4},{7,5},{8,10},{9,11},{10,... | collective-permute-start | bytes 1179656 | tf_op jit(solution)/shard_map/ppermute | solution.py:864
  154.4 21.1 %collective-permute-start.39 = (bf16[256,768]{1,0:T(8,128)(2,1)S(1)}, bf16[256,768]{1,0:T(8,128)(2,1)S(1)}, u32[]{:S(2)}, u32[]{:S(2)}) collective-permute-start(bf16[256,768]{1,0:T(8,128)(2,1)S(1)} %far_sum.7.refs_2_), channel_id=1, source_target_pairs={{0,2},{1,3},{2,0},{3,1},{4,6},{5,7},{6,4},{7,5},{8,10},{9,11},{10,... | collective-permute-start | bytes 1179656 | tf_op jit(solution)/shard_map/ppermute | solution.py:864
  160.5 9.6 %collective-permute-start.34 = (bf16[96,768]{1,0:T(8,128)(2,1)S(1)}, bf16[96,768]{1,0:T(8,128)(2,1)S(1)}, u32[]{:S(2)}, u32[]{:S(2)}) collective-permute-start(bf16[96,768]{1,0:T(8,128)(2,1)S(1)} %close.3.refs_2_.refs_0_), channel_id=1, source_target_pairs={{0,16},{4,20},{8,24},{12,28},{16,0},{20,4},{24,8},{28,12},{1,17},{... | collective-permute-start | bytes 442376 | tf_op jit(solution)/shard_map/ppermute | solution.py:864
  166.8 16.7 %collective-permute-start.43 = (bf16[2,96,768]{2,1,0:T(8,128)(2,1)S(1)}, bf16[2,96,768]{2,1,0:T(8,128)(2,1)S(1)}, u32[]{:S(2)}, u32[]{:S(2)}) collective-permute-start(bf16[2,96,768]{2,1,0:T(8,128)(2,1)S(1)} %get-tuple-element.219.refs_2_), channel_id=1, source_target_pairs={{0,8},{4,12},{8,0},{12,4},{16,24},{20,28},{24,16},{28,20},{1,9},{5... | collective-permute-start | bytes 884744 | tf_op jit(solution)/shard_map/ppermute | solution.py:864
  169.5 10.0 %collective-permute-start.38 = (bf16[96,768]{1,0:T(8,128)(2,1)S(1)}, bf16[96,768]{1,0:T(8,128)(2,1)S(1)}, u32[]{:S(2)}, u32[]{:S(2)}) collective-permute-start(bf16[96,768]{1,0:T(8,128)(2,1)S(1)} %get-tuple-element.220.refs_2_), channel_id=1, source_target_pairs={{0,16},{4,20},{8,24},{12,28},{16,0},{20,4},{24,8},{28,12},{1,17},{... | collective-permute-start | bytes 442376 | tf_op jit(solution)/shard_map/ppermute | solution.py:864
  170.7 16.9 %collective-permute-start.41 = (bf16[2,96,768]{2,1,0:T(8,128)(2,1)S(1)}, bf16[2,96,768]{2,1,0:T(8,128)(2,1)S(1)}, u32[]{:S(2)}, u32[]{:S(2)}) collective-permute-start(bf16[2,96,768]{2,1,0:T(8,128)(2,1)S(1)} %join.7.refs_4_.refs_0_), channel_id=1, source_target_pairs={{0,8},{4,12},{8,0},{12,4},{16,24},{20,28},{24,16},{28,20},{1,9},{5... | collective-permute-start | bytes 884744 | tf_op jit(solution)/shard_map/ppermute | solution.py:864
  174.9 13.8 %collective-permute-start.37 = (bf16[256,768]{1,0:T(8,128)(2,1)S(1)}, bf16[256,768]{1,0:T(8,128)(2,1)S(1)}, u32[]{:S(2)}, u32[]{:S(2)}) collective-permute-start(bf16[256,768]{1,0:T(8,128)(2,1)S(1)} %block_end.1.refs_6_.refs_0_), channel_id=1, source_target_pairs={{0,2},{1,3},{2,0},{3,1},{4,6},{5,7},{6,4},{7,5},{8,10},{9,11},{10,... | collective-permute-start | bytes 1179656 | tf_op jit(solution)/shard_map/ppermute | solution.py:864
  176.7 16.3 %collective-permute-start.44 = (bf16[256,768]{1,0:T(8,128)(2,1)S(1)}, bf16[256,768]{1,0:T(8,128)(2,1)S(1)}, u32[]{:S(2)}, u32[]{:S(2)}) collective-permute-start(bf16[256,768]{1,0:T(8,128)(2,1)S(1)} %get-tuple-element.238.refs_2_.refs_0_), channel_id=1, source_target_pairs={{0,2},{1,3},{2,0},{3,1},{4,6},{5,7},{6,4},{7,5},{8,10},{9,11},{10,... | collective-permute-start | bytes 1179656 | tf_op jit(solution)/shard_map/ppermute | solution.py:864
  180.1 10.5 %collective-permute-start.40 = (bf16[96,768]{1,0:T(8,128)(2,1)S(1)}, bf16[96,768]{1,0:T(8,128)(2,1)S(1)}, u32[]{:S(2)}, u32[]{:S(2)}) collective-permute-start(bf16[96,768]{1,0:T(8,128)(2,1)S(1)} %close.4.refs_2_.refs_0_), channel_id=1, source_target_pairs={{0,16},{4,20},{8,24},{12,28},{16,0},{20,4},{24,8},{28,12},{1,17},{... | collective-permute-start | bytes 442376 | tf_op jit(solution)/shard_map/ppermute | solution.py:864
  184.8 11.2 %collective-permute-start.46 = (bf16[96,768]{1,0:T(8,128)(2,1)S(1)}, bf16[96,768]{1,0:T(8,128)(2,1)}, u32[]{:S(2)}, u32[]{:S(2)}) collective-permute-start(bf16[96,768]{1,0:T(8,128)(2,1)S(1)} %get-tuple-element.229.refs_2_), channel_id=1, source_target_pairs={{0,16},{4,20},{8,24},{12,28},{16,0},{20,4},{24,8},{28,12},{1,17},{... | collective-permute-start | bytes 442376 | tf_op jit(solution)/shard_map/ppermute | solution.py:864
  187.5 6.4 %collective-permute-start.47 = (f32[6,768]{1,0:T(8,128)S(1)}, f32[6,768]{1,0:T(8,128)S(1)}, u32[]{:S(2)}, u32[]{:S(2)}) collective-permute-start(f32[6,768]{1,0:T(8,128)S(1)} %vec_add.2.refs_2_.refs_0_), channel_id=1, source_target_pairs={{0,2},{1,3},{2,0},{3,1},{4,6},{5,7},{6,4},{7,5},{8,10},{9,11},{10,... | collective-permute-start | bytes 55304 | tf_op jit(solution)/shard_map/ppermute | solution.py:864
  188.7 16.4 %collective-permute-start.52 = (bf16[4,96,768]{2,1,0:T(8,128)(2,1)S(1)}, bf16[4,96,768]{2,1,0:T(8,128)(2,1)S(1)}, u32[]{:S(2)}, u32[]{:S(2)}) collective-permute-start(bf16[4,96,768]{2,1,0:T(8,128)(2,1)S(1)} %join.8.refs_2_.refs_5_), channel_id=1, source_target_pairs={{0,4},{4,0},{8,12},{12,8},{16,20},{20,16},{24,28},{28,24},{1,5},{5... | collective-permute-start | bytes 1769480 | tf_op jit(solution)/shard_map/ppermute | solution.py:864
  193.5 9.4 %collective-permute-start.45 = (bf16[2,96,768]{2,1,0:T(8,128)(2,1)S(1)}, bf16[2,96,768]{2,1,0:T(8,128)(2,1)}, u32[]{:S(2)}, u32[]{:S(2)}) collective-permute-start(bf16[2,96,768]{2,1,0:T(8,128)(2,1)S(1)} %join.9.refs_2_.refs_3_.refs_0_), channel_id=1, source_target_pairs={{0,8},{4,12},{8,0},{12,4},{16,24},{20,28},{24,16},{28,20},{1,9},{5... | collective-permute-start | bytes 884744 | tf_op jit(solution)/shard_map/ppermute | solution.py:864
  198.5 14.0 %collective-permute-start.49 = (bf16[112,768]{1,0:T(8,128)(2,1)S(1)}, bf16[112,768]{1,0:T(8,128)(2,1)S(1)}, u32[]{:S(2)}, u32[]{:S(2)}) collective-permute-start(bf16[112,768]{1,0:T(8,128)(2,1)S(1)} %close.5.refs_2_.refs_0_), channel_id=1, source_target_pairs={{0,16},{4,20},{8,24},{12,28},{16,0},{20,4},{24,8},{28,12},{1,17},{... | collective-permute-start | bytes 516104 | tf_op jit(solution)/shard_map/ppermute | solution.py:864
  199.3 14.0 %collective-permute-start.50 = (bf16[112,768]{1,0:T(8,128)(2,1)S(1)}, bf16[112,768]{1,0:T(8,128)(2,1)S(1)}, u32[]{:S(2)}, u32[]{:S(2)}) collective-permute-start(bf16[112,768]{1,0:T(8,128)(2,1)S(1)} %close.5.refs_2_.refs_0_), channel_id=1, source_target_pairs={{0,8},{4,12},{8,0},{12,4},{16,24},{20,28},{24,16},{28,20},{1,9},{5... | collective-permute-start | bytes 516104 | tf_op jit(solution)/shard_map/ppermute | solution.py:864
  201.1 12.2 %collective-permute-start.51 = (bf16[112,768]{1,0:T(8,128)(2,1)S(1)}, bf16[112,768]{1,0:T(8,128)(2,1)S(1)}, u32[]{:S(2)}, u32[]{:S(2)}) collective-permute-start(bf16[112,768]{1,0:T(8,128)(2,1)S(1)} %close.5.refs_2_.refs_0_), channel_id=1, source_target_pairs={{0,24},{4,28},{8,16},{12,20},{16,8},{20,12},{24,0},{28,4},{1,25},{... | collective-permute-start | bytes 516104 | tf_op jit(solution)/shard_map/ppermute | solution.py:864
  204.5 16.3 %collective-permute-start.48 = (bf16[4,96,768]{2,1,0:T(8,128)(2,1)S(1)}, bf16[4,96,768]{2,1,0:T(8,128)(2,1)S(1)}, u32[]{:S(2)}, u32[]{:S(2)}) collective-permute-start(bf16[4,96,768]{2,1,0:T(8,128)(2,1)S(1)} %join.10.refs_7_.refs_5_), channel_id=1, source_target_pairs={{0,4},{4,0},{8,12},{12,8},{16,20},{20,16},{24,28},{28,24},{1,5},{5... | collective-permute-start | bytes 1769480 | tf_op jit(solution)/shard_map/ppermute | solution.py:864
  213.8 19.9 %collective-permute-start.57 = (bf16[4,112,768]{2,1,0:T(8,128)(2,1)S(1)}, bf16[4,112,768]{2,1,0:T(8,128)(2,1)S(1)}, u32[]{:S(2)}, u32[]{:S(2)}) collective-permute-start(bf16[4,112,768]{2,1,0:T(8,128)(2,1)S(1)} %join.11.refs_10_), channel_id=1, source_target_pairs={{0,4},{4,0},{8,12},{12,8},{16,20},{20,16},{24,28},{28,24},{1,5},{5... | collective-permute-start | bytes 2064392 | tf_op jit(solution)/shard_map/ppermute | solution.py:864
  (43 other events, 298.5 us)

commit v6 on v5

--- a/solution.py
+++ b/solution.py
@@ -669,7 +669,7 @@
     return run(kernel, (1,), ins, fulls(ins), out, fulls(out), idx, "close", tick, (), after)[0]
 
 
-def join(parts, idx, after=(), tick=2 * TICK):
+def join(parts, idx, after=(), tick=2 * TICK, hbm=()):
     shapes = [x.shape if len(x.shape) == 3 else (1, *x.shape) for x in parts]
 
     def kernel(idx, *refs):
@@ -679,7 +679,7 @@
             at += shape[0]
 
     out = [sds((sum(x[0] for x in shapes), *shapes[0][1:]), BF)]
-    return run(kernel, (1,), parts, fulls(parts), out, fulls(out), idx, "join", tick, (), after)[0]
+    return run(kernel, (1,), parts, fulls(parts), out, fulls(out), idx, "join", tick, (), after, hbm)[0]
 
 
 def block_end(h, keep, got, last, idx, after=()):
@@ -974,46 +974,46 @@
     down_z2, up_z1 = dp(down_low, 4), dp(up_low, 2)
     qkv_x = dp(qkv_send, 1)
     da_got = mp(da_send, 1)
-    bo_sum = far_sum(bo_last, bo_got, idx, [qkv_send], 0)
-    bo_far = mp(bo_sum, 2)
-    da_sum = far_sum(da_last, da_got, idx, [bo_sum])
+    down_done = fine_sum(close(down_t, [down_z2], idx, [qkv_send], tick=20))
+    down_r4 = dp(down_done, 4)
+    up_t, up_low = fold(up_t, up_z1, idx, [down_done], 20)
+    up_z2 = dp(up_low, 4)
+    da_sum = far_sum(da_last, da_got, idx, [up_low])
     da_far = mp(da_sum, 2)
-    down_done = fine_sum(close(down_t, [down_z2], idx, [da_sum]))
-    down_r4 = dp(down_done, 4)
-    qkv_t, qkv_low = fold(qkv_keep, qkv_x, idx, [down_done], 0)
+    bo_sum = far_sum(bo_last, bo_got, idx, [da_sum], 0)
+    down_two = join([down_done, down_r4], idx, [bo_sum])
+    down_r2 = dp(down_two, 2)
+    qkv_t, qkv_low = fold(qkv_keep, qkv_x, idx, [down_two], 0)
     qkv_z1 = dp(qkv_low, 2)
-    up_t, up_low = fold(up_t, up_z1, idx, [qkv_low])
-    up_z2 = dp(up_low, 4)
-    down_two = join([down_done, down_r4], idx, [up_low])
-    down_r2 = dp(down_two, 2)
-    out_own = block_end(hidden, bo_keep, bo_got, bo_far, idx, [down_two])
-    out_far = mp(out_own, 2)
-    gt, outer_early = shard_end(da_keep, da_got, da_far, tokens, outer_norms, dh, idx, [out_own])
-    gt_far = mp(gt, 2)
+    gt, outer_early = shard_end(da_keep, da_got, da_far, tokens, outer_norms, dh, idx, [qkv_low])
     lanes = outer_late.shape[1]
     vec = jnp.concatenate([outer_early, outer_late, attn_grads.reshape(-1, lanes)])
     vec_got = mp(vec, 1)
     up_done = fine_sum(close(up_t, [up_z2], idx, [gt]))
     up_r4 = dp(up_done, 4)
-    qkv_t, qkv_low = fold(qkv_t, qkv_z1, idx, [up_done])
-    qkv_z2 = dp(qkv_low, 4)
-    vec = vec_add(vec, vec_got, idx, [qkv_low])
+    vec = vec_add(vec, vec_got, idx, [up_done])
     vec_got = mp(vec, 2)
+    gt_far = mp(after(gt, vec), 2)
     down_four = join([down_two, down_r2], idx, [vec])
     down_other = dp(down_four, 1)
-    up_two = join([up_done, up_r4], idx, [down_four, gt_far, out_far])
+    vec = vec_add(vec, vec_got, idx, [down_four])
+    bo_far = mp(after(bo_sum, vec), 2)
+    qkv_t, qkv_low = fold(qkv_t, qkv_z1, idx, [vec])
+    qkv_z2 = dp(qkv_low, 4)
+    up_two = join([up_done, up_r4], idx, [qkv_low], hbm=(0, 1))
     up_r2 = dp(up_two, 2)
-    vec = vec_add(vec, vec_got, idx, [up_two])
     attn_own = lax.dynamic_slice_in_dim(vec[4:].reshape(n_mp, -1), mp_at, 1, 0)
     attn_own = jnp.pad(attn_own, ((0, 0), (0, lanes - attn_own.shape[1])))
     vec = jnp.concatenate([vec[:4], attn_own, ffn_grads, jnp.zeros((1, lanes), F32)])
     vec = fine_sum(vec)
-    qkv_own = close(qkv_t, [qkv_z2], idx, [up_two], None if fine > 1 else vec)
+    qkv_own = close(qkv_t, [qkv_z2], idx, [up_two, down_other, gt_far], None if fine > 1 else vec)
     if fine > 1:
         high = vec.astype(BF)
         qkv_own = jnp.concatenate([fine_sum(qkv_own), high, (vec - high.astype(F32)).astype(BF)])
     qkv_z = [dp(qkv_own, k) for k in ORDER[1:]]
     up_four = join([up_two, up_r2], idx, [qkv_own])
+    out_own = block_end(hidden, bo_keep, bo_got, bo_far, idx, [up_four])
+    out_far = mp(out_own, 2)
     up_other = dp(up_four, 1)
     down_mats = [x[0] for x in (w_down, left_down, right_down, left_root_down, right_root_down)]
     *down_res, token = update_one(down_mats, down_four, down_other, total, idx, "update_down", [up_four])

time: 239 us -> 236 us (0.987)
  waiting for transfers between devices: 53.4 us -> 42.7 us
  Pallas kernels: 117 us -> 121 us
    ppermute x58, waiting for transfers between devices: 53.4 us -> 42.7 us  [swap(): return lax.ppermute(x, axis, [(i, i ^ k) for i in range(size)])]
    pallas_call x42, Pallas kernels: 117 us -> 121 us  [run(): pl.pallas_call(kernel, grid_spec=pltpu.PrefetchScalarGridSpec(num_scalar_...]
  transfers between devices with their start and end apart: 58 -> 58, of which waited for: 21 -> 18; matrix products, arithmetic and copies ran while one was open for 1% -> 2% of each run, Pallas kernels for 41% -> 43%
where the time goes in v6:
time: 236 us; the launch traced here: 234 us
  Pallas kernels  121 us (51%)
  starting transfers between devices  56.5 us (24%)
  waiting for transfers between devices  42.7 us (18%)
  blocking collectives  5.59 us (2%)
  local copies, waits for them, and re-layouts  4.46 us (2%)
    pallas_call x42, Pallas kernels, run(): pl.pallas_call(kernel, grid_spec=pltpu.PrefetchScalarGridSpec(num_scalar_...  121 us
    ppermute x58, starting transfers between devices, swap(): return lax.ppermute(x, axis, [(i, i ^ k) for i in range(size)])  56.5 us
    ppermute x58, waiting for transfers between devices, swap(): return lax.ppermute(x, axis, [(i, i ^ k) for i in range(size)])  42.7 us
    all_gather x1, blocking collectives, body(): stats = lax.all_gather(stats, 'mp')  5.59 us
  transfers between devices with their start and end apart: 58, of which 18 were waited for; matrix products, arithmetic and copies ran while one was open for 2% of the time, Pallas kernels for 43%

profile of v6, /device:TPU:0, one launch (start us, length us, event | category | flops | bytes accessed | tf_op | source)
XLA Modules:
  0.0 233.5 jit_solution(1048855453920771172)
XLA Ops:
  0.8 2.4 %pack_weights.1.refs_2_ = bf16[96,768]{1,0:T(8,128)(2,1)} custom-call(s32[3]{0:T(128)S(1)} %pad_add_fusion.idx, f32[96,576]{1,0:T(8,128)} %bitcast.75, f32[24,768]{1,0:T(8,128)} %bitcast.82), custom_call_target="tpu_custom_call" | custom-call | flops 400000000 | bytes 1024 | tf_op jit(solution)/shard_map/pack_weights/pallas_call | solution.py:44
  3.1 2.9 %collective-permute-start = (bf16[96,768]{1,0:T(8,128)(2,1)}, bf16[96,768]{1,0:T(8,128)(2,1)}, u32[]{:S(2)}, u32[]{:S(2)}) collective-permute-start(bf16[96,768]{1,0:T(8,128)(2,1)} %pack_weights.1.refs_2_), channel_id=1, source_target_pairs={{0,4},{4,0},{8,12},{12,8},{16,20},{20,16},{24,28},{28,24},{1,5},{5... | collective-permute-start | bytes 442376 | tf_op jit(solution)/shard_map/ppermute | solution.py:864
  7.6 2.6 %collective-permute-start.4 = (bf16[96,768]{1,0:T(8,128)(2,1)}, bf16[96,768]{1,0:T(8,128)(2,1)}, u32[]{:S(2)}, u32[]{:S(2)}) collective-permute-start(bf16[96,768]{1,0:T(8,128)(2,1)} %pack_weights.1.refs_2_), channel_id=1, source_target_pairs={{0,16},{4,20},{8,24},{12,28},{16,0},{20,4},{24,8},{28,12},{1,17},{... | collective-permute-start | bytes 442376 | tf_op jit(solution)/shard_map/ppermute | solution.py:864
  10.4 1.6 cast_pair.1
  13.4 3.9 %collective-permute-done.2 = bf16[96,768]{1,0:T(8,128)(2,1)S(1)} collective-permute-done((bf16[96,768]{1,0:T(8,128)(2,1)S(1)}, bf16[96,768]{1,0:T(8,128)(2,1)S(1)}, u32[]{:S(2)}, u32[]{:S(2)}) %collective-permute-start.2) | collective-permute-done | bytes 147488 | tf_op jit(solution)/shard_map/ppermute | solution.py:864
  17.7 4.1 %collective-permute-done.4.refs_6_ = bf16[96,768]{1,0:T(8,128)(2,1)} collective-permute-done((bf16[96,768]{1,0:T(8,128)(2,1)}, bf16[96,768]{1,0:T(8,128)(2,1)}, u32[]{:S(2)}, u32[]{:S(2)}) %collective-permute-start.4) | collective-permute-done | bytes 147488 | tf_op jit(solution)/shard_map/ppermute | solution.py:864
  25.0 1.7 collective-permute-start.8
  27.9 1.6 collective-permute-start.10
  30.3 5.2 %project.1 = (bf16[1024,192]{1,0:T(8,128)(2,1)}, bf16[1024,192]{1,0:T(8,128)(2,1)}, bf16[1024,192]{1,0:T(8,128)(2,1)}, bf16[768,576]{1,0:T(8,128)(2,1)}, bf16[208,768]{1,0:T(8,128)(2,1)}) custom-call(s32[3]{0:T(128)S(1)} %pad_add_fusion.idx, bf16[1024,768]{1,0:T(8,128)(2,1)S(1)} %fusion.5.refs_0_, f32[2,192]{1,0:T(2,128)S(1)} %copy-done.30, ...), custom_call_target="tpu_custom_call" | custom-call | flops 16000000000 | bytes 1024 | tf_op jit(solution)/shard_map/project/pallas_call | solution.py:44
  37.0 9.8 %attend.1 = (bf16[1024,192]{1,0:T(8,128)(2,1)}, bf16[3,256,256]{2,1,0:T(8,128)(2,1)}, bf16[3,256,512]{2,1,0:T(8,128)(2,1)}, bf16[3,256,768]{2,1,0:T(8,128)(2,1)}, bf16[3,256,1024]{2,1,0:T(8,128)(2,1)}) custom-call(s32[3]{0:T(128)S(1)} %pad_add_fusion.idx, s32[1024,1]{1,0:T(8,128)S(1)} %copy.55.refs_0_, bf16[1024,192]{1,0:T(8,128)(2,1)} %get-tuple-element.159.refs_1_.refs_0_, ...), custom_call_target="tpu_custom_call" | custom-call | flops 4000000000 | bytes 1024 | tf_op jit(solution)/shard_map/attend/pallas_call | solution.py:44
  46.8 4.7 %collective-permute-done.14.refs_1_ = bf16[2,96,768]{2,1,0:T(8,128)(2,1)S(1)} collective-permute-done((bf16[2,96,768]{2,1,0:T(8,128)(2,1)S(1)}, bf16[2,96,768]{2,1,0:T(8,128)(2,1)S(1)}, u32[]{:S(2)}, u32[]{:S(2)}) %collective-permute-start.14) | collective-permute-done | bytes 294944 | tf_op jit(solution)/shard_map/ppermute | solution.py:864
  56.0 10.4 %collective-permute-done.11.refs_4_.refs_8_ = bf16[1024,192]{1,0:T(8,128)(2,1)S(1)} collective-permute-done((bf16[1024,192]{1,0:T(8,128)(2,1)}, bf16[1024,192]{1,0:T(8,128)(2,1)S(1)}, u32[]{:S(2)}, u32[]{:S(2)}) %collective-permute-start.11) | collective-permute-done | bytes 393248 | tf_op jit(solution)/shard_map/ppermute | solution.py:864
  66.9 1.9 collective-permute-done.18.refs_10_.refs_4_
  69.1 6.8 %outproj.1 = (f32[1024,768]{1,0:T(8,128)}, bf16[1024,768]{1,0:T(8,128)(2,1)S(1)}) custom-call(s32[3]{0:T(128)S(1)} %pad_add_fusion.idx, f32[4,768]{1,0:T(4,128)S(1)} %copy-done.15, bf16[1024,768]{1,0:T(8,128)(2,1)} %refs_3_.1, bf16[1024,192]{1,0:T(8,128)(2,1)S(1)} %copy-done.2, bf16[1024,192]{1,0:T(8,128)(2,1)S(1)} %collective-permute-done.12.refs_3_.refs_7_, ...), custom_call_target="tpu_custom_call" | custom-call | bytes 1024 | tf_op jit(solution)/shard_map/outproj/pallas_call | solution.py:44
  75.9 7.2 %ffn_up.1 = (f32[1024,768]{1,0:T(8,128)S(1)}, f32[1024,768]{1,0:T(8,128)S(1)}, f32[1024,768]{1,0:T(8,128)S(1)}, f32[8,1024]{1,0:T(8,128)S(1)}, bf16[768,768]{1,0:T(8,128)(2,1)S(1)}, /*index=5*/bf16[768,768]{1,0:T(8,128)(2,1)}) custom-call(s32[3]{0:T(128)S(1)} %pad_add_fusion.idx, bf16[1024,768]{1,0:T(8,128)(2,1)S(1)} %get-tuple-element.178.refs_0_, ...), custom_call_target="tpu_custom_call" | custom-call | flops 3000000000 | bytes 1024 | tf_op jit(solution)/shard_map/ffn_up/pallas_call | solution.py:44
  83.1 5.6 %all-gather = f32[32,1024]{1,0:T(8,128)S(1)} all-gather(f32[8,1024]{1,0:T(8,128)S(1)} %get-tuple-element.182), channel_id=2, replica_groups=mesh['dp'=8,'mp'=4] {'mp'}, dimensions={0}, use_global_device_ids=true | all-gather | bytes 163840 | tf_op jit(solution)/shard_map/all_gather | solution.py:947
  88.7 6.3 %ffn_mid.1 = (bf16[1024,768]{1,0:T(8,128)(2,1)}, bf16[1024,768]{1,0:T(8,128)(2,1)}, bf16[2,256,768]{2,1,0:T(8,128)(2,1)S(1)}, f32[256,768]{1,0:T(8,128)}, f32[256,768]{1,0:T(8,128)S(1)}, /*index=5*/f32[2,768]{1,0:T(2,128)S(1)}) custom-call(s32[3]{0:T(128)S(1)} %pad_add_fusion.idx, f32[1024,768]{1,0:T(8,128)S(1)} %get-tuple-element.179.refs_0_, ...), custom_call_target="tpu_custom_call" | custom-call | flops 2600000000 | bytes 1024 | tf_op jit(solution)/shard_map/ffn_mid/pallas_call | solution.py:44
  95.3 1.9 collective-permute-done.20.refs_1_
  97.9 1.6 collective-permute-start.21
  99.5 3.5 %grad_down.1 = (bf16[4,96,768]{2,1,0:T(8,128)(2,1)S(1)}, bf16[4,96,768]{2,1,0:T(8,128)(2,1)}) custom-call(s32[3]{0:T(128)S(1)} %pad_add_fusion.idx, bf16[1024,768]{1,0:T(8,128)(2,1)S(1)} %copy-done.7, bf16[1024,768]{1,0:T(8,128)(2,1)S(1)} %copy-done.8, bf16[256,768]{1,0:T(8,128)(2,1)S(1)} %far_sum.4.refs_2_), custom_call_target="tpu_custom_call" | custom-call | flops 1400000000 | bytes 1024 | tf_op jit(solution)/shard_map/grad_down/pallas_call | solution.py:44
  104.5 3.5 %grad_up.1 = (bf16[4,96,768]{2,1,0:T(8,128)(2,1)S(1)}, bf16[4,96,768]{2,1,0:T(8,128)(2,1)}) custom-call(s32[3]{0:T(128)S(1)} %pad_add_fusion.idx, bf16[1024,768]{1,0:T(8,128)(2,1)S(1)} %get-tuple-element.178.refs_0_, bf16[1024,768]{1,0:T(8,128)(2,1)S(1)} %copy-done.26, bf16[4,96,768]{2,1,0:T(8,128)(2,1)S(1)} %get-tuple-element.190.refs_2_), custom_call_target="tpu_custom_call" | custom-call | flops 1400000000 | bytes 1024 | tf_op jit(solution)/shard_map/grad_up/pallas_call | solution.py:44
  109.4 5.1 %shard_back.1 = (f32[256,768]{1,0:T(8,128)}, f32[2,768]{1,0:T(2,128)S(1)}, f32[4,2,192]{2,1,0:T(2,128)S(1)}, bf16[256,192]{1,0:T(8,128)(2,1)S(1)}, bf16[256,192]...) custom-call(s32[3]{0:T(128)S(1)} %pad_add_fusion.idx, ...), custom_call_target="tpu_custom_call" | custom-call | bytes 1024 | tf_op jit(solution)/shard_map/shard_back/pallas_call | solution.py:44
  118.8 5.5 %ffn_out.1 = (bf16[2,256,768]{2,1,0:T(8,128)(2,1)S(1)}, f32[256,768]{1,0:T(8,128)}, f32[256,768]{1,0:T(8,128)S(1)}) custom-call(s32[3]{0:T(128)S(1)} %pad_add_fusion.idx, bf16[1024,768]{1,0:T(8,128)(2,1)} %get-tuple-element.184.refs_0_, bf16[768,768]{1,0:T(8,128)(2,1)} %get-tuple-element.185.refs_1_, bf16[256,192]{1,0:T(8,128)(2,1)S(1)} %collective-permute-done.22.refs_2_.refs_8_), custom_call_target="tpu_custom_call" | custom-call | bytes 1024 | tf_op jit(solution)/shard_map/ffn_out/pallas_call | solution.py:44
  124.3 1.8 fold.6
  126.8 1.6 collective-permute-start.28
  128.4 11.2 %attend_back.1.refs_2_.refs_1_ = bf16[1024,576]{1,0:T(8,128)(2,1)S(1)} custom-call(s32[3]{0:T(128)S(1)} %pad_add_fusion.idx, bf16[1024,192]{1,0:T(8,128)(2,1)} %get-tuple-element.159.refs_1_.refs_0_, bf16[1024,192]{1,0:T(8,128)(2,1)} %get-tuple-element.160.refs_2_.refs_1_, bf16[1024,192]{1,0:T(8,128)(2,1)} %get-tuple-element.161.refs_3_.refs_2_, ...), custom_call_target="tpu_custom_call" | custom-call | flops 4400000000 | bytes 1024 | tf_op jit(solution)/shard_map/attend_back/pallas_call | solution.py:44
  140.3 2.5 %collective-permute-start.33 = (bf16[96,768]{1,0:T(8,128)(2,1)S(1)}, bf16[96,768]{1,0:T(8,128)(2,1)S(1)}, u32[]{:S(2)}, u32[]{:S(2)}) collective-permute-start(bf16[96,768]{1,0:T(8,128)(2,1)S(1)} %get-tuple-element.213.refs_2_), channel_id=1, source_target_pairs={{0,16},{4,20},{8,24},{12,28},{16,0},{20,4},{24,8},{28,12},{1,17},{... | collective-permute-start | bytes 442376 | tf_op jit(solution)/shard_map/ppermute | solution.py:864
  142.8 1.7 fold.8
  144.6 6.5 %qkv_back.1 = (bf16[4,96,768]{2,1,0:T(8,128)(2,1)}, bf16[4,96,768]{2,1,0:T(8,128)(2,1)}, bf16[2,256,768]{2,1,0:T(8,128)(2,1)S(1)}, f32[256,768]{1,0:T(8,128)}, f32[256,768]{1,0:T(8,128)S(1)}) custom-call(s32[3]{0:T(128)S(1)} %pad_add_fusion.idx, bf16[1024,768]{1,0:T(8,128)(2,1)} %copy-done.6, bf16[1024,576]{1,0:T(8,128)(2,1)S(1)} %attend_back.1.refs_2_.refs_1_, ...), custom_call_target="tpu_custom_call" | custom-call | flops 16000000000 | bytes 1024 | tf_op jit(solution)/shard_map/qkv_back/pallas_call | solution.py:44
  153.1 2.2 collective-permute-start.36
  161.1 5.6 %collective-permute-done.36.refs_1_ = bf16[96,768]{1,0:T(8,128)(2,1)} collective-permute-done((bf16[96,768]{1,0:T(8,128)(2,1)}, bf16[96,768]{1,0:T(8,128)(2,1)}, u32[]{:S(2)}, u32[]{:S(2)}) %collective-permute-start.36) | collective-permute-done | bytes 147488 | tf_op jit(solution)/shard_map/ppermute | solution.py:864
  168.4 1.9 fold.10
  170.3 2.1 collective-permute-start.43
  172.4 2.3 shard_end.1
  176.6 1.7 collective-permute-done.40.refs_1_
  181.3 1.7 collective-permute-start.41
  187.7 2.5 %collective-permute-start.44 = (bf16[2,96,768]{2,1,0:T(8,128)(2,1)S(1)}, bf16[2,96,768]{2,1,0:T(8,128)(2,1)S(1)}, u32[]{:S(2)}, u32[]{:S(2)}) collective-permute-start(bf16[2,96,768]{2,1,0:T(8,128)(2,1)S(1)} %join.9.refs_3_.refs_0_), channel_id=1, source_target_pairs={{0,8},{4,12},{8,0},{12,4},{16,24},{20,28},{24,16},{28,20},{1,9},{5... | collective-permute-start | bytes 884744 | tf_op jit(solution)/shard_map/ppermute | solution.py:864
  190.3 3.1 %collective-permute-done.45.refs_1_ = bf16[96,768]{1,0:T(8,128)(2,1)} collective-permute-done((bf16[96,768]{1,0:T(8,128)(2,1)}, bf16[96,768]{1,0:T(8,128)(2,1)}, u32[]{:S(2)}, u32[]{:S(2)}) %collective-permute-start.45) | collective-permute-done | bytes 147488 | tf_op jit(solution)/shard_map/ppermute | solution.py:864
  195.0 1.7 collective-permute-start.50
  197.5 1.9 collective-permute-start.52
  201.9 1.9 block_end.1.refs_0_
  203.8 3.3 %collective-permute-start.48 = (bf16[256,768]{1,0:T(8,128)(2,1)S(1)}, bf16[256,768]{1,0:T(8,128)(2,1)S(1)}, u32[]{:S(2)}, u32[]{:S(2)}) collective-permute-start(bf16[256,768]{1,0:T(8,128)(2,1)S(1)} %block_end.1.refs_0_), channel_id=1, source_target_pairs={{0,2},{1,3},{2,0},{3,1},{4,6},{5,7},{6,4},{7,5},{8,10},{9,11},{10,... | collective-permute-start | bytes 1179656 | tf_op jit(solution)/shard_map/ppermute | solution.py:864
  207.1 5.1 %update_down.1 = (f32[768,768]{1,0:T(8,128)}, f32[96,768]{1,0:T(8,128)}, f32[96,768]{1,0:T(8,128)}, f32[96,768]{1,0:T(8,128)}, bf16[96,768]{1,0:T(8,128)(2,1)}, /*index=5*/f32[8,128]{1,0:T(8,128)S(1)}) custom-call(s32[3]{0:T(128)S(1)} %pad_add_fusion.idx, f32[96,768]{1,0:T(8,128)} %bitcast.63, f32[96,768]{1,0:T(8,128)} %bitcast.64, f32[96,768]{1,0:T(8,128)} %bitcast.65, ...), custom_call_target="tpu_custom_call" | custom-call | bytes 1024 | tf_op jit(solution)/shard_map/update_down/pallas_call | solution.py:44
  213.4 3.5 %warm.1 = (f32[96,576]{1,0:T(8,128)S(1)}, f32[96,768]{1,0:T(8,128)S(1)}, f32[72,576]{1,0:T(8,128)S(1)}, f32[96,768]{1,0:T(8,128)S(1)}, f32[576,576]{1,0:T(8,128)...) custom-call(s32[3]{0:T(128)S(1)} %pad_add_fusion.idx, ...), custom_call_target="tpu_custom_call" | custom-call | bytes 1024 | tf_op jit(solution)/shard_map/warm/pallas_call | solution.py:44
  216.9 5.1 %update_up.1 = (f32[768,768]{1,0:T(8,128)}, f32[96,768]{1,0:T(8,128)}, f32[96,768]{1,0:T(8,128)}, f32[96,768]{1,0:T(8,128)}, bf16[96,768]{1,0:T(8,128)(2,1)}, /*index=5*/f32[8,128]{1,0:T(8,128)S(1)}) custom-call(s32[3]{0:T(128)S(1)} %pad_add_fusion.idx, f32[96,768]{1,0:T(8,128)} %bitcast.68, f32[96,768]{1,0:T(8,128)} %bitcast.69, f32[96,768]{1,0:T(8,128)} %bitcast.70, ...), custom_call_target="tpu_custom_call" | custom-call | bytes 1024 | tf_op jit(solution)/shard_map/update_up/pallas_call | solution.py:44
  224.3 1.8 spread_tokens.1
  226.1 1.8 spread_out.1
  228.8 4.5 %update_qkv.1 = (f32[576,768]{1,0:T(8,128)}, f32[96,768]{1,0:T(8,128)}, f32[72,576]{1,0:T(8,128)}, f32[96,576]{1,0:T(8,128)}, bf16[96,576]{1,0:T(8,128)(2,1)}, /...) custom-call(s32[3]{0:T(128)S(1)} %pad_add_fusion.idx, ...), custom_call_target="tpu_custom_call" | custom-call | flops 2400000000 | bytes 1024 | tf_op jit(solution)/shard_map/update_qkv/pallas_call | solution.py:44
  (210 shorter events, 53.0 us)
Async XLA Ops:
  3.1 23.6 %collective-permute-start = (bf16[96,768]{1,0:T(8,128)(2,1)}, bf16[96,768]{1,0:T(8,128)(2,1)}, u32[]{:S(2)}, u32[]{:S(2)}) collective-permute-start(bf16[96,768]{1,0:T(8,128)(2,1)} %pack_weights.1.refs_2_), channel_id=1, source_target_pairs={{0,4},{4,0},{8,12},{12,8},{16,20},{20,16},{24,28},{28,24},{1,5},{5... | collective-permute-start | bytes 442376 | tf_op jit(solution)/shard_map/ppermute | solution.py:864
  6.1 11.3 %collective-permute-start.1 = (bf16[96,768]{1,0:T(8,128)(2,1)}, bf16[96,768]{1,0:T(8,128)(2,1)}, u32[]{:S(2)}, u32[]{:S(2)}) collective-permute-start(bf16[96,768]{1,0:T(8,128)(2,1)} %pack_weights.1.refs_2_), channel_id=1, source_target_pairs={{0,8},{4,12},{8,0},{12,4},{16,24},{20,28},{24,16},{28,20},{1,9},{5... | collective-permute-start | bytes 442376 | tf_op jit(solution)/shard_map/ppermute | solution.py:864
  7.6 14.2 %collective-permute-start.4 = (bf16[96,768]{1,0:T(8,128)(2,1)}, bf16[96,768]{1,0:T(8,128)(2,1)}, u32[]{:S(2)}, u32[]{:S(2)}) collective-permute-start(bf16[96,768]{1,0:T(8,128)(2,1)} %pack_weights.1.refs_2_), channel_id=1, source_target_pairs={{0,16},{4,20},{8,24},{12,28},{16,0},{20,4},{24,8},{28,12},{1,17},{... | collective-permute-start | bytes 442376 | tf_op jit(solution)/shard_map/ppermute | solution.py:864
  10.2 12.2 %collective-permute-start.6 = (bf16[96,768]{1,0:T(8,128)(2,1)}, bf16[96,768]{1,0:T(8,128)(2,1)}, u32[]{:S(2)}, u32[]{:S(2)}) collective-permute-start(bf16[96,768]{1,0:T(8,128)(2,1)} %pack_weights.1.refs_2_), channel_id=1, source_target_pairs={{0,24},{4,28},{8,16},{12,20},{16,8},{20,12},{24,0},{28,4},{1,25},{... | collective-permute-start | bytes 442376 | tf_op jit(solution)/shard_map/ppermute | solution.py:864
  12.1 5.2 %collective-permute-start.2 = (bf16[96,768]{1,0:T(8,128)(2,1)S(1)}, bf16[96,768]{1,0:T(8,128)(2,1)S(1)}, u32[]{:S(2)}, u32[]{:S(2)}) collective-permute-start(bf16[96,768]{1,0:T(8,128)(2,1)S(1)} %get-tuple-element.155), channel_id=1, source_target_pairs={{0,4},{4,0},{8,12},{12,8},{16,20},{20,16},{24,28},{28,24},{1,5},{5... | collective-permute-start | bytes 442376 | tf_op jit(solution)/shard_map/ppermute | solution.py:864
  17.3 10.6 %collective-permute-start.3 = (bf16[96,768]{1,0:T(8,128)(2,1)}, bf16[96,768]{1,0:T(8,128)(2,1)}, u32[]{:S(2)}, u32[]{:S(2)}) collective-permute-start(bf16[96,768]{1,0:T(8,128)(2,1)} %collective-permute-done.1.refs_4_), channel_id=1, source_target_pairs={{0,4},{4,0},{8,12},{12,8},{16,20},{20,16},{24,28},{28,24},{1,5},{5... | collective-permute-start | bytes 442376 | tf_op jit(solution)/shard_map/ppermute | solution.py:864
  21.8 7.7 %collective-permute-start.5 = (bf16[96,768]{1,0:T(8,128)(2,1)}, bf16[96,768]{1,0:T(8,128)(2,1)}, u32[]{:S(2)}, u32[]{:S(2)}) collective-permute-start(bf16[96,768]{1,0:T(8,128)(2,1)} %collective-permute-done.4.refs_6_), channel_id=1, source_target_pairs={{0,4},{4,0},{8,12},{12,8},{16,20},{20,16},{24,28},{28,24},{1,5},{5... | collective-permute-start | bytes 442376 | tf_op jit(solution)/shard_map/ppermute | solution.py:864
  22.4 7.9 %collective-permute-start.7 = (bf16[96,768]{1,0:T(8,128)(2,1)}, bf16[96,768]{1,0:T(8,128)(2,1)}, u32[]{:S(2)}, u32[]{:S(2)}) collective-permute-start(bf16[96,768]{1,0:T(8,128)(2,1)} %collective-permute-done.6.refs_8_), channel_id=1, source_target_pairs={{0,4},{4,0},{8,12},{12,8},{16,20},{20,16},{24,28},{28,24},{1,5},{5... | collective-permute-start | bytes 442376 | tf_op jit(solution)/shard_map/ppermute | solution.py:864
  25.0 21.8 %collective-permute-start.8 = (bf16[96,768]{1,0:T(8,128)(2,1)}, bf16[96,768]{1,0:T(8,128)(2,1)S(1)}, u32[]{:S(2)}, u32[]{:S(2)}) collective-permute-start(bf16[96,768]{1,0:T(8,128)(2,1)} %copy-done.16), channel_id=1, source_target_pairs={{0,16},{4,20},{8,24},{12,28},{16,0},{20,4},{24,8},{28,12},{1,17},{... | collective-permute-start | bytes 442376 | tf_op jit(solution)/shard_map/ppermute | solution.py:864
  26.8 20.1 %collective-permute-start.9 = (bf16[96,768]{1,0:T(8,128)(2,1)}, bf16[96,768]{1,0:T(8,128)(2,1)S(1)}, u32[]{:S(2)}, u32[]{:S(2)}) collective-permute-start(bf16[96,768]{1,0:T(8,128)(2,1)} %copy-done.16), channel_id=1, source_target_pairs={{0,8},{4,12},{8,0},{12,4},{16,24},{20,28},{24,16},{28,20},{1,9},{5... | collective-permute-start | bytes 442376 | tf_op jit(solution)/shard_map/ppermute | solution.py:864
  27.9 18.9 %collective-permute-start.10 = (bf16[96,768]{1,0:T(8,128)(2,1)}, bf16[96,768]{1,0:T(8,128)(2,1)S(1)}, u32[]{:S(2)}, u32[]{:S(2)}) collective-permute-start(bf16[96,768]{1,0:T(8,128)(2,1)} %copy-done.16), channel_id=1, source_target_pairs={{0,24},{4,28},{8,16},{12,20},{16,8},{20,12},{24,0},{28,4},{1,25},{... | collective-permute-start | bytes 442376 | tf_op jit(solution)/shard_map/ppermute | solution.py:864
  29.5 22.0 %collective-permute-start.14 = (bf16[2,96,768]{2,1,0:T(8,128)(2,1)S(1)}, bf16[2,96,768]{2,1,0:T(8,128)(2,1)S(1)}, u32[]{:S(2)}, u32[]{:S(2)}) collective-permute-start(bf16[2,96,768]{2,1,0:T(8,128)(2,1)S(1)} %pad_maximum_fusion.1.refs_0_), channel_id=1, source_target_pairs={{0,16},{4,20},{8,24},{12,28},{16,0},{20,4},{24,8},{28,12},{1,17},{... | collective-permute-start | bytes 884744 | tf_op jit(solution)/shard_map/ppermute | solution.py:864
  35.5 16.3 %collective-permute-start.16 = (bf16[208,768]{1,0:T(8,128)(2,1)}, bf16[208,768]{1,0:T(8,128)(2,1)S(1)}, u32[]{:S(2)}, u32[]{:S(2)}) collective-permute-start(bf16[208,768]{1,0:T(8,128)(2,1)} %get-tuple-element.175.refs_6_.refs_10_), channel_id=1, source_target_pairs={{0,2},{1,3},{2,0},{3,1},{4,6},{5,7},{6,4},{7,5},{8,10},{9,11},{10,... | collective-permute-start | bytes 958472 | tf_op jit(solution)/shard_map/ppermute | solution.py:864
  51.7 3.6 %collective-permute-start.15 = (bf16[208,768]{1,0:T(8,128)(2,1)S(1)}, bf16[208,768]{1,0:T(8,128)(2,1)S(1)}, u32[]{:S(2)}, u32[]{:S(2)}) collective-permute-start(bf16[208,768]{1,0:T(8,128)(2,1)S(1)} %copy-done.9), channel_id=1, source_target_pairs={{0,1},{1,0},{2,3},{3,2},{4,5},{5,4},{6,7},{7,6},{8,9},{9,8},{10,11... | collective-permute-start | bytes 958472 | tf_op jit(solution)/shard_map/ppermute | solution.py:864
  52.2 14.1 %collective-permute-start.11 = (bf16[1024,192]{1,0:T(8,128)(2,1)}, bf16[1024,192]{1,0:T(8,128)(2,1)S(1)}, u32[]{:S(2)}, u32[]{:S(2)}) collective-permute-start(bf16[1024,192]{1,0:T(8,128)(2,1)} %get-tuple-element.166.refs_2_.refs_6_), channel_id=1, source_target_pairs={{0,2},{1,3},{2,0},{3,1},{4,6},{5,7},{6,4},{7,5},{8,10},{9,11},{10,... | collective-permute-start | bytes 1179656 | tf_op jit(solution)/shard_map/ppermute | solution.py:864
  53.8 15.0 %collective-permute-start.18 = (bf16[4,96,768]{2,1,0:T(8,128)(2,1)S(1)}, bf16[4,96,768]{2,1,0:T(8,128)(2,1)S(1)}, u32[]{:S(2)}, u32[]{:S(2)}) collective-permute-start(bf16[4,96,768]{2,1,0:T(8,128)(2,1)S(1)} %pad_maximum_fusion.refs_2_.refs_3_), channel_id=1, source_target_pairs={{0,4},{4,0},{8,12},{12,8},{16,20},{20,16},{24,28},{28,24},{1,5},{5... | collective-permute-start | bytes 1769480 | tf_op jit(solution)/shard_map/ppermute | solution.py:864
  55.9 20.0 %collective-permute-start.19 = (bf16[4,96,768]{2,1,0:T(8,128)(2,1)S(1)}, bf16[4,96,768]{2,1,0:T(8,128)(2,1)S(1)}, u32[]{:S(2)}, u32[]{:S(2)}) collective-permute-start(bf16[4,96,768]{2,1,0:T(8,128)(2,1)S(1)} %join.6.refs_5_), channel_id=1, source_target_pairs={{0,8},{4,12},{8,0},{12,4},{16,24},{20,28},{24,16},{28,20},{1,9},{5... | collective-permute-start | bytes 1769480 | tf_op jit(solution)/shard_map/ppermute | solution.py:864
  97.9 11.4 %collective-permute-start.21 = (bf16[256,768]{1,0:T(8,128)(2,1)S(1)}, bf16[256,768]{1,0:T(8,128)(2,1)S(1)}, u32[]{:S(2)}, u32[]{:S(2)}) collective-permute-start(bf16[256,768]{1,0:T(8,128)(2,1)S(1)} %far_sum.4.refs_2_), channel_id=1, source_target_pairs={{0,2},{1,3},{2,0},{3,1},{4,6},{5,7},{6,4},{7,5},{8,10},{9,11},{10,... | collective-permute-start | bytes 1179656 | tf_op jit(solution)/shard_map/ppermute | solution.py:864
  103.0 21.3 %collective-permute-start.26 = (bf16[4,96,768]{2,1,0:T(8,128)(2,1)S(1)}, bf16[4,96,768]{2,1,0:T(8,128)(2,1)S(1)}, u32[]{:S(2)}, u32[]{:S(2)}) collective-permute-start(bf16[4,96,768]{2,1,0:T(8,128)(2,1)S(1)} %get-tuple-element.190.refs_2_), channel_id=1, source_target_pairs={{0,4},{4,0},{8,12},{12,8},{16,20},{20,16},{24,28},{28,24},{1,5},{5... | collective-permute-start | bytes 1769480 | tf_op jit(solution)/shard_map/ppermute | solution.py:864
  115.0 11.1 %collective-permute-start.25 = (bf16[2,192,768]{2,1,0:T(8,128)(2,1)S(1)}, bf16[2,192,768]{2,1,0:T(8,128)(2,1)S(1)}, u32[]{:S(2)}, u32[]{:S(2)}) collective-permute-start(bf16[2,192,768]{2,1,0:T(8,128)(2,1)S(1)} %get-tuple-element.203), channel_id=1, source_target_pairs={{0,1},{1,0},{2,3},{3,2},{4,5},{5,4},{6,7},{7,6},{8,9},{9,8},{10,11... | collective-permute-start | bytes 1769480 | tf_op jit(solution)/shard_map/ppermute | solution.py:864
  115.6 12.8 %collective-permute-start.23 = (bf16[256,192]{1,0:T(8,128)(2,1)S(1)}, bf16[256,192]{1,0:T(8,128)(2,1)S(1)}, u32[]{:S(2)}, u32[]{:S(2)}) collective-permute-start(bf16[256,192]{1,0:T(8,128)(2,1)S(1)} %get-tuple-element.200), channel_id=1, source_target_pairs={{0,2},{1,3},{2,0},{3,1},{4,6},{5,7},{6,4},{7,5},{8,10},{9,11},{10,... | collective-permute-start | bytes 294920 | tf_op jit(solution)/shard_map/ppermute | solution.py:864
  117.1 11.3 %collective-permute-start.24 = (bf16[256,192]{1,0:T(8,128)(2,1)S(1)}, bf16[256,192]{1,0:T(8,128)(2,1)S(1)}, u32[]{:S(2)}, u32[]{:S(2)}) collective-permute-start(bf16[256,192]{1,0:T(8,128)(2,1)S(1)} %get-tuple-element.201), channel_id=1, source_target_pairs={{0,3},{1,2},{2,1},{3,0},{4,7},{5,6},{6,5},{7,4},{8,11},{9,10},{10,... | collective-permute-start | bytes 294920 | tf_op jit(solution)/shard_map/ppermute | solution.py:864
  117.2 25.5 %collective-permute-start.29 = (bf16[4,96,768]{2,1,0:T(8,128)(2,1)S(1)}, bf16[4,96,768]{2,1,0:T(8,128)(2,1)S(1)}, u32[]{:S(2)}, u32[]{:S(2)}) collective-permute-start(bf16[4,96,768]{2,1,0:T(8,128)(2,1)S(1)} %get-tuple-element.211.refs_14_), channel_id=1, source_target_pairs={{0,4},{4,0},{8,12},{12,8},{16,20},{20,16},{24,28},{28,24},{1,5},{5... | collective-permute-start | bytes 1769480 | tf_op jit(solution)/shard_map/ppermute | solution.py:864
  126.1 13.6 %collective-permute-start.30 = (bf16[2,96,768]{2,1,0:T(8,128)(2,1)S(1)}, bf16[2,96,768]{2,1,0:T(8,128)(2,1)S(1)}, u32[]{:S(2)}, u32[]{:S(2)}) collective-permute-start(bf16[2,96,768]{2,1,0:T(8,128)(2,1)S(1)} %get-tuple-element.205.refs_2_), channel_id=1, source_target_pairs={{0,8},{4,12},{8,0},{12,4},{16,24},{20,28},{24,16},{28,20},{1,9},{5... | collective-permute-start | bytes 884744 | tf_op jit(solution)/shard_map/ppermute | solution.py:864
  126.8 17.8 %collective-permute-start.28 = (bf16[192,768]{1,0:T(8,128)(2,1)S(1)}, bf16[192,768]{1,0:T(8,128)(2,1)S(1)}, u32[]{:S(2)}, u32[]{:S(2)}) collective-permute-start(bf16[192,768]{1,0:T(8,128)(2,1)S(1)} %far_sum.5.refs_11_), channel_id=1, source_target_pairs={{0,2},{1,3},{2,0},{3,1},{4,6},{5,7},{6,4},{7,5},{8,10},{9,11},{10,... | collective-permute-start | bytes 884744 | tf_op jit(solution)/shard_map/ppermute | solution.py:864
  139.6 20.9 %collective-permute-start.27 = (bf16[2,256,768]{2,1,0:T(8,128)(2,1)S(1)}, bf16[2,256,768]{2,1,0:T(8,128)(2,1)S(1)}, u32[]{:S(2)}, u32[]{:S(2)}) collective-permute-start(bf16[2,256,768]{2,1,0:T(8,128)(2,1)S(1)} %get-tuple-element.206.refs_2_), channel_id=1, source_target_pairs={{0,1},{1,0},{2,3},{3,2},{4,5},{5,4},{6,7},{7,6},{8,9},{9,8},{10,11... | collective-permute-start | bytes 2359304 | tf_op jit(solution)/shard_map/ppermute | solution.py:864
  140.3 11.6 %collective-permute-start.33 = (bf16[96,768]{1,0:T(8,128)(2,1)S(1)}, bf16[96,768]{1,0:T(8,128)(2,1)S(1)}, u32[]{:S(2)}, u32[]{:S(2)}) collective-permute-start(bf16[96,768]{1,0:T(8,128)(2,1)S(1)} %get-tuple-element.213.refs_2_), channel_id=1, source_target_pairs={{0,16},{4,20},{8,24},{12,28},{16,0},{20,4},{24,8},{28,12},{1,17},{... | collective-permute-start | bytes 442376 | tf_op jit(solution)/shard_map/ppermute | solution.py:864
  144.5 10.8 %collective-permute-start.32 = (bf16[2,96,768]{2,1,0:T(8,128)(2,1)S(1)}, bf16[2,96,768]{2,1,0:T(8,128)(2,1)S(1)}, u32[]{:S(2)}, u32[]{:S(2)}) collective-permute-start(bf16[2,96,768]{2,1,0:T(8,128)(2,1)S(1)} %get-tuple-element.214.refs_6_), channel_id=1, source_target_pairs={{0,8},{4,12},{8,0},{12,4},{16,24},{20,28},{24,16},{28,20},{1,9},{5... | collective-permute-start | bytes 884744 | tf_op jit(solution)/shard_map/ppermute | solution.py:864
  151.1 5.5 %collective-permute-start.31 = (bf16[2,256,768]{2,1,0:T(8,128)(2,1)S(1)}, bf16[2,256,768]{2,1,0:T(8,128)(2,1)S(1)}, u32[]{:S(2)}, u32[]{:S(2)}) collective-permute-start(bf16[2,256,768]{2,1,0:T(8,128)(2,1)S(1)} %get-tuple-element.216), channel_id=1, source_target_pairs={{0,1},{1,0},{2,3},{3,2},{4,5},{5,4},{6,7},{7,6},{8,9},{9,8},{10,11... | collective-permute-start | bytes 2359304 | tf_op jit(solution)/shard_map/ppermute | solution.py:864
  151.3 17.1 %collective-permute-start.35 = (bf16[4,96,768]{2,1,0:T(8,128)(2,1)}, bf16[4,96,768]{2,1,0:T(8,128)(2,1)}, u32[]{:S(2)}, u32[]{:S(2)}) collective-permute-start(bf16[4,96,768]{2,1,0:T(8,128)(2,1)} %get-tuple-element.219.refs_2_), channel_id=1, source_target_pairs={{0,4},{4,0},{8,12},{12,8},{16,20},{20,16},{24,28},{28,24},{1,5},{5... | collective-permute-start | bytes 1769480 | tf_op jit(solution)/shard_map/ppermute | solution.py:864
  153.1 13.7 %collective-permute-start.36 = (bf16[96,768]{1,0:T(8,128)(2,1)}, bf16[96,768]{1,0:T(8,128)(2,1)}, u32[]{:S(2)}, u32[]{:S(2)}) collective-permute-start(bf16[96,768]{1,0:T(8,128)(2,1)} %close.3.refs_2_.refs_0_), channel_id=1, source_target_pairs={{0,16},{4,20},{8,24},{12,28},{16,0},{20,4},{24,8},{28,12},{1,17},{... | collective-permute-start | bytes 442376 | tf_op jit(solution)/shard_map/ppermute | solution.py:864
  157.3 15.1 %collective-permute-start.34 = (bf16[256,768]{1,0:T(8,128)(2,1)S(1)}, bf16[256,768]{1,0:T(8,128)(2,1)}, u32[]{:S(2)}, u32[]{:S(2)}) collective-permute-start(bf16[256,768]{1,0:T(8,128)(2,1)S(1)} %far_sum.6.refs_2_), channel_id=1, source_target_pairs={{0,2},{1,3},{2,0},{3,1},{4,6},{5,7},{6,4},{7,5},{8,10},{9,11},{10,... | collective-permute-start | bytes 1179656 | tf_op jit(solution)/shard_map/ppermute | solution.py:864
  159.8 15.0 %collective-permute-start.38 = (bf16[96,768]{1,0:T(8,128)(2,1)}, bf16[96,768]{1,0:T(8,128)(2,1)S(1)}, u32[]{:S(2)}, u32[]{:S(2)}) collective-permute-start(bf16[96,768]{1,0:T(8,128)(2,1)} %copy-done.28), channel_id=1, source_target_pairs={{0,16},{4,20},{8,24},{12,28},{16,0},{20,4},{24,8},{28,12},{1,17},{... | collective-permute-start | bytes 442376 | tf_op jit(solution)/shard_map/ppermute | solution.py:864
  168.3 10.0 %collective-permute-start.40 = (bf16[2,96,768]{2,1,0:T(8,128)(2,1)S(1)}, bf16[2,96,768]{2,1,0:T(8,128)(2,1)S(1)}, u32[]{:S(2)}, u32[]{:S(2)}) collective-permute-start(bf16[2,96,768]{2,1,0:T(8,128)(2,1)S(1)} %join.7.refs_2_.refs_0_), channel_id=1, source_target_pairs={{0,8},{4,12},{8,0},{12,4},{16,24},{20,28},{24,16},{28,20},{1,9},{5... | collective-permute-start | bytes 884744 | tf_op jit(solution)/shard_map/ppermute | solution.py:864
  170.3 13.5 %collective-permute-start.43 = (bf16[2,96,768]{2,1,0:T(8,128)(2,1)S(1)}, bf16[2,96,768]{2,1,0:T(8,128)(2,1)S(1)}, u32[]{:S(2)}, u32[]{:S(2)}) collective-permute-start(bf16[2,96,768]{2,1,0:T(8,128)(2,1)S(1)} %get-tuple-element.224.refs_6_), channel_id=1, source_target_pairs={{0,8},{4,12},{8,0},{12,4},{16,24},{20,28},{24,16},{28,20},{1,9},{5... | collective-permute-start | bytes 884744 | tf_op jit(solution)/shard_map/ppermute | solution.py:864
  175.4 10.7 %collective-permute-start.42 = (bf16[96,768]{1,0:T(8,128)(2,1)S(1)}, bf16[96,768]{1,0:T(8,128)(2,1)}, u32[]{:S(2)}, u32[]{:S(2)}) collective-permute-start(bf16[96,768]{1,0:T(8,128)(2,1)S(1)} %close.4.refs_2_.refs_0_), channel_id=1, source_target_pairs={{0,16},{4,20},{8,24},{12,28},{16,0},{20,4},{24,8},{28,12},{1,17},{... | collective-permute-start | bytes 442376 | tf_op jit(solution)/shard_map/ppermute | solution.py:864
  176.5 4.2 %collective-permute-start.39 = (f32[6,768]{1,0:T(8,128)S(1)}, f32[6,768]{1,0:T(8,128)S(1)}, u32[]{:S(2)}, u32[]{:S(2)}) collective-permute-start(f32[6,768]{1,0:T(8,128)S(1)} %vec_add.2.refs_2_.refs_0_), channel_id=1, source_target_pairs={{0,2},{1,3},{2,0},{3,1},{4,6},{5,7},{6,4},{7,5},{8,10},{9,11},{10,... | collective-permute-start | bytes 55304 | tf_op jit(solution)/shard_map/ppermute | solution.py:864
  178.9 14.6 %collective-permute-start.46 = (bf16[4,96,768]{2,1,0:T(8,128)(2,1)S(1)}, bf16[4,96,768]{2,1,0:T(8,128)(2,1)S(1)}, u32[]{:S(2)}, u32[]{:S(2)}) collective-permute-start(bf16[4,96,768]{2,1,0:T(8,128)(2,1)S(1)} %join.8.refs_2_.refs_5_), channel_id=1, source_target_pairs={{0,4},{4,0},{8,12},{12,8},{16,20},{20,16},{24,28},{28,24},{1,5},{5... | collective-permute-start | bytes 1769480 | tf_op jit(solution)/shard_map/ppermute | solution.py:864
  180.4 13.0 %collective-permute-start.47 = (bf16[256,768]{1,0:T(8,128)(2,1)S(1)}, bf16[256,768]{1,0:T(8,128)(2,1)S(1)}, u32[]{:S(2)}, u32[]{:S(2)}) collective-permute-start(bf16[256,768]{1,0:T(8,128)(2,1)S(1)} %get-tuple-element.242.refs_2_.refs_0_), channel_id=1, source_target_pairs={{0,2},{1,3},{2,0},{3,1},{4,6},{5,7},{6,4},{7,5},{8,10},{9,11},{10,... | collective-permute-start | bytes 1179656 | tf_op jit(solution)/shard_map/ppermute | solution.py:864
  181.3 20.5 %collective-permute-start.41 = (bf16[256,768]{1,0:T(8,128)(2,1)S(1)}, bf16[256,768]{1,0:T(8,128)(2,1)}, u32[]{:S(2)}, u32[]{:S(2)}) collective-permute-start(bf16[256,768]{1,0:T(8,128)(2,1)S(1)} %far_sum.7.refs_2_), channel_id=1, source_target_pairs={{0,2},{1,3},{2,0},{3,1},{4,6},{5,7},{6,4},{7,5},{8,10},{9,11},{10,... | collective-permute-start | bytes 1179656 | tf_op jit(solution)/shard_map/ppermute | solution.py:864
  185.8 7.6 %collective-permute-start.45 = (bf16[96,768]{1,0:T(8,128)(2,1)}, bf16[96,768]{1,0:T(8,128)(2,1)}, u32[]{:S(2)}, u32[]{:S(2)}) collective-permute-start(bf16[96,768]{1,0:T(8,128)(2,1)} %get-tuple-element.232.refs_2_), channel_id=1, source_target_pairs={{0,16},{4,20},{8,24},{12,28},{16,0},{20,4},{24,8},{28,12},{1,17},{... | collective-permute-start | bytes 442376 | tf_op jit(solution)/shard_map/ppermute | solution.py:864
  187.7 12.1 %collective-permute-start.44 = (bf16[2,96,768]{2,1,0:T(8,128)(2,1)S(1)}, bf16[2,96,768]{2,1,0:T(8,128)(2,1)S(1)}, u32[]{:S(2)}, u32[]{:S(2)}) collective-permute-start(bf16[2,96,768]{2,1,0:T(8,128)(2,1)S(1)} %join.9.refs_3_.refs_0_), channel_id=1, source_target_pairs={{0,8},{4,12},{8,0},{12,4},{16,24},{20,28},{24,16},{28,20},{1,9},{5... | collective-permute-start | bytes 884744 | tf_op jit(solution)/shard_map/ppermute | solution.py:864
  195.0 17.3 %collective-permute-start.50 = (bf16[112,768]{1,0:T(8,128)(2,1)S(1)}, bf16[112,768]{1,0:T(8,128)(2,1)S(1)}, u32[]{:S(2)}, u32[]{:S(2)}) collective-permute-start(bf16[112,768]{1,0:T(8,128)(2,1)S(1)} %close.5.refs_2_.refs_0_), channel_id=1, source_target_pairs={{0,16},{4,20},{8,24},{12,28},{16,0},{20,4},{24,8},{28,12},{1,17},{... | collective-permute-start | bytes 516104 | tf_op jit(solution)/shard_map/ppermute | solution.py:864
  196.7 15.6 %collective-permute-start.51 = (bf16[112,768]{1,0:T(8,128)(2,1)S(1)}, bf16[112,768]{1,0:T(8,128)(2,1)S(1)}, u32[]{:S(2)}, u32[]{:S(2)}) collective-permute-start(bf16[112,768]{1,0:T(8,128)(2,1)S(1)} %close.5.refs_2_.refs_0_), channel_id=1, source_target_pairs={{0,8},{4,12},{8,0},{12,4},{16,24},{20,28},{24,16},{28,20},{1,9},{5... | collective-permute-start | bytes 516104 | tf_op jit(solution)/shard_map/ppermute | solution.py:864
  197.5 14.8 %collective-permute-start.52 = (bf16[112,768]{1,0:T(8,128)(2,1)S(1)}, bf16[112,768]{1,0:T(8,128)(2,1)S(1)}, u32[]{:S(2)}, u32[]{:S(2)}) collective-permute-start(bf16[112,768]{1,0:T(8,128)(2,1)S(1)} %close.5.refs_2_.refs_0_), channel_id=1, source_target_pairs={{0,24},{4,28},{8,16},{12,20},{16,8},{20,12},{24,0},{28,4},{1,25},{... | collective-permute-start | bytes 516104 | tf_op jit(solution)/shard_map/ppermute | solution.py:864
  200.4 16.5 %collective-permute-start.49 = (bf16[4,96,768]{2,1,0:T(8,128)(2,1)S(1)}, bf16[4,96,768]{2,1,0:T(8,128)(2,1)S(1)}, u32[]{:S(2)}, u32[]{:S(2)}) collective-permute-start(bf16[4,96,768]{2,1,0:T(8,128)(2,1)S(1)} %join.10.refs_4_.refs_7_.refs_5_), channel_id=1, source_target_pairs={{0,4},{4,0},{8,12},{12,8},{16,20},{20,16},{24,28},{28,24},{1,5},{5... | collective-permute-start | bytes 1769480 | tf_op jit(solution)/shard_map/ppermute | solution.py:864
  203.8 18.2 %collective-permute-start.48 = (bf16[256,768]{1,0:T(8,128)(2,1)S(1)}, bf16[256,768]{1,0:T(8,128)(2,1)S(1)}, u32[]{:S(2)}, u32[]{:S(2)}) collective-permute-start(bf16[256,768]{1,0:T(8,128)(2,1)S(1)} %block_end.1.refs_0_), channel_id=1, source_target_pairs={{0,2},{1,3},{2,0},{3,1},{4,6},{5,7},{6,4},{7,5},{8,10},{9,11},{10,... | collective-permute-start | bytes 1179656 | tf_op jit(solution)/shard_map/ppermute | solution.py:864
  212.9 16.0 %collective-permute-start.57 = (bf16[4,112,768]{2,1,0:T(8,128)(2,1)S(1)}, bf16[4,112,768]{2,1,0:T(8,128)(2,1)S(1)}, u32[]{:S(2)}, u32[]{:S(2)}) collective-permute-start(bf16[4,112,768]{2,1,0:T(8,128)(2,1)S(1)} %join.11.refs_10_), channel_id=1, source_target_pairs={{0,4},{4,0},{8,12},{12,8},{16,20},{20,16},{24,28},{28,24},{1,5},{5... | collective-permute-start | bytes 2064392 | tf_op jit(solution)/shard_map/ppermute | solution.py:864
  (50 other events, 343.3 us)

commit v7 on v6

--- a/solution.py
+++ b/solution.py
@@ -736,6 +736,14 @@
 
     outs = [near(x.shape, x.dtype) for x in arrays]
     return run(kernel, (1,), arrays, fulls(arrays), outs, fulls(outs), idx, "warm", 0, (), after, range(count))
+
+
+def mark(idx, after, tick=0):
+    def kernel(idx, out_ref):
+        out_ref[...] = jnp.zeros(out_ref.shape, F32)
+
+    out = [sds((8, 128), F32)]
+    return run(kernel, (1,), [], [], out, fulls(out), idx, "mark", tick, (), after)[0]
 
 
 def one_hot(place, count, width):
@@ -934,10 +942,10 @@
     o, *probs = attend(start, q, k, v, idx)
     o, *up_z = lax.optimization_barrier((o, *up_z))
     o_far = mp(o, 2)
-    up_four = jnp.stack([up_own, *lax.optimization_barrier((*up_z, down_z2))[:-1]])
+    up_four = jnp.stack([up_own, *up_z])
     up_x = dp(up_four, 1)
     wo_near, wo_last = mp(after(wo, up_four), 1), mp(after(wo_far, up_four), 1)
-    down_four = join([down_two, down_z2], idx, [up_four, wo_near, wo_last])
+    down_four = join([down_two, down_z2], idx, [wo_near, wo_last, mark(idx, [down_z2], 20)])
     down_z1 = dp(down_four, 2)
     o_near = mp(after(o, o_far), 1)
     o_all = [o, o_near, o_far, mp(o_far, 1)]

time: 236 us -> 230 us (0.975)
  waiting for transfers between devices: 42.7 us -> 39.2 us
    ppermute x58, waiting for transfers between devices: 42.7 us -> 39.2 us  [swap(): return lax.ppermute(x, axis, [(i, i ^ k) for i in range(size)])]
    pallas_call x42 -> x43, Pallas kernels: 121 us -> 121 us  [run(): pl.pallas_call(kernel, grid_spec=pltpu.PrefetchScalarGridSpec(num_scalar_...]
  transfers between devices with their start and end apart: 58 -> 58, of which waited for: 18 -> 17; matrix products, arithmetic and copies ran while one was open for 2% -> 2% of each run, Pallas kernels for 43% -> 44%
where the time goes in v7:
time: 230 us; the launch traced here: 229 us
  Pallas kernels  121 us (53%)
  starting transfers between devices  54.7 us (24%)
  waiting for transfers between devices  39.2 us (17%)
  blocking collectives  5.59 us (2%)
  local copies, waits for them, and re-layouts  5.13 us (2%)
    pallas_call x43, Pallas kernels, run(): pl.pallas_call(kernel, grid_spec=pltpu.PrefetchScalarGridSpec(num_scalar_...  121 us
    ppermute x58, starting transfers between devices, swap(): return lax.ppermute(x, axis, [(i, i ^ k) for i in range(size)])  54.7 us
    ppermute x58, waiting for transfers between devices, swap(): return lax.ppermute(x, axis, [(i, i ^ k) for i in range(size)])  39.2 us
    all_gather x1, blocking collectives, body(): stats = lax.all_gather(stats, 'mp')  5.59 us
  transfers between devices with their start and end apart: 58, of which 17 were waited for; matrix products, arithmetic and copies ran while one was open for 2% of the time, Pallas kernels for 44%

profile of v7, /device:TPU:0, one launch (start us, length us, event | category | flops | bytes accessed | tf_op | source)
XLA Modules:
  0.0 229.4 jit_solution(6797145600975203923)
XLA Ops:
  0.8 2.4 %pack_weights.1.refs_2_ = bf16[96,768]{1,0:T(8,128)(2,1)} custom-call(s32[3]{0:T(128)S(1)} %pad_add_fusion.idx, f32[96,576]{1,0:T(8,128)} %bitcast.75, f32[24,768]{1,0:T(8,128)} %bitcast.82), custom_call_target="tpu_custom_call" | custom-call | flops 400000000 | bytes 1024 | tf_op jit(solution)/shard_map/pack_weights/pallas_call | solution.py:44
  3.1 2.9 %collective-permute-start = (bf16[96,768]{1,0:T(8,128)(2,1)}, bf16[96,768]{1,0:T(8,128)(2,1)}, u32[]{:S(2)}, u32[]{:S(2)}) collective-permute-start(bf16[96,768]{1,0:T(8,128)(2,1)} %pack_weights.1.refs_2_), channel_id=1, source_target_pairs={{0,4},{4,0},{8,12},{12,8},{16,20},{20,16},{24,28},{28,24},{1,5},{5... | collective-permute-start | bytes 442376 | tf_op jit(solution)/shard_map/ppermute | solution.py:872
  6.1 1.6 collective-permute-start.1
  7.6 2.6 %collective-permute-start.4 = (bf16[96,768]{1,0:T(8,128)(2,1)}, bf16[96,768]{1,0:T(8,128)(2,1)}, u32[]{:S(2)}, u32[]{:S(2)}) collective-permute-start(bf16[96,768]{1,0:T(8,128)(2,1)} %pack_weights.1.refs_2_), channel_id=1, source_target_pairs={{0,16},{4,20},{8,24},{12,28},{16,0},{20,4},{24,8},{28,12},{1,17},{... | collective-permute-start | bytes 442376 | tf_op jit(solution)/shard_map/ppermute | solution.py:872
  10.4 1.6 cast_pair.1
  13.4 3.9 %collective-permute-done.2 = bf16[96,768]{1,0:T(8,128)(2,1)S(1)} collective-permute-done((bf16[96,768]{1,0:T(8,128)(2,1)S(1)}, bf16[96,768]{1,0:T(8,128)(2,1)S(1)}, u32[]{:S(2)}, u32[]{:S(2)}) %collective-permute-start.2) | collective-permute-done | bytes 147488 | tf_op jit(solution)/shard_map/ppermute | solution.py:872
  17.7 4.1 %collective-permute-done.4.refs_6_ = bf16[96,768]{1,0:T(8,128)(2,1)} collective-permute-done((bf16[96,768]{1,0:T(8,128)(2,1)}, bf16[96,768]{1,0:T(8,128)(2,1)}, u32[]{:S(2)}, u32[]{:S(2)}) %collective-permute-start.4) | collective-permute-done | bytes 147488 | tf_op jit(solution)/shard_map/ppermute | solution.py:872
  25.0 1.7 collective-permute-start.8
  27.9 1.6 collective-permute-start.10
  30.3 5.2 %project.1 = (bf16[1024,192]{1,0:T(8,128)(2,1)}, bf16[1024,192]{1,0:T(8,128)(2,1)}, bf16[1024,192]{1,0:T(8,128)(2,1)}, bf16[768,576]{1,0:T(8,128)(2,1)}, bf16[208,768]{1,0:T(8,128)(2,1)}) custom-call(s32[3]{0:T(128)S(1)} %pad_add_fusion.idx, bf16[1024,768]{1,0:T(8,128)(2,1)S(1)} %fusion.5.refs_0_, f32[2,192]{1,0:T(2,128)S(1)} %copy-done.30, ...), custom_call_target="tpu_custom_call" | custom-call | flops 16000000000 | bytes 1024 | tf_op jit(solution)/shard_map/project/pallas_call | solution.py:44
  35.5 1.6 collective-permute-start.15
  37.0 9.8 %attend.1 = (bf16[1024,192]{1,0:T(8,128)(2,1)}, bf16[3,256,256]{2,1,0:T(8,128)(2,1)}, bf16[3,256,512]{2,1,0:T(8,128)(2,1)}, bf16[3,256,768]{2,1,0:T(8,128)(2,1)}, bf16[3,256,1024]{2,1,0:T(8,128)(2,1)}) custom-call(s32[3]{0:T(128)S(1)} %pad_add_fusion.idx, s32[1024,1]{1,0:T(8,128)S(1)} %copy.55.refs_0_, bf16[1024,192]{1,0:T(8,128)(2,1)} %get-tuple-element.156.refs_1_.refs_0_, ...), custom_call_target="tpu_custom_call" | custom-call | flops 4000000000 | bytes 1024 | tf_op jit(solution)/shard_map/attend/pallas_call | solution.py:44
  46.9 1.6 collective-permute-start.17
  49.5 2.0 collective-permute-done.18.refs_0_.refs_1_
  52.9 6.5 %collective-permute-done.11.refs_4_.refs_8_ = bf16[1024,192]{1,0:T(8,128)(2,1)S(1)} collective-permute-done((bf16[1024,192]{1,0:T(8,128)(2,1)}, bf16[1024,192]{1,0:T(8,128)(2,1)S(1)}, u32[]{:S(2)}, u32[]{:S(2)}) %collective-permute-start.11) | collective-permute-done | bytes 393248 | tf_op jit(solution)/shard_map/ppermute | solution.py:872
  62.0 6.8 %outproj.1 = (f32[1024,768]{1,0:T(8,128)}, bf16[1024,768]{1,0:T(8,128)(2,1)S(1)}) custom-call(s32[3]{0:T(128)S(1)} %pad_add_fusion.idx, f32[4,768]{1,0:T(4,128)S(1)} %copy-done.15, bf16[1024,768]{1,0:T(8,128)(2,1)} %refs_3_.1, bf16[1024,192]{1,0:T(8,128)(2,1)S(1)} %copy-done.2, bf16[1024,192]{1,0:T(8,128)(2,1)S(1)} %collective-permute-done.12.refs_3_.refs_7_, ...), custom_call_target="tpu_custom_call" | custom-call | bytes 1024 | tf_op jit(solution)/shard_map/outproj/pallas_call | solution.py:44
  68.9 7.2 %ffn_up.1 = (f32[1024,768]{1,0:T(8,128)S(1)}, f32[1024,768]{1,0:T(8,128)S(1)}, f32[1024,768]{1,0:T(8,128)S(1)}, f32[8,1024]{1,0:T(8,128)S(1)}, bf16[768,768]{1,0:T(8,128)(2,1)S(1)}, /*index=5*/bf16[768,768]{1,0:T(8,128)(2,1)}) custom-call(s32[3]{0:T(128)S(1)} %pad_add_fusion.idx, bf16[1024,768]{1,0:T(8,128)(2,1)S(1)} %get-tuple-element.171.refs_0_, ...), custom_call_target="tpu_custom_call" | custom-call | flops 3000000000 | bytes 1024 | tf_op jit(solution)/shard_map/ffn_up/pallas_call | solution.py:44
  76.1 5.6 %all-gather = f32[32,1024]{1,0:T(8,128)S(1)} all-gather(f32[8,1024]{1,0:T(8,128)S(1)} %get-tuple-element.176), channel_id=2, replica_groups=mesh['dp'=8,'mp'=4] {'mp'}, dimensions={0}, use_global_device_ids=true | all-gather | bytes 163840 | tf_op jit(solution)/shard_map/all_gather | solution.py:955
  81.7 6.3 %ffn_mid.1 = (bf16[1024,768]{1,0:T(8,128)(2,1)}, bf16[1024,768]{1,0:T(8,128)(2,1)}, bf16[2,256,768]{2,1,0:T(8,128)(2,1)S(1)}, f32[256,768]{1,0:T(8,128)}, f32[256,768]{1,0:T(8,128)S(1)}, /*index=5*/f32[2,768]{1,0:T(2,128)S(1)}) custom-call(s32[3]{0:T(128)S(1)} %pad_add_fusion.idx, f32[1024,768]{1,0:T(8,128)S(1)} %get-tuple-element.173.refs_0_, ...), custom_call_target="tpu_custom_call" | custom-call | flops 2600000000 | bytes 1024 | tf_op jit(solution)/shard_map/ffn_mid/pallas_call | solution.py:44
  88.3 1.9 collective-permute-done.20.refs_1_
  92.1 3.5 %grad_down.1 = (bf16[4,96,768]{2,1,0:T(8,128)(2,1)S(1)}, bf16[4,96,768]{2,1,0:T(8,128)(2,1)}) custom-call(s32[3]{0:T(128)S(1)} %pad_add_fusion.idx, bf16[1024,768]{1,0:T(8,128)(2,1)S(1)} %copy-done.7, bf16[1024,768]{1,0:T(8,128)(2,1)S(1)} %copy-done.8, bf16[256,768]{1,0:T(8,128)(2,1)S(1)} %far_sum.4.refs_2_), custom_call_target="tpu_custom_call" | custom-call | flops 1400000000 | bytes 1024 | tf_op jit(solution)/shard_map/grad_down/pallas_call | solution.py:44
  96.1 3.5 %grad_up.1 = (bf16[4,96,768]{2,1,0:T(8,128)(2,1)S(1)}, bf16[4,96,768]{2,1,0:T(8,128)(2,1)}) custom-call(s32[3]{0:T(128)S(1)} %pad_add_fusion.idx, bf16[1024,768]{1,0:T(8,128)(2,1)S(1)} %get-tuple-element.171.refs_0_, bf16[1024,768]{1,0:T(8,128)(2,1)S(1)} %copy-done.26, bf16[4,96,768]{2,1,0:T(8,128)(2,1)S(1)} %get-tuple-element.184.refs_2_), custom_call_target="tpu_custom_call" | custom-call | flops 1400000000 | bytes 1024 | tf_op jit(solution)/shard_map/grad_up/pallas_call | solution.py:44
  99.6 2.7 %collective-permute-done.21.refs_2_ = bf16[256,768]{1,0:T(8,128)(2,1)S(1)} collective-permute-done((bf16[256,768]{1,0:T(8,128)(2,1)S(1)}, bf16[256,768]{1,0:T(8,128)(2,1)S(1)}, u32[]{:S(2)}, u32[]{:S(2)}) %collective-permute-start.21) | collective-permute-done | bytes 393248 | tf_op jit(solution)/shard_map/ppermute | solution.py:872
  102.3 5.1 %shard_back.1 = (f32[256,768]{1,0:T(8,128)}, f32[2,768]{1,0:T(2,128)S(1)}, f32[4,2,192]{2,1,0:T(2,128)S(1)}, bf16[256,192]{1,0:T(8,128)(2,1)S(1)}, bf16[256,192]...) custom-call(s32[3]{0:T(128)S(1)} %pad_add_fusion.idx, ...), custom_call_target="tpu_custom_call" | custom-call | bytes 1024 | tf_op jit(solution)/shard_map/shard_back/pallas_call | solution.py:44
  110.7 5.5 %ffn_out.1 = (bf16[2,256,768]{2,1,0:T(8,128)(2,1)S(1)}, f32[256,768]{1,0:T(8,128)}, f32[256,768]{1,0:T(8,128)S(1)}) custom-call(s32[3]{0:T(128)S(1)} %pad_add_fusion.idx, bf16[1024,768]{1,0:T(8,128)(2,1)} %get-tuple-element.178.refs_0_, bf16[768,768]{1,0:T(8,128)(2,1)} %get-tuple-element.179.refs_1_, bf16[256,192]{1,0:T(8,128)(2,1)S(1)} %collective-permute-done.22.refs_2_.refs_8_), custom_call_target="tpu_custom_call" | custom-call | bytes 1024 | tf_op jit(solution)/shard_map/ffn_out/pallas_call | solution.py:44
  116.2 1.8 fold.6
  121.1 11.2 %attend_back.1.refs_2_.refs_1_ = bf16[1024,576]{1,0:T(8,128)(2,1)S(1)} custom-call(s32[3]{0:T(128)S(1)} %pad_add_fusion.idx, bf16[1024,192]{1,0:T(8,128)(2,1)} %get-tuple-element.156.refs_1_.refs_0_, bf16[1024,192]{1,0:T(8,128)(2,1)} %get-tuple-element.157.refs_2_.refs_1_, bf16[1024,192]{1,0:T(8,128)(2,1)} %get-tuple-element.158.refs_3_.refs_2_, ...), custom_call_target="tpu_custom_call" | custom-call | flops 4400000000 | bytes 1024 | tf_op jit(solution)/shard_map/attend_back/pallas_call | solution.py:44
  133.3 1.7 fold.8
  136.5 6.5 %qkv_back.1 = (bf16[4,96,768]{2,1,0:T(8,128)(2,1)}, bf16[4,96,768]{2,1,0:T(8,128)(2,1)}, bf16[2,256,768]{2,1,0:T(8,128)(2,1)S(1)}, f32[256,768]{1,0:T(8,128)}, f32[256,768]{1,0:T(8,128)S(1)}) custom-call(s32[3]{0:T(128)S(1)} %pad_add_fusion.idx, bf16[1024,768]{1,0:T(8,128)(2,1)} %copy-done.6, bf16[1024,576]{1,0:T(8,128)(2,1)S(1)} %attend_back.1.refs_2_.refs_1_, ...), custom_call_target="tpu_custom_call" | custom-call | flops 16000000000 | bytes 1024 | tf_op jit(solution)/shard_map/qkv_back/pallas_call | solution.py:44
  145.5 1.9 collective-permute-start.36
  159.0 1.9 fold.10
  161.7 2.3 shard_end.1
  164.7 4.3 %collective-permute-start.42 = (bf16[96,768]{1,0:T(8,128)(2,1)S(1)}, bf16[96,768]{1,0:T(8,128)(2,1)}, u32[]{:S(2)}, u32[]{:S(2)}) collective-permute-start(bf16[96,768]{1,0:T(8,128)(2,1)S(1)} %close.4.refs_2_.refs_0_), channel_id=1, source_target_pairs={{0,16},{4,20},{8,24},{12,28},{16,0},{20,4},{24,8},{28,12},{1,17},{... | collective-permute-start | bytes 442376 | tf_op jit(solution)/shard_map/ppermute | solution.py:872
  169.6 1.6 collective-permute-start.39
  174.0 1.6 collective-permute-start.41
  175.6 2.2 collective-permute-done.43.refs_1_
  179.9 1.5 join.9.refs_3_.refs_0_
  181.9 6.7 %collective-permute-done.45.refs_1_ = bf16[96,768]{1,0:T(8,128)(2,1)} collective-permute-done((bf16[96,768]{1,0:T(8,128)(2,1)}, bf16[96,768]{1,0:T(8,128)(2,1)}, u32[]{:S(2)}, u32[]{:S(2)}) %collective-permute-start.45) | collective-permute-done | bytes 147488 | tf_op jit(solution)/shard_map/ppermute | solution.py:872
  191.4 3.2 %collective-permute-start.52 = (bf16[112,768]{1,0:T(8,128)(2,1)S(1)}, bf16[112,768]{1,0:T(8,128)(2,1)S(1)}, u32[]{:S(2)}, u32[]{:S(2)}) collective-permute-start(bf16[112,768]{1,0:T(8,128)(2,1)S(1)} %close.5.refs_2_.refs_0_), channel_id=1, source_target_pairs={{0,24},{4,28},{8,16},{12,20},{16,8},{20,12},{24,0},{28,4},{1,25},{... | collective-permute-start | bytes 516104 | tf_op jit(solution)/shard_map/ppermute | solution.py:872
  195.2 2.4 %collective-permute-start.49 = (bf16[4,96,768]{2,1,0:T(8,128)(2,1)S(1)}, bf16[4,96,768]{2,1,0:T(8,128)(2,1)S(1)}, u32[]{:S(2)}, u32[]{:S(2)}) collective-permute-start(bf16[4,96,768]{2,1,0:T(8,128)(2,1)S(1)} %join.10.refs_4_.refs_7_.refs_5_), channel_id=1, source_target_pairs={{0,4},{4,0},{8,12},{12,8},{16,20},{20,16},{24,28},{28,24},{1,5},{5... | collective-permute-start | bytes 1769480 | tf_op jit(solution)/shard_map/ppermute | solution.py:872
  197.6 1.9 block_end.1.refs_0_
  200.2 5.1 %update_down.1 = (f32[768,768]{1,0:T(8,128)}, f32[96,768]{1,0:T(8,128)}, f32[96,768]{1,0:T(8,128)}, f32[96,768]{1,0:T(8,128)}, bf16[96,768]{1,0:T(8,128)(2,1)}, /*index=5*/f32[8,128]{1,0:T(8,128)S(1)}) custom-call(s32[3]{0:T(128)S(1)} %pad_add_fusion.idx, f32[96,768]{1,0:T(8,128)} %bitcast.63, f32[96,768]{1,0:T(8,128)} %bitcast.64, f32[96,768]{1,0:T(8,128)} %bitcast.65, ...), custom_call_target="tpu_custom_call" | custom-call | bytes 1024 | tf_op jit(solution)/shard_map/update_down/pallas_call | solution.py:44
  207.3 3.5 %warm.1 = (f32[96,576]{1,0:T(8,128)S(1)}, f32[96,768]{1,0:T(8,128)S(1)}, f32[72,576]{1,0:T(8,128)S(1)}, f32[96,768]{1,0:T(8,128)S(1)}, f32[576,576]{1,0:T(8,128)...) custom-call(s32[3]{0:T(128)S(1)} %pad_add_fusion.idx, ...), custom_call_target="tpu_custom_call" | custom-call | bytes 1024 | tf_op jit(solution)/shard_map/warm/pallas_call | solution.py:44
  211.8 5.1 %update_up.1 = (f32[768,768]{1,0:T(8,128)}, f32[96,768]{1,0:T(8,128)}, f32[96,768]{1,0:T(8,128)}, f32[96,768]{1,0:T(8,128)}, bf16[96,768]{1,0:T(8,128)(2,1)}, /*index=5*/f32[8,128]{1,0:T(8,128)S(1)}) custom-call(s32[3]{0:T(128)S(1)} %pad_add_fusion.idx, f32[96,768]{1,0:T(8,128)} %bitcast.68, f32[96,768]{1,0:T(8,128)} %bitcast.69, f32[96,768]{1,0:T(8,128)} %bitcast.70, ...), custom_call_target="tpu_custom_call" | custom-call | bytes 1024 | tf_op jit(solution)/shard_map/update_up/pallas_call | solution.py:44
  219.2 1.8 spread_tokens.1
  221.0 1.8 spread_out.1
  222.8 1.9 collective-permute-done.57.refs_11_
  224.7 4.5 %update_qkv.1 = (f32[576,768]{1,0:T(8,128)}, f32[96,768]{1,0:T(8,128)}, f32[72,576]{1,0:T(8,128)}, f32[96,576]{1,0:T(8,128)}, bf16[96,576]{1,0:T(8,128)(2,1)}, /...) custom-call(s32[3]{0:T(128)S(1)} %pad_add_fusion.idx, ...), custom_call_target="tpu_custom_call" | custom-call | flops 2400000000 | bytes 1024 | tf_op jit(solution)/shard_map/update_qkv/pallas_call | solution.py:44
  (211 shorter events, 54.4 us)
Async XLA Ops:
  3.1 23.6 %collective-permute-start = (bf16[96,768]{1,0:T(8,128)(2,1)}, bf16[96,768]{1,0:T(8,128)(2,1)}, u32[]{:S(2)}, u32[]{:S(2)}) collective-permute-start(bf16[96,768]{1,0:T(8,128)(2,1)} %pack_weights.1.refs_2_), channel_id=1, source_target_pairs={{0,4},{4,0},{8,12},{12,8},{16,20},{20,16},{24,28},{28,24},{1,5},{5... | collective-permute-start | bytes 442376 | tf_op jit(solution)/shard_map/ppermute | solution.py:872
  6.1 11.3 %collective-permute-start.1 = (bf16[96,768]{1,0:T(8,128)(2,1)}, bf16[96,768]{1,0:T(8,128)(2,1)}, u32[]{:S(2)}, u32[]{:S(2)}) collective-permute-start(bf16[96,768]{1,0:T(8,128)(2,1)} %pack_weights.1.refs_2_), channel_id=1, source_target_pairs={{0,8},{4,12},{8,0},{12,4},{16,24},{20,28},{24,16},{28,20},{1,9},{5... | collective-permute-start | bytes 442376 | tf_op jit(solution)/shard_map/ppermute | solution.py:872
  7.6 14.2 %collective-permute-start.4 = (bf16[96,768]{1,0:T(8,128)(2,1)}, bf16[96,768]{1,0:T(8,128)(2,1)}, u32[]{:S(2)}, u32[]{:S(2)}) collective-permute-start(bf16[96,768]{1,0:T(8,128)(2,1)} %pack_weights.1.refs_2_), channel_id=1, source_target_pairs={{0,16},{4,20},{8,24},{12,28},{16,0},{20,4},{24,8},{28,12},{1,17},{... | collective-permute-start | bytes 442376 | tf_op jit(solution)/shard_map/ppermute | solution.py:872
  10.2 12.2 %collective-permute-start.6 = (bf16[96,768]{1,0:T(8,128)(2,1)}, bf16[96,768]{1,0:T(8,128)(2,1)}, u32[]{:S(2)}, u32[]{:S(2)}) collective-permute-start(bf16[96,768]{1,0:T(8,128)(2,1)} %pack_weights.1.refs_2_), channel_id=1, source_target_pairs={{0,24},{4,28},{8,16},{12,20},{16,8},{20,12},{24,0},{28,4},{1,25},{... | collective-permute-start | bytes 442376 | tf_op jit(solution)/shard_map/ppermute | solution.py:872
  12.1 5.2 %collective-permute-start.2 = (bf16[96,768]{1,0:T(8,128)(2,1)S(1)}, bf16[96,768]{1,0:T(8,128)(2,1)S(1)}, u32[]{:S(2)}, u32[]{:S(2)}) collective-permute-start(bf16[96,768]{1,0:T(8,128)(2,1)S(1)} %get-tuple-element.152), channel_id=1, source_target_pairs={{0,4},{4,0},{8,12},{12,8},{16,20},{20,16},{24,28},{28,24},{1,5},{5... | collective-permute-start | bytes 442376 | tf_op jit(solution)/shard_map/ppermute | solution.py:872
  17.3 10.6 %collective-permute-start.3 = (bf16[96,768]{1,0:T(8,128)(2,1)}, bf16[96,768]{1,0:T(8,128)(2,1)}, u32[]{:S(2)}, u32[]{:S(2)}) collective-permute-start(bf16[96,768]{1,0:T(8,128)(2,1)} %collective-permute-done.1.refs_4_), channel_id=1, source_target_pairs={{0,4},{4,0},{8,12},{12,8},{16,20},{20,16},{24,28},{28,24},{1,5},{5... | collective-permute-start | bytes 442376 | tf_op jit(solution)/shard_map/ppermute | solution.py:872
  21.8 7.7 %collective-permute-start.5 = (bf16[96,768]{1,0:T(8,128)(2,1)}, bf16[96,768]{1,0:T(8,128)(2,1)}, u32[]{:S(2)}, u32[]{:S(2)}) collective-permute-start(bf16[96,768]{1,0:T(8,128)(2,1)} %collective-permute-done.4.refs_6_), channel_id=1, source_target_pairs={{0,4},{4,0},{8,12},{12,8},{16,20},{20,16},{24,28},{28,24},{1,5},{5... | collective-permute-start | bytes 442376 | tf_op jit(solution)/shard_map/ppermute | solution.py:872
  22.4 7.9 %collective-permute-start.7 = (bf16[96,768]{1,0:T(8,128)(2,1)}, bf16[96,768]{1,0:T(8,128)(2,1)}, u32[]{:S(2)}, u32[]{:S(2)}) collective-permute-start(bf16[96,768]{1,0:T(8,128)(2,1)} %collective-permute-done.6.refs_8_), channel_id=1, source_target_pairs={{0,4},{4,0},{8,12},{12,8},{16,20},{20,16},{24,28},{28,24},{1,5},{5... | collective-permute-start | bytes 442376 | tf_op jit(solution)/shard_map/ppermute | solution.py:872
  25.0 21.8 %collective-permute-start.8 = (bf16[96,768]{1,0:T(8,128)(2,1)}, bf16[96,768]{1,0:T(8,128)(2,1)S(1)}, u32[]{:S(2)}, u32[]{:S(2)}) collective-permute-start(bf16[96,768]{1,0:T(8,128)(2,1)} %copy-done.16), channel_id=1, source_target_pairs={{0,16},{4,20},{8,24},{12,28},{16,0},{20,4},{24,8},{28,12},{1,17},{... | collective-permute-start | bytes 442376 | tf_op jit(solution)/shard_map/ppermute | solution.py:872
  26.8 20.1 %collective-permute-start.9 = (bf16[96,768]{1,0:T(8,128)(2,1)}, bf16[96,768]{1,0:T(8,128)(2,1)S(1)}, u32[]{:S(2)}, u32[]{:S(2)}) collective-permute-start(bf16[96,768]{1,0:T(8,128)(2,1)} %copy-done.16), channel_id=1, source_target_pairs={{0,8},{4,12},{8,0},{12,4},{16,24},{20,28},{24,16},{28,20},{1,9},{5... | collective-permute-start | bytes 442376 | tf_op jit(solution)/shard_map/ppermute | solution.py:872
  27.9 18.9 %collective-permute-start.10 = (bf16[96,768]{1,0:T(8,128)(2,1)}, bf16[96,768]{1,0:T(8,128)(2,1)S(1)}, u32[]{:S(2)}, u32[]{:S(2)}) collective-permute-start(bf16[96,768]{1,0:T(8,128)(2,1)} %copy-done.16), channel_id=1, source_target_pairs={{0,24},{4,28},{8,16},{12,20},{16,8},{20,12},{24,0},{28,4},{1,25},{... | collective-permute-start | bytes 442376 | tf_op jit(solution)/shard_map/ppermute | solution.py:872
  29.5 22.0 %collective-permute-start.18 = (bf16[2,96,768]{2,1,0:T(8,128)(2,1)S(1)}, bf16[2,96,768]{2,1,0:T(8,128)(2,1)S(1)}, u32[]{:S(2)}, u32[]{:S(2)}) collective-permute-start(bf16[2,96,768]{2,1,0:T(8,128)(2,1)S(1)} %pad_maximum_fusion.1.refs_0_), channel_id=1, source_target_pairs={{0,16},{4,20},{8,24},{12,28},{16,0},{20,4},{24,8},{28,12},{1,17},{... | collective-permute-start | bytes 884744 | tf_op jit(solution)/shard_map/ppermute | solution.py:872
  35.5 13.6 %collective-permute-start.15 = (bf16[208,768]{1,0:T(8,128)(2,1)}, bf16[208,768]{1,0:T(8,128)(2,1)S(1)}, u32[]{:S(2)}, u32[]{:S(2)}) collective-permute-start(bf16[208,768]{1,0:T(8,128)(2,1)} %get-tuple-element.168.refs_6_.refs_10_), channel_id=1, source_target_pairs={{0,2},{1,3},{2,0},{3,1},{4,6},{5,7},{6,4},{7,5},{8,10},{9,11},{10,... | collective-permute-start | bytes 958472 | tf_op jit(solution)/shard_map/ppermute | solution.py:872
  46.9 12.9 %collective-permute-start.17 = (bf16[4,96,768]{2,1,0:T(8,128)(2,1)S(1)}, bf16[4,96,768]{2,1,0:T(8,128)(2,1)S(1)}, u32[]{:S(2)}, u32[]{:S(2)}) collective-permute-start(bf16[4,96,768]{2,1,0:T(8,128)(2,1)S(1)} %pad_maximum_fusion.refs_3_), channel_id=1, source_target_pairs={{0,4},{4,0},{8,12},{12,8},{16,20},{20,16},{24,28},{28,24},{1,5},{5... | collective-permute-start | bytes 1769480 | tf_op jit(solution)/shard_map/ppermute | solution.py:872
  48.5 10.8 %collective-permute-start.11 = (bf16[1024,192]{1,0:T(8,128)(2,1)}, bf16[1024,192]{1,0:T(8,128)(2,1)S(1)}, u32[]{:S(2)}, u32[]{:S(2)}) collective-permute-start(bf16[1024,192]{1,0:T(8,128)(2,1)} %get-tuple-element.163.refs_2_.refs_6_), channel_id=1, source_target_pairs={{0,2},{1,3},{2,0},{3,1},{4,6},{5,7},{6,4},{7,5},{8,10},{9,11},{10,... | collective-permute-start | bytes 1179656 | tf_op jit(solution)/shard_map/ppermute | solution.py:872
  52.8 16.1 %collective-permute-start.19 = (bf16[4,96,768]{2,1,0:T(8,128)(2,1)S(1)}, bf16[4,96,768]{2,1,0:T(8,128)(2,1)S(1)}, u32[]{:S(2)}, u32[]{:S(2)}) collective-permute-start(bf16[4,96,768]{2,1,0:T(8,128)(2,1)S(1)} %join.6.refs_5_), channel_id=1, source_target_pairs={{0,8},{4,12},{8,0},{12,4},{16,24},{20,28},{24,16},{28,20},{1,9},{5... | collective-permute-start | bytes 1769480 | tf_op jit(solution)/shard_map/ppermute | solution.py:872
  90.9 11.4 %collective-permute-start.21 = (bf16[256,768]{1,0:T(8,128)(2,1)S(1)}, bf16[256,768]{1,0:T(8,128)(2,1)S(1)}, u32[]{:S(2)}, u32[]{:S(2)}) collective-permute-start(bf16[256,768]{1,0:T(8,128)(2,1)S(1)} %far_sum.4.refs_2_), channel_id=1, source_target_pairs={{0,2},{1,3},{2,0},{3,1},{4,6},{5,7},{6,4},{7,5},{8,10},{9,11},{10,... | collective-permute-start | bytes 1179656 | tf_op jit(solution)/shard_map/ppermute | solution.py:872
  95.6 20.6 %collective-permute-start.26 = (bf16[4,96,768]{2,1,0:T(8,128)(2,1)S(1)}, bf16[4,96,768]{2,1,0:T(8,128)(2,1)S(1)}, u32[]{:S(2)}, u32[]{:S(2)}) collective-permute-start(bf16[4,96,768]{2,1,0:T(8,128)(2,1)S(1)} %get-tuple-element.184.refs_2_), channel_id=1, source_target_pairs={{0,4},{4,0},{8,12},{12,8},{16,20},{20,16},{24,28},{28,24},{1,5},{5... | collective-permute-start | bytes 1769480 | tf_op jit(solution)/shard_map/ppermute | solution.py:872
  108.0 11.3 %collective-permute-start.25 = (bf16[2,192,768]{2,1,0:T(8,128)(2,1)S(1)}, bf16[2,192,768]{2,1,0:T(8,128)(2,1)S(1)}, u32[]{:S(2)}, u32[]{:S(2)}) collective-permute-start(bf16[2,192,768]{2,1,0:T(8,128)(2,1)S(1)} %get-tuple-element.197), channel_id=1, source_target_pairs={{0,1},{1,0},{2,3},{3,2},{4,5},{5,4},{6,7},{7,6},{8,9},{9,8},{10,11... | collective-permute-start | bytes 1769480 | tf_op jit(solution)/shard_map/ppermute | solution.py:872
  108.5 12.6 %collective-permute-start.23 = (bf16[256,192]{1,0:T(8,128)(2,1)S(1)}, bf16[256,192]{1,0:T(8,128)(2,1)S(1)}, u32[]{:S(2)}, u32[]{:S(2)}) collective-permute-start(bf16[256,192]{1,0:T(8,128)(2,1)S(1)} %get-tuple-element.194), channel_id=1, source_target_pairs={{0,2},{1,3},{2,0},{3,1},{4,6},{5,7},{6,4},{7,5},{8,10},{9,11},{10,... | collective-permute-start | bytes 294920 | tf_op jit(solution)/shard_map/ppermute | solution.py:872
  109.0 12.1 %collective-permute-start.24 = (bf16[256,192]{1,0:T(8,128)(2,1)S(1)}, bf16[256,192]{1,0:T(8,128)(2,1)S(1)}, u32[]{:S(2)}, u32[]{:S(2)}) collective-permute-start(bf16[256,192]{1,0:T(8,128)(2,1)S(1)} %get-tuple-element.195), channel_id=1, source_target_pairs={{0,3},{1,2},{2,1},{3,0},{4,7},{5,6},{6,5},{7,4},{8,11},{9,10},{10,... | collective-permute-start | bytes 294920 | tf_op jit(solution)/shard_map/ppermute | solution.py:872
  110.2 23.2 %collective-permute-start.29 = (bf16[4,96,768]{2,1,0:T(8,128)(2,1)S(1)}, bf16[4,96,768]{2,1,0:T(8,128)(2,1)S(1)}, u32[]{:S(2)}, u32[]{:S(2)}) collective-permute-start(bf16[4,96,768]{2,1,0:T(8,128)(2,1)S(1)} %get-tuple-element.205.refs_14_), channel_id=1, source_target_pairs={{0,4},{4,0},{8,12},{12,8},{16,20},{20,16},{24,28},{28,24},{1,5},{5... | collective-permute-start | bytes 1769480 | tf_op jit(solution)/shard_map/ppermute | solution.py:872
  118.0 14.4 %collective-permute-start.30 = (bf16[2,96,768]{2,1,0:T(8,128)(2,1)S(1)}, bf16[2,96,768]{2,1,0:T(8,128)(2,1)S(1)}, u32[]{:S(2)}, u32[]{:S(2)}) collective-permute-start(bf16[2,96,768]{2,1,0:T(8,128)(2,1)S(1)} %get-tuple-element.199.refs_2_), channel_id=1, source_target_pairs={{0,8},{4,12},{8,0},{12,4},{16,24},{20,28},{24,16},{28,20},{1,9},{5... | collective-permute-start | bytes 884744 | tf_op jit(solution)/shard_map/ppermute | solution.py:872
  119.9 16.6 %collective-permute-start.28 = (bf16[192,768]{1,0:T(8,128)(2,1)S(1)}, bf16[192,768]{1,0:T(8,128)(2,1)S(1)}, u32[]{:S(2)}, u32[]{:S(2)}) collective-permute-start(bf16[192,768]{1,0:T(8,128)(2,1)S(1)} %far_sum.5.refs_11_), channel_id=1, source_target_pairs={{0,2},{1,3},{2,0},{3,1},{4,6},{5,7},{6,4},{7,5},{8,10},{9,11},{10,... | collective-permute-start | bytes 884744 | tf_op jit(solution)/shard_map/ppermute | solution.py:872
  132.3 21.6 %collective-permute-start.27 = (bf16[2,256,768]{2,1,0:T(8,128)(2,1)S(1)}, bf16[2,256,768]{2,1,0:T(8,128)(2,1)S(1)}, u32[]{:S(2)}, u32[]{:S(2)}) collective-permute-start(bf16[2,256,768]{2,1,0:T(8,128)(2,1)S(1)} %get-tuple-element.200.refs_2_), channel_id=1, source_target_pairs={{0,1},{1,0},{2,3},{3,2},{4,5},{5,4},{6,7},{7,6},{8,9},{9,8},{10,11... | collective-permute-start | bytes 2359304 | tf_op jit(solution)/shard_map/ppermute | solution.py:872
  133.0 11.3 %collective-permute-start.33 = (bf16[96,768]{1,0:T(8,128)(2,1)S(1)}, bf16[96,768]{1,0:T(8,128)(2,1)S(1)}, u32[]{:S(2)}, u32[]{:S(2)}) collective-permute-start(bf16[96,768]{1,0:T(8,128)(2,1)S(1)} %get-tuple-element.207.refs_2_), channel_id=1, source_target_pairs={{0,16},{4,20},{8,24},{12,28},{16,0},{20,4},{24,8},{28,12},{1,17},{... | collective-permute-start | bytes 442376 | tf_op jit(solution)/shard_map/ppermute | solution.py:872
  135.1 12.4 %collective-permute-start.32 = (bf16[2,96,768]{2,1,0:T(8,128)(2,1)S(1)}, bf16[2,96,768]{2,1,0:T(8,128)(2,1)S(1)}, u32[]{:S(2)}, u32[]{:S(2)}) collective-permute-start(bf16[2,96,768]{2,1,0:T(8,128)(2,1)S(1)} %get-tuple-element.208.refs_6_), channel_id=1, source_target_pairs={{0,8},{4,12},{8,0},{12,4},{16,24},{20,28},{24,16},{28,20},{1,9},{5... | collective-permute-start | bytes 884744 | tf_op jit(solution)/shard_map/ppermute | solution.py:872
  143.0 5.8 %collective-permute-start.31 = (bf16[2,256,768]{2,1,0:T(8,128)(2,1)S(1)}, bf16[2,256,768]{2,1,0:T(8,128)(2,1)S(1)}, u32[]{:S(2)}, u32[]{:S(2)}) collective-permute-start(bf16[2,256,768]{2,1,0:T(8,128)(2,1)S(1)} %get-tuple-element.210), channel_id=1, source_target_pairs={{0,1},{1,0},{2,3},{3,2},{4,5},{5,4},{6,7},{7,6},{8,9},{9,8},{10,11... | collective-permute-start | bytes 2359304 | tf_op jit(solution)/shard_map/ppermute | solution.py:872
  143.0 16.1 %collective-permute-start.35 = (bf16[4,96,768]{2,1,0:T(8,128)(2,1)}, bf16[4,96,768]{2,1,0:T(8,128)(2,1)}, u32[]{:S(2)}, u32[]{:S(2)}) collective-permute-start(bf16[4,96,768]{2,1,0:T(8,128)(2,1)} %get-tuple-element.213.refs_2_), channel_id=1, source_target_pairs={{0,4},{4,0},{8,12},{12,8},{16,20},{20,16},{24,28},{28,24},{1,5},{5... | collective-permute-start | bytes 1769480 | tf_op jit(solution)/shard_map/ppermute | solution.py:872
  145.5 10.4 %collective-permute-start.36 = (bf16[96,768]{1,0:T(8,128)(2,1)}, bf16[96,768]{1,0:T(8,128)(2,1)}, u32[]{:S(2)}, u32[]{:S(2)}) collective-permute-start(bf16[96,768]{1,0:T(8,128)(2,1)} %close.3.refs_2_.refs_0_), channel_id=1, source_target_pairs={{0,16},{4,20},{8,24},{12,28},{16,0},{20,4},{24,8},{28,12},{1,17},{... | collective-permute-start | bytes 442376 | tf_op jit(solution)/shard_map/ppermute | solution.py:872
  149.4 12.3 %collective-permute-start.34 = (bf16[256,768]{1,0:T(8,128)(2,1)S(1)}, bf16[256,768]{1,0:T(8,128)(2,1)}, u32[]{:S(2)}, u32[]{:S(2)}) collective-permute-start(bf16[256,768]{1,0:T(8,128)(2,1)S(1)} %far_sum.6.refs_2_), channel_id=1, source_target_pairs={{0,2},{1,3},{2,0},{3,1},{4,6},{5,7},{6,4},{7,5},{8,10},{9,11},{10,... | collective-permute-start | bytes 1179656 | tf_op jit(solution)/shard_map/ppermute | solution.py:872
  152.7 11.4 %collective-permute-start.38 = (bf16[96,768]{1,0:T(8,128)(2,1)}, bf16[96,768]{1,0:T(8,128)(2,1)S(1)}, u32[]{:S(2)}, u32[]{:S(2)}) collective-permute-start(bf16[96,768]{1,0:T(8,128)(2,1)} %copy-done.28), channel_id=1, source_target_pairs={{0,16},{4,20},{8,24},{12,28},{16,0},{20,4},{24,8},{28,12},{1,17},{... | collective-permute-start | bytes 442376 | tf_op jit(solution)/shard_map/ppermute | solution.py:872
  157.4 13.7 %collective-permute-start.40 = (bf16[2,96,768]{2,1,0:T(8,128)(2,1)S(1)}, bf16[2,96,768]{2,1,0:T(8,128)(2,1)S(1)}, u32[]{:S(2)}, u32[]{:S(2)}) collective-permute-start(bf16[2,96,768]{2,1,0:T(8,128)(2,1)S(1)} %join.7.refs_2_.refs_0_), channel_id=1, source_target_pairs={{0,8},{4,12},{8,0},{12,4},{16,24},{20,28},{24,16},{28,20},{1,9},{5... | collective-permute-start | bytes 884744 | tf_op jit(solution)/shard_map/ppermute | solution.py:872
  161.0 16.9 %collective-permute-start.43 = (bf16[2,96,768]{2,1,0:T(8,128)(2,1)S(1)}, bf16[2,96,768]{2,1,0:T(8,128)(2,1)S(1)}, u32[]{:S(2)}, u32[]{:S(2)}) collective-permute-start(bf16[2,96,768]{2,1,0:T(8,128)(2,1)S(1)} %get-tuple-element.218.refs_6_), channel_id=1, source_target_pairs={{0,8},{4,12},{8,0},{12,4},{16,24},{20,28},{24,16},{28,20},{1,9},{5... | collective-permute-start | bytes 884744 | tf_op jit(solution)/shard_map/ppermute | solution.py:872
  164.0 4.9 %collective-permute-start.37 = (f32[6,768]{1,0:T(8,128)S(1)}, f32[6,768]{1,0:T(8,128)S(1)}, u32[]{:S(2)}, u32[]{:S(2)}) collective-permute-start(f32[6,768]{1,0:T(8,128)S(1)} %pad_maximum_fusion.2.refs_0_), channel_id=1, source_target_pairs={{0,1},{1,0},{2,3},{3,2},{4,5},{5,4},{6,7},{7,6},{8,9},{9,8},{10,11... | collective-permute-start | bytes 55304 | tf_op jit(solution)/shard_map/ppermute | solution.py:872
  164.7 15.1 %collective-permute-start.42 = (bf16[96,768]{1,0:T(8,128)(2,1)S(1)}, bf16[96,768]{1,0:T(8,128)(2,1)}, u32[]{:S(2)}, u32[]{:S(2)}) collective-permute-start(bf16[96,768]{1,0:T(8,128)(2,1)S(1)} %close.4.refs_2_.refs_0_), channel_id=1, source_target_pairs={{0,16},{4,20},{8,24},{12,28},{16,0},{20,4},{24,8},{28,12},{1,17},{... | collective-permute-start | bytes 442376 | tf_op jit(solution)/shard_map/ppermute | solution.py:872
  169.6 3.9 %collective-permute-start.39 = (f32[6,768]{1,0:T(8,128)S(1)}, f32[6,768]{1,0:T(8,128)S(1)}, u32[]{:S(2)}, u32[]{:S(2)}) collective-permute-start(f32[6,768]{1,0:T(8,128)S(1)} %vec_add.2.refs_2_.refs_0_), channel_id=1, source_target_pairs={{0,2},{1,3},{2,0},{3,1},{4,6},{5,7},{6,4},{7,5},{8,10},{9,11},{10,... | collective-permute-start | bytes 55304 | tf_op jit(solution)/shard_map/ppermute | solution.py:872
  171.7 16.9 %collective-permute-start.46 = (bf16[4,96,768]{2,1,0:T(8,128)(2,1)S(1)}, bf16[4,96,768]{2,1,0:T(8,128)(2,1)S(1)}, u32[]{:S(2)}, u32[]{:S(2)}) collective-permute-start(bf16[4,96,768]{2,1,0:T(8,128)(2,1)S(1)} %join.8.refs_2_.refs_5_), channel_id=1, source_target_pairs={{0,4},{4,0},{8,12},{12,8},{16,20},{20,16},{24,28},{28,24},{1,5},{5... | collective-permute-start | bytes 1769480 | tf_op jit(solution)/shard_map/ppermute | solution.py:872
  172.3 16.3 %collective-permute-start.47 = (bf16[256,768]{1,0:T(8,128)(2,1)S(1)}, bf16[256,768]{1,0:T(8,128)(2,1)S(1)}, u32[]{:S(2)}, u32[]{:S(2)}) collective-permute-start(bf16[256,768]{1,0:T(8,128)(2,1)S(1)} %get-tuple-element.236.refs_2_.refs_0_), channel_id=1, source_target_pairs={{0,2},{1,3},{2,0},{3,1},{4,6},{5,7},{6,4},{7,5},{8,10},{9,11},{10,... | collective-permute-start | bytes 1179656 | tf_op jit(solution)/shard_map/ppermute | solution.py:872
  174.0 23.5 %collective-permute-start.41 = (bf16[256,768]{1,0:T(8,128)(2,1)S(1)}, bf16[256,768]{1,0:T(8,128)(2,1)}, u32[]{:S(2)}, u32[]{:S(2)}) collective-permute-start(bf16[256,768]{1,0:T(8,128)(2,1)S(1)} %far_sum.7.refs_2_), channel_id=1, source_target_pairs={{0,2},{1,3},{2,0},{3,1},{4,6},{5,7},{6,4},{7,5},{8,10},{9,11},{10,... | collective-permute-start | bytes 1179656 | tf_op jit(solution)/shard_map/ppermute | solution.py:872
  179.8 8.8 %collective-permute-start.45 = (bf16[96,768]{1,0:T(8,128)(2,1)}, bf16[96,768]{1,0:T(8,128)(2,1)}, u32[]{:S(2)}, u32[]{:S(2)}) collective-permute-start(bf16[96,768]{1,0:T(8,128)(2,1)} %get-tuple-element.226.refs_2_), channel_id=1, source_target_pairs={{0,16},{4,20},{8,24},{12,28},{16,0},{20,4},{24,8},{28,12},{1,17},{... | collective-permute-start | bytes 442376 | tf_op jit(solution)/shard_map/ppermute | solution.py:872
  181.4 13.2 %collective-permute-start.44 = (bf16[2,96,768]{2,1,0:T(8,128)(2,1)S(1)}, bf16[2,96,768]{2,1,0:T(8,128)(2,1)S(1)}, u32[]{:S(2)}, u32[]{:S(2)}) collective-permute-start(bf16[2,96,768]{2,1,0:T(8,128)(2,1)S(1)} %join.9.refs_3_.refs_0_), channel_id=1, source_target_pairs={{0,8},{4,12},{8,0},{12,4},{16,24},{20,28},{24,16},{28,20},{1,9},{5... | collective-permute-start | bytes 884744 | tf_op jit(solution)/shard_map/ppermute | solution.py:872
  190.1 15.3 %collective-permute-start.50 = (bf16[112,768]{1,0:T(8,128)(2,1)S(1)}, bf16[112,768]{1,0:T(8,128)(2,1)S(1)}, u32[]{:S(2)}, u32[]{:S(2)}) collective-permute-start(bf16[112,768]{1,0:T(8,128)(2,1)S(1)} %close.5.refs_2_.refs_0_), channel_id=1, source_target_pairs={{0,16},{4,20},{8,24},{12,28},{16,0},{20,4},{24,8},{28,12},{1,17},{... | collective-permute-start | bytes 516104 | tf_op jit(solution)/shard_map/ppermute | solution.py:872
  190.2 15.2 %collective-permute-start.51 = (bf16[112,768]{1,0:T(8,128)(2,1)S(1)}, bf16[112,768]{1,0:T(8,128)(2,1)S(1)}, u32[]{:S(2)}, u32[]{:S(2)}) collective-permute-start(bf16[112,768]{1,0:T(8,128)(2,1)S(1)} %close.5.refs_2_.refs_0_), channel_id=1, source_target_pairs={{0,8},{4,12},{8,0},{12,4},{16,24},{20,28},{24,16},{28,20},{1,9},{5... | collective-permute-start | bytes 516104 | tf_op jit(solution)/shard_map/ppermute | solution.py:872
  191.4 14.0 %collective-permute-start.52 = (bf16[112,768]{1,0:T(8,128)(2,1)S(1)}, bf16[112,768]{1,0:T(8,128)(2,1)S(1)}, u32[]{:S(2)}, u32[]{:S(2)}) collective-permute-start(bf16[112,768]{1,0:T(8,128)(2,1)S(1)} %close.5.refs_2_.refs_0_), channel_id=1, source_target_pairs={{0,24},{4,28},{8,16},{12,20},{16,8},{20,12},{24,0},{28,4},{1,25},{... | collective-permute-start | bytes 516104 | tf_op jit(solution)/shard_map/ppermute | solution.py:872
  195.2 16.6 %collective-permute-start.49 = (bf16[4,96,768]{2,1,0:T(8,128)(2,1)S(1)}, bf16[4,96,768]{2,1,0:T(8,128)(2,1)S(1)}, u32[]{:S(2)}, u32[]{:S(2)}) collective-permute-start(bf16[4,96,768]{2,1,0:T(8,128)(2,1)S(1)} %join.10.refs_4_.refs_7_.refs_5_), channel_id=1, source_target_pairs={{0,4},{4,0},{8,12},{12,8},{16,20},{20,16},{24,28},{28,24},{1,5},{5... | collective-permute-start | bytes 1769480 | tf_op jit(solution)/shard_map/ppermute | solution.py:872
  199.5 17.4 %collective-permute-start.48 = (bf16[256,768]{1,0:T(8,128)(2,1)S(1)}, bf16[256,768]{1,0:T(8,128)(2,1)S(1)}, u32[]{:S(2)}, u32[]{:S(2)}) collective-permute-start(bf16[256,768]{1,0:T(8,128)(2,1)S(1)} %block_end.1.refs_0_), channel_id=1, source_target_pairs={{0,2},{1,3},{2,0},{3,1},{4,6},{5,7},{6,4},{7,5},{8,10},{9,11},{10,... | collective-permute-start | bytes 1179656 | tf_op jit(solution)/shard_map/ppermute | solution.py:872
  206.0 18.7 %collective-permute-start.57 = (bf16[4,112,768]{2,1,0:T(8,128)(2,1)S(1)}, bf16[4,112,768]{2,1,0:T(8,128)(2,1)S(1)}, u32[]{:S(2)}, u32[]{:S(2)}) collective-permute-start(bf16[4,112,768]{2,1,0:T(8,128)(2,1)S(1)} %join.11.refs_10_), channel_id=1, source_target_pairs={{0,4},{4,0},{8,12},{12,8},{16,20},{20,16},{24,28},{28,24},{1,5},{5... | collective-permute-start | bytes 2064392 | tf_op jit(solution)/shard_map/ppermute | solution.py:872
  (50 other events, 301.1 us)
